TPU v7x, 32 devices: a whole 2x2x4 slice. The times are simulated.
32 devices in a mesh: groups: 1, expert: 32 (over z, y, x, core).
Axes of the slice: x: 2, y: 2, z: 4, core: 2. Of those that a mesh axis runs over, the one named last changes fastest.
Arguments:
- tokens: bfloat16 [256, 3584], P(('groups', 'expert')), may hold values from -6 to 6
- cotangent: bfloat16 [256, 3584], P(('groups', 'expert')), may hold values from -4 to 4
- route_probs: float32 [256, 8], P(('groups', 'expert')), may hold values from 0.02 to 0.5
- expert_ids: int32 [256, 8], P(('groups', 'expert')), may hold values from 0 to 15, all different within a row; in each aligned block of 8 rows (0 to 7, 8 to 15, ...) at most 6 rows name the same one
- gate_weight: bfloat16 [3584, 16384], P(None, 'expert'), as said below
- up_weight: bfloat16 [3584, 16384], P(None, 'expert'), as said below
- down_weight: bfloat16 [16384, 3584], P('expert'), as said below
- narrow_factors: bfloat16 [3, 16, 16384], P(None, None, 'expert'), may hold values from -1.5 to 1.5
- wide_factors: bfloat16 [3, 16, 57344], P(None, None, 'expert'), may hold values from -1.5 to 1.5
Outputs:
- grad_tokens: bfloat16 [256, 3584], P(('groups', 'expert'))
- grad_probs: float32 [256, 8], P(('groups', 'expert'))
- grad_narrow: float32 [3, 16, 16384], P('groups', None, 'expert')
- grad_wide: float32 [3, 16, 57344], P('groups', None, 'expert')
Inputs may be any that keep to these rules, and one draw needn't show every extreme that they name: `expert_ids`: in each aligned block of 8 rows no expert is named more than 6 times, a bound that some block reaches. `gate_weight`: of every four consecutive rows of a column, two entries are zero. `up_weight`: of every four consecutive rows of a column, two entries are zero. `down_weight`: of every four consecutive rows of a column, two entries are zero.
All inputs are finite; a program needn't handle non-finite values.
Results may differ from a plain program's by a relative error of at most 0.0088.
Values may be sent and summed in bfloat16 or wider, within the bound.
No kernel may reach another device: no remote copies, remote signals or barrier semaphores. Data moves between devices by JAX's collectives and lax.ppermute only.
A program may use at most 128 MiB of HBM per device.

v0:
```python
import jax
import jax.numpy as jnp
from jax import lax
from jax.sharding import PartitionSpec as P


def from_partner(value, axis, bit):
    mask = 2**bit
    pairs = [(source, source ^ mask) for source in range(lax.axis_size(axis))]
    return lax.ppermute(value, axis, pairs)


def join_halves(mine, other, is_lower):
    return jnp.where(
        is_lower, jnp.concatenate([mine, other], axis=-1), jnp.concatenate([other, mine], axis=-1)
    )


def expert_half(slot_inputs, slot_grads, gate_half, up_half, down_half, narrow_rows, wide_rows):
    highest = lax.Precision.HIGHEST
    rows_dims = (((1,), (1,)), ((), ()))
    cols_dims = (((0,), (0,)), ((), ()))
    gate_eff = (
        gate_half.astype(jnp.float32)
        * (1.0 + jnp.einsum("rd,rf->df", wide_rows[0], narrow_rows[0], precision=highest))
    ).astype(jnp.bfloat16)
    up_eff = (
        up_half.astype(jnp.float32)
        * (1.0 + jnp.einsum("rd,rf->df", wide_rows[1], narrow_rows[1], precision=highest))
    ).astype(jnp.bfloat16)
    down_eff = (
        down_half.astype(jnp.float32)
        * (1.0 + jnp.einsum("rf,rd->fd", narrow_rows[2], wide_rows[2], precision=highest))
    ).astype(jnp.bfloat16)
    pre_gate = jnp.dot(slot_inputs, gate_eff, preferred_element_type=jnp.float32)
    pre_up = jnp.dot(slot_inputs, up_eff, preferred_element_type=jnp.float32)
    sigmoid_gate = jax.nn.sigmoid(pre_gate)
    activated = pre_gate * sigmoid_gate
    hidden = (activated * pre_up).astype(jnp.bfloat16)
    part_out = jnp.dot(hidden, down_eff, preferred_element_type=jnp.float32).astype(jnp.bfloat16)
    grad_hidden = lax.dot_general(
        slot_grads, down_eff, rows_dims, preferred_element_type=jnp.float32
    )
    grad_gate = (
        grad_hidden * pre_up * sigmoid_gate * (1.0 + pre_gate * (1.0 - sigmoid_gate))
    ).astype(jnp.bfloat16)
    grad_up = (grad_hidden * activated).astype(jnp.bfloat16)
    part_in = (
        lax.dot_general(grad_gate, gate_eff, rows_dims, preferred_element_type=jnp.float32)
        + lax.dot_general(grad_up, up_eff, rows_dims, preferred_element_type=jnp.float32)
    ).astype(jnp.bfloat16)
    masked_gate = lax.dot_general(
        slot_inputs, grad_gate, cols_dims, preferred_element_type=jnp.float32
    ) * gate_half.astype(jnp.float32)
    masked_up = lax.dot_general(
        slot_inputs, grad_up, cols_dims, preferred_element_type=jnp.float32
    ) * up_half.astype(jnp.float32)
    masked_down = lax.dot_general(
        hidden, slot_grads, cols_dims, preferred_element_type=jnp.float32
    ) * down_half.astype(jnp.float32)
    narrow_grad = jnp.stack(
        [
            jnp.einsum("rd,df->rf", wide_rows[0], masked_gate, precision=highest),
            jnp.einsum("rd,df->rf", wide_rows[1], masked_up, precision=highest),
            jnp.einsum("rd,fd->rf", wide_rows[2], masked_down, precision=highest),
        ]
    )
    wide_grad = jnp.stack(
        [
            jnp.einsum("rf,df->rd", narrow_rows[0], masked_gate, precision=highest),
            jnp.einsum("rf,df->rd", narrow_rows[1], masked_up, precision=highest),
            jnp.einsum("rf,fd->rd", narrow_rows[2], masked_down, precision=highest),
        ]
    )
    return (part_out, part_in, narrow_grad, wide_grad)


def body(
    tokens,
    cotangent,
    route_probs,
    expert_ids,
    gate_weight,
    up_weight,
    down_weight,
    narrow_factors,
    wide_factors,
):
    tok_rows, model_width = tokens.shape
    top_count = expert_ids.shape[1]
    devices = lax.axis_size("expert")
    experts = devices // 2
    capacity = min(tok_rows, max(2, (3 * tok_rows * top_count + 2 * experts - 1) // (2 * experts)))
    half_width = model_width // 2
    is_lower = lax.axis_index("expert") % 2 == 0
    assigned = tok_rows * top_count
    slot_count = devices * capacity
    partner_factors = from_partner(wide_factors, "expert", 0)
    wide_rows = join_halves(wide_factors, partner_factors, is_lower).astype(jnp.float32)
    narrow_rows = narrow_factors.astype(jnp.float32)
    flat_ids = expert_ids.reshape(assigned)
    chosen = (flat_ids[:, None] == jnp.arange(experts, dtype=jnp.int32)[None, :]).astype(jnp.int32)
    before = jnp.cumsum(chosen, axis=0) - chosen
    slot_index = jnp.sum(before * chosen, axis=1)
    target = flat_ids * capacity + slot_index
    placing = (jnp.arange(experts * capacity, dtype=jnp.int32)[:, None] == target[None, :]).astype(
        jnp.bfloat16
    )
    placing_tok = jnp.sum(placing.reshape(experts * capacity, tok_rows, top_count), axis=2)
    send_inputs = jnp.dot(placing_tok, tokens, preferred_element_type=jnp.float32).astype(
        jnp.bfloat16
    )
    scaled = (route_probs[:, :, None] * cotangent[:, None, :].astype(jnp.float32)).astype(
        jnp.bfloat16
    )
    send_grads = jnp.dot(
        placing, scaled.reshape(assigned, model_width), preferred_element_type=jnp.float32
    ).astype(jnp.bfloat16)

    def copy_twice(block):
        shaped = block.reshape(experts, 1, capacity, model_width)
        return jnp.broadcast_to(shaped, (experts, 2, capacity, model_width)).reshape(
            devices, capacity, model_width
        )

    slot_inputs, slot_grads = (
        lax.all_to_all(copy_twice(send_inputs), "expert", split_axis=0, concat_axis=0, tiled=True),
        lax.all_to_all(copy_twice(send_grads), "expert", split_axis=0, concat_axis=0, tiled=True),
    )
    slot_inputs = slot_inputs.reshape(slot_count, model_width)
    slot_grads = slot_grads.reshape(slot_count, model_width)
    part_out, part_in, grad_narrow, wide_part = expert_half(
        slot_inputs, slot_grads, gate_weight, up_weight, down_weight, narrow_rows, wide_rows
    )
    keep_part = jnp.where(is_lower, wide_part[:, :, :half_width], wide_part[:, :, half_width:])
    give_part = jnp.where(is_lower, wide_part[:, :, half_width:], wide_part[:, :, :half_width])
    grad_wide = keep_part + from_partner(give_part.astype(jnp.bfloat16), "expert", 0).astype(
        give_part.dtype
    )
    back_out, back_in = (
        lax.all_to_all(
            part_out.reshape(devices, capacity, model_width),
            "expert",
            split_axis=0,
            concat_axis=0,
            tiled=True,
        ),
        lax.all_to_all(
            part_in.reshape(devices, capacity, model_width),
            "expert",
            split_axis=0,
            concat_axis=0,
            tiled=True,
        ),
    )

    def add_pairs(block):
        shaped = block.reshape(experts, 2, capacity, model_width).astype(jnp.float32)
        return (
            (shaped[:, 0] + shaped[:, 1])
            .astype(jnp.bfloat16)
            .reshape(experts * capacity, model_width)
        )

    expert_out = add_pairs(back_out)
    slot_in = add_pairs(back_in)
    picked_out = lax.dot_general(
        placing, expert_out, (((0,), (0,)), ((), ())), preferred_element_type=jnp.float32
    )
    picked_out = picked_out.reshape(tok_rows, top_count, model_width)
    grad_probs = jnp.einsum("td,tkd->tk", cotangent.astype(jnp.float32), picked_out)
    grad_tokens = lax.dot_general(
        placing_tok, slot_in, (((0,), (0,)), ((), ())), preferred_element_type=jnp.float32
    ).astype(jnp.bfloat16)
    return (grad_tokens, grad_probs, grad_narrow, grad_wide)


def solution(mesh):
    in_specs = (
        P(("groups", "expert"), None),
        P(("groups", "expert"), None),
        P(("groups", "expert"), None),
        P(("groups", "expert"), None),
        P(None, "expert"),
        P(None, "expert"),
        P("expert", None),
        P(None, None, "expert"),
        P(None, None, "expert"),
    )
    out_specs = (
        P(("groups", "expert"), None),
        P(("groups", "expert"), None),
        P("groups", None, "expert"),
        P("groups", None, "expert"),
    )
    return jax.shard_map(body, mesh=mesh, in_specs=in_specs, out_specs=out_specs, check_vma=False)
```

profile of v0, /device:TPU:0, one launch (start us, length us, event | category | flops | bytes accessed | tf_op | source)
XLA Modules:
  0.0 222.6 jit_solution(16364679246706791390)
XLA Ops:
  0.6 0.8 eq.56
  1.4 0.1 fusion.17
  1.5 0.1 reduce_window_sum.11
  1.6 0.2 select_reduce_fusion
  1.8 0.1 reduce_sum.24
  1.9 0.7 multiply_add_fusion
  2.6 0.1 fusion.23
  2.7 0.4 convolution_convert_fusion.1
  3.1 0.2 broadcast_in_dim.10
  3.3 1.4 broadcast_in_dim.22
  4.7 7.3 %all-to-all-start.1 = ((bf16[32,6,3584]{2,1,0:T(8,128)(2,1)}), bf16[32,6,3584]{2,1,0:T(8,128)(2,1)S(1)}, u32[]{:S(2)}, u32[]{:S(2)}) async-start(bf16[32,6,3584]{2,1,0:T(8,128)(2,1)} %bitcast.121), calls=%async_computation.1 | async-start | bytes 3670016 | tf_op jit(solution)/shard_map/all_to_all | solution.py:127
  12.0 0.1 mul.80
  12.1 1.3 convolution_convert_fusion.2
  13.4 1.4 broadcast_in_dim.8
  14.8 40.5 %all-to-all-done.1 = bf16[32,6,3584]{2,1,0:T(8,128)(2,1)S(1)} async-done(((bf16[32,6,3584]{2,1,0:T(8,128)(2,1)}), bf16[32,6,3584]{2,1,0:T(8,128)(2,1)S(1)}, u32[]{:S(2)}, u32[]{:S(2)}) %all-to-all-start.1) | async-done | bytes 1376288 | tf_op jit(solution)/shard_map/all_to_all | solution.py:127
  55.2 1.4 broadcast_in_dim.9
  56.6 4.1 %all-to-all-start = ((bf16[32,6,3584]{2,1,0:T(8,128)(2,1)}), bf16[32,6,3584]{2,1,0:T(8,128)(2,1)}, u32[]{:S(2)}, u32[]{:S(2)}) async-start(bf16[32,6,3584]{2,1,0:T(8,128)(2,1)} %bitcast.120), calls=%async_computation | async-start | bytes 3670016 | tf_op jit(solution)/shard_map/all_to_all | solution.py:128
  60.8 0.3 collective-permute-start
  61.0 6.0 %copy.21 = bf16[512,3584]{0,1:T(8,128)(2,1)} copy(bf16[512,3584]{1,0:T(8,128)(2,1)} %param.15) | data formatting | bytes 7340032 | tf_op args[6]
  67.0 0.1 maximum_select_fusion
  67.1 5.1 %fusion.2 = bf16[3584,512]{1,0:T(8,128)(2,1)} fusion(bf16[3584,512]{1,0:T(8,128)(2,1)} %param.13, bf16[3,16,3584]{2,1,0:T(8,128)(2,1)S(1)} %maximum_select_fusion, bf16[3,16,512]{2,1,0:T(8,128)(2,1)S(1)} %copy-done.15), kind=kOutput, calls=%fused_computation.8 | convolution fusion | flops 66060288 | bytes 7471104 | tf_op jit(solution)/shard_map/rd,rf->df/dot_general | solution.py:25
  72.3 3.0 %fusion.1 = bf16[3584,512]{1,0:T(8,128)(2,1)} fusion(bf16[3584,512]{1,0:T(8,128)(2,1)S(1)} %copy-done.7, bf16[3,16,3584]{2,1,0:T(8,128)(2,1)S(1)} %maximum_select_fusion, bf16[3,16,512]{2,1,0:T(8,128)(2,1)S(1)} %copy-done.15), kind=kOutput, calls=%fused_computation.7 | convolution fusion | flops 66060288 | bytes 7471104 | tf_op jit(solution)/shard_map/rd,rf->df/dot_general | solution.py:29
  75.2 3.0 %fusion = bf16[512,3584]{0,1:T(8,128)(2,1)} fusion(bf16[512,3584]{0,1:T(8,128)(2,1)S(1)} %copy-done.3, bf16[3,16,3584]{2,1,0:T(8,128)(2,1)S(1)} %maximum_select_fusion, bf16[3,16,512]{2,1,0:T(8,128)(2,1)S(1)} %copy-done.15), kind=kOutput, calls=%fused_computation.6 | convolution fusion | flops 66060288 | bytes 7471104 | tf_op jit(solution)/shard_map/rf,rd->fd/dot_general | solution.py:33
  78.2 0.5 reshape.101
  78.7 3.7 %fusion.39 = f32[192,512]{1,0:T(8,128)} fusion(bf16[192,3584]{1,0:T(8,128)(2,1)S(1)} %reshape.101, bf16[3584,512]{1,0:T(8,128)(2,1)} %fusion.2), kind=kOutput, calls=%fused_computation.75 | convolution fusion | flops 704643072 | bytes 5439488 | tf_op jit(solution)/shard_map/dot_general | solution.py:35
  82.4 21.6 %all-to-all-done = bf16[32,6,3584]{2,1,0:T(8,128)(2,1)} async-done(((bf16[32,6,3584]{2,1,0:T(8,128)(2,1)}), bf16[32,6,3584]{2,1,0:T(8,128)(2,1)}, u32[]{:S(2)}, u32[]{:S(2)}) %all-to-all-start) | async-done | bytes 1376288 | tf_op jit(solution)/shard_map/all_to_all | solution.py:128
  104.0 2.4 %reshape.99 = bf16[192,3584]{1,0:T(8,128)(2,1)S(1)} reshape(bf16[32,6,3584]{2,1,0:T(8,128)(2,1)} %all-to-all-done) | data formatting | bytes 2752512 | tf_op jit(solution)/shard_map/reshape | solution.py:131
  106.4 3.1 %fusion.38 = f32[192,512]{1,0:T(8,128)S(1)} fusion(bf16[192,3584]{1,0:T(8,128)(2,1)S(1)} %reshape.99, bf16[512,3584]{0,1:T(8,128)(2,1)} %fusion), kind=kOutput, calls=%fused_computation.74 | convolution fusion | flops 704643072 | bytes 5439488 | tf_op jit(solution)/shard_map/dot_general | solution.py:41
  109.5 0.1 copy-done.14
  109.6 1.0 multiply_convert_fusion
  110.6 1.1 copy-done.5
  111.7 1.3 fusion.40
  113.0 0.7 copy-done.6
  113.7 4.2 %convert_multiply_fusion = f32[3584,512]{1,0:T(8,128)} fusion(bf16[3584,512]{1,0:T(8,128)(2,1)S(1)} %copy-done.6, bf16[192,3584]{1,0:T(8,128)(2,1)S(1)} %reshape.101, bf16[192,512]{1,0:T(8,128)(2,1)S(1)} %get-tuple-element.5), kind=kOutput, calls=%fused_computation | convolution fusion | flops 708313088 | bytes 12582912 | tf_op jit(solution)/shard_map/dot_general | solution.py:52
  117.9 2.5 %fusion.3 = bf16[192,3584]{1,0:T(8,128)(2,1)} fusion(f32[192,3584]{1,0:T(8,128)S(1)} %fusion.40, bf16[192,512]{1,0:T(8,128)(2,1)S(1)} %get-tuple-element.6, bf16[3584,512]{1,0:T(8,128)(2,1)S(1)} %copy-done.9), kind=kOutput, calls=%fused_computation.10 | convolution fusion | flops 706019328 | bytes 7995392 | tf_op jit(solution)/shard_map/dot_general | solution.py:50
  120.3 3.4 %reshape.102 = bf16[32,6,3584]{2,1,0:T(8,128)(2,1)} reshape(bf16[192,3584]{1,0:T(8,128)(2,1)} %fusion.3) | data formatting | bytes 2752512 | tf_op jit(solution)/shard_map/reshape | solution.py:149
  123.7 4.3 %all-to-all-start.2 = ((bf16[32,6,3584]{2,1,0:T(8,128)(2,1)}), bf16[32,6,3584]{2,1,0:T(8,128)(2,1)}, u32[]{:S(2)}, u32[]{:S(2)}) async-start(bf16[32,6,3584]{2,1,0:T(8,128)(2,1)} %reshape.102), calls=%async_computation.2 | async-start | bytes 3670016 | tf_op jit(solution)/shard_map/all_to_all | solution.py:148
  128.1 6.4 %convert_multiply_fusion.4 = f32[512,3584]{0,1:T(8,128)} fusion(bf16[512,3584]{0,1:T(8,128)(2,1)} %copy.21, bf16[192,512]{1,0:T(8,128)(2,1)S(1)} %get-tuple-element.4, bf16[192,3584]{1,0:T(8,128)(2,1)S(1)} %reshape.99), kind=kOutput, calls=%fused_computation.4 | convolution fusion | flops 708313088 | bytes 12582912 | tf_op jit(solution)/shard_map/dot_general | solution.py:58
  134.5 1.4 convolution_convert_fusion
  135.9 1.5 reshape.103
  137.4 6.4 %convolution_bitcast_fusion = f32[1,16,3584]{2,1,0:T(8,128)S(1)} fusion(f32[512,3584]{0,1:T(8,128)} %convert_multiply_fusion.4, bf16[3,16,512]{2,1,0:T(8,128)(2,1)S(1)} %copy-done.15), kind=kOutput, calls=%fused_computation.14 | convolution fusion | flops 352321536 | bytes 7585792 | tf_op jit(solution)/shard_map/rf,fd->rd/dot_general | solution.py:72
  143.9 6.6 %convolution_bitcast_fusion.2 = f32[1,16,3584]{2,1,0:T(8,128)S(1)} fusion(f32[3584,512]{1,0:T(8,128)} %convert_multiply_fusion, bf16[3,16,512]{2,1,0:T(8,128)(2,1)S(1)} %copy-done.15), kind=kOutput, calls=%fused_computation.16 | convolution fusion | flops 352321536 | bytes 7585792 | tf_op jit(solution)/shard_map/rf,df->rd/dot_general | solution.py:70
  150.5 1.2 convert_multiply_fusion.2
  151.7 3.4 %convolution_bitcast_fusion.1 = f32[1,16,3584]{2,1,0:T(8,128)S(1)} fusion(f32[3584,512]{1,0:T(8,128)S(1)} %convert_multiply_fusion.2, bf16[3,16,512]{2,1,0:T(8,128)(2,1)S(1)} %copy-done.15), kind=kOutput, calls=%fused_computation.15 | convolution fusion | flops 352321536 | bytes 7585792 | tf_op jit(solution)/shard_map/rf,df->rd/dot_general | solution.py:71
  155.2 0.8 copy-done.10
  156.0 0.7 select_convert_fusion
  156.7 14.5 %all-to-all-done.2 = bf16[32,6,3584]{2,1,0:T(8,128)(2,1)} async-done(((bf16[32,6,3584]{2,1,0:T(8,128)(2,1)}), bf16[32,6,3584]{2,1,0:T(8,128)(2,1)}, u32[]{:S(2)}, u32[]{:S(2)}) %all-to-all-start.2) | async-done | bytes 1376288 | tf_op jit(solution)/shard_map/all_to_all | solution.py:148
  171.2 4.3 %all-to-all-start.3 = ((bf16[32,6,3584]{2,1,0:T(8,128)(2,1)}), bf16[32,6,3584]{2,1,0:T(8,128)(2,1)}, u32[]{:S(2)}, u32[]{:S(2)}) async-start(bf16[32,6,3584]{2,1,0:T(8,128)(2,1)} %reshape.103), calls=%async_computation.3 | async-start | bytes 3670016 | tf_op jit(solution)/shard_map/all_to_all | solution.py:141
  175.5 5.7 %convolution_bitcast_fusion.3 = f32[1,16,512]{2,1,0:T(8,128)S(1)} fusion(f32[512,3584]{0,1:T(8,128)} %convert_multiply_fusion.4, bf16[3,16,3584]{2,1,0:T(8,128)(2,1)S(1)} %copy-done.13), kind=kOutput, calls=%fused_computation.28 | convolution fusion | flops 352321536 | bytes 7487488 | tf_op jit(solution)/shard_map/rd,fd->rf/dot_general | solution.py:65
  181.1 0.1 collective-permute-start.1
  181.2 5.5 %convolution_bitcast_fusion.5 = f32[1,16,512]{2,1,0:T(8,128)S(1)} fusion(f32[3584,512]{1,0:T(8,128)} %convert_multiply_fusion, bf16[3,16,3584]{2,1,0:T(8,128)(2,1)S(1)} %copy-done.13), kind=kOutput, calls=%fused_computation.30 | convolution fusion | flops 352321536 | bytes 7487488 | tf_op jit(solution)/shard_map/rd,df->rf/dot_general | solution.py:63
  186.8 2.5 %convolution_bitcast_fusion.4 = f32[1,16,512]{2,1,0:T(8,128)S(1)} fusion(f32[3584,512]{1,0:T(8,128)S(1)} %bitcast.119, bf16[3,16,3584]{2,1,0:T(8,128)(2,1)S(1)} %copy-done.13), kind=kOutput, calls=%fused_computation.29 | convolution fusion | flops 352321536 | bytes 7487488 | tf_op jit(solution)/shard_map/rd,df->rf/dot_general | solution.py:64
  189.3 0.7 pad_maximum_fusion.1
  190.0 0.8 convert_add_fusion
  190.8 1.9 convert.3
  192.7 0.2 fusion.7
  192.9 0.2 convert_element_type.115
  193.1 0.8 convolution_convert_fusion.3
  194.0 24.6 %all-to-all-done.3 = bf16[32,6,3584]{2,1,0:T(8,128)(2,1)} async-done(((bf16[32,6,3584]{2,1,0:T(8,128)(2,1)}), bf16[32,6,3584]{2,1,0:T(8,128)(2,1)}, u32[]{:S(2)}, u32[]{:S(2)}) %all-to-all-start.3) | async-done | bytes 1376288 | tf_op jit(solution)/shard_map/all_to_all | solution.py:141
  218.6 1.9 convert.4
  220.5 0.2 fusion.5
  220.7 0.2 reshape.106
  221.0 0.4 copy-done.19
  221.3 1.3 fusion.8
  (47 shorter events, 0.2 us)
Async XLA Ops:
  0.6 2.0 copy-start
  3.1 9.0 %copy-start.20 = (f32[8,8]{1,0:T(8,128)S(1)}, f32[8,8]{1,0:T(8,128)}, u32[]{:S(2)}) copy-start(f32[8,8]{1,0:T(8,128)} %param.11) | copy-start | bytes 772
  3.1 9.0 %copy-start.18 = (bf16[8,3584]{1,0:T(8,128)(2,1)S(1)}, bf16[8,3584]{1,0:T(8,128)(2,1)}, u32[]{:S(2)}) copy-start(bf16[8,3584]{1,0:T(8,128)(2,1)} %param.10) | copy-start | bytes 172036
  4.7 50.5 %all-to-all-start.1 = ((bf16[32,6,3584]{2,1,0:T(8,128)(2,1)}), bf16[32,6,3584]{2,1,0:T(8,128)(2,1)S(1)}, u32[]{:S(2)}, u32[]{:S(2)}) async-start(bf16[32,6,3584]{2,1,0:T(8,128)(2,1)} %bitcast.121), calls=%async_computation.1 | async-start | bytes 3670016 | tf_op jit(solution)/shard_map/all_to_all | solution.py:127
  13.4 47.4 %copy-start.17 = (bf16[3,16,1792]{2,1,0:T(8,128)(2,1)S(1)}, bf16[3,16,1792]{2,1,0:T(8,128)(2,1)}, u32[]{:S(2)}) copy-start(bf16[3,16,1792]{2,1,0:T(8,128)(2,1)} %param.17) | copy-start | bytes 516100
  56.6 47.4 %all-to-all-start = ((bf16[32,6,3584]{2,1,0:T(8,128)(2,1)}), bf16[32,6,3584]{2,1,0:T(8,128)(2,1)}, u32[]{:S(2)}, u32[]{:S(2)}) async-start(bf16[32,6,3584]{2,1,0:T(8,128)(2,1)} %bitcast.120), calls=%async_computation | async-start | bytes 3670016 | tf_op jit(solution)/shard_map/all_to_all | solution.py:128
  60.8 6.2 %collective-permute-start = (bf16[3,16,1792]{2,1,0:T(8,128)(2,1)S(1)}, bf16[3,16,1792]{2,1,0:T(8,128)(2,1)S(1)}, u32[]{:S(2)}, u32[]{:S(2)}) collective-permute-start(bf16[3,16,1792]{2,1,0:T(8,128)(2,1)S(1)} %copy-done.17), channel_id=1, source_target_pairs={{0,1},{1,0},{2,3},{3,2},{4,5},{5,4},{6,7},{7,6},{8,9},{9,8},{10,11... | collective-permute-start | bytes 516104 | tf_op jit(solution)/shard_map/ppermute | solution.py:10
  61.0 6.1 %copy-start.15 = (bf16[3,16,512]{2,1,0:T(8,128)(2,1)S(1)}, bf16[3,16,512]{2,1,0:T(8,128)(2,1)}, u32[]{:S(2)}) copy-start(bf16[3,16,512]{2,1,0:T(8,128)(2,1)} %param.16) | copy-start | bytes 147460
  67.1 8.1 %copy-start.12 = (bf16[3,16,3584]{2,1,0:T(8,128)(2,1)}, bf16[3,16,3584]{2,1,0:T(8,128)(2,1)S(1)}, u32[]{:S(2)}) copy-start(bf16[3,16,3584]{2,1,0:T(8,128)(2,1)S(1)} %maximum_select_fusion) | copy-start | bytes 1032196
  67.1 5.1 %copy-start.7 = (bf16[3584,512]{1,0:T(8,128)(2,1)S(1)}, bf16[3584,512]{1,0:T(8,128)(2,1)}, u32[]{:S(2)}) copy-start(bf16[3584,512]{1,0:T(8,128)(2,1)} %param.14) | copy-start | bytes 11010052
  72.3 3.0 %copy-start.3 = (bf16[512,3584]{0,1:T(8,128)(2,1)S(1)}, bf16[512,3584]{0,1:T(8,128)(2,1)}, u32[]{:S(2)}) copy-start(bf16[512,3584]{0,1:T(8,128)(2,1)} %copy.21) | copy-start | bytes 11010052
  106.4 3.1 %copy-start.9 = (bf16[3584,512]{1,0:T(8,128)(2,1)S(1)}, bf16[3584,512]{1,0:T(8,128)(2,1)}, u32[]{:S(2)}) copy-start(bf16[3584,512]{1,0:T(8,128)(2,1)} %fusion.1) | copy-start | bytes 11010052
  106.4 3.2 %copy-start.14 = (f32[192,512]{1,0:T(8,128)S(1)}, f32[192,512]{1,0:T(8,128)}, u32[]{:S(2)}) copy-start(f32[192,512]{1,0:T(8,128)} %fusion.39) | copy-start | bytes 1179652
  109.6 2.0 copy-start.5
  111.6 2.0 copy-start.6
  123.7 47.5 %all-to-all-start.2 = ((bf16[32,6,3584]{2,1,0:T(8,128)(2,1)}), bf16[32,6,3584]{2,1,0:T(8,128)(2,1)}, u32[]{:S(2)}, u32[]{:S(2)}) async-start(bf16[32,6,3584]{2,1,0:T(8,128)(2,1)} %reshape.102), calls=%async_computation.2 | async-start | bytes 3670016 | tf_op jit(solution)/shard_map/all_to_all | solution.py:148
  128.0 6.5 %copy-start.4 = (bf16[512,3584]{0,1:T(8,128)(2,1)S(1)}, bf16[512,3584]{0,1:T(8,128)(2,1)}, u32[]{:S(2)}) copy-start(bf16[512,3584]{0,1:T(8,128)(2,1)} %fusion) | copy-start | bytes 11010052
  143.9 6.6 %copy-start.8 = (bf16[3584,512]{1,0:T(8,128)(2,1)S(1)}, bf16[3584,512]{1,0:T(8,128)(2,1)}, u32[]{:S(2)}) copy-start(bf16[3584,512]{1,0:T(8,128)(2,1)} %param.14) | copy-start | bytes 11010052
  151.7 3.4 %copy-start.2 = (f32[3584,512]{1,0:T(8,128)}, f32[3584,512]{1,0:T(8,128)S(1)}, u32[]{:S(2)}) copy-start(f32[3584,512]{1,0:T(8,128)S(1)} %convert_multiply_fusion.2) | copy-start | bytes 22020100
  155.1 20.3 %copy-start.13 = (bf16[3,16,3584]{2,1,0:T(8,128)(2,1)S(1)}, bf16[3,16,3584]{2,1,0:T(8,128)(2,1)}, u32[]{:S(2)}) copy-start(bf16[3,16,3584]{2,1,0:T(8,128)(2,1)} %copy-done.12) | copy-start | bytes 1032196
  155.2 0.8 copy-start.10
  171.2 15.6 %slice-start = ((s8[7340032]{0:T(1024)(128)(4,1)}), s8[3145728]{0:T(1024)(128)(4,1)S(1)}, s32[]{:S(2)}) async-start(s8[7340032]{0:T(1024)(128)(4,1)} %bitcast.118), calls=%async_computation.4 | async-start | bytes 6291456
  171.2 47.4 %all-to-all-start.3 = ((bf16[32,6,3584]{2,1,0:T(8,128)(2,1)}), bf16[32,6,3584]{2,1,0:T(8,128)(2,1)}, u32[]{:S(2)}, u32[]{:S(2)}) async-start(bf16[32,6,3584]{2,1,0:T(8,128)(2,1)} %reshape.103), calls=%async_computation.3 | async-start | bytes 3670016 | tf_op jit(solution)/shard_map/all_to_all | solution.py:141
  175.4 5.7 %copy-start.16 = (bf16[3,16,1792]{2,1,0:T(8,128)(2,1)S(1)}, bf16[3,16,1792]{2,1,0:T(8,128)(2,1)}, u32[]{:S(2)}) copy-start(bf16[3,16,1792]{2,1,0:T(8,128)(2,1)} %select_convert_fusion) | copy-start | bytes 516100
  175.5 11.3 %slice-start.1 = ((s8[7340032]{0:T(1024)(128)(4,1)}), s8[4194304]{0:T(1024)(128)(4,1)S(1)}, s32[]{:S(2)}) async-start(s8[7340032]{0:T(1024)(128)(4,1)} %bitcast.118), calls=%async_computation.5 | async-start | bytes 8388608
  181.1 8.8 %collective-permute-start.1 = (bf16[3,16,1792]{2,1,0:T(8,128)(2,1)S(1)}, bf16[3,16,1792]{2,1,0:T(8,128)(2,1)S(1)}, u32[]{:S(2)}, u32[]{:S(2)}) collective-permute-start(bf16[3,16,1792]{2,1,0:T(8,128)(2,1)S(1)} %copy-done.16), channel_id=1, source_target_pairs={{0,1},{1,0},{2,3},{3,2},{4,5},{5,4},{6,7},{7,6},{8,9},{9,8},{10,11... | collective-permute-start | bytes 516104 | tf_op jit(solution)/shard_map/ppermute | solution.py:10
  186.8 3.2 %copy-start.11 = (f32[3,16,3584]{2,1,0:T(8,128)S(1)}, f32[3,16,3584]{2,1,0:T(8,128)}, u32[]{:S(2)}) copy-start(f32[3,16,3584]{2,1,0:T(8,128)} %copy-done.10) | copy-start | bytes 2064388
  218.6 4.0 %copy-start.1 = (bf16[8,3584]{1,0:T(8,128)(2,1)S(1)}, bf16[8,3584]{1,0:T(8,128)(2,1)}, u32[]{:S(2)}) copy-start(bf16[8,3584]{1,0:T(8,128)(2,1)} %param.9) | copy-start | bytes 172036
  220.5 0.8 copy-start.19
where the time goes:
time: 224 us; the launch traced here: 223 us
  waiting for transfers between devices  101 us (45%)
  matrix products  69.7 us (31%)
  local copies, waits for them, and re-layouts  22.7 us (10%)
  starting transfers between devices  20.4 us (9%)
  other arithmetic  7.74 us (3%)
    all_to_all x1, waiting for transfers between devices, body(): lax.all_to_all(copy_twice(send_inputs), 'expert', split_axis=0, concat_ax...  40.5 us
    all_to_all x1, waiting for transfers between devices, body(): lax.all_to_all(part_out.reshape(devices, capacity, model_width), 'expert'...  24.6 us
    all_to_all x1, waiting for transfers between devices, body(): lax.all_to_all(copy_twice(send_grads), 'expert', split_axis=0, concat_axi...  21.6 us
    all_to_all x1, waiting for transfers between devices, body(): lax.all_to_all(part_in.reshape(devices, capacity, model_width), 'expert',...  14.5 us
    unnamed x47, local copies, waits for them, and re-layouts  9.12 us
    all_to_all x1, starting transfers between devices, body(): lax.all_to_all(copy_twice(send_inputs), 'expert', split_axis=0, concat_ax...  7.3 us
    dot_general x1, matrix products, expert_half(): jnp.einsum('rf,df->rd', narrow_rows[0], masked_gate, precision=highest)  6.61 us
    dot_general x1, matrix products, expert_half(): jnp.einsum('rf,fd->rd', narrow_rows[2], masked_down, precision=highest)  6.45 us
  transfers between devices with their start and end apart: 6, of which 4 were waited for; matrix products, arithmetic and copies ran while one was open for 31% of the time, Pallas kernels for 0%

commit v1 on v0

v1 whole, which is shorter than its diff:
```python
import jax
import jax.numpy as jnp
from jax import lax
from jax.sharding import PartitionSpec as P

ROWS = (((1,), (1,)), ((), ()))
COLS = (((0,), (0,)), ((), ()))


def send(value, mask):
    pairs = [(source, source ^ mask) for source in range(lax.axis_size("expert"))]
    return lax.ppermute(value, "expert", pairs)


def stages():
    found, bit, top = [], 1, lax.axis_size("expert").bit_length() - 1
    while bit < top:
        if bit + 1 < top:
            found.append((2**bit, 2 ** (bit + 1), 3 * 2**bit))
        else:
            found.append((2**bit,))
        bit += 2
    return found


def gather_rows(block):
    for masks in reversed(stages()):
        block = jnp.concatenate([block] + [send(block, mask) for mask in masks], axis=0)
    return jnp.concatenate([block, send(block, 1)], axis=0)


def scatter_rows(block):
    half = block.shape[0] // 2
    total = block[:half].astype(jnp.float32) + send(block[half:], 1).astype(jnp.float32)
    for masks in stages():
        parts = jnp.split(total.astype(jnp.bfloat16), len(masks) + 1, axis=0)
        total = parts[0].astype(jnp.float32)
        for part, mask in zip(parts[1:], masks):
            total = total + send(part, mask).astype(jnp.float32)
    return total


def two_terms(value):
    high = value.astype(jnp.bfloat16)
    low = (value - high.astype(jnp.float32)).astype(jnp.bfloat16)
    return jnp.concatenate([high, low], axis=-1)


def dot32(left, right, dims=(((1,), (0,)), ((), ()))):
    return lax.dot_general(left, right, dims, preferred_element_type=jnp.float32)


def join_halves(mine, other, is_lower):
    return jnp.where(
        is_lower, jnp.concatenate([mine, other], axis=-1), jnp.concatenate([other, mine], axis=-1)
    )


def scaled_weight(weight, left, right):
    return (weight.astype(jnp.float32) * (1.0 + dot32(left, right, COLS))).astype(jnp.bfloat16)


def body(
    tokens,
    cotangent,
    route_probs,
    expert_ids,
    gate_weight,
    up_weight,
    down_weight,
    narrow_factors,
    wide_factors,
):
    tok_rows, width = tokens.shape
    devices = lax.axis_size("expert")
    experts = devices // 2
    me = lax.axis_index("expert")
    is_lower = me % 2 == 0
    half_width = width // 2
    chosen = expert_ids[:, :, None] == jnp.arange(experts, dtype=jnp.int32)[None, None, :]
    dense_probs = jnp.sum(jnp.where(chosen, route_probs[:, :, None], 0.0), axis=1)
    lanes = -(-2 * experts // 128) * 128
    extra = jnp.pad(two_terms(dense_probs), ((0, 0), (0, lanes - 2 * experts)))
    all_tokens = gather_rows(jnp.concatenate([tokens, extra], axis=1))
    all_cot = gather_rows(cotangent)
    wide = join_halves(wide_factors, send(wide_factors, 1), is_lower)
    narrow = narrow_factors
    gate_eff = scaled_weight(gate_weight, wide[0], narrow[0])
    up_eff = scaled_weight(up_weight, wide[1], narrow[1])
    down_eff = scaled_weight(down_weight, narrow[2], wide[2])
    inputs = all_tokens[:, :width]
    lane = jnp.arange(lanes, dtype=jnp.int32)
    own_lanes = (lane % experts == me // 2) & (lane < 2 * experts)
    probs = jnp.sum(
        jnp.where(own_lanes[None, :], all_tokens[:, width:].astype(jnp.float32), 0.0),
        axis=1,
        keepdims=True,
    )
    routed = probs > 0.0
    pre_gate = dot32(inputs, gate_eff)
    pre_up = dot32(inputs, up_eff)
    sigmoid_gate = jax.nn.sigmoid(pre_gate)
    activated = pre_gate * sigmoid_gate
    hidden = jnp.where(routed, activated * pre_up, 0.0)
    grad_full = dot32(all_cot, down_eff, ROWS)
    grad_hidden = probs * grad_full
    own_probs = jnp.sum(hidden * grad_full, axis=1, keepdims=True)
    hidden_scaled = (hidden * probs).astype(jnp.bfloat16)
    grad_gate = jnp.where(
        routed, grad_hidden * pre_up * sigmoid_gate * (1.0 + pre_gate * (1.0 - sigmoid_gate)), 0.0
    ).astype(jnp.bfloat16)
    grad_up = jnp.where(routed, grad_hidden * activated, 0.0).astype(jnp.bfloat16)
    part_in = (dot32(grad_gate, gate_eff, ROWS) + dot32(grad_up, up_eff, ROWS)).astype(jnp.bfloat16)
    prob_lanes = jnp.where(
        own_lanes[None, :],
        jnp.where(lane[None, :] < experts, own_probs, own_probs - own_probs.astype(jnp.bfloat16).astype(jnp.float32)),
        0.0,
    ).astype(jnp.bfloat16)
    summed = scatter_rows(jnp.concatenate([part_in, prob_lanes], axis=1))
    masked_gate = (dot32(inputs, grad_gate, COLS) * gate_weight.astype(jnp.float32)).astype(jnp.bfloat16)
    masked_up = (dot32(inputs, grad_up, COLS) * up_weight.astype(jnp.float32)).astype(jnp.bfloat16)
    masked_down = (dot32(hidden_scaled, all_cot, COLS) * down_weight.astype(jnp.float32)).astype(jnp.bfloat16)
    grad_narrow = jnp.stack(
        [dot32(wide[0], masked_gate), dot32(wide[1], masked_up), dot32(wide[2], masked_down, ROWS)]
    )
    wide_part = jnp.stack(
        [dot32(narrow[0], masked_gate, ROWS), dot32(narrow[1], masked_up, ROWS), dot32(narrow[2], masked_down)]
    )
    keep_part = jnp.where(is_lower, wide_part[:, :, :half_width], wide_part[:, :, half_width:])
    give_part = jnp.where(is_lower, wide_part[:, :, half_width:], wide_part[:, :, :half_width])
    grad_wide = keep_part + send(give_part.astype(jnp.bfloat16), 1).astype(jnp.float32)
    grad_tokens = summed[:, :width].astype(jnp.bfloat16)
    dense_grads = summed[:, width : width + experts] + summed[:, width + experts : width + 2 * experts]
    grad_probs = jnp.sum(jnp.where(chosen, dense_grads[:, None, :], 0.0), axis=2)
    return (grad_tokens, grad_probs, grad_narrow, grad_wide)


def solution(mesh):
    in_specs = (
        P(("groups", "expert"), None),
        P(("groups", "expert"), None),
        P(("groups", "expert"), None),
        P(("groups", "expert"), None),
        P(None, "expert"),
        P(None, "expert"),
        P("expert", None),
        P(None, None, "expert"),
        P(None, None, "expert"),
    )
    out_specs = (
        P(("groups", "expert"), None),
        P(("groups", "expert"), None),
        P("groups", None, "expert"),
        P("groups", None, "expert"),
    )
    return jax.shard_map(body, mesh=mesh, in_specs=in_specs, out_specs=out_specs, check_vma=False)
```

time: 224 us -> 106 us (0.47)
  waiting for transfers between devices: 101 us -> 28.1 us
  matrix products: 69.7 us -> 24.4 us
  starting transfers between devices: 20.4 us -> 26.1 us
    all_to_all x4 -> x0, waiting for transfers between devices: 101 us -> none  [the longest x1 40.5 us: body(): lax.all_to_all(copy_twice(send_inputs), 'expert', split_axis=0, concat_ax...]
    dot_general x22 -> x16, matrix products: 69.7 us -> 24.4 us  [dot32(): lax.dot_general(left, right, dims, preferred_element_type=jnp.float32)]
    ppermute x2 -> x23, waiting for transfers between devices: 0.01 us -> 28.1 us  [send(): return lax.ppermute(value, 'expert', pairs)]
    ppermute x2 -> x23, starting transfers between devices: 0.32 us -> 26.1 us  [send(): return lax.ppermute(value, 'expert', pairs)]
    all_to_all x4 -> x0, starting transfers between devices: 20 us -> none  [the longest x1 7.3 us: body(): lax.all_to_all(copy_twice(send_inputs), 'expert', split_axis=0, concat_ax...]
    unnamed x47 -> x42, local copies, waits for them, and re-layouts: 9.12 us -> 19 us
    reshape x4 -> x0, local copies, waits for them, and re-layouts: 7.83 us -> none  [the longest x1 3.37 us: body(): part_in.reshape(devices, capacity, model_width)]
    broadcast_in_dim x4 -> x0, local copies, waits for them, and re-layouts: 4.36 us -> none  [copy_twice(): jnp.broadcast_to(shaped, (experts, 2, capacity, model_width))]
  transfers between devices with their start and end apart: 6 -> 23, of which waited for: 4 -> 9; matrix products, arithmetic and copies ran while one was open for 31% -> 21% of each run, Pallas kernels for 0% -> 0%
where the time goes in v1:
time: 106 us
  waiting for transfers between devices  28.1 us (27%)
  starting transfers between devices  26.1 us (25%)
  matrix products  24.4 us (23%)
  local copies, waits for them, and re-layouts  20.8 us (20%)
  other arithmetic  5.55 us (5%)
    ppermute x23, waiting for transfers between devices, send(): return lax.ppermute(value, 'expert', pairs)  28.1 us
    ppermute x23, starting transfers between devices, send(): return lax.ppermute(value, 'expert', pairs)  26.1 us
    dot_general x16, matrix products, dot32(): lax.dot_general(left, right, dims, preferred_element_type=jnp.float32)  24.4 us
    unnamed x42, local copies, waits for them, and re-layouts  19 us
  transfers between devices with their start and end apart: 23, of which 9 were waited for; matrix products, arithmetic and copies ran while one was open for 21% of the time, Pallas kernels for 0%

profile of v1, /device:TPU:0, one launch (start us, length us, event | category | flops | bytes accessed | tf_op | source)
XLA Modules:
  0.0 105.9 jit_solution(7379890832840961236)
XLA Ops:
  0.6 4.1 %collective-permute-start.8 = (bf16[8,3584]{1,0:T(8,128)(2,1)}, bf16[8,3584]{1,0:T(8,128)(2,1)S(1)}, u32[]{:S(2)}, u32[]{:S(2)}) collective-permute-start(bf16[8,3584]{1,0:T(8,128)(2,1)} %param.10), channel_id=1, source_target_pairs={{0,16},{1,17},{2,18},{3,19},{4,20},{5,21},{6,22},{7,23},{8,24},{9,... | collective-permute-start | bytes 172040 | tf_op jit(solution)/shard_map/ppermute | solution.py:12
  4.7 1.6 %collective-permute-start.7 = (bf16[8,3584]{1,0:T(8,128)(2,1)}, bf16[8,3584]{1,0:T(8,128)(2,1)S(1)}, u32[]{:S(2)}, u32[]{:S(2)}) collective-permute-start(bf16[8,3584]{1,0:T(8,128)(2,1)} %param.10), channel_id=1, source_target_pairs={{0,8},{1,9},{2,10},{3,11},{4,12},{5,13},{6,14},{7,15},{8,0},{9,1},... | collective-permute-start | bytes 172040 | tf_op jit(solution)/shard_map/ppermute | solution.py:12
  6.3 0.8 select_reduce_fusion.2
  7.2 1.4 %constant_dynamic-update-slice_fusion.6 = (bf16[128,3712]{1,0:T(8,128)(2,1)}, bf16[256,3712]{1,0:T(8,128)(2,1)S(1)}, bf16[8,3712]{1,0:T(8,128)(2,1)S(1)}) fusion(bf16[8,128]{1,0:T(8,128)(2,1)S(1)} %fusion.33, bf16[8,3584]{1,0:T(8,128)(2,1)} %param.9), kind=kLoop, calls=%fused_computation.60 | loop fusion | flops 118782 | bytes 237568
  8.6 1.9 %collective-permute-start.1 = (bf16[8,3712]{1,0:T(8,128)(2,1)S(1)}, bf16[8,3712]{1,0:T(8,128)(2,1)S(1)}, u32[]{:S(2)}, u32[]{:S(2)}) collective-permute-start(bf16[8,3712]{1,0:T(8,128)(2,1)S(1)} %get-tuple-element.35), channel_id=1, source_target_pairs={{0,16},{1,17},{2,18},{3,19},{4,20},{5,21},{6,22},{7,23},{8,24},{9,... | collective-permute-start | bytes 178184 | tf_op jit(solution)/shard_map/ppermute | solution.py:12
  10.6 2.5 %collective-permute-start = (bf16[8,3712]{1,0:T(8,128)(2,1)S(1)}, bf16[8,3712]{1,0:T(8,128)(2,1)S(1)}, u32[]{:S(2)}, u32[]{:S(2)}) collective-permute-start(bf16[8,3712]{1,0:T(8,128)(2,1)S(1)} %get-tuple-element.35), channel_id=1, source_target_pairs={{0,8},{1,9},{2,10},{3,11},{4,12},{5,13},{6,14},{7,15},{8,0},{9,1},... | collective-permute-start | bytes 178184 | tf_op jit(solution)/shard_map/ppermute | solution.py:12
  13.0 1.5 %constant_dynamic-update-slice_fusion.25 = (bf16[128,3584]{1,0:T(8,128)(2,1)}, bf16[32,3584]{1,0:T(8,128)(2,1)S(1)}, bf16[256,3584]{1,0:T(8,128)(2,1)}) fusion(bf16[8,3584]{1,0:T(8,128)(2,1)} %param.10), kind=kLoop, calls=%fused_computation.79 | loop fusion | bytes 229376
  14.5 6.0 %copy.15 = bf16[512,3584]{0,1:T(8,128)(2,1)} copy(bf16[512,3584]{1,0:T(8,128)(2,1)} %param.15) | data formatting | bytes 7340032 | tf_op args[6]
  20.6 0.6 constant_dynamic-update-slice_fusion.24
  21.3 0.7 constant_dynamic-update-slice_fusion.23
  21.9 0.7 constant_dynamic-update-slice_fusion.22
  22.6 2.7 %collective-permute-start.12 = (bf16[32,3584]{1,0:T(8,128)(2,1)S(1)}, bf16[32,3584]{1,0:T(8,128)(2,1)S(1)}, u32[]{:S(2)}, u32[]{:S(2)}) collective-permute-start(bf16[32,3584]{1,0:T(8,128)(2,1)S(1)} %get-tuple-element.38), channel_id=1, source_target_pairs={{0,6},{1,7},{2,4},{3,5},{4,2},{5,3},{6,0},{7,1},{8,14},{9,15},{10,... | collective-permute-start | bytes 688136 | tf_op jit(solution)/shard_map/ppermute | solution.py:12
  25.3 0.5 collective-permute-start.11
  25.8 0.3 collective-permute-start.10
  26.1 0.5 collective-permute-done.2
  26.6 2.5 %collective-permute-start.5 = (bf16[32,3712]{1,0:T(8,128)(2,1)S(1)}, bf16[32,3712]{1,0:T(8,128)(2,1)S(1)}, u32[]{:S(2)}, u32[]{:S(2)}) collective-permute-start(bf16[32,3712]{1,0:T(8,128)(2,1)S(1)} %pad_maximum_fusion.2), channel_id=1, source_target_pairs={{0,6},{1,7},{2,4},{3,5},{4,2},{5,3},{6,0},{7,1},{8,14},{9,15},{10,... | collective-permute-start | bytes 712712 | tf_op jit(solution)/shard_map/ppermute | solution.py:12
  29.1 0.6 constant_dynamic-update-slice_fusion.5
  29.7 0.6 constant_dynamic-update-slice_fusion.4
  30.4 0.6 constant_dynamic-update-slice_fusion.3
  31.0 0.5 collective-permute-start.4
  31.6 5.5 %collective-permute-done.10 = bf16[32,3584]{1,0:T(8,128)(2,1)S(1)} collective-permute-done((bf16[32,3584]{1,0:T(8,128)(2,1)S(1)}, bf16[32,3584]{1,0:T(8,128)(2,1)S(1)}, u32[]{:S(2)}, u32[]{:S(2)}) %collective-permute-start.10) | collective-permute-done | bytes 229408 | tf_op jit(solution)/shard_map/ppermute | solution.py:12
  37.1 1.5 %collective-permute-start.3 = (bf16[32,3712]{1,0:T(8,128)(2,1)S(1)}, bf16[32,3712]{1,0:T(8,128)(2,1)S(1)}, u32[]{:S(2)}, u32[]{:S(2)}) collective-permute-start(bf16[32,3712]{1,0:T(8,128)(2,1)S(1)} %pad_maximum_fusion.2), channel_id=1, source_target_pairs={{0,2},{1,3},{2,0},{3,1},{4,6},{5,7},{6,4},{7,5},{8,10},{9,11},{10,... | collective-permute-start | bytes 712712 | tf_op jit(solution)/shard_map/ppermute | solution.py:12
  38.6 0.8 constant_dynamic-update-slice_fusion.21
  39.4 0.8 constant_dynamic-update-slice_fusion.20
  40.3 0.8 constant_dynamic-update-slice_fusion.19
  41.1 5.9 %collective-permute-done.3 = bf16[32,3712]{1,0:T(8,128)(2,1)S(1)} collective-permute-done((bf16[32,3712]{1,0:T(8,128)(2,1)S(1)}, bf16[32,3712]{1,0:T(8,128)(2,1)S(1)}, u32[]{:S(2)}, u32[]{:S(2)}) %collective-permute-start.3) | collective-permute-done | bytes 237600 | tf_op jit(solution)/shard_map/ppermute | solution.py:12
  47.2 1.1 %fusion.4 = bf16[3584,512]{1,0:T(8,128)(2,1)S(1)} fusion(bf16[3584,512]{1,0:T(8,128)(2,1)S(1)} %copy-done.2, bf16[3,16,3584]{2,1,0:T(8,128)(2,1)S(1)} %maximum_select_fusion, bf16[3,16,512]{2,1,0:T(8,128)(2,1)S(1)} %copy-done.12), kind=kOutput, calls=%fused_computation.10 | convolution fusion | flops 66060288 | bytes 7471104 | tf_op jit(solution)/shard_map/dot_general | solution.py:50
  48.4 0.8 copy-done
  49.2 1.1 %fusion.2 = bf16[3584,512]{1,0:T(8,128)(2,1)S(1)} fusion(bf16[3584,512]{1,0:T(8,128)(2,1)S(1)} %copy-done, bf16[3,16,3584]{2,1,0:T(8,128)(2,1)S(1)} %maximum_select_fusion, bf16[3,16,512]{2,1,0:T(8,128)(2,1)S(1)} %copy-done.12), kind=kOutput, calls=%fused_computation.8 | convolution fusion | flops 66060288 | bytes 7471104 | tf_op jit(solution)/shard_map/dot_general | solution.py:50
  50.3 1.7 %copy-done.8 = bf16[256,3584]{1,0:T(8,128)(2,1)S(1)} copy-done((bf16[256,3584]{1,0:T(8,128)(2,1)S(1)}, bf16[256,3584]{1,0:T(8,128)(2,1)}, u32[]{:S(2)}) %copy-start.8) | copy-done | bytes 1835032
  52.4 1.1 %fusion.10 = f32[256,512]{1,0:T(8,128)S(1)} fusion(bf16[3584,512]{1,0:T(8,128)(2,1)S(1)} %fusion.4, bf16[256,3712]{1,0:T(8,128)(2,1)S(1)} %constant_dynamic-update-slice_fusion.7), kind=kOutput, calls=%fused_computation.23 | convolution fusion | flops 939524096 | bytes 6029312 | tf_op jit(solution)/shard_map/dot_general | solution.py:50
  53.5 1.9 %fusion.12 = f32[256,512]{1,0:T(8,128)} fusion(bf16[3584,512]{1,0:T(8,128)(2,1)S(1)} %fusion.2, bf16[256,3712]{1,0:T(8,128)(2,1)S(1)} %constant_dynamic-update-slice_fusion.7), kind=kOutput, calls=%fused_computation.25 | convolution fusion | flops 939524096 | bytes 6029312 | tf_op jit(solution)/shard_map/dot_general | solution.py:50
  55.4 5.1 %select_convert_fusion.1 = (bf16[256,512]{1,0:T(8,128)(2,1)S(1)}, f32[256]{0:T(256)S(1)}, bf16[256,512]{1,0:T(8,128)(2,1)S(1)}) fusion(f32[256,512]{1,0:T(8,128)S(1)} %fusion.10, f32[256,512]{1,0:T(8,128)} %fusion.12, f32[256]{0:T(256)S(1)} %select_reduce_fusion, pred[256]{0:T(512)(128)(4,1)S(1)} %broadcast_compare_fusion, bf16[256,3584]{1,0:T(8,128)(2,1)} %copy-done.9, ...), kind=kOutput, calls=%fused_computation.37 | convolution fusion | flops 1008205568 | bytes 7211520 | tf_op jit(solution)/shard_map/dot_general | solution.py:50
  60.5 4.1 %fusion.1 = bf16[512,3584]{0,1:T(8,128)(2,1)S(1)} fusion(bf16[512,3584]{0,1:T(8,128)(2,1)} %copy.15, bf16[256,3584]{1,0:T(8,128)(2,1)} %copy-done.9, f32[256]{0:T(256)S(1)} %select_reduce_fusion, f32[256,512]{1,0:T(8,128)} %fusion.12, pred[256]{0:T(512)(128)(4,1)S(1)} %broadcast_compare_fusion, f32[256,512]{1,0:T(8,128)S(1)} %fusion.10), kind=kOutput, calls=%fused_computation.7 | convolution fusion | flops 946077696 | bytes 10224896 | tf_op jit(solution)/shard_map/dot_general | solution.py:50
  64.7 0.6 convolution_bitcast_fusion.3
  65.2 1.1 %convolution_bitcast_fusion = f32[1,16,3584]{2,1,0:T(8,128)S(1)} fusion(bf16[512,3584]{0,1:T(8,128)(2,1)S(1)} %fusion.1, bf16[3,16,512]{2,1,0:T(8,128)(2,1)S(1)} %copy-done.12), kind=kOutput, calls=%fused_computation.14 | convolution fusion | flops 58720256 | bytes 3915776 | tf_op jit(solution)/shard_map/dot_general | solution.py:50
  66.3 1.0 copy-done.1
  67.3 1.2 %fusion.3 = bf16[3584,512]{1,0:T(8,128)(2,1)S(1)} fusion(bf16[3584,512]{1,0:T(8,128)(2,1)S(1)} %copy-done.1, bf16[256,512]{1,0:T(8,128)(2,1)S(1)} %get-tuple-element.8, bf16[256,3712]{1,0:T(8,128)(2,1)S(1)} %constant_dynamic-update-slice_fusion.7), kind=kOutput, calls=%fused_computation.9 | convolution fusion | flops 945029120 | bytes 9437184 | tf_op jit(solution)/shard_map/dot_general | solution.py:50
  68.5 0.6 convolution_bitcast_fusion.4
  69.0 1.1 %convolution_bitcast_fusion.1 = f32[1,16,3584]{2,1,0:T(8,128)S(1)} fusion(bf16[3584,512]{1,0:T(8,128)(2,1)S(1)} %fusion.3, bf16[3,16,512]{2,1,0:T(8,128)(2,1)S(1)} %copy-done.12), kind=kOutput, calls=%fused_computation.15 | convolution fusion | flops 58720256 | bytes 3915776 | tf_op jit(solution)/shard_map/dot_general | solution.py:50
  70.1 1.0 copy-done.7
  71.1 1.2 %fusion.39 = f32[256,3584]{1,0:T(8,128)S(1)} fusion(bf16[256,512]{1,0:T(8,128)(2,1)S(1)} %get-tuple-element.6, bf16[3584,512]{1,0:T(8,128)(2,1)S(1)} %copy-done.7), kind=kOutput, calls=%fused_computation.118 | convolution fusion | flops 939524096 | bytes 7602176 | tf_op jit(solution)/shard_map/dot_general | solution.py:50
  72.3 0.8 copy-done.3
  73.1 1.4 %fusion.5 = bf16[3584,512]{1,0:T(8,128)(2,1)S(1)} fusion(bf16[3584,512]{1,0:T(8,128)(2,1)S(1)} %copy-done.3, bf16[256,512]{1,0:T(8,128)(2,1)S(1)} %get-tuple-element.6, bf16[256,3712]{1,0:T(8,128)(2,1)S(1)} %constant_dynamic-update-slice_fusion.7), kind=kOutput, calls=%fused_computation.11 | convolution fusion | flops 945029120 | bytes 9437184 | tf_op jit(solution)/shard_map/dot_general | solution.py:50
  74.5 0.7 copy-done.5
  75.2 1.3 %fusion.6 = bf16[256,3584]{1,0:T(8,128)(2,1)S(1)} fusion(f32[256,3584]{1,0:T(8,128)S(1)} %fusion.39, bf16[256,512]{1,0:T(8,128)(2,1)S(1)} %get-tuple-element.8, bf16[3584,512]{1,0:T(8,128)(2,1)S(1)} %copy-done.5), kind=kOutput, calls=%fused_computation.13 | convolution fusion | flops 941359104 | bytes 9437184 | tf_op jit(solution)/shard_map/dot_general | solution.py:50
  76.7 1.1 convolution_bitcast_fusion.2
  77.9 1.3 %collective-permute-done.15 = bf16[128,3712]{1,0:T(8,128)(2,1)S(1)} collective-permute-done((bf16[128,3712]{1,0:T(8,128)(2,1)S(1)}, bf16[128,3712]{1,0:T(8,128)(2,1)S(1)}, u32[]{:S(2)}, u32[]{:S(2)}) %collective-permute-start.15) | collective-permute-done | bytes 950304 | tf_op jit(solution)/shard_map/ppermute | solution.py:12
  79.5 1.6 %collective-permute-start.16 = (bf16[32,3712]{1,0:T(8,128)(2,1)S(1)}, bf16[32,3712]{1,0:T(8,128)(2,1)S(1)}, u32[]{:S(2)}, u32[]{:S(2)}) collective-permute-start(bf16[32,3712]{1,0:T(8,128)(2,1)S(1)} %get-tuple-element.9), channel_id=1, source_target_pairs={{0,2},{1,3},{2,0},{3,1},{4,6},{5,7},{6,4},{7,5},{8,10},{9,11},{10,... | collective-permute-start | bytes 712712 | tf_op jit(solution)/shard_map/ppermute | solution.py:12
  81.1 1.3 %collective-permute-start.18 = (bf16[32,3712]{1,0:T(8,128)(2,1)S(1)}, bf16[32,3712]{1,0:T(8,128)(2,1)S(1)}, u32[]{:S(2)}, u32[]{:S(2)}) collective-permute-start(bf16[32,3712]{1,0:T(8,128)(2,1)S(1)} %get-tuple-element.10), channel_id=1, source_target_pairs={{0,6},{1,7},{2,4},{3,5},{4,2},{5,3},{6,0},{7,1},{8,14},{9,15},{10,... | collective-permute-start | bytes 712712 | tf_op jit(solution)/shard_map/ppermute | solution.py:12
  82.4 0.7 collective-permute-start.17
  83.1 0.6 convolution_bitcast_fusion.5
  83.7 0.7 pad_maximum_fusion.3
  84.3 3.9 %collective-permute-done.16 = bf16[32,3712]{1,0:T(8,128)(2,1)S(1)} collective-permute-done((bf16[32,3712]{1,0:T(8,128)(2,1)S(1)}, bf16[32,3712]{1,0:T(8,128)(2,1)S(1)}, u32[]{:S(2)}, u32[]{:S(2)}) %collective-permute-start.16) | collective-permute-done | bytes 237600 | tf_op jit(solution)/shard_map/ppermute | solution.py:12
  88.2 5.1 %collective-permute-done.18 = bf16[32,3712]{1,0:T(8,128)(2,1)S(1)} collective-permute-done((bf16[32,3712]{1,0:T(8,128)(2,1)S(1)}, bf16[32,3712]{1,0:T(8,128)(2,1)S(1)}, u32[]{:S(2)}, u32[]{:S(2)}) %collective-permute-start.18) | collective-permute-done | bytes 237600 | tf_op jit(solution)/shard_map/ppermute | solution.py:12
  93.4 1.4 %collective-permute-done.17 = bf16[32,3712]{1,0:T(8,128)(2,1)S(1)} collective-permute-done((bf16[32,3712]{1,0:T(8,128)(2,1)S(1)}, bf16[32,3712]{1,0:T(8,128)(2,1)S(1)}, u32[]{:S(2)}, u32[]{:S(2)}) %collective-permute-start.17) | collective-permute-done | bytes 237600 | tf_op jit(solution)/shard_map/ppermute | solution.py:12
  94.9 0.4 collective-permute-start.19
  95.3 3.3 %collective-permute-start.21 = (bf16[8,3712]{1,0:T(8,128)(2,1)S(1)}, bf16[8,3712]{1,0:T(8,128)(2,1)S(1)}, u32[]{:S(2)}, u32[]{:S(2)}) collective-permute-start(bf16[8,3712]{1,0:T(8,128)(2,1)S(1)} %get-tuple-element.13), channel_id=1, source_target_pairs={{0,24},{1,25},{2,26},{3,27},{4,28},{5,29},{6,30},{7,31},{8,16},{9,... | collective-permute-start | bytes 178184 | tf_op jit(solution)/shard_map/ppermute | solution.py:12
  98.7 0.5 collective-permute-start.20
  99.1 0.8 convert_add_fusion
  99.9 2.0 %collective-permute-done.21 = bf16[8,3712]{1,0:T(8,128)(2,1)S(1)} collective-permute-done((bf16[8,3712]{1,0:T(8,128)(2,1)S(1)}, bf16[8,3712]{1,0:T(8,128)(2,1)S(1)}, u32[]{:S(2)}, u32[]{:S(2)}) %collective-permute-start.21) | collective-permute-done | bytes 59424 | tf_op jit(solution)/shard_map/ppermute | solution.py:12
  101.9 2.5 %collective-permute-done.20 = bf16[8,3712]{1,0:T(8,128)(2,1)S(1)} collective-permute-done((bf16[8,3712]{1,0:T(8,128)(2,1)S(1)}, bf16[8,3712]{1,0:T(8,128)(2,1)S(1)}, u32[]{:S(2)}, u32[]{:S(2)}) %collective-permute-start.20) | collective-permute-done | bytes 59424 | tf_op jit(solution)/shard_map/ppermute | solution.py:12
  104.5 0.6 slice.140
  105.1 0.7 select_reduce_fusion.1
  (69 shorter events, 1.8 us)
Async XLA Ops:
  0.6 20.6 %collective-permute-start.8 = (bf16[8,3584]{1,0:T(8,128)(2,1)}, bf16[8,3584]{1,0:T(8,128)(2,1)S(1)}, u32[]{:S(2)}, u32[]{:S(2)}) collective-permute-start(bf16[8,3584]{1,0:T(8,128)(2,1)} %param.10), channel_id=1, source_target_pairs={{0,16},{1,17},{2,18},{3,19},{4,20},{5,21},{6,22},{7,23},{8,24},{9,... | collective-permute-start | bytes 172040 | tf_op jit(solution)/shard_map/ppermute | solution.py:12
  4.7 15.8 %collective-permute-start.7 = (bf16[8,3584]{1,0:T(8,128)(2,1)}, bf16[8,3584]{1,0:T(8,128)(2,1)S(1)}, u32[]{:S(2)}, u32[]{:S(2)}) collective-permute-start(bf16[8,3584]{1,0:T(8,128)(2,1)} %param.10), channel_id=1, source_target_pairs={{0,8},{1,9},{2,10},{3,11},{4,12},{5,13},{6,14},{7,15},{8,0},{9,1},... | collective-permute-start | bytes 172040 | tf_op jit(solution)/shard_map/ppermute | solution.py:12
  6.3 15.6 %collective-permute-start.9 = (bf16[8,3584]{1,0:T(8,128)(2,1)}, bf16[8,3584]{1,0:T(8,128)(2,1)S(1)}, u32[]{:S(2)}, u32[]{:S(2)}) collective-permute-start(bf16[8,3584]{1,0:T(8,128)(2,1)} %param.10), channel_id=1, source_target_pairs={{0,24},{1,25},{2,26},{3,27},{4,28},{5,29},{6,30},{7,31},{8,16},{9,... | collective-permute-start | bytes 172040 | tf_op jit(solution)/shard_map/ppermute | solution.py:12
  8.6 16.6 %collective-permute-start.1 = (bf16[8,3712]{1,0:T(8,128)(2,1)S(1)}, bf16[8,3712]{1,0:T(8,128)(2,1)S(1)}, u32[]{:S(2)}, u32[]{:S(2)}) collective-permute-start(bf16[8,3712]{1,0:T(8,128)(2,1)S(1)} %get-tuple-element.35), channel_id=1, source_target_pairs={{0,16},{1,17},{2,18},{3,19},{4,20},{5,21},{6,22},{7,23},{8,24},{9,... | collective-permute-start | bytes 178184 | tf_op jit(solution)/shard_map/ppermute | solution.py:12
  10.6 15.2 %collective-permute-start = (bf16[8,3712]{1,0:T(8,128)(2,1)S(1)}, bf16[8,3712]{1,0:T(8,128)(2,1)S(1)}, u32[]{:S(2)}, u32[]{:S(2)}) collective-permute-start(bf16[8,3712]{1,0:T(8,128)(2,1)S(1)} %get-tuple-element.35), channel_id=1, source_target_pairs={{0,8},{1,9},{2,10},{3,11},{4,12},{5,13},{6,14},{7,15},{8,0},{9,1},... | collective-permute-start | bytes 178184 | tf_op jit(solution)/shard_map/ppermute | solution.py:12
  14.5 6.7 %copy-start.11 = (bf16[3,16,1792]{2,1,0:T(8,128)(2,1)S(1)}, bf16[3,16,1792]{2,1,0:T(8,128)(2,1)}, u32[]{:S(2)}) copy-start(bf16[3,16,1792]{2,1,0:T(8,128)(2,1)} %param.17) | copy-start | bytes 516100
  14.5 12.1 %copy-start.10 = (bf16[8,3584]{1,0:T(8,128)(2,1)S(1)}, bf16[8,3584]{1,0:T(8,128)(2,1)}, u32[]{:S(2)}) copy-start(bf16[8,3584]{1,0:T(8,128)(2,1)} %param.9) | copy-start | bytes 172036
  20.5 6.1 %collective-permute-start.2 = (bf16[8,3712]{1,0:T(8,128)(2,1)S(1)}, bf16[8,3712]{1,0:T(8,128)(2,1)S(1)}, u32[]{:S(2)}, u32[]{:S(2)}) collective-permute-start(bf16[8,3712]{1,0:T(8,128)(2,1)S(1)} %get-tuple-element.35), channel_id=1, source_target_pairs={{0,24},{1,25},{2,26},{3,27},{4,28},{5,29},{6,30},{7,31},{8,16},{9,... | collective-permute-start | bytes 178184 | tf_op jit(solution)/shard_map/ppermute | solution.py:12
  21.3 9.7 %collective-permute-start.14 = (bf16[3,16,1792]{2,1,0:T(8,128)(2,1)S(1)}, bf16[3,16,1792]{2,1,0:T(8,128)(2,1)S(1)}, u32[]{:S(2)}, u32[]{:S(2)}) collective-permute-start(bf16[3,16,1792]{2,1,0:T(8,128)(2,1)S(1)} %copy-done.11), channel_id=1, source_target_pairs={{0,1},{1,0},{2,3},{3,2},{4,5},{5,4},{6,7},{7,6},{8,9},{9,8},{10,11... | collective-permute-start | bytes 516104 | tf_op jit(solution)/shard_map/ppermute | solution.py:12
  22.6 17.7 %collective-permute-start.12 = (bf16[32,3584]{1,0:T(8,128)(2,1)S(1)}, bf16[32,3584]{1,0:T(8,128)(2,1)S(1)}, u32[]{:S(2)}, u32[]{:S(2)}) collective-permute-start(bf16[32,3584]{1,0:T(8,128)(2,1)S(1)} %get-tuple-element.38), channel_id=1, source_target_pairs={{0,6},{1,7},{2,4},{3,5},{4,2},{5,3},{6,0},{7,1},{8,14},{9,15},{10,... | collective-permute-start | bytes 688136 | tf_op jit(solution)/shard_map/ppermute | solution.py:12
  25.3 14.2 %collective-permute-start.11 = (bf16[32,3584]{1,0:T(8,128)(2,1)S(1)}, bf16[32,3584]{1,0:T(8,128)(2,1)S(1)}, u32[]{:S(2)}, u32[]{:S(2)}) collective-permute-start(bf16[32,3584]{1,0:T(8,128)(2,1)S(1)} %get-tuple-element.38), channel_id=1, source_target_pairs={{0,4},{1,5},{2,6},{3,7},{4,0},{5,1},{6,2},{7,3},{8,12},{9,13},{10,... | collective-permute-start | bytes 688136 | tf_op jit(solution)/shard_map/ppermute | solution.py:12
  25.8 11.4 %collective-permute-start.10 = (bf16[32,3584]{1,0:T(8,128)(2,1)S(1)}, bf16[32,3584]{1,0:T(8,128)(2,1)S(1)}, u32[]{:S(2)}, u32[]{:S(2)}) collective-permute-start(bf16[32,3584]{1,0:T(8,128)(2,1)S(1)} %get-tuple-element.38), channel_id=1, source_target_pairs={{0,2},{1,3},{2,0},{3,1},{4,6},{5,7},{6,4},{7,5},{8,10},{9,11},{10,... | collective-permute-start | bytes 688136 | tf_op jit(solution)/shard_map/ppermute | solution.py:12
  26.6 20.5 %collective-permute-start.5 = (bf16[32,3712]{1,0:T(8,128)(2,1)S(1)}, bf16[32,3712]{1,0:T(8,128)(2,1)S(1)}, u32[]{:S(2)}, u32[]{:S(2)}) collective-permute-start(bf16[32,3712]{1,0:T(8,128)(2,1)S(1)} %pad_maximum_fusion.2), channel_id=1, source_target_pairs={{0,6},{1,7},{2,4},{3,5},{4,2},{5,3},{6,0},{7,1},{8,14},{9,15},{10,... | collective-permute-start | bytes 712712 | tf_op jit(solution)/shard_map/ppermute | solution.py:12
  31.0 16.0 %copy-start.14 = (bf16[128,3712]{1,0:T(8,128)(2,1)S(1)}, bf16[128,3712]{1,0:T(8,128)(2,1)}, u32[]{:S(2)}) copy-start(bf16[128,3712]{1,0:T(8,128)(2,1)} %get-tuple-element.27) | copy-start | bytes 2850820
  31.0 16.0 %collective-permute-start.4 = (bf16[32,3712]{1,0:T(8,128)(2,1)S(1)}, bf16[32,3712]{1,0:T(8,128)(2,1)S(1)}, u32[]{:S(2)}, u32[]{:S(2)}) collective-permute-start(bf16[32,3712]{1,0:T(8,128)(2,1)S(1)} %pad_maximum_fusion.2), channel_id=1, source_target_pairs={{0,4},{1,5},{2,6},{3,7},{4,0},{5,1},{6,2},{7,3},{8,12},{9,13},{10,... | collective-permute-start | bytes 712712 | tf_op jit(solution)/shard_map/ppermute | solution.py:12
  37.1 9.8 %collective-permute-start.3 = (bf16[32,3712]{1,0:T(8,128)(2,1)S(1)}, bf16[32,3712]{1,0:T(8,128)(2,1)S(1)}, u32[]{:S(2)}, u32[]{:S(2)}) collective-permute-start(bf16[32,3712]{1,0:T(8,128)(2,1)S(1)} %pad_maximum_fusion.2), channel_id=1, source_target_pairs={{0,2},{1,3},{2,0},{3,1},{4,6},{5,7},{6,4},{7,5},{8,10},{9,11},{10,... | collective-permute-start | bytes 712712 | tf_op jit(solution)/shard_map/ppermute | solution.py:12
  38.6 8.6 %copy-start.2 = (bf16[3584,512]{1,0:T(8,128)(2,1)S(1)}, bf16[3584,512]{1,0:T(8,128)(2,1)}, u32[]{:S(2)}) copy-start(bf16[3584,512]{1,0:T(8,128)(2,1)} %param.13) | copy-start | bytes 11010052
  39.4 7.8 %copy-start.12 = (bf16[3,16,512]{2,1,0:T(8,128)(2,1)S(1)}, bf16[3,16,512]{2,1,0:T(8,128)(2,1)}, u32[]{:S(2)}) copy-start(bf16[3,16,512]{2,1,0:T(8,128)(2,1)} %param.16) | copy-start | bytes 147460
  41.1 9.2 %collective-permute-start.13 = (bf16[128,3584]{1,0:T(8,128)(2,1)}, bf16[128,3584]{1,0:T(8,128)(2,1)S(1)}, u32[]{:S(2)}, u32[]{:S(2)}) collective-permute-start(bf16[128,3584]{1,0:T(8,128)(2,1)} %get-tuple-element.21), channel_id=1, source_target_pairs={{0,1},{1,0},{2,3},{3,2},{4,5},{5,4},{6,7},{7,6},{8,9},{9,8},{10,11... | collective-permute-start | bytes 2752520 | tf_op jit(solution)/shard_map/ppermute | solution.py:12
  47.1 2.0 %copy-start = (bf16[3584,512]{1,0:T(8,128)(2,1)S(1)}, bf16[3584,512]{1,0:T(8,128)(2,1)}, u32[]{:S(2)}) copy-start(bf16[3584,512]{1,0:T(8,128)(2,1)} %param.14) | copy-start | bytes 11010052
  47.1 5.0 %collective-permute-start.6 = (bf16[128,3712]{1,0:T(8,128)(2,1)S(1)}, bf16[128,3712]{1,0:T(8,128)(2,1)S(1)}, u32[]{:S(2)}, u32[]{:S(2)}) collective-permute-start(bf16[128,3712]{1,0:T(8,128)(2,1)S(1)} %get-tuple-element.15), channel_id=1, source_target_pairs={{0,1},{1,0},{2,3},{3,2},{4,5},{5,4},{6,7},{7,6},{8,9},{9,8},{10,11... | collective-permute-start | bytes 2850824 | tf_op jit(solution)/shard_map/ppermute | solution.py:12
  49.2 3.2 %copy-start.6 = (bf16[3584,512]{1,0:T(8,128)(2,1)}, bf16[3584,512]{1,0:T(8,128)(2,1)S(1)}, u32[]{:S(2)}) copy-start(bf16[3584,512]{1,0:T(8,128)(2,1)S(1)} %fusion.4) | copy-start | bytes 11010052
  49.2 2.8 %copy-start.8 = (bf16[256,3584]{1,0:T(8,128)(2,1)S(1)}, bf16[256,3584]{1,0:T(8,128)(2,1)}, u32[]{:S(2)}) copy-start(bf16[256,3584]{1,0:T(8,128)(2,1)} %get-tuple-element.22) | copy-start | bytes 5505028
  50.3 3.2 %copy-start.4 = (bf16[3584,512]{1,0:T(8,128)(2,1)}, bf16[3584,512]{1,0:T(8,128)(2,1)S(1)}, u32[]{:S(2)}) copy-start(bf16[3584,512]{1,0:T(8,128)(2,1)S(1)} %fusion.2) | copy-start | bytes 11010052
  52.1 1.4 %copy-start.9 = (bf16[256,3584]{1,0:T(8,128)(2,1)}, bf16[256,3584]{1,0:T(8,128)(2,1)S(1)}, u32[]{:S(2)}) copy-start(bf16[256,3584]{1,0:T(8,128)(2,1)S(1)} %constant_dynamic-update-slice_fusion.26) | copy-start | bytes 5505028
  65.2 2.1 %copy-start.1 = (bf16[3584,512]{1,0:T(8,128)(2,1)S(1)}, bf16[3584,512]{1,0:T(8,128)(2,1)}, u32[]{:S(2)}) copy-start(bf16[3584,512]{1,0:T(8,128)(2,1)} %param.14) | copy-start | bytes 11010052
  69.0 2.1 %copy-start.7 = (bf16[3584,512]{1,0:T(8,128)(2,1)S(1)}, bf16[3584,512]{1,0:T(8,128)(2,1)}, u32[]{:S(2)}) copy-start(bf16[3584,512]{1,0:T(8,128)(2,1)} %copy-done.6) | copy-start | bytes 11010052
  71.1 2.0 %copy-start.3 = (bf16[3584,512]{1,0:T(8,128)(2,1)S(1)}, bf16[3584,512]{1,0:T(8,128)(2,1)}, u32[]{:S(2)}) copy-start(bf16[3584,512]{1,0:T(8,128)(2,1)} %param.13) | copy-start | bytes 11010052
  73.1 2.0 %copy-start.5 = (bf16[3584,512]{1,0:T(8,128)(2,1)S(1)}, bf16[3584,512]{1,0:T(8,128)(2,1)}, u32[]{:S(2)}) copy-start(bf16[3584,512]{1,0:T(8,128)(2,1)} %copy-done.4) | copy-start | bytes 11010052
  76.7 2.6 %collective-permute-start.15 = (bf16[128,3712]{1,0:T(8,128)(2,1)S(1)}, bf16[128,3712]{1,0:T(8,128)(2,1)S(1)}, u32[]{:S(2)}, u32[]{:S(2)}) collective-permute-start(bf16[128,3712]{1,0:T(8,128)(2,1)S(1)} %pad_maximum_fusion), channel_id=1, source_target_pairs={{0,1},{1,0},{2,3},{3,2},{4,5},{5,4},{6,7},{7,6},{8,9},{9,8},{10,11... | collective-permute-start | bytes 2850824 | tf_op jit(solution)/shard_map/ppermute | solution.py:12
  79.5 8.7 %collective-permute-start.16 = (bf16[32,3712]{1,0:T(8,128)(2,1)S(1)}, bf16[32,3712]{1,0:T(8,128)(2,1)S(1)}, u32[]{:S(2)}, u32[]{:S(2)}) collective-permute-start(bf16[32,3712]{1,0:T(8,128)(2,1)S(1)} %get-tuple-element.9), channel_id=1, source_target_pairs={{0,2},{1,3},{2,0},{3,1},{4,6},{5,7},{6,4},{7,5},{8,10},{9,11},{10,... | collective-permute-start | bytes 712712 | tf_op jit(solution)/shard_map/ppermute | solution.py:12
  81.1 12.3 %collective-permute-start.18 = (bf16[32,3712]{1,0:T(8,128)(2,1)S(1)}, bf16[32,3712]{1,0:T(8,128)(2,1)S(1)}, u32[]{:S(2)}, u32[]{:S(2)}) collective-permute-start(bf16[32,3712]{1,0:T(8,128)(2,1)S(1)} %get-tuple-element.10), channel_id=1, source_target_pairs={{0,6},{1,7},{2,4},{3,5},{4,2},{5,3},{6,0},{7,1},{8,14},{9,15},{10,... | collective-permute-start | bytes 712712 | tf_op jit(solution)/shard_map/ppermute | solution.py:12
  82.4 12.4 %collective-permute-start.17 = (bf16[32,3712]{1,0:T(8,128)(2,1)S(1)}, bf16[32,3712]{1,0:T(8,128)(2,1)S(1)}, u32[]{:S(2)}, u32[]{:S(2)}) collective-permute-start(bf16[32,3712]{1,0:T(8,128)(2,1)S(1)} %get-tuple-element.11), channel_id=1, source_target_pairs={{0,4},{1,5},{2,6},{3,7},{4,0},{5,1},{6,2},{7,3},{8,12},{9,13},{10,... | collective-permute-start | bytes 712712 | tf_op jit(solution)/shard_map/ppermute | solution.py:12
  83.7 21.5 %copy-start.13 = (s32[8,8]{1,0:T(8,128)S(1)}, s32[8,8]{1,0:T(8,128)}, u32[]{:S(2)}) copy-start(s32[8,8]{1,0:T(8,128)} %param.12) | copy-start | bytes 772
  83.7 15.5 %collective-permute-start.22 = (bf16[3,16,1792]{2,1,0:T(8,128)(2,1)S(1)}, bf16[3,16,1792]{2,1,0:T(8,128)(2,1)S(1)}, u32[]{:S(2)}, u32[]{:S(2)}) collective-permute-start(bf16[3,16,1792]{2,1,0:T(8,128)(2,1)S(1)} %select_convert_fusion.2), channel_id=1, source_target_pairs={{0,1},{1,0},{2,3},{3,2},{4,5},{5,4},{6,7},{7,6},{8,9},{9,8},{10,11... | collective-permute-start | bytes 516104 | tf_op jit(solution)/shard_map/ppermute | solution.py:12
  94.9 5.0 %collective-permute-start.19 = (bf16[8,3712]{1,0:T(8,128)(2,1)S(1)}, bf16[8,3712]{1,0:T(8,128)(2,1)S(1)}, u32[]{:S(2)}, u32[]{:S(2)}) collective-permute-start(bf16[8,3712]{1,0:T(8,128)(2,1)S(1)} %get-tuple-element.12), channel_id=1, source_target_pairs={{0,8},{1,9},{2,10},{3,11},{4,12},{5,13},{6,14},{7,15},{8,0},{9,1},... | collective-permute-start | bytes 178184 | tf_op jit(solution)/shard_map/ppermute | solution.py:12
  95.3 6.6 %collective-permute-start.21 = (bf16[8,3712]{1,0:T(8,128)(2,1)S(1)}, bf16[8,3712]{1,0:T(8,128)(2,1)S(1)}, u32[]{:S(2)}, u32[]{:S(2)}) collective-permute-start(bf16[8,3712]{1,0:T(8,128)(2,1)S(1)} %get-tuple-element.13), channel_id=1, source_target_pairs={{0,24},{1,25},{2,26},{3,27},{4,28},{5,29},{6,30},{7,31},{8,16},{9,... | collective-permute-start | bytes 178184 | tf_op jit(solution)/shard_map/ppermute | solution.py:12
  98.7 5.7 %collective-permute-start.20 = (bf16[8,3712]{1,0:T(8,128)(2,1)S(1)}, bf16[8,3712]{1,0:T(8,128)(2,1)S(1)}, u32[]{:S(2)}, u32[]{:S(2)}) collective-permute-start(bf16[8,3712]{1,0:T(8,128)(2,1)S(1)} %get-tuple-element.14), channel_id=1, source_target_pairs={{0,16},{1,17},{2,18},{3,19},{4,20},{5,21},{6,22},{7,23},{8,24},{9,... | collective-permute-start | bytes 178184 | tf_op jit(solution)/shard_map/ppermute | solution.py:12

commit v2 on v1

v2 whole, which is shorter than its diff:
```python
import functools

import jax
import jax.numpy as jnp
from jax import lax
from jax.experimental import pallas as pl
from jax.experimental.pallas import tpu as pltpu
from jax.sharding import PartitionSpec as P

NN = (((1,), (0,)), ((), ()))
NT = (((1,), (1,)), ((), ()))
TN = (((0,), (0,)), ((), ()))
F32, B16 = jnp.float32, jnp.bfloat16


def send(value, mask):
    pairs = [(source, source ^ mask) for source in range(lax.axis_size("expert"))]
    return lax.ppermute(value, "expert", pairs)


def stages():
    found, bit, top = [], 1, lax.axis_size("expert").bit_length() - 1
    while bit < top:
        if bit + 1 < top:
            found.append((2**bit, 2 ** (bit + 1), 3 * 2**bit))
        else:
            found.append((2**bit,))
        bit += 2
    return found


def dot32(left, right, dims=NN):
    return lax.dot_general(left, right, dims, preferred_element_type=F32)


def in_vmem(kernel, outs, args, flops=0):
    moved = sum(a.size * a.dtype.itemsize for a in args)
    moved += sum(s[0] * s[1] * jnp.dtype(d).itemsize for s, d in outs)
    return pl.pallas_call(
        kernel,
        out_shape=[pltpu.VMEM(shape, dtype) for shape, dtype in outs],
        in_specs=[pl.BlockSpec(memory_space=pltpu.VMEM)] * len(args),
        out_specs=[pl.BlockSpec(memory_space=pltpu.VMEM)] * len(outs),
        compiler_params=pltpu.CompilerParams(vmem_limit_bytes=20 * 2**20),
        cost_estimate=pl.CostEstimate(flops=flops, bytes_accessed=moved, transcendentals=0),
    )(*[pltpu.with_memory_space_constraint(a, pltpu.VMEM) for a in args])


def stacked(refs):
    return jnp.concatenate([ref[...].astype(F32) for ref in refs], axis=0)


def chunks_of(width):
    step = next(s for s in (512, 256, 128) if width % s == 0)
    return [pl.ds(at, step) for at in range(0, width, step)]


def weights_kernel(
    gate_ref, up_ref, down_ref, narrow_ref, wide_ref, gate_out, up_out, down_out
):
    for part in chunks_of(gate_ref.shape[0]):
        for i, (src, dst) in enumerate(((gate_ref, gate_out), (up_ref, up_out))):
            factor = 1.0 + dot32(wide_ref[i, :, part], narrow_ref[i], TN)
            dst[part, :] = (src[part, :].astype(F32) * factor).astype(B16)
        factor = 1.0 + dot32(narrow_ref[2], wide_ref[2, :, part], TN)
        down_out[:, part] = (down_ref[:, part].astype(F32) * factor).astype(B16)


def pack_tokens_kernel(masks, rows, capacity, experts, width, *refs):
    pieces, outs = refs[: -len(masks) - 2], refs[-len(masks) - 2 :]
    block = stacked(pieces)
    held = block.astype(B16)
    outs[0][...] = held
    count = block.shape[0]
    slots = count // rows * capacity
    me = lax.axis_index("expert")
    extra = block[:, width:]
    named = (extra > 0.0).astype(B16)
    lane = lax.broadcasted_iota(jnp.int32, (8, extra.shape[1]), 1)
    line = lax.broadcasted_iota(jnp.int32, (8, extra.shape[1]), 0)
    wanted = jnp.zeros((8, extra.shape[1]), F32)
    for i, mask in enumerate(masks):
        wanted = jnp.where((line == i) & (lane == (me ^ mask) // 2), 1.0, wanted)
    chosen = dot32(wanted.astype(B16), named, NT)
    earlier = lax.broadcasted_iota(jnp.int32, (count, count), 0)
    later = lax.broadcasted_iota(jnp.int32, (count, count), 1)
    before = (earlier // rows == later // rows) & (earlier < later)
    slot = dot32(chosen.astype(B16), before.astype(F32).astype(B16))
    to = lax.broadcasted_iota(jnp.int32, (slots, count), 0)
    of = lax.broadcasted_iota(jnp.int32, (slots, count), 1)
    in_block = to // capacity == of // rows
    place = (to % capacity).astype(F32)
    picks = []
    for i in range(len(masks)):
        pick = in_block & (place == slot[i : i + 1, :]) & (chosen[i : i + 1, :] > 0.5)
        pick = jnp.where(pick, 1.0, 0.0)
        picks.append(pick)
        outs[1 + i][...] = dot32(pick.astype(B16), held).astype(B16)
    outs[-1][...] = jnp.concatenate(picks, axis=0)


def pack_kernel(*refs):
    pick_ref, refs = refs[0], refs[1:]
    ways = pick_ref.shape[0] // refs[-1].shape[0]
    pieces, outs = refs[: -ways - 1], refs[-ways - 1 :]
    held = stacked(pieces).astype(B16)
    outs[0][...] = held
    slots = pick_ref.shape[0] // ways
    for i in range(ways):
        pick = pick_ref[i * slots : (i + 1) * slots, :].astype(B16)
        outs[1 + i][...] = dot32(pick, held).astype(B16)


def pre_kernel(experts, width, gate_ref, up_ref, *refs):
    pieces, (x_ref, prob_ref, pre_gate_ref, pre_up_ref) = refs[:-4], refs[-4:]
    for part in chunks_of(width):
        x_ref[:, part] = jnp.concatenate(
            [piece[:, part].astype(F32) for piece in pieces], axis=0
        ).astype(B16)
    extra = jnp.concatenate([piece[:, width:].astype(F32) for piece in pieces], axis=0)
    lane = lax.broadcasted_iota(jnp.int32, extra.shape, 1)
    own = (lane % experts == lax.axis_index("expert") // 2) & (lane < 2 * experts)
    probs = jnp.sum(jnp.where(own, extra, 0.0), axis=1, keepdims=True)
    prob_ref[...] = jnp.broadcast_to(probs, prob_ref.shape)
    pre_gate_ref[...] = dot32(x_ref[...], gate_ref[...])
    pre_up_ref[...] = dot32(x_ref[...], up_ref[...])


def mid_kernel(
    experts, width, gate_ref, up_ref, down_ref, prob_ref, pre_gate_ref, pre_up_ref, *refs
):
    pieces, outs = refs[:-6], refs[-6:]
    y_ref, hidden_ref, grad_gate_ref, grad_up_ref, mine_ref, give_ref = outs
    for part in chunks_of(width):
        y_ref[:, part] = jnp.concatenate(
            [piece[:, part].astype(F32) for piece in pieces], axis=0
        ).astype(B16)
    grad_full = dot32(y_ref[...], down_ref[...], NT)
    pre_gate, pre_up = pre_gate_ref[...], pre_up_ref[...]
    probs = prob_ref[:, :1]
    routed = probs > 0.0
    sigmoid_gate = jax.nn.sigmoid(pre_gate)
    activated = pre_gate * sigmoid_gate
    hidden = jnp.where(routed, activated * pre_up, 0.0)
    hidden_ref[...] = (hidden * probs).astype(B16)
    own_probs = jnp.sum(hidden * grad_full, axis=1, keepdims=True)
    grad_hidden = grad_full * probs
    grad_gate_ref[...] = jnp.where(
        routed, grad_hidden * pre_up * sigmoid_gate * (1.0 + pre_gate * (1.0 - sigmoid_gate)), 0.0
    ).astype(B16)
    grad_up_ref[...] = jnp.where(routed, grad_hidden * activated, 0.0).astype(B16)
    half = mine_ref.shape[0]
    for part in chunks_of(width):
        product = dot32(grad_gate_ref[...], gate_ref[part, :], NT)
        product = product + dot32(grad_up_ref[...], up_ref[part, :], NT)
        mine_ref[:, part] = product[:half].astype(B16)
        give_ref[:, part] = product[half:].astype(B16)
    lanes = mine_ref.shape[1] - width
    lane = lax.broadcasted_iota(jnp.int32, (2 * half, lanes), 1)
    expert = lax.axis_index("expert") // 2
    high = own_probs.astype(B16).astype(F32)
    extra = jnp.where(lane == expert, high, jnp.where(lane == expert + experts, own_probs - high, 0.0))
    mine_ref[:, width:] = extra[:half].astype(B16)
    give_ref[:, width:] = extra[half:].astype(B16)


def first_sum_kernel(experts, width, mine_ref, other_ref, own_ref, *outs):
    total = mine_ref[...].astype(F32) + other_ref[...].astype(F32)
    count = own_ref.shape[0]
    own_ref[...] = total[:count]
    rest, extra = total[count:, :width], total[count:, width:]
    lane = lax.broadcasted_iota(jnp.int32, extra.shape, 1)
    lost = jnp.where(lane < experts, extra - extra.astype(B16).astype(F32), 0.0)
    extra = extra + pltpu.roll(lost, experts, 1) - lost
    slots = outs[0].shape[0]
    for i, out in enumerate(outs):
        out[:, :width] = rest[i * slots : (i + 1) * slots].astype(B16)
        out[:, width:] = extra[i * slots : (i + 1) * slots].astype(B16)


def second_sum_kernel(pick_ref, own_ref, *refs):
    came, out = refs[:-1], refs[-1]
    out[...] = own_ref[...] + dot32(pick_ref[...].astype(B16), stacked(came).astype(B16), TN)


def grads_kernel(
    x_ref, y_ref, hidden_ref, grad_gate_ref, grad_up_ref, gate_ref, up_ref, down_ref,
    narrow_ref, wide_ref, after_ref, narrow_out, wide_out,
):
    del after_ref
    narrow_out[...] = jnp.zeros_like(narrow_out)
    rank = narrow_ref.shape[1]
    for part in chunks_of(x_ref.shape[1]):
        for i, (grad, weight) in enumerate(((grad_gate_ref, gate_ref), (grad_up_ref, up_ref))):
            masked = dot32(x_ref[:, part], grad[...], TN) * weight[part, :].astype(F32)
            masked = masked.astype(B16)
            lines = pl.ds(i * rank, rank)
            narrow_out[lines, :] += dot32(wide_ref[i, :, part], masked)
            wide_out[lines, part] = dot32(narrow_ref[i], masked, NT)
        masked = dot32(hidden_ref[...], y_ref[:, part], TN) * down_ref[:, part].astype(F32)
        masked = masked.astype(B16)
        lines = pl.ds(2 * rank, rank)
        narrow_out[lines, :] += dot32(wide_ref[2, :, part], masked, NT)
        wide_out[lines, part] = dot32(narrow_ref[2], masked)


def join_halves(mine, other, is_lower):
    return jnp.where(
        is_lower, jnp.concatenate([mine, other], axis=-1), jnp.concatenate([other, mine], axis=-1)
    )


def body(
    tokens,
    cotangent,
    route_probs,
    expert_ids,
    gate_weight,
    up_weight,
    down_weight,
    narrow,
    wide_factors,
):
    rows, width = tokens.shape
    hidden_units = gate_weight.shape[1]
    top_count = expert_ids.shape[1]
    devices = lax.axis_size("expert")
    experts = devices // 2
    capacity = min(rows, max(2, (3 * rows * top_count + 2 * experts - 1) // (2 * experts)))
    is_lower = lax.axis_index("expert") % 2 == 0
    half_width = width // 2
    near, far = stages()[0], stages()[1:]
    count = rows * devices // 2 // (len(near) + 1)
    slots = count // rows * capacity
    half = count + len(near) * slots
    lanes = -(-2 * experts // 128) * 128
    full = width + lanes

    chosen = expert_ids[:, :, None] == jnp.arange(experts, dtype=jnp.int32)[None, None, :]
    dense = jnp.sum(jnp.where(chosen, route_probs[:, :, None], 0.0), axis=1)
    high = dense.astype(B16)
    low = (dense - high.astype(F32)).astype(B16)
    tail = jnp.zeros((rows, lanes - 2 * experts), B16)
    message = jnp.concatenate([tokens, high, low, tail], axis=1)

    def pieces_of(block):
        for masks in reversed(far[1:]):
            block = jnp.concatenate([block] + [send(block, mask) for mask in masks], axis=0)
        if far:
            return [block] + [send(block, mask) for mask in far[0]]
        return [block]

    def all_of(held, packed):
        mine = jnp.concatenate([held] + [send(p, mask) for p, mask in zip(packed, near)], axis=0)
        return [mine, send(mine, 1)]

    token_pieces = pieces_of(message)
    packed_type = [((slots, full), B16)] * len(near)
    held, *packed, pick = in_vmem(
        functools.partial(pack_tokens_kernel, near, rows, capacity, experts, width),
        [((count, full), B16)] + packed_type + [((len(near) * slots, count), F32)],
        token_pieces,
    )
    token_rows = all_of(held, packed)
    cot_pieces = pieces_of(cotangent)
    cot_held, *cot_packed = in_vmem(
        pack_kernel,
        [((count, width), B16)] + [((slots, width), B16)] * len(near),
        [pick] + cot_pieces,
    )
    cot_rows = all_of(cot_held, cot_packed)

    wide = join_halves(wide_factors, send(wide_factors, 1), is_lower)
    matmul = 2 * 2 * half * width * hidden_units
    weight_type = [((width, hidden_units), B16)] * 2 + [((hidden_units, width), B16)]
    weights = (gate_weight, up_weight, down_weight)
    gate_eff, up_eff, down_eff = in_vmem(
        weights_kernel, weight_type, (*weights, narrow, wide), 3 * matmul
    )
    wide_type, unit_type = ((2 * half, width), B16), ((2 * half, hidden_units), B16)
    x, probs, pre_gate, pre_up = in_vmem(
        functools.partial(pre_kernel, experts, width),
        [wide_type, ((2 * half, 128), F32)] + [((2 * half, hidden_units), F32)] * 2,
        (gate_eff, up_eff, *token_rows),
        2 * matmul,
    )
    y, hidden, grad_gate, grad_up, mine, give = in_vmem(
        functools.partial(mid_kernel, experts, width),
        [wide_type] + [unit_type] * 3 + [((half, full), B16)] * 2,
        (gate_eff, up_eff, down_eff, probs, pre_gate, pre_up, *cot_rows),
        3 * matmul,
    )
    own, *parts = in_vmem(
        functools.partial(first_sum_kernel, experts, width),
        [((count, full), F32)] + packed_type,
        (mine, send(give, 1)),
    )
    rank = narrow.shape[1]
    grad_narrow, wide_part = in_vmem(
        grads_kernel,
        [((3 * rank, hidden_units), F32), ((3 * rank, width), F32)],
        (x, y, hidden, grad_gate, grad_up, *weights, narrow, wide, parts[0]),
        9 * matmul,
    )
    (total,) = in_vmem(
        second_sum_kernel,
        [((count, full), F32)],
        (pick, own, *[send(part, mask) for part, mask in zip(parts, near)]),
    )
    for masks in far:
        pieces = jnp.split(total, len(masks) + 1, axis=0)
        total = pieces[0]
        for piece, mask in zip(pieces[1:], masks):
            total = total + send(piece.astype(B16), mask).astype(F32)
    grad_narrow = grad_narrow.reshape(3, rank, hidden_units)
    wide_part = wide_part.reshape(3, rank, width)
    keep_part = jnp.where(is_lower, wide_part[:, :, :half_width], wide_part[:, :, half_width:])
    give_part = jnp.where(is_lower, wide_part[:, :, half_width:], wide_part[:, :, :half_width])
    grad_wide = keep_part + send(give_part.astype(B16), 1).astype(F32)
    grad_tokens = total[:, :width].astype(B16)
    dense_grads = total[:, width : width + experts] + total[:, width + experts : width + 2 * experts]
    grad_probs = jnp.sum(jnp.where(chosen, dense_grads[:, None, :], 0.0), axis=2)
    return (grad_tokens, grad_probs, grad_narrow, grad_wide)


def solution(mesh):
    in_specs = (
        P(("groups", "expert"), None),
        P(("groups", "expert"), None),
        P(("groups", "expert"), None),
        P(("groups", "expert"), None),
        P(None, "expert"),
        P(None, "expert"),
        P("expert", None),
        P(None, None, "expert"),
        P(None, None, "expert"),
    )
    out_specs = (
        P(("groups", "expert"), None),
        P(("groups", "expert"), None),
        P("groups", None, "expert"),
        P("groups", None, "expert"),
    )
    return jax.shard_map(body, mesh=mesh, in_specs=in_specs, out_specs=out_specs, check_vma=False)
```

time: 106 us -> 83.2 us (0.78)
  matrix products: 24.4 us -> 0 us
  Pallas kernels: 0 us -> 19 us
  local copies, waits for them, and re-layouts: 20.8 us -> 7.25 us
  waiting for transfers between devices: 28.1 us -> 23.1 us
  starting transfers between devices: 26.1 us -> 28.9 us
  other arithmetic: 5.55 us -> 3.6 us
    dot_general x16 -> x0, matrix products: 24.4 us -> none  [dot32(): lax.dot_general(left, right, dims, preferred_element_type=jnp.float32)]
    pallas_call x0 -> x8, Pallas kernels: none -> 19 us  [in_vmem(): pl.pallas_call(kernel, out_shape=[pltpu.VMEM(shape, dtype) for shape, dty...]
    unnamed x42 -> x23, local copies, waits for them, and re-layouts: 19 us -> 5.66 us
    ppermute x23, waiting for transfers between devices: 28.1 us -> 23.1 us  [send(): return lax.ppermute(value, 'expert', pairs)]
    ppermute x23, starting transfers between devices: 26.1 us -> 28.9 us  [send(): return lax.ppermute(value, 'expert', pairs)]
    unnamed x1 -> x0, other arithmetic: 1.45 us -> none
  transfers between devices with their start and end apart: 23 -> 23, of which waited for: 9 -> 7; matrix products, arithmetic and copies ran while one was open for 21% -> 3% of each run, Pallas kernels for 0% -> 18%
where the time goes in v2:
time: 83.2 us; the launch traced here: 82.8 us
  starting transfers between devices  28.9 us (35%)
  waiting for transfers between devices  23.1 us (28%)
  Pallas kernels  19 us (23%)
  local copies, waits for them, and re-layouts  7.25 us (9%)
  other arithmetic  3.6 us (4%)
  between operations  0.92 us (1%)
    ppermute x23, starting transfers between devices, send(): return lax.ppermute(value, 'expert', pairs)  28.9 us
    ppermute x23, waiting for transfers between devices, send(): return lax.ppermute(value, 'expert', pairs)  23.1 us
    pallas_call x8, Pallas kernels, in_vmem(): pl.pallas_call(kernel, out_shape=[pltpu.VMEM(shape, dtype) for shape, dty...  19 us
    unnamed x23, local copies, waits for them, and re-layouts  5.66 us
  transfers between devices with their start and end apart: 23, of which 7 were waited for; matrix products, arithmetic and copies ran while one was open for 3% of the time, Pallas kernels for 18%

profile of v2, /device:TPU:0, one launch (start us, length us, event | category | flops | bytes accessed | tf_op | source)
XLA Modules:
  0.0 82.8 jit_solution(17209609266593836462)
XLA Ops:
  0.6 0.8 select_reduce_fusion.1
  1.5 0.9 %concatenate.15.refs_0_ = bf16[8,3712]{1,0:T(8,128)(2,1)S(1)} concatenate(bf16[8,3584]{1,0:T(8,128)(2,1)} %param.9, bf16[8,16]{1,0:T(8,128)(2,1)S(1)} %get-tuple-element.61, bf16[8,16]{1,0:T(8,128)(2,1)S(1)} %get-tuple-element.60, bf16[8,96]{1,0:T(8,128)(2,1)S(1)} %broadcast_in_dim.31), dimensions={1} | concatenate | bytes 118784 | tf_op jit(solution)/shard_map/concatenate | solution.py:244
  2.4 5.0 %collective-permute-start.2 = (bf16[8,3712]{1,0:T(8,128)(2,1)S(1)}, bf16[8,3712]{1,0:T(8,128)(2,1)S(1)}, u32[]{:S(2)}, u32[]{:S(2)}) collective-permute-start(bf16[8,3712]{1,0:T(8,128)(2,1)S(1)} %concatenate.15.refs_0_), channel_id=1, source_target_pairs={{0,24},{1,25},{2,26},{3,27},{4,28},{5,29},{6,30},{7,31},{8,16},{9,... | collective-permute-start | bytes 178184 | tf_op jit(solution)/shard_map/ppermute | solution.py:18
  7.4 0.0 collective-permute-start.1
  7.4 0.6 collective-permute-start
  8.1 2.3 %collective-permute-start.9 = (bf16[8,3584]{1,0:T(8,128)(2,1)}, bf16[8,3584]{1,0:T(8,128)(2,1)S(1)}, u32[]{:S(2)}, u32[]{:S(2)}) collective-permute-start(bf16[8,3584]{1,0:T(8,128)(2,1)} %refs_1_.1), channel_id=1, source_target_pairs={{0,16},{1,17},{2,18},{3,19},{4,20},{5,21},{6,22},{7,23},{8,24},{9,... | collective-permute-start | bytes 172040 | tf_op jit(solution)/shard_map/ppermute | solution.py:18
  10.4 2.0 %collective-permute-start.8 = (bf16[8,3584]{1,0:T(8,128)(2,1)}, bf16[8,3584]{1,0:T(8,128)(2,1)S(1)}, u32[]{:S(2)}, u32[]{:S(2)}) collective-permute-start(bf16[8,3584]{1,0:T(8,128)(2,1)} %refs_1_.1), channel_id=1, source_target_pairs={{0,8},{1,9},{2,10},{3,11},{4,12},{5,13},{6,14},{7,15},{8,0},{9,1},... | collective-permute-start | bytes 172040 | tf_op jit(solution)/shard_map/ppermute | solution.py:18
  12.4 0.0 collective-permute-done.2.refs_3_
  12.4 1.7 %collective-permute-start.10 = (bf16[8,3584]{1,0:T(8,128)(2,1)}, bf16[8,3584]{1,0:T(8,128)(2,1)S(1)}, u32[]{:S(2)}, u32[]{:S(2)}) collective-permute-start(bf16[8,3584]{1,0:T(8,128)(2,1)} %refs_1_.1), channel_id=1, source_target_pairs={{0,24},{1,25},{2,26},{3,27},{4,28},{5,29},{6,30},{7,31},{8,16},{9,... | collective-permute-start | bytes 172040 | tf_op jit(solution)/shard_map/ppermute | solution.py:18
  14.1 0.0 collective-permute-done.1.refs_2_
  14.1 0.0 collective-permute-start.3
  14.1 0.0 collective-permute-done.refs_1_
  14.1 0.6 shard_map.120
  14.7 1.6 %collective-permute-start.4 = (bf16[24,3712]{1,0:T(8,128)(2,1)S(1)}, bf16[24,3712]{1,0:T(8,128)(2,1)S(1)}, u32[]{:S(2)}, u32[]{:S(2)}) collective-permute-start(bf16[24,3712]{1,0:T(8,128)(2,1)S(1)} %get-tuple-element.37), channel_id=1, source_target_pairs={{0,2},{1,3},{2,0},{3,1},{4,6},{5,7},{6,4},{7,5},{8,10},{9,11},{10,... | collective-permute-start | bytes 534536 | tf_op jit(solution)/shard_map/ppermute | solution.py:18
  16.3 0.0 collective-permute-done.9.refs_3_
  16.3 1.6 %collective-permute-start.5 = (bf16[24,3712]{1,0:T(8,128)(2,1)S(1)}, bf16[24,3712]{1,0:T(8,128)(2,1)S(1)}, u32[]{:S(2)}, u32[]{:S(2)}) collective-permute-start(bf16[24,3712]{1,0:T(8,128)(2,1)S(1)} %get-tuple-element.38), channel_id=1, source_target_pairs={{0,4},{1,5},{2,6},{3,7},{4,0},{5,1},{6,2},{7,3},{8,12},{9,13},{10,... | collective-permute-start | bytes 534536 | tf_op jit(solution)/shard_map/ppermute | solution.py:18
  17.9 0.0 collective-permute-done.8.refs_2_
  17.9 1.4 %collective-permute-start.6 = (bf16[24,3712]{1,0:T(8,128)(2,1)S(1)}, bf16[24,3712]{1,0:T(8,128)(2,1)S(1)}, u32[]{:S(2)}, u32[]{:S(2)}) collective-permute-start(bf16[24,3712]{1,0:T(8,128)(2,1)S(1)} %get-tuple-element.39), channel_id=1, source_target_pairs={{0,6},{1,7},{2,4},{3,5},{4,2},{5,3},{6,0},{7,1},{8,14},{9,15},{10,... | collective-permute-start | bytes 534536 | tf_op jit(solution)/shard_map/ppermute | solution.py:18
  19.2 0.0 collective-permute-done.10.refs_4_
  19.2 0.8 copy-done.5
  20.0 0.3 shard_map.123
  20.4 0.9 %collective-permute-start.11 = (bf16[24,3584]{1,0:T(8,128)(2,1)S(1)}, bf16[24,3584]{1,0:T(8,128)(2,1)S(1)}, u32[]{:S(2)}, u32[]{:S(2)}) collective-permute-start(bf16[24,3584]{1,0:T(8,128)(2,1)S(1)} %get-tuple-element.44), channel_id=1, source_target_pairs={{0,2},{1,3},{2,0},{3,1},{4,6},{5,7},{6,4},{7,5},{8,10},{9,11},{10,... | collective-permute-start | bytes 516104 | tf_op jit(solution)/shard_map/ppermute | solution.py:18
  21.3 7.9 %collective-permute-done.11 = bf16[24,3584]{1,0:T(8,128)(2,1)S(1)} collective-permute-done((bf16[24,3584]{1,0:T(8,128)(2,1)S(1)}, bf16[24,3584]{1,0:T(8,128)(2,1)S(1)}, u32[]{:S(2)}, u32[]{:S(2)}) %collective-permute-start.11) | collective-permute-done | bytes 172064 | tf_op jit(solution)/shard_map/ppermute | solution.py:18
  29.2 1.5 %collective-permute-start.12 = (bf16[24,3584]{1,0:T(8,128)(2,1)S(1)}, bf16[24,3584]{1,0:T(8,128)(2,1)S(1)}, u32[]{:S(2)}, u32[]{:S(2)}) collective-permute-start(bf16[24,3584]{1,0:T(8,128)(2,1)S(1)} %get-tuple-element.45), channel_id=1, source_target_pairs={{0,4},{1,5},{2,6},{3,7},{4,0},{5,1},{6,2},{7,3},{8,12},{9,13},{10,... | collective-permute-start | bytes 516104 | tf_op jit(solution)/shard_map/ppermute | solution.py:18
  30.7 4.5 %collective-permute-done.12 = bf16[24,3584]{1,0:T(8,128)(2,1)S(1)} collective-permute-done((bf16[24,3584]{1,0:T(8,128)(2,1)S(1)}, bf16[24,3584]{1,0:T(8,128)(2,1)S(1)}, u32[]{:S(2)}, u32[]{:S(2)}) %collective-permute-start.12) | collective-permute-done | bytes 172064 | tf_op jit(solution)/shard_map/ppermute | solution.py:18
  35.2 2.4 %collective-permute-start.13 = (bf16[24,3584]{1,0:T(8,128)(2,1)S(1)}, bf16[24,3584]{1,0:T(8,128)(2,1)S(1)}, u32[]{:S(2)}, u32[]{:S(2)}) collective-permute-start(bf16[24,3584]{1,0:T(8,128)(2,1)S(1)} %get-tuple-element.46), channel_id=1, source_target_pairs={{0,6},{1,7},{2,4},{3,5},{4,2},{5,3},{6,0},{7,1},{8,14},{9,15},{10,... | collective-permute-start | bytes 516104 | tf_op jit(solution)/shard_map/ppermute | solution.py:18
  37.7 0.0 collective-permute-done.4
  37.7 0.0 collective-permute-done.5
  37.7 0.0 collective-permute-done.6
  37.8 0.1 collective-permute-start.7
  37.9 3.7 %collective-permute-done.13 = bf16[24,3584]{1,0:T(8,128)(2,1)S(1)} collective-permute-done((bf16[24,3584]{1,0:T(8,128)(2,1)S(1)}, bf16[24,3584]{1,0:T(8,128)(2,1)S(1)}, u32[]{:S(2)}, u32[]{:S(2)}) %collective-permute-start.13) | collective-permute-done | bytes 172064 | tf_op jit(solution)/shard_map/ppermute | solution.py:18
  41.5 0.1 collective-permute-start.14
  41.6 1.1 %maximum_select_fusion.wide_ref = bf16[3,16,3584]{2,1,0:T(8,128)(2,1)S(1)} fusion(bf16[3,16,1792]{2,1,0:T(8,128)(2,1)S(1)} %collective-permute-done.3, bf16[3,16,1792]{2,1,0:T(8,128)(2,1)} %param.17, pred[]{:T(512)S(6)} %eq.21), kind=kLoop, calls=%fused_computation | loop fusion | flops 1548288 | bytes 688129 | tf_op jit(solution)/shard_map/jit(_where)/select_n | solution.py:208
  42.7 0.0 copy-start.1
  42.8 2.0 %copy-done.1 = bf16[3584,512]{1,0:T(8,128)(2,1)S(1)} copy-done((bf16[3584,512]{1,0:T(8,128)(2,1)S(1)}, bf16[3584,512]{1,0:T(8,128)(2,1)}, u32[]{:S(2)}) %copy-start.1) | copy-done | bytes 3670040
  44.8 2.0 %copy-done.3 = bf16[512,3584]{1,0:T(8,128)(2,1)S(1)} copy-done((bf16[512,3584]{1,0:T(8,128)(2,1)S(1)}, bf16[512,3584]{1,0:T(8,128)(2,1)}, u32[]{:S(2)}) %copy-start.3) | copy-done | bytes 3670040
  46.8 3.0 %shard_map.121 = (bf16[3584,512]{1,0:T(8,128)(2,1)S(1)}, bf16[3584,512]{1,0:T(8,128)(2,1)S(1)}, bf16[512,3584]{1,0:T(8,128)(2,1)S(1)}) custom-call(bf16[3584,512]{1,0:T(8,128)(2,1)S(1)} %copy-done, bf16[3584,512]{1,0:T(8,128)(2,1)S(1)} %copy-done.1, bf16[512,3584]{1,0:T(8,128)(2,1)S(1)} %copy-done.3, bf16[3,16,512]{2,1,0:T(8,128)(2,1)S(1)} %copy-done.6, ...), custom_call_target="tpu_custom_call" | custom-call | flops 2290089984 | bytes 22413312 | tf_op jit(solution)/shard_map/pallas_call | solution.py:39
  49.9 0.0 collective-permute-done.7.refs_1_
  49.9 1.7 %shard_map.122 = (bf16[208,3584]{1,0:T(8,128)(2,1)S(1)}, f32[208,128]{1,0:T(8,128)S(1)}, f32[208,512]{1,0:T(8,128)S(1)}, f32[208,512]{1,0:T(8,128)S(1)}) custom-call(bf16[3584,512]{1,0:T(8,128)(2,1)S(1)} %get-tuple-element.33.gate_ref, bf16[3584,512]{1,0:T(8,128)(2,1)S(1)} %get-tuple-element.34.up_ref, ...), custom_call_target="tpu_custom_call" | custom-call | flops 1526726656 | bytes 11333632 | tf_op jit(solution)/shard_map/pallas_call | solution.py:39
  51.6 0.0 copy-start.2
  51.6 0.0 copy-start.4
  51.6 3.8 %shard_map.124 = (bf16[208,3584]{1,0:T(8,128)(2,1)S(1)}, bf16[208,512]{1,0:T(8,128)(2,1)S(1)}, bf16[208,512]{1,0:T(8,128)(2,1)S(1)}, bf16[208,512]{1,0:T(8,128)(...) custom-call(bf16[3584,512]{1,0:T(8,128)(2,1)S(1)} %get-tuple-element.33.gate_ref, ...), custom_call_target="tpu_custom_call" | custom-call | flops 2290089984 | bytes 17133568 | tf_op jit(solution)/shard_map/pallas_call | solution.py:39
  55.5 0.6 collective-permute-start.15
  56.1 1.9 %collective-permute-done.15.other_ref = bf16[104,3712]{1,0:T(8,128)(2,1)S(1)} collective-permute-done((bf16[104,3712]{1,0:T(8,128)(2,1)S(1)}, bf16[104,3712]{1,0:T(8,128)(2,1)S(1)}, u32[]{:S(2)}, u32[]{:S(2)}) %collective-permute-start.15) | collective-permute-done | bytes 772128 | tf_op jit(solution)/shard_map/ppermute | solution.py:18
  58.0 0.3 shard_map.125
  58.3 1.6 %collective-permute-start.17 = (bf16[24,3712]{1,0:T(8,128)(2,1)S(1)}, bf16[24,3712]{1,0:T(8,128)(2,1)S(1)}, u32[]{:S(2)}, u32[]{:S(2)}) collective-permute-start(bf16[24,3712]{1,0:T(8,128)(2,1)S(1)} %get-tuple-element.51), channel_id=1, source_target_pairs={{0,4},{1,5},{2,6},{3,7},{4,0},{5,1},{6,2},{7,3},{8,12},{9,13},{10,... | collective-permute-start | bytes 534536 | tf_op jit(solution)/shard_map/ppermute | solution.py:18
  59.9 1.4 %collective-permute-start.18 = (bf16[24,3712]{1,0:T(8,128)(2,1)S(1)}, bf16[24,3712]{1,0:T(8,128)(2,1)S(1)}, u32[]{:S(2)}, u32[]{:S(2)}) collective-permute-start(bf16[24,3712]{1,0:T(8,128)(2,1)S(1)} %get-tuple-element.52), channel_id=1, source_target_pairs={{0,6},{1,7},{2,4},{3,5},{4,2},{5,3},{6,0},{7,1},{8,14},{9,15},{10,... | collective-permute-start | bytes 534536 | tf_op jit(solution)/shard_map/ppermute | solution.py:18
  61.3 0.5 collective-permute-start.16
  61.9 8.9 %shard_map.127 = (f32[48,512]{1,0:T(8,128)S(1)}, f32[48,3584]{1,0:T(8,128)S(1)}) custom-call(bf16[208,3584]{1,0:T(8,128)(2,1)S(1)} %get-tuple-element.53.x_ref, bf16[208,3584]{1,0:T(8,128)(2,1)S(1)} %get-tuple-element.54.y_ref, bf16[208,512]{1,0:T(8,128)(2,1)S(1)} %get-tuple-element.55.hidden_ref, bf16[208,512]{1,0:T(8,128)(2,1)S(1)} %get-tuple-element.56.grad_gate_ref, ...), custom_call_target="tpu_custom_call" | custom-call | flops 6870269952 | bytes 15988736 | tf_op jit(solution)/shard_map/pallas_call | solution.py:39
  70.9 0.6 copy.19
  71.5 0.0 collective-permute-start.22
  71.5 0.0 collective-permute-done.17.refs_1_
  71.5 0.0 collective-permute-done.18.refs_2_
  71.5 0.3 shard_map.126
  71.9 0.1 collective-permute-start.19
  71.9 2.4 %collective-permute-start.21 = (bf16[8,3712]{1,0:T(8,128)(2,1)S(1)}, bf16[8,3712]{1,0:T(8,128)(2,1)S(1)}, u32[]{:S(2)}, u32[]{:S(2)}) collective-permute-start(bf16[8,3712]{1,0:T(8,128)(2,1)S(1)} %get-tuple-element.63), channel_id=1, source_target_pairs={{0,24},{1,25},{2,26},{3,27},{4,28},{5,29},{6,30},{7,31},{8,16},{9,... | collective-permute-start | bytes 178184 | tf_op jit(solution)/shard_map/ppermute | solution.py:18
  74.3 1.1 %collective-permute-start.20 = (bf16[8,3712]{1,0:T(8,128)(2,1)S(1)}, bf16[8,3712]{1,0:T(8,128)(2,1)S(1)}, u32[]{:S(2)}, u32[]{:S(2)}) collective-permute-start(bf16[8,3712]{1,0:T(8,128)(2,1)S(1)} %get-tuple-element.64), channel_id=1, source_target_pairs={{0,16},{1,17},{2,18},{3,19},{4,20},{5,21},{6,22},{7,23},{8,24},{9,... | collective-permute-start | bytes 178184 | tf_op jit(solution)/shard_map/ppermute | solution.py:18
  75.4 0.8 convert_add_fusion
  76.2 0.1 collective-permute-done.19
  76.3 2.0 %collective-permute-done.21 = bf16[8,3712]{1,0:T(8,128)(2,1)S(1)} collective-permute-done((bf16[8,3712]{1,0:T(8,128)(2,1)S(1)}, bf16[8,3712]{1,0:T(8,128)(2,1)S(1)}, u32[]{:S(2)}, u32[]{:S(2)}) %collective-permute-start.21) | collective-permute-done | bytes 59424 | tf_op jit(solution)/shard_map/ppermute | solution.py:18
  78.3 3.1 %collective-permute-done.20 = bf16[8,3712]{1,0:T(8,128)(2,1)S(1)} collective-permute-done((bf16[8,3712]{1,0:T(8,128)(2,1)S(1)}, bf16[8,3712]{1,0:T(8,128)(2,1)S(1)}, u32[]{:S(2)}, u32[]{:S(2)}) %collective-permute-start.20) | collective-permute-done | bytes 59424 | tf_op jit(solution)/shard_map/ppermute | solution.py:18
  81.4 0.1 slice_add_fusion.1
  81.5 0.6 slice.35
  82.1 0.7 select_reduce_fusion
  (28 shorter events, 0.3 us)
Async XLA Ops:
  0.6 42.1 %copy-start.6 = (bf16[3,16,512]{2,1,0:T(8,128)(2,1)S(1)}, bf16[3,16,512]{2,1,0:T(8,128)(2,1)}, u32[]{:S(2)}) copy-start(bf16[3,16,512]{2,1,0:T(8,128)(2,1)} %narrow_ref.3) | copy-start | bytes 147460
  2.4 10.0 %collective-permute-start.2 = (bf16[8,3712]{1,0:T(8,128)(2,1)S(1)}, bf16[8,3712]{1,0:T(8,128)(2,1)S(1)}, u32[]{:S(2)}, u32[]{:S(2)}) collective-permute-start(bf16[8,3712]{1,0:T(8,128)(2,1)S(1)} %concatenate.15.refs_0_), channel_id=1, source_target_pairs={{0,24},{1,25},{2,26},{3,27},{4,28},{5,29},{6,30},{7,31},{8,16},{9,... | collective-permute-start | bytes 178184 | tf_op jit(solution)/shard_map/ppermute | solution.py:18
  7.4 6.7 %collective-permute-start.1 = (bf16[8,3712]{1,0:T(8,128)(2,1)S(1)}, bf16[8,3712]{1,0:T(8,128)(2,1)S(1)}, u32[]{:S(2)}, u32[]{:S(2)}) collective-permute-start(bf16[8,3712]{1,0:T(8,128)(2,1)S(1)} %concatenate.15.refs_0_), channel_id=1, source_target_pairs={{0,16},{1,17},{2,18},{3,19},{4,20},{5,21},{6,22},{7,23},{8,24},{9,... | collective-permute-start | bytes 178184 | tf_op jit(solution)/shard_map/ppermute | solution.py:18
  7.4 6.7 %collective-permute-start = (bf16[8,3712]{1,0:T(8,128)(2,1)S(1)}, bf16[8,3712]{1,0:T(8,128)(2,1)S(1)}, u32[]{:S(2)}, u32[]{:S(2)}) collective-permute-start(bf16[8,3712]{1,0:T(8,128)(2,1)S(1)} %concatenate.15.refs_0_), channel_id=1, source_target_pairs={{0,8},{1,9},{2,10},{3,11},{4,12},{5,13},{6,14},{7,15},{8,0},{9,1},... | collective-permute-start | bytes 178184 | tf_op jit(solution)/shard_map/ppermute | solution.py:18
  8.1 8.2 %collective-permute-start.9 = (bf16[8,3584]{1,0:T(8,128)(2,1)}, bf16[8,3584]{1,0:T(8,128)(2,1)S(1)}, u32[]{:S(2)}, u32[]{:S(2)}) collective-permute-start(bf16[8,3584]{1,0:T(8,128)(2,1)} %refs_1_.1), channel_id=1, source_target_pairs={{0,16},{1,17},{2,18},{3,19},{4,20},{5,21},{6,22},{7,23},{8,24},{9,... | collective-permute-start | bytes 172040 | tf_op jit(solution)/shard_map/ppermute | solution.py:18
  10.4 7.5 %collective-permute-start.8 = (bf16[8,3584]{1,0:T(8,128)(2,1)}, bf16[8,3584]{1,0:T(8,128)(2,1)S(1)}, u32[]{:S(2)}, u32[]{:S(2)}) collective-permute-start(bf16[8,3584]{1,0:T(8,128)(2,1)} %refs_1_.1), channel_id=1, source_target_pairs={{0,8},{1,9},{2,10},{3,11},{4,12},{5,13},{6,14},{7,15},{8,0},{9,1},... | collective-permute-start | bytes 172040 | tf_op jit(solution)/shard_map/ppermute | solution.py:18
  12.4 30.3 %copy-start = (bf16[3584,512]{1,0:T(8,128)(2,1)S(1)}, bf16[3584,512]{1,0:T(8,128)(2,1)}, u32[]{:S(2)}) copy-start(bf16[3584,512]{1,0:T(8,128)(2,1)} %gate_ref.3) | copy-start | bytes 11010052
  12.4 6.8 %collective-permute-start.10 = (bf16[8,3584]{1,0:T(8,128)(2,1)}, bf16[8,3584]{1,0:T(8,128)(2,1)S(1)}, u32[]{:S(2)}, u32[]{:S(2)}) collective-permute-start(bf16[8,3584]{1,0:T(8,128)(2,1)} %refs_1_.1), channel_id=1, source_target_pairs={{0,24},{1,25},{2,26},{3,27},{4,28},{5,29},{6,30},{7,31},{8,16},{9,... | collective-permute-start | bytes 172040 | tf_op jit(solution)/shard_map/ppermute | solution.py:18
  14.1 27.5 %collective-permute-start.3 = (bf16[3,16,1792]{2,1,0:T(8,128)(2,1)}, bf16[3,16,1792]{2,1,0:T(8,128)(2,1)S(1)}, u32[]{:S(2)}, u32[]{:S(2)}) collective-permute-start(bf16[3,16,1792]{2,1,0:T(8,128)(2,1)} %param.17), channel_id=1, source_target_pairs={{0,1},{1,0},{2,3},{3,2},{4,5},{5,4},{6,7},{7,6},{8,9},{9,8},{10,11... | collective-permute-start | bytes 516104 | tf_op jit(solution)/shard_map/ppermute | solution.py:18
  14.7 23.0 %collective-permute-start.4 = (bf16[24,3712]{1,0:T(8,128)(2,1)S(1)}, bf16[24,3712]{1,0:T(8,128)(2,1)S(1)}, u32[]{:S(2)}, u32[]{:S(2)}) collective-permute-start(bf16[24,3712]{1,0:T(8,128)(2,1)S(1)} %get-tuple-element.37), channel_id=1, source_target_pairs={{0,2},{1,3},{2,0},{3,1},{4,6},{5,7},{6,4},{7,5},{8,10},{9,11},{10,... | collective-permute-start | bytes 534536 | tf_op jit(solution)/shard_map/ppermute | solution.py:18
  16.3 21.4 %collective-permute-start.5 = (bf16[24,3712]{1,0:T(8,128)(2,1)S(1)}, bf16[24,3712]{1,0:T(8,128)(2,1)S(1)}, u32[]{:S(2)}, u32[]{:S(2)}) collective-permute-start(bf16[24,3712]{1,0:T(8,128)(2,1)S(1)} %get-tuple-element.38), channel_id=1, source_target_pairs={{0,4},{1,5},{2,6},{3,7},{4,0},{5,1},{6,2},{7,3},{8,12},{9,13},{10,... | collective-permute-start | bytes 534536 | tf_op jit(solution)/shard_map/ppermute | solution.py:18
  17.9 19.9 %collective-permute-start.6 = (bf16[24,3712]{1,0:T(8,128)(2,1)S(1)}, bf16[24,3712]{1,0:T(8,128)(2,1)S(1)}, u32[]{:S(2)}, u32[]{:S(2)}) collective-permute-start(bf16[24,3712]{1,0:T(8,128)(2,1)S(1)} %get-tuple-element.39), channel_id=1, source_target_pairs={{0,6},{1,7},{2,4},{3,5},{4,2},{5,3},{6,0},{7,1},{8,14},{9,15},{10,... | collective-permute-start | bytes 534536 | tf_op jit(solution)/shard_map/ppermute | solution.py:18
  19.2 0.8 copy-start.5
  20.4 8.8 %collective-permute-start.11 = (bf16[24,3584]{1,0:T(8,128)(2,1)S(1)}, bf16[24,3584]{1,0:T(8,128)(2,1)S(1)}, u32[]{:S(2)}, u32[]{:S(2)}) collective-permute-start(bf16[24,3584]{1,0:T(8,128)(2,1)S(1)} %get-tuple-element.44), channel_id=1, source_target_pairs={{0,2},{1,3},{2,0},{3,1},{4,6},{5,7},{6,4},{7,5},{8,10},{9,11},{10,... | collective-permute-start | bytes 516104 | tf_op jit(solution)/shard_map/ppermute | solution.py:18
  29.2 6.0 %collective-permute-start.12 = (bf16[24,3584]{1,0:T(8,128)(2,1)S(1)}, bf16[24,3584]{1,0:T(8,128)(2,1)S(1)}, u32[]{:S(2)}, u32[]{:S(2)}) collective-permute-start(bf16[24,3584]{1,0:T(8,128)(2,1)S(1)} %get-tuple-element.45), channel_id=1, source_target_pairs={{0,4},{1,5},{2,6},{3,7},{4,0},{5,1},{6,2},{7,3},{8,12},{9,13},{10,... | collective-permute-start | bytes 516104 | tf_op jit(solution)/shard_map/ppermute | solution.py:18
  35.2 6.3 %collective-permute-start.13 = (bf16[24,3584]{1,0:T(8,128)(2,1)S(1)}, bf16[24,3584]{1,0:T(8,128)(2,1)S(1)}, u32[]{:S(2)}, u32[]{:S(2)}) collective-permute-start(bf16[24,3584]{1,0:T(8,128)(2,1)S(1)} %get-tuple-element.46), channel_id=1, source_target_pairs={{0,6},{1,7},{2,4},{3,5},{4,2},{5,3},{6,0},{7,1},{8,14},{9,15},{10,... | collective-permute-start | bytes 516104 | tf_op jit(solution)/shard_map/ppermute | solution.py:18
  37.8 12.1 %collective-permute-start.7 = (bf16[104,3712]{1,0:T(8,128)(2,1)S(1)}, bf16[104,3712]{1,0:T(8,128)(2,1)S(1)}, u32[]{:S(2)}, u32[]{:S(2)}) collective-permute-start(bf16[104,3712]{1,0:T(8,128)(2,1)S(1)} %constant_dynamic-update-slice_fusion.refs_0_), channel_id=1, source_target_pairs={{0,1},{1,0},{2,3},{3,2},{4,5},{5,4},{6,7},{7,6},{8,9},{9,8},{10,11... | collective-permute-start | bytes 2316296 | tf_op jit(solution)/shard_map/ppermute | solution.py:18
  41.5 10.1 %collective-permute-start.14 = (bf16[104,3584]{1,0:T(8,128)(2,1)S(1)}, bf16[104,3584]{1,0:T(8,128)(2,1)S(1)}, u32[]{:S(2)}, u32[]{:S(2)}) collective-permute-start(bf16[104,3584]{1,0:T(8,128)(2,1)S(1)} %constant_dynamic-update-slice_fusion.4.refs_0_), channel_id=1, source_target_pairs={{0,1},{1,0},{2,3},{3,2},{4,5},{5,4},{6,7},{7,6},{8,9},{9,8},{10,11... | collective-permute-start | bytes 2236424 | tf_op jit(solution)/shard_map/ppermute | solution.py:18
  42.7 2.0 %copy-start.1 = (bf16[3584,512]{1,0:T(8,128)(2,1)S(1)}, bf16[3584,512]{1,0:T(8,128)(2,1)}, u32[]{:S(2)}) copy-start(bf16[3584,512]{1,0:T(8,128)(2,1)} %up_ref.3) | copy-start | bytes 11010052
  44.8 2.0 %copy-start.3 = (bf16[512,3584]{1,0:T(8,128)(2,1)S(1)}, bf16[512,3584]{1,0:T(8,128)(2,1)}, u32[]{:S(2)}) copy-start(bf16[512,3584]{1,0:T(8,128)(2,1)} %down_ref.3) | copy-start | bytes 11010052
  51.6 10.3 %copy-start.2 = (bf16[3584,512]{1,0:T(8,128)(2,1)S(1)}, bf16[3584,512]{1,0:T(8,128)(2,1)}, u32[]{:S(2)}) copy-start(bf16[3584,512]{1,0:T(8,128)(2,1)} %up_ref.3) | copy-start | bytes 11010052
  51.6 10.2 %copy-start.4 = (bf16[512,3584]{1,0:T(8,128)(2,1)S(1)}, bf16[512,3584]{1,0:T(8,128)(2,1)}, u32[]{:S(2)}) copy-start(bf16[512,3584]{1,0:T(8,128)(2,1)} %down_ref.3) | copy-start | bytes 11010052
  55.5 2.5 %collective-permute-start.15 = (bf16[104,3712]{1,0:T(8,128)(2,1)S(1)}, bf16[104,3712]{1,0:T(8,128)(2,1)S(1)}, u32[]{:S(2)}, u32[]{:S(2)}) collective-permute-start(bf16[104,3712]{1,0:T(8,128)(2,1)S(1)} %get-tuple-element.48), channel_id=1, source_target_pairs={{0,1},{1,0},{2,3},{3,2},{4,5},{5,4},{6,7},{7,6},{8,9},{9,8},{10,11... | collective-permute-start | bytes 2316296 | tf_op jit(solution)/shard_map/ppermute | solution.py:18
  58.3 13.2 %collective-permute-start.17 = (bf16[24,3712]{1,0:T(8,128)(2,1)S(1)}, bf16[24,3712]{1,0:T(8,128)(2,1)S(1)}, u32[]{:S(2)}, u32[]{:S(2)}) collective-permute-start(bf16[24,3712]{1,0:T(8,128)(2,1)S(1)} %get-tuple-element.51), channel_id=1, source_target_pairs={{0,4},{1,5},{2,6},{3,7},{4,0},{5,1},{6,2},{7,3},{8,12},{9,13},{10,... | collective-permute-start | bytes 534536 | tf_op jit(solution)/shard_map/ppermute | solution.py:18
  59.9 11.6 %collective-permute-start.18 = (bf16[24,3712]{1,0:T(8,128)(2,1)S(1)}, bf16[24,3712]{1,0:T(8,128)(2,1)S(1)}, u32[]{:S(2)}, u32[]{:S(2)}) collective-permute-start(bf16[24,3712]{1,0:T(8,128)(2,1)S(1)} %get-tuple-element.52), channel_id=1, source_target_pairs={{0,6},{1,7},{2,4},{3,5},{4,2},{5,3},{6,0},{7,1},{8,14},{9,15},{10,... | collective-permute-start | bytes 534536 | tf_op jit(solution)/shard_map/ppermute | solution.py:18
  61.3 10.2 %collective-permute-start.16 = (bf16[24,3712]{1,0:T(8,128)(2,1)S(1)}, bf16[24,3712]{1,0:T(8,128)(2,1)S(1)}, u32[]{:S(2)}, u32[]{:S(2)}) collective-permute-start(bf16[24,3712]{1,0:T(8,128)(2,1)S(1)} %get-tuple-element.50.after_ref), channel_id=1, source_target_pairs={{0,2},{1,3},{2,0},{3,1},{4,6},{5,7},{6,4},{7,5},{8,10},{9,11},{10,... | collective-permute-start | bytes 534536 | tf_op jit(solution)/shard_map/ppermute | solution.py:18
  70.8 11.3 %copy-start.7 = (s32[8,8]{1,0:T(8,128)S(1)}, s32[8,8]{1,0:T(8,128)}, u32[]{:S(2)}) copy-start(s32[8,8]{1,0:T(8,128)} %param.12) | copy-start | bytes 772
  71.5 3.9 %collective-permute-start.22 = (bf16[3,16,1792]{2,1,0:T(8,128)(2,1)S(1)}, bf16[3,16,1792]{2,1,0:T(8,128)(2,1)S(1)}, u32[]{:S(2)}, u32[]{:S(2)}) collective-permute-start(bf16[3,16,1792]{2,1,0:T(8,128)(2,1)S(1)} %select_convert_fusion), channel_id=1, source_target_pairs={{0,1},{1,0},{2,3},{3,2},{4,5},{5,4},{6,7},{7,6},{8,9},{9,8},{10,11... | collective-permute-start | bytes 516104 | tf_op jit(solution)/shard_map/ppermute | solution.py:18
  71.9 4.4 %collective-permute-start.19 = (bf16[8,3712]{1,0:T(8,128)(2,1)S(1)}, bf16[8,3712]{1,0:T(8,128)(2,1)S(1)}, u32[]{:S(2)}, u32[]{:S(2)}) collective-permute-start(bf16[8,3712]{1,0:T(8,128)(2,1)S(1)} %get-tuple-element.62), channel_id=1, source_target_pairs={{0,8},{1,9},{2,10},{3,11},{4,12},{5,13},{6,14},{7,15},{8,0},{9,1},... | collective-permute-start | bytes 178184 | tf_op jit(solution)/shard_map/ppermute | solution.py:18
  71.9 6.3 %collective-permute-start.21 = (bf16[8,3712]{1,0:T(8,128)(2,1)S(1)}, bf16[8,3712]{1,0:T(8,128)(2,1)S(1)}, u32[]{:S(2)}, u32[]{:S(2)}) collective-permute-start(bf16[8,3712]{1,0:T(8,128)(2,1)S(1)} %get-tuple-element.63), channel_id=1, source_target_pairs={{0,24},{1,25},{2,26},{3,27},{4,28},{5,29},{6,30},{7,31},{8,16},{9,... | collective-permute-start | bytes 178184 | tf_op jit(solution)/shard_map/ppermute | solution.py:18
  74.3 7.1 %collective-permute-start.20 = (bf16[8,3712]{1,0:T(8,128)(2,1)S(1)}, bf16[8,3712]{1,0:T(8,128)(2,1)S(1)}, u32[]{:S(2)}, u32[]{:S(2)}) collective-permute-start(bf16[8,3712]{1,0:T(8,128)(2,1)S(1)} %get-tuple-element.64), channel_id=1, source_target_pairs={{0,16},{1,17},{2,18},{3,19},{4,20},{5,21},{6,22},{7,23},{8,24},{9,... | collective-permute-start | bytes 178184 | tf_op jit(solution)/shard_map/ppermute | solution.py:18

commit v3 on v2

v3 whole, which is shorter than its diff:
```python
import functools

import jax
import jax.numpy as jnp
from jax import lax
from jax.experimental import pallas as pl
from jax.experimental.pallas import tpu as pltpu
from jax.sharding import PartitionSpec as P

NN = (((1,), (0,)), ((), ()))
NT = (((1,), (1,)), ((), ()))
TN = (((0,), (0,)), ((), ()))
F32, B16 = jnp.float32, jnp.bfloat16


def send(value, mask):
    pairs = [(source, source ^ mask) for source in range(lax.axis_size("expert"))]
    return lax.ppermute(value, "expert", pairs)


def stages():
    found, bit, top = [], 1, lax.axis_size("expert").bit_length() - 1
    while bit < top:
        if bit + 1 < top:
            found.append((2**bit, 2 ** (bit + 1), 3 * 2**bit))
        else:
            found.append((2**bit,))
        bit += 2
    return found


def dot32(left, right, dims=NN):
    return lax.dot_general(left, right, dims, preferred_element_type=F32)


def in_vmem(kernel, outs, args, flops=0, outside=0, results=(), scratch=()):
    moved = sum(a.size * a.dtype.itemsize for a in args)
    spaces = [pltpu.HBM] * outside + [pltpu.VMEM] * (len(args) - outside)
    return pl.pallas_call(
        kernel,
        out_shape=[
            (jax.ShapeDtypeStruct if i in results else pltpu.VMEM)(shape, dtype)
            for i, (shape, dtype) in enumerate(outs)
        ],
        in_specs=[pl.BlockSpec(memory_space=space) for space in spaces],
        out_specs=[pl.BlockSpec(memory_space=pltpu.VMEM)] * len(outs),
        scratch_shapes=list(scratch),
        compiler_params=pltpu.CompilerParams(vmem_limit_bytes=20 * 2**20),
        cost_estimate=pl.CostEstimate(flops=flops, bytes_accessed=moved, transcendentals=0),
    )(*[pltpu.with_memory_space_constraint(a, space) for a, space in zip(args, spaces)])


def stacked(refs):
    return jnp.concatenate([ref[...].astype(F32) for ref in refs], axis=0)


def chunks_of(width, step=512):
    return [pl.ds(at, step) for at in range(0, width, step)]


def copied(sources, targets, sems):
    copies = [pltpu.make_async_copy(*pair, sems.at[i]) for i, pair in enumerate(zip(sources, targets))]
    for copy in copies:
        copy.start()
    return copies


def message_kernel(experts, width, *refs):
    sources, out_ref, probs_ref, ids_ref, sems = refs[:4], refs[4], refs[5], refs[6], refs[7]
    tail = out_ref.shape[1] - width
    targets = (out_ref.at[:, :width], out_ref.at[:, tail:], probs_ref, ids_ref)
    copies = copied(sources, targets, sems)
    for copy in copies[2:]:
        copy.wait()
    ids, probs = ids_ref[...], probs_ref[...]
    high = probs.astype(B16).astype(F32)
    low = probs - high
    lane = lax.broadcasted_iota(jnp.int32, (ids.shape[0], tail - width), 1)
    extra = jnp.zeros(lane.shape, F32)
    for k in range(ids.shape[1]):
        one = slice(k, k + 1)
        extra = jnp.where(lane == ids[:, one], high[:, one], extra)
        extra = jnp.where(lane == ids[:, one] + experts, low[:, one], extra)
    out_ref[:, width:tail] = extra.astype(B16)
    for copy in copies[:2]:
        copy.wait()


def weights_into(which, sources, raws, outs, narrow_ref, wide_ref, sems):
    pieces = sems.shape[0] // len(sources)
    parts = []
    for i, (source, raw) in enumerate(zip(sources, raws)):
        step = source.shape[0] // pieces
        for j in range(pieces):
            rows = pl.ds(j * step, step)
            sem = sems.at[i * pieces + j]
            parts.append((i, rows, pltpu.make_async_copy(source.at[rows, :], raw.at[rows, :], sem)))
    ahead = 5
    for _, _, copy in parts[:ahead]:
        copy.start()
    for at, (i, rows, copy) in enumerate(parts):
        copy.wait()
        if at + ahead < len(parts):
            parts[at + ahead][2].start()
        raw, out, kind = raws[i], outs[i], which + i
        if kind < 2:
            for line in range(rows.start, rows.start + rows.size, 128):
                lines = pl.ds(line, 128)
                factor = 1.0 + dot32(wide_ref[kind, :, lines], narrow_ref[kind], TN)
                out[lines, :] = (raw[lines, :].astype(F32) * factor).astype(B16)
        else:
            for lanes in chunks_of(raw.shape[1]):
                factor = 1.0 + dot32(narrow_ref[kind, :, rows], wide_ref[kind, :, lanes], TN)
                out[rows, lanes] = (raw[rows, lanes].astype(F32) * factor).astype(B16)


def weights_kernel(gate_ref, up_ref, down_ref, narrow_hbm, mine_hbm, other_ref, *refs):
    raws, outs, (narrow_out, wide_out, mine_ref, small_sems, sems) = refs[:3], refs[3:6], refs[6:]
    for copy in copied((narrow_hbm, mine_hbm), (narrow_out, mine_ref), small_sems):
        copy.wait()
    half = mine_ref.shape[2]
    is_lower = lax.axis_index("expert") % 2 == 0

    @pl.when(is_lower)
    def _():
        wide_out[:, :, :half] = mine_ref[...]
        wide_out[:, :, half:] = other_ref[...]

    @pl.when(jnp.logical_not(is_lower))
    def _():
        wide_out[:, :, :half] = other_ref[...]
        wide_out[:, :, half:] = mine_ref[...]

    weights_into(0, (gate_ref, up_ref, down_ref), raws, outs, narrow_out, wide_out, sems)


def picks_of(extra, wanted_experts, rows, capacity):
    count, lanes = extra.shape
    slots = count // rows * capacity
    named = (extra > 0.0).astype(B16)
    lane = lax.broadcasted_iota(jnp.int32, (8, lanes), 1)
    line = lax.broadcasted_iota(jnp.int32, (8, lanes), 0)
    wanted = jnp.zeros((8, lanes), F32)
    for i, expert in enumerate(wanted_experts):
        wanted = jnp.where((line == i) & (lane == expert), 1.0, wanted)
    chosen = dot32(wanted.astype(B16), named, NT)
    earlier = lax.broadcasted_iota(jnp.int32, (count, count), 0)
    later = lax.broadcasted_iota(jnp.int32, (count, count), 1)
    before = (earlier // rows == later // rows) & (earlier < later)
    slot = dot32(chosen.astype(B16), before.astype(F32).astype(B16))
    to = lax.broadcasted_iota(jnp.int32, (slots, count), 0)
    of = lax.broadcasted_iota(jnp.int32, (slots, count), 1)
    in_block = to // capacity == of // rows
    place = (to % capacity).astype(F32)
    picks = []
    for i in range(len(wanted_experts)):
        pick = in_block & (place == slot[i : i + 1, :]) & (chosen[i : i + 1, :] > 0.5)
        picks.append(jnp.where(pick, 1.0, 0.0))
    return picks


def pack_kernel(masks, rows, capacity, waits, *refs):
    refs, ways = refs[waits:], min(len(masks), 2)
    pieces, (tokens_out, cot_out, pick_out), outs = (
        refs[: -3 - ways], refs[-3 - ways : -ways], refs[-ways:]
    )
    block = stacked(pieces)
    held = block.astype(B16)
    full, width = tokens_out.shape[1], cot_out.shape[1]
    tokens_out[...] = held[:, :full]
    cot_out[...] = held[:, full:]
    me = lax.axis_index("expert")
    wanted = [(me ^ mask) // 2 for mask in masks]
    picks = picks_of(block[:, width:full], wanted, rows, capacity)
    for pick, out in zip(picks, outs):
        out[...] = dot32(pick.astype(B16), held).astype(B16)
    pick_out[...] = jnp.concatenate(picks, axis=0)


def stack_kernel(tokens_ref, cot_ref, *refs):
    pieces, (tokens_out, cot_out) = refs[:-2], refs[-2:]
    full = tokens_out.shape[1]
    for out, first, own in ((tokens_out, 0, tokens_ref), (cot_out, full, cot_ref)):
        parts = [own[...].astype(F32)]
        parts += [piece[:, first : first + out.shape[1]].astype(F32) for piece in pieces]
        out[...] = jnp.concatenate(parts, axis=0).astype(B16)


def pre_kernel(experts, width, rows, capacity, gate_ref, up_ref, *refs):
    pieces, (x_ref, prob_ref, pre_gate_ref, pre_up_ref, pick_ref) = refs[:-5], refs[-5:]
    count = pick_ref.shape[1]
    crossed = pieces[0][:, width:].astype(F32)[-count:]
    (pick_ref[...],) = picks_of(crossed, [lax.axis_index("expert") // 2], rows, capacity)
    for part in chunks_of(width):
        x_ref[:, part] = jnp.concatenate(
            [piece[:, part].astype(F32) for piece in pieces], axis=0
        ).astype(B16)
    extra = jnp.concatenate([piece[:, width:].astype(F32) for piece in pieces], axis=0)
    lane = lax.broadcasted_iota(jnp.int32, extra.shape, 1)
    own = (lane % experts == lax.axis_index("expert") // 2) & (lane < 2 * experts)
    probs = jnp.sum(jnp.where(own, extra, 0.0), axis=1, keepdims=True)
    prob_ref[...] = jnp.broadcast_to(probs, prob_ref.shape)
    pre_gate_ref[...] = dot32(x_ref[...], gate_ref[...])
    pre_up_ref[...] = dot32(x_ref[...], up_ref[...])


def mid_kernel(
    experts, width, gate_ref, up_ref, down_ref, prob_ref, pre_gate_ref, pre_up_ref, *refs
):
    pieces, outs = refs[:-6], refs[-6:]
    y_ref, hidden_ref, grad_gate_ref, grad_up_ref, mine_ref, give_ref = outs
    for part in chunks_of(width):
        y_ref[:, part] = jnp.concatenate(
            [piece[:, part].astype(F32) for piece in pieces], axis=0
        ).astype(B16)
    grad_full = dot32(y_ref[...], down_ref[...], NT)
    pre_gate, pre_up = pre_gate_ref[...], pre_up_ref[...]
    probs = prob_ref[:, :1]
    routed = probs > 0.0
    sigmoid_gate = jax.nn.sigmoid(pre_gate)
    activated = pre_gate * sigmoid_gate
    hidden = jnp.where(routed, activated * pre_up, 0.0)
    hidden_ref[...] = (hidden * probs).astype(B16)
    own_probs = jnp.sum(hidden * grad_full, axis=1, keepdims=True)
    grad_hidden = grad_full * probs
    grad_gate_ref[...] = jnp.where(
        routed, grad_hidden * pre_up * sigmoid_gate * (1.0 + pre_gate * (1.0 - sigmoid_gate)), 0.0
    ).astype(B16)
    grad_up_ref[...] = jnp.where(routed, grad_hidden * activated, 0.0).astype(B16)
    half = mine_ref.shape[0]
    for part in chunks_of(width):
        product = dot32(grad_gate_ref[...], gate_ref[part, :], NT)
        product = product + dot32(grad_up_ref[...], up_ref[part, :], NT)
        mine_ref[:, part] = product[:half].astype(B16)
        give_ref[:, part] = product[half:].astype(B16)
    lanes = mine_ref.shape[1] - width
    lane = lax.broadcasted_iota(jnp.int32, (2 * half, lanes), 1)
    expert = lax.axis_index("expert") // 2
    high = own_probs.astype(B16).astype(F32)
    extra = jnp.where(lane == expert, high, jnp.where(lane == expert + experts, own_probs - high, 0.0))
    mine_ref[:, width:] = extra[:half].astype(B16)
    give_ref[:, width:] = extra[half:].astype(B16)


def first_sum_kernel(experts, width, mine_ref, other_ref, pick_ref, after_ref, own_ref, *outs):
    del after_ref
    total = mine_ref[...].astype(F32) + other_ref[...].astype(F32)
    count = own_ref.shape[0]
    own_ref[...] = total[:count]
    extra = total[count:, width:]
    lane = lax.broadcasted_iota(jnp.int32, extra.shape, 1)
    lost = jnp.where(lane < experts, extra - extra.astype(B16).astype(F32), 0.0)
    extra = extra + pltpu.roll(lost, experts, 1) - lost
    slots = outs[0].shape[0]
    for i, out in enumerate(outs):
        if i < 2:
            part = slice(i * slots, (i + 1) * slots)
            out[:, :width] = total[count:, :width][part].astype(B16)
            out[:, width:] = extra[part].astype(B16)
        else:
            pick = pick_ref[...].astype(B16)
            out[:, :width] = dot32(pick, total[-count:, :width].astype(B16)).astype(B16)
            out[:, width:] = dot32(pick, extra[-count:].astype(B16)).astype(B16)


def second_sum_kernel(ways, pick_ref, own_ref, *refs):
    came, own_out, outs = refs[: -2 - ways], refs[-1 - ways], refs[len(refs) - ways :]
    total = own_ref[...] + dot32(pick_ref[...].astype(B16), stacked(came).astype(B16), TN)
    count = own_out.shape[0]
    own_out[...] = total[:count]
    for i, out in enumerate(outs):
        out[...] = total[(i + 1) * count : (i + 2) * count].astype(B16)


def down_grads_kernel(y_ref, hidden_ref, down_ref, narrow_ref, wide_ref, narrow_out, wide_out):
    width = y_ref.shape[1]
    narrow_out[...] = jnp.zeros_like(narrow_out)
    for part in chunks_of(width, width // 2):
        masked = dot32(hidden_ref[...], y_ref[:, part], TN) * down_ref[:, part].astype(F32)
        masked = masked.astype(B16)
        narrow_out[...] += dot32(wide_ref[2, :, part], masked, NT)
        wide_out[:, part] = dot32(narrow_ref[2], masked)


def feature_grads_kernel(
    x_ref, grad_gate_ref, grad_up_ref, gate_ref, up_ref, narrow_ref, wide_ref, after_ref,
    down_narrow_ref, down_wide_ref, narrow_out, keep_out, give_out, wide_all,
):
    del after_ref
    width, rank = x_ref.shape[1], narrow_ref.shape[1]
    lines = pl.ds(2 * rank, rank)
    narrow_out[lines, :] = down_narrow_ref[...]
    wide_all[lines, :] = down_wide_ref[...]
    for i, (grad, raw) in enumerate(((grad_gate_ref, gate_ref), (grad_up_ref, up_ref))):
        lines = pl.ds(i * rank, rank)
        narrow_out[lines, :] = jnp.zeros((rank, narrow_out.shape[1]), F32)
        for part in chunks_of(width, width // 2):
            masked = dot32(x_ref[:, part], grad[...], TN) * raw[part, :].astype(F32)
            masked = masked.astype(B16)
            narrow_out[lines, :] += dot32(wide_ref[i, :, part], masked)
            wide_all[lines, part] = dot32(narrow_ref[i], masked, NT)
    half = keep_out.shape[1]
    is_lower = lax.axis_index("expert") % 2 == 0

    @pl.when(is_lower)
    def _():
        keep_out[...] = wide_all[:, :half]
        give_out[...] = wide_all[:, half:].astype(B16)

    @pl.when(jnp.logical_not(is_lower))
    def _():
        keep_out[...] = wide_all[:, half:]
        give_out[...] = wide_all[:, :half].astype(B16)


def last_kernel(experts, width, ids_ref, keep_ref, given_ref, own_ref, *refs):
    came, (tokens_out, probs_out, wide_out) = refs[:-3], refs[-3:]
    total = own_ref[...]
    for ref in came:
        total = total + ref[...].astype(F32)
    tokens_out[...] = total[:, :width].astype(B16)
    extra, ids = total[:, width:], ids_ref[...]
    lane = lax.broadcasted_iota(jnp.int32, extra.shape, 1)
    spot = lax.broadcasted_iota(jnp.int32, ids.shape, 1)
    probs = jnp.zeros(ids.shape, F32)
    for k in range(ids.shape[1]):
        wanted = ids[:, k : k + 1]
        found = jnp.where((lane == wanted) | (lane == wanted + experts), extra, 0.0)
        probs = jnp.where(spot == k, jnp.sum(found, axis=1, keepdims=True), probs)
    probs_out[...] = probs
    wide_out[...] = keep_ref[...] + given_ref[...].astype(F32)


def body(
    tokens,
    cotangent,
    route_probs,
    expert_ids,
    gate_weight,
    up_weight,
    down_weight,
    narrow,
    wide_factors,
):
    rows, width = tokens.shape
    hidden_units = gate_weight.shape[1]
    top_count = expert_ids.shape[1]
    rank = narrow.shape[1]
    devices = lax.axis_size("expert")
    experts = devices // 2
    capacity = min(rows, max(2, (3 * rows * top_count + 2 * experts - 1) // (2 * experts)))
    near, far = stages()[0], stages()[1:]
    count = rows * devices // 2 // (len(near) + 1)
    slots = count // rows * capacity
    half = count + len(near[:2]) * slots + len(near[2:]) * count
    lanes = -(-2 * experts // 128) * 128
    full = width + lanes

    def pieces_of(block):
        for masks in reversed(far[1:]):
            block = jnp.concatenate([block] + [send(block, mask) for mask in masks], axis=0)
        if far:
            return [block] + [send(block, mask) for mask in far[0]]
        return [block]

    (message,) = in_vmem(
        functools.partial(message_kernel, experts, width),
        [((rows, full + width), B16)],
        (tokens, cotangent, route_probs, expert_ids),
        outside=4,
        scratch=[
            pltpu.VMEM(route_probs.shape, F32),
            pltpu.VMEM(expert_ids.shape, jnp.int32),
            pltpu.SemaphoreType.DMA((4,)),
        ],
    )
    pieces = pieces_of(message)
    crossed = [send(message, mask) for mask in near[2:]]
    matmul = 2 * 2 * half * width * hidden_units
    weights = (gate_weight, up_weight, down_weight)
    gate_raw, up_raw, down_raw, gate_eff, up_eff, down_eff, narrow, wide = in_vmem(
        weights_kernel,
        [(weight.shape, B16) for weight in weights] * 2
        + [(narrow.shape, B16), ((3, rank, width), B16)],
        (*weights, narrow, wide_factors, send(wide_factors, 1)),
        3 * matmul,
        outside=5,
        scratch=[
            pltpu.VMEM(wide_factors.shape, B16),
            pltpu.SemaphoreType.DMA((2,)),
            pltpu.SemaphoreType.DMA((12,)),
        ],
    )
    held, cot_held, pick, *packed = in_vmem(
        functools.partial(pack_kernel, near, rows, capacity, 1 + len(crossed)),
        [((count, full), B16), ((count, width), B16), ((len(near) * slots, count), F32)]
        + [((slots, full + width), B16)] * len(near[:2]),
        [wide] + crossed + pieces,
    )
    came = [send(block, mask) for block, mask in zip(packed, near)]
    for block in crossed:
        came += pieces_of(block)
    mine_rows, cot_mine = in_vmem(
        stack_kernel, [((half, full), B16), ((half, width), B16)], [held, cot_held, *came]
    )
    token_rows = [mine_rows, send(mine_rows, 1)]
    cot_rows = [cot_mine, send(cot_mine, 1)]
    packed_type = [((slots, full), B16)] * len(near)

    wide_type, unit_type = ((2 * half, width), B16), ((2 * half, hidden_units), B16)
    x, probs, pre_gate, pre_up, cross_pick = in_vmem(
        functools.partial(pre_kernel, experts, width, rows, capacity),
        [wide_type, ((2 * half, 128), F32)]
        + [((2 * half, hidden_units), F32)] * 2
        + [((slots, count), F32)],
        (gate_eff, up_eff, *token_rows),
        2 * matmul,
    )
    y, hidden, grad_gate, grad_up, mine, give = in_vmem(
        functools.partial(mid_kernel, experts, width),
        [wide_type] + [unit_type] * 3 + [((half, full), B16)] * 2,
        (gate_eff, up_eff, down_eff, probs, pre_gate, pre_up, *cot_rows),
        3 * matmul,
    )
    other = send(give, 1)
    down_narrow, down_wide = in_vmem(
        down_grads_kernel,
        [((rank, hidden_units), F32), ((rank, width), F32)],
        (y, hidden, down_raw, narrow, wide),
        2 * matmul,
    )
    own, *parts = in_vmem(
        functools.partial(first_sum_kernel, experts, width),
        [((count, full), F32)] + packed_type,
        (mine, other, cross_pick, down_narrow),
    )
    grad_narrow, keep, give = in_vmem(
        feature_grads_kernel,
        [((3 * rank, hidden_units), F32), ((3 * rank, width // 2), F32), ((3 * rank, width // 2), B16)],
        (x, grad_gate, grad_up, gate_raw, up_raw, narrow, wide, parts[0], down_narrow, down_wide),
        4 * matmul,
        results=(0,),
        scratch=[pltpu.VMEM((3 * rank, width), F32)],
    )
    ways = len(far[0]) if far else 0
    own, *parts = in_vmem(
        functools.partial(second_sum_kernel, ways),
        [((count // (ways + 1), full), F32)] + [((count // (ways + 1), full), B16)] * ways,
        (pick, own, *[send(part, mask) for part, mask in zip(parts, near)], keep),
    )
    came = [send(part, mask) for part, mask in zip(parts, far[0] if far else ())]
    for masks in far[1:]:
        total = own
        for part in came:
            total = total + part.astype(F32)
        own, *parts = jnp.split(total, len(masks) + 1, axis=0)
        came = [send(part.astype(B16), mask) for part, mask in zip(parts, masks)]
    grad_tokens, grad_probs, grad_wide = in_vmem(
        functools.partial(last_kernel, experts, width),
        [((rows, width), B16), (expert_ids.shape, F32), ((3 * rank, width // 2), F32)],
        (expert_ids, keep, send(give, 1), own, *came),
        results=(0, 1, 2),
    )
    return (
        grad_tokens,
        grad_probs,
        grad_narrow.reshape(3, rank, hidden_units),
        grad_wide.reshape(3, rank, width // 2),
    )


def solution(mesh):
    in_specs = (
        P(("groups", "expert"), None),
        P(("groups", "expert"), None),
        P(("groups", "expert"), None),
        P(("groups", "expert"), None),
        P(None, "expert"),
        P(None, "expert"),
        P("expert", None),
        P(None, None, "expert"),
        P(None, None, "expert"),
    )
    out_specs = (
        P(("groups", "expert"), None),
        P(("groups", "expert"), None),
        P("groups", None, "expert"),
        P("groups", None, "expert"),
    )
    return jax.shard_map(body, mesh=mesh, in_specs=in_specs, out_specs=out_specs, check_vma=False)
```

time: 83.2 us -> 65.7 us (0.79)
  waiting for transfers between devices: 23.1 us -> 15.6 us
  local copies, waits for them, and re-layouts: 7.25 us -> 0.01 us
  Pallas kernels: 19 us -> 24.5 us
  starting transfers between devices: 28.9 us -> 24.6 us
  other arithmetic: 3.6 us -> 0 us
    ppermute x23 -> x20, waiting for transfers between devices: 23.1 us -> 15.6 us  [send(): return lax.ppermute(value, 'expert', pairs)]
    unnamed x23 -> x2, local copies, waits for them, and re-layouts: 5.66 us -> 0.01 us
    pallas_call x8 -> x11, Pallas kernels: 19 us -> 24.5 us  [in_vmem(): pl.pallas_call(kernel, out_shape=[(jax.ShapeDtypeStruct if i in results e...]
    ppermute x23 -> x20, starting transfers between devices: 28.9 us -> 24.6 us  [send(): return lax.ppermute(value, 'expert', pairs)]
    reduce_sum x2 -> x0, other arithmetic: 1.55 us -> none  [the longest x1 0.8 us: body(): dense = jnp.sum(jnp.where(chosen, route_probs[:, :, None], 0.0), axis=1)]
    select_n x1 -> x0, other arithmetic: 1.09 us -> none  [join_halves(): jnp.where(is_lower, jnp.concatenate([mine, other], axis=-1), jnp.concaten...]
    concatenate x3 -> x0, local copies, waits for them, and re-layouts: 0.94 us -> none  [the longest x1 0.91 us: body(): message = jnp.concatenate([tokens, high, low, tail], axis=1)]
    add x3 -> x0, other arithmetic: 0.89 us -> none  [the longest x1 0.78 us: body(): grad_wide = keep_part + send(give_part.astype(B16), 1).astype(F32)]
  transfers between devices with their start and end apart: 23 -> 20, of which waited for: 7 -> 7; matrix products, arithmetic and copies ran while one was open for 3% -> 0% of each run, Pallas kernels for 18% -> 29%
where the time goes in v3:
time: 65.7 us; the launch traced here: 65.5 us
  starting transfers between devices  24.6 us (37%)
  Pallas kernels  24.5 us (37%)
  waiting for transfers between devices  15.6 us (24%)
  between operations  0.76 us (1%)
    ppermute x20, starting transfers between devices, send(): return lax.ppermute(value, 'expert', pairs)  24.6 us
    pallas_call x11, Pallas kernels, in_vmem(): pl.pallas_call(kernel, out_shape=[(jax.ShapeDtypeStruct if i in results e...  24.5 us
    ppermute x20, waiting for transfers between devices, send(): return lax.ppermute(value, 'expert', pairs)  15.6 us
  transfers between devices with their start and end apart: 20, of which 7 were waited for; matrix products, arithmetic and copies ran while one was open for 0% of the time, Pallas kernels for 29%

profile of v3, /device:TPU:0, one launch (start us, length us, event | category | flops | bytes accessed | tf_op | source)
XLA Modules:
  0.0 65.5 jit_solution(696261773138060876)
XLA Ops:
  0.6 0.5 collective-permute-start
  1.1 0.9 %shard_map.121.refs_2_ = bf16[8,7296]{1,0:T(8,128)(2,1)S(1)} custom-call(bf16[8,3584]{1,0:T(8,128)(2,1)} %refs_0_.1, bf16[8,3584]{1,0:T(8,128)(2,1)} %refs_1_.1, f32[8,8]{1,0:T(8,128)} %refs_2_.1, s32[8,8]{1,0:T(8,128)} %ids_ref.1), custom_call_target="tpu_custom_call" | custom-call | bytes 115200 | tf_op jit(solution)/shard_map/pallas_call | solution.py:39
  2.1 4.7 %collective-permute-start.4 = (bf16[8,7296]{1,0:T(8,128)(2,1)S(1)}, bf16[8,7296]{1,0:T(8,128)(2,1)S(1)}, u32[]{:S(2)}, u32[]{:S(2)}) collective-permute-start(bf16[8,7296]{1,0:T(8,128)(2,1)S(1)} %shard_map.121.refs_2_), channel_id=1, source_target_pairs={{0,24},{1,25},{2,26},{3,27},{4,28},{5,29},{6,30},{7,31},{8,16},{9,... | collective-permute-start | bytes 350216 | tf_op jit(solution)/shard_map/ppermute | solution.py:18
  6.7 0.0 collective-permute-start.3
  6.7 0.6 collective-permute-start.2
  7.4 2.6 %collective-permute-start.1 = (bf16[8,7296]{1,0:T(8,128)(2,1)S(1)}, bf16[8,7296]{1,0:T(8,128)(2,1)S(1)}, u32[]{:S(2)}, u32[]{:S(2)}) collective-permute-start(bf16[8,7296]{1,0:T(8,128)(2,1)S(1)} %shard_map.121.refs_2_), channel_id=1, source_target_pairs={{0,6},{1,7},{2,4},{3,5},{4,2},{5,3},{6,0},{7,1},{8,14},{9,15},{10,... | collective-permute-start | bytes 350216 | tf_op jit(solution)/shard_map/ppermute | solution.py:18
  10.0 0.0 collective-permute-done.other_ref
  10.0 7.3 %shard_map.120 = (bf16[3584,512]{1,0:T(8,128)(2,1)S(1)}, bf16[3584,512]{1,0:T(8,128)(2,1)S(1)}, bf16[512,3584]{1,0:T(8,128)(2,1)S(1)}, bf16[3584,512]{1,0:T(8,12...) custom-call(bf16[3584,512]{1,0:T(8,128)(2,1)} %gate_ref.1, ...), custom_call_target="tpu_custom_call" | custom-call | flops 2466250752 | bytes 11403264 | tf_op jit(solution)/shard_map/pallas_call | solution.py:39
  17.3 0.0 collective-permute-done.4.refs_5_
  17.3 0.0 collective-permute-done.3.refs_4_
  17.3 0.0 collective-permute-done.2.refs_3_
  17.4 0.0 collective-permute-done.1.refs_1_.refs_2_
  17.4 0.6 shard_map.122
  18.0 1.4 %collective-permute-start.5 = (bf16[24,7296]{1,0:T(8,128)(2,1)S(1)}, bf16[24,7296]{1,0:T(8,128)(2,1)S(1)}, u32[]{:S(2)}, u32[]{:S(2)}) collective-permute-start(bf16[24,7296]{1,0:T(8,128)(2,1)S(1)} %get-tuple-element.51), channel_id=1, source_target_pairs={{0,2},{1,3},{2,0},{3,1},{4,6},{5,7},{6,4},{7,5},{8,10},{9,11},{10,... | collective-permute-start | bytes 1050632 | tf_op jit(solution)/shard_map/ppermute | solution.py:18
  19.4 1.5 %collective-permute-start.6 = (bf16[24,7296]{1,0:T(8,128)(2,1)S(1)}, bf16[24,7296]{1,0:T(8,128)(2,1)S(1)}, u32[]{:S(2)}, u32[]{:S(2)}) collective-permute-start(bf16[24,7296]{1,0:T(8,128)(2,1)S(1)} %get-tuple-element.52), channel_id=1, source_target_pairs={{0,4},{1,5},{2,6},{3,7},{4,0},{5,1},{6,2},{7,3},{8,12},{9,13},{10,... | collective-permute-start | bytes 1050632 | tf_op jit(solution)/shard_map/ppermute | solution.py:18
  21.0 2.5 %collective-permute-start.9 = (bf16[8,7296]{1,0:T(8,128)(2,1)S(1)}, bf16[8,7296]{1,0:T(8,128)(2,1)S(1)}, u32[]{:S(2)}, u32[]{:S(2)}) collective-permute-start(bf16[8,7296]{1,0:T(8,128)(2,1)S(1)} %collective-permute-done.1.refs_1_.refs_2_), channel_id=1, source_target_pairs={{0,24},{1,25},{2,26},{3,27},{4,28},{5,29},{6,30},{7,31},{8,16},{9,... | collective-permute-start | bytes 350216 | tf_op jit(solution)/shard_map/ppermute | solution.py:18
  23.4 0.0 collective-permute-start.8
  23.4 1.9 %collective-permute-start.7 = (bf16[8,7296]{1,0:T(8,128)(2,1)S(1)}, bf16[8,7296]{1,0:T(8,128)(2,1)S(1)}, u32[]{:S(2)}, u32[]{:S(2)}) collective-permute-start(bf16[8,7296]{1,0:T(8,128)(2,1)S(1)} %collective-permute-done.1.refs_1_.refs_2_), channel_id=1, source_target_pairs={{0,8},{1,9},{2,10},{3,11},{4,12},{5,13},{6,14},{7,15},{8,0},{9,1},... | collective-permute-start | bytes 350216 | tf_op jit(solution)/shard_map/ppermute | solution.py:18
  25.4 3.5 %collective-permute-done.9.refs_5_ = bf16[8,7296]{1,0:T(8,128)(2,1)S(1)} collective-permute-done((bf16[8,7296]{1,0:T(8,128)(2,1)S(1)}, bf16[8,7296]{1,0:T(8,128)(2,1)S(1)}, u32[]{:S(2)}, u32[]{:S(2)}) %collective-permute-start.9) | collective-permute-done | bytes 116768 | tf_op jit(solution)/shard_map/ppermute | solution.py:18
  28.9 4.0 %collective-permute-done.8.refs_4_ = bf16[8,7296]{1,0:T(8,128)(2,1)S(1)} collective-permute-done((bf16[8,7296]{1,0:T(8,128)(2,1)S(1)}, bf16[8,7296]{1,0:T(8,128)(2,1)S(1)}, u32[]{:S(2)}, u32[]{:S(2)}) %collective-permute-start.8) | collective-permute-done | bytes 116768 | tf_op jit(solution)/shard_map/ppermute | solution.py:18
  32.9 0.0 collective-permute-done.7.refs_3_
  32.9 0.0 collective-permute-done.5.refs_0_
  32.9 0.0 collective-permute-done.6.refs_1_
  32.9 0.1 shard_map.123
  33.0 0.1 collective-permute-start.10
  33.1 0.5 collective-permute-start.11
  33.6 1.8 %collective-permute-done.10.refs_1_ = bf16[112,3712]{1,0:T(8,128)(2,1)S(1)} collective-permute-done((bf16[112,3712]{1,0:T(8,128)(2,1)S(1)}, bf16[112,3712]{1,0:T(8,128)(2,1)S(1)}, u32[]{:S(2)}, u32[]{:S(2)}) %collective-permute-start.10) | collective-permute-done | bytes 831520 | tf_op jit(solution)/shard_map/ppermute | solution.py:18
  35.4 1.9 %shard_map.124 = (bf16[224,3584]{1,0:T(8,128)(2,1)S(1)}, f32[224,128]{1,0:T(8,128)S(1)}, f32[224,512]{1,0:T(8,128)S(1)}, f32[224,512]{1,0:T(8,128)S(1)}, f32[24,32]{1,0:T(8,128)S(1)}) custom-call(bf16[3584,512]{1,0:T(8,128)(2,1)S(1)} %get-tuple-element.46.gate_ref, bf16[3584,512]{1,0:T(8,128)(2,1)S(1)} %get-tuple-element.47.up_ref, ...), custom_call_target="tpu_custom_call" | custom-call | flops 1644167168 | bytes 9003008 | tf_op jit(solution)/shard_map/pallas_call | solution.py:39
  37.4 0.0 collective-permute-done.11.refs_1_
  37.4 3.7 %shard_map.125 = (bf16[224,3584]{1,0:T(8,128)(2,1)S(1)}, bf16[224,512]{1,0:T(8,128)(2,1)S(1)}, bf16[224,512]{1,0:T(8,128)(2,1)S(1)}, bf16[224,512]{1,0:T(8,128)(...) custom-call(bf16[3584,512]{1,0:T(8,128)(2,1)S(1)} %get-tuple-element.46.gate_ref, ...), custom_call_target="tpu_custom_call" | custom-call | flops 2466250752 | bytes 13647872 | tf_op jit(solution)/shard_map/pallas_call | solution.py:39
  41.1 0.2 collective-permute-start.12
  41.3 2.5 %shard_map.126 = (f32[16,512]{1,0:T(8,128)S(1)}, f32[16,3584]{1,0:T(8,128)S(1)}) custom-call(bf16[224,3584]{1,0:T(8,128)(2,1)S(1)} %get-tuple-element.68.y_ref, bf16[224,512]{1,0:T(8,128)(2,1)S(1)} %get-tuple-element.69.hidden_ref, bf16[512,3584]{1,0:T(8,128)(2,1)S(1)} %get-tuple-element.70.down_ref, bf16[3,16,512]{2,1,0:T(8,128)(2,1)S(1)} %get-tuple-element.64.narrow_ref, ...), custom_call_target="tpu_custom_call" | custom-call | flops 1644167168 | bytes 5898240 | tf_op jit(solution)/shard_map/pallas_call | solution.py:39
  43.8 0.0 collective-permute-done.12.other_ref
  43.8 0.3 shard_map.127
  44.1 0.8 %collective-permute-start.15 = (bf16[24,3712]{1,0:T(8,128)(2,1)S(1)}, bf16[24,3712]{1,0:T(8,128)(2,1)S(1)}, u32[]{:S(2)}, u32[]{:S(2)}) collective-permute-start(bf16[24,3712]{1,0:T(8,128)(2,1)S(1)} %get-tuple-element.78), channel_id=1, source_target_pairs={{0,4},{1,5},{2,6},{3,7},{4,0},{5,1},{6,2},{7,3},{8,12},{9,13},{10,... | collective-permute-start | bytes 534536 | tf_op jit(solution)/shard_map/ppermute | solution.py:18
  45.0 1.4 %collective-permute-start.16 = (bf16[24,3712]{1,0:T(8,128)(2,1)S(1)}, bf16[24,3712]{1,0:T(8,128)(2,1)S(1)}, u32[]{:S(2)}, u32[]{:S(2)}) collective-permute-start(bf16[24,3712]{1,0:T(8,128)(2,1)S(1)} %get-tuple-element.79), channel_id=1, source_target_pairs={{0,6},{1,7},{2,4},{3,5},{4,2},{5,3},{6,0},{7,1},{8,14},{9,15},{10,... | collective-permute-start | bytes 534536 | tf_op jit(solution)/shard_map/ppermute | solution.py:18
  46.4 1.3 %collective-permute-start.14 = (bf16[24,3712]{1,0:T(8,128)(2,1)S(1)}, bf16[24,3712]{1,0:T(8,128)(2,1)S(1)}, u32[]{:S(2)}, u32[]{:S(2)}) collective-permute-start(bf16[24,3712]{1,0:T(8,128)(2,1)S(1)} %get-tuple-element.72.after_ref), channel_id=1, source_target_pairs={{0,2},{1,3},{2,0},{3,1},{4,6},{5,7},{6,4},{7,5},{8,10},{9,11},{10,... | collective-permute-start | bytes 534536 | tf_op jit(solution)/shard_map/ppermute | solution.py:18
  47.7 0.0 copy-start
  47.7 5.9 %shard_map.128 = (f32[48,512]{1,0:T(8,128)}, f32[48,1792]{1,0:T(8,128)S(1)}, bf16[48,1792]{1,0:T(8,128)(2,1)S(1)}) custom-call(bf16[224,3584]{1,0:T(8,128)(2,1)S(1)} %get-tuple-element.54.x_ref, bf16[224,512]{1,0:T(8,128)(2,1)S(1)} %get-tuple-element.60.grad_gate_ref, bf16[224,512]{1,0:T(8,128)(2,1)S(1)} %get-tuple-element.61.grad_up_ref, ...), custom_call_target="tpu_custom_call" | custom-call | flops 3288334336 | bytes 10237952 | tf_op jit(solution)/shard_map/pallas_call | solution.py:39
  53.6 0.0 collective-permute-start.13
  53.6 1.2 %collective-permute-done.15.refs_1_ = bf16[24,3712]{1,0:T(8,128)(2,1)S(1)} collective-permute-done((bf16[24,3712]{1,0:T(8,128)(2,1)S(1)}, bf16[24,3712]{1,0:T(8,128)(2,1)S(1)}, u32[]{:S(2)}, u32[]{:S(2)}) %collective-permute-start.15) | collective-permute-done | bytes 178208 | tf_op jit(solution)/shard_map/ppermute | solution.py:18
  54.8 0.0 collective-permute-done.16.refs_2_
  54.8 1.2 %collective-permute-done.14.refs_0_ = bf16[24,3712]{1,0:T(8,128)(2,1)S(1)} collective-permute-done((bf16[24,3712]{1,0:T(8,128)(2,1)S(1)}, bf16[24,3712]{1,0:T(8,128)(2,1)S(1)}, u32[]{:S(2)}, u32[]{:S(2)}) %collective-permute-start.14) | collective-permute-done | bytes 178208 | tf_op jit(solution)/shard_map/ppermute | solution.py:18
  56.0 0.3 shard_map.129
  56.3 0.1 collective-permute-start.17
  56.4 2.2 %collective-permute-start.18 = (bf16[8,3712]{1,0:T(8,128)(2,1)S(1)}, bf16[8,3712]{1,0:T(8,128)(2,1)S(1)}, u32[]{:S(2)}, u32[]{:S(2)}) collective-permute-start(bf16[8,3712]{1,0:T(8,128)(2,1)S(1)} %get-tuple-element.82), channel_id=1, source_target_pairs={{0,16},{1,17},{2,18},{3,19},{4,20},{5,21},{6,22},{7,23},{8,24},{9,... | collective-permute-start | bytes 178184 | tf_op jit(solution)/shard_map/ppermute | solution.py:18
  58.6 2.2 %collective-permute-start.19 = (bf16[8,3712]{1,0:T(8,128)(2,1)S(1)}, bf16[8,3712]{1,0:T(8,128)(2,1)S(1)}, u32[]{:S(2)}, u32[]{:S(2)}) collective-permute-start(bf16[8,3712]{1,0:T(8,128)(2,1)S(1)} %get-tuple-element.83), channel_id=1, source_target_pairs={{0,24},{1,25},{2,26},{3,27},{4,28},{5,29},{6,30},{7,31},{8,16},{9,... | collective-permute-start | bytes 178184 | tf_op jit(solution)/shard_map/ppermute | solution.py:18
  60.8 0.0 collective-permute-done.13.given_ref
  60.8 0.0 collective-permute-done.17.refs_0_
  60.8 1.0 %collective-permute-done.18.refs_1_ = bf16[8,3712]{1,0:T(8,128)(2,1)S(1)} collective-permute-done((bf16[8,3712]{1,0:T(8,128)(2,1)S(1)}, bf16[8,3712]{1,0:T(8,128)(2,1)S(1)}, u32[]{:S(2)}, u32[]{:S(2)}) %collective-permute-start.18) | collective-permute-done | bytes 59424 | tf_op jit(solution)/shard_map/ppermute | solution.py:18
  61.7 2.8 %collective-permute-done.19.refs_2_ = bf16[8,3712]{1,0:T(8,128)(2,1)S(1)} collective-permute-done((bf16[8,3712]{1,0:T(8,128)(2,1)S(1)}, bf16[8,3712]{1,0:T(8,128)(2,1)S(1)}, u32[]{:S(2)}, u32[]{:S(2)}) %collective-permute-start.19) | collective-permute-done | bytes 59424 | tf_op jit(solution)/shard_map/ppermute | solution.py:18
  64.6 0.0 copy-done
  64.6 0.9 %shard_map.130 = (bf16[8,3584]{1,0:T(8,128)(2,1)}, f32[8,8]{1,0:T(8,128)}, f32[48,1792]{1,0:T(8,128)}) custom-call(s32[8,8]{1,0:T(8,128)S(1)} %copy-done, f32[48,1792]{1,0:T(8,128)S(1)} %get-tuple-element.74.refs_3_.keep_ref, bf16[48,1792]{1,0:T(8,128)(2,1)S(1)} %collective-permute-done.13.given_ref, f32[8,3712]{1,0:T(8,128)S(1)} %get-tuple-element.80.own_ref, ...), custom_call_target="tpu_custom_call" | custom-call | bytes 813312 | tf_op jit(solution)/shard_map/pallas_call | solution.py:39
Async XLA Ops:
  0.6 9.3 %collective-permute-start = (bf16[3,16,1792]{2,1,0:T(8,128)(2,1)}, bf16[3,16,1792]{2,1,0:T(8,128)(2,1)S(1)}, u32[]{:S(2)}, u32[]{:S(2)}) collective-permute-start(bf16[3,16,1792]{2,1,0:T(8,128)(2,1)} %mine_hbm.1), channel_id=1, source_target_pairs={{0,1},{1,0},{2,3},{3,2},{4,5},{5,4},{6,7},{7,6},{8,9},{9,8},{10,11... | collective-permute-start | bytes 516104 | tf_op jit(solution)/shard_map/ppermute | solution.py:18
  2.1 15.3 %collective-permute-start.4 = (bf16[8,7296]{1,0:T(8,128)(2,1)S(1)}, bf16[8,7296]{1,0:T(8,128)(2,1)S(1)}, u32[]{:S(2)}, u32[]{:S(2)}) collective-permute-start(bf16[8,7296]{1,0:T(8,128)(2,1)S(1)} %shard_map.121.refs_2_), channel_id=1, source_target_pairs={{0,24},{1,25},{2,26},{3,27},{4,28},{5,29},{6,30},{7,31},{8,16},{9,... | collective-permute-start | bytes 350216 | tf_op jit(solution)/shard_map/ppermute | solution.py:18
  6.7 10.6 %collective-permute-start.3 = (bf16[8,7296]{1,0:T(8,128)(2,1)S(1)}, bf16[8,7296]{1,0:T(8,128)(2,1)S(1)}, u32[]{:S(2)}, u32[]{:S(2)}) collective-permute-start(bf16[8,7296]{1,0:T(8,128)(2,1)S(1)} %shard_map.121.refs_2_), channel_id=1, source_target_pairs={{0,16},{1,17},{2,18},{3,19},{4,20},{5,21},{6,22},{7,23},{8,24},{9,... | collective-permute-start | bytes 350216 | tf_op jit(solution)/shard_map/ppermute | solution.py:18
  6.7 10.6 %collective-permute-start.2 = (bf16[8,7296]{1,0:T(8,128)(2,1)S(1)}, bf16[8,7296]{1,0:T(8,128)(2,1)S(1)}, u32[]{:S(2)}, u32[]{:S(2)}) collective-permute-start(bf16[8,7296]{1,0:T(8,128)(2,1)S(1)} %shard_map.121.refs_2_), channel_id=1, source_target_pairs={{0,8},{1,9},{2,10},{3,11},{4,12},{5,13},{6,14},{7,15},{8,0},{9,1},... | collective-permute-start | bytes 350216 | tf_op jit(solution)/shard_map/ppermute | solution.py:18
  7.4 10.0 %collective-permute-start.1 = (bf16[8,7296]{1,0:T(8,128)(2,1)S(1)}, bf16[8,7296]{1,0:T(8,128)(2,1)S(1)}, u32[]{:S(2)}, u32[]{:S(2)}) collective-permute-start(bf16[8,7296]{1,0:T(8,128)(2,1)S(1)} %shard_map.121.refs_2_), channel_id=1, source_target_pairs={{0,6},{1,7},{2,4},{3,5},{4,2},{5,3},{6,0},{7,1},{8,14},{9,15},{10,... | collective-permute-start | bytes 350216 | tf_op jit(solution)/shard_map/ppermute | solution.py:18
  18.0 14.9 %collective-permute-start.5 = (bf16[24,7296]{1,0:T(8,128)(2,1)S(1)}, bf16[24,7296]{1,0:T(8,128)(2,1)S(1)}, u32[]{:S(2)}, u32[]{:S(2)}) collective-permute-start(bf16[24,7296]{1,0:T(8,128)(2,1)S(1)} %get-tuple-element.51), channel_id=1, source_target_pairs={{0,2},{1,3},{2,0},{3,1},{4,6},{5,7},{6,4},{7,5},{8,10},{9,11},{10,... | collective-permute-start | bytes 1050632 | tf_op jit(solution)/shard_map/ppermute | solution.py:18
  19.4 13.5 %collective-permute-start.6 = (bf16[24,7296]{1,0:T(8,128)(2,1)S(1)}, bf16[24,7296]{1,0:T(8,128)(2,1)S(1)}, u32[]{:S(2)}, u32[]{:S(2)}) collective-permute-start(bf16[24,7296]{1,0:T(8,128)(2,1)S(1)} %get-tuple-element.52), channel_id=1, source_target_pairs={{0,4},{1,5},{2,6},{3,7},{4,0},{5,1},{6,2},{7,3},{8,12},{9,13},{10,... | collective-permute-start | bytes 1050632 | tf_op jit(solution)/shard_map/ppermute | solution.py:18
  21.0 7.9 %collective-permute-start.9 = (bf16[8,7296]{1,0:T(8,128)(2,1)S(1)}, bf16[8,7296]{1,0:T(8,128)(2,1)S(1)}, u32[]{:S(2)}, u32[]{:S(2)}) collective-permute-start(bf16[8,7296]{1,0:T(8,128)(2,1)S(1)} %collective-permute-done.1.refs_1_.refs_2_), channel_id=1, source_target_pairs={{0,24},{1,25},{2,26},{3,27},{4,28},{5,29},{6,30},{7,31},{8,16},{9,... | collective-permute-start | bytes 350216 | tf_op jit(solution)/shard_map/ppermute | solution.py:18
  23.4 9.5 %collective-permute-start.8 = (bf16[8,7296]{1,0:T(8,128)(2,1)S(1)}, bf16[8,7296]{1,0:T(8,128)(2,1)S(1)}, u32[]{:S(2)}, u32[]{:S(2)}) collective-permute-start(bf16[8,7296]{1,0:T(8,128)(2,1)S(1)} %collective-permute-done.1.refs_1_.refs_2_), channel_id=1, source_target_pairs={{0,16},{1,17},{2,18},{3,19},{4,20},{5,21},{6,22},{7,23},{8,24},{9,... | collective-permute-start | bytes 350216 | tf_op jit(solution)/shard_map/ppermute | solution.py:18
  23.4 9.5 %collective-permute-start.7 = (bf16[8,7296]{1,0:T(8,128)(2,1)S(1)}, bf16[8,7296]{1,0:T(8,128)(2,1)S(1)}, u32[]{:S(2)}, u32[]{:S(2)}) collective-permute-start(bf16[8,7296]{1,0:T(8,128)(2,1)S(1)} %collective-permute-done.1.refs_1_.refs_2_), channel_id=1, source_target_pairs={{0,8},{1,9},{2,10},{3,11},{4,12},{5,13},{6,14},{7,15},{8,0},{9,1},... | collective-permute-start | bytes 350216 | tf_op jit(solution)/shard_map/ppermute | solution.py:18
  33.0 2.4 %collective-permute-start.10 = (bf16[112,3712]{1,0:T(8,128)(2,1)S(1)}, bf16[112,3712]{1,0:T(8,128)(2,1)S(1)}, u32[]{:S(2)}, u32[]{:S(2)}) collective-permute-start(bf16[112,3712]{1,0:T(8,128)(2,1)S(1)} %get-tuple-element.53.refs_0_), channel_id=1, source_target_pairs={{0,1},{1,0},{2,3},{3,2},{4,5},{5,4},{6,7},{7,6},{8,9},{9,8},{10,11... | collective-permute-start | bytes 2494472 | tf_op jit(solution)/shard_map/ppermute | solution.py:18
  33.1 4.3 %collective-permute-start.11 = (bf16[112,3584]{1,0:T(8,128)(2,1)S(1)}, bf16[112,3584]{1,0:T(8,128)(2,1)S(1)}, u32[]{:S(2)}, u32[]{:S(2)}) collective-permute-start(bf16[112,3584]{1,0:T(8,128)(2,1)S(1)} %get-tuple-element.59.refs_0_), channel_id=1, source_target_pairs={{0,1},{1,0},{2,3},{3,2},{4,5},{5,4},{6,7},{7,6},{8,9},{9,8},{10,11... | collective-permute-start | bytes 2408456 | tf_op jit(solution)/shard_map/ppermute | solution.py:18
  41.1 2.7 %collective-permute-start.12 = (bf16[112,3712]{1,0:T(8,128)(2,1)S(1)}, bf16[112,3712]{1,0:T(8,128)(2,1)S(1)}, u32[]{:S(2)}, u32[]{:S(2)}) collective-permute-start(bf16[112,3712]{1,0:T(8,128)(2,1)S(1)} %get-tuple-element.66), channel_id=1, source_target_pairs={{0,1},{1,0},{2,3},{3,2},{4,5},{5,4},{6,7},{7,6},{8,9},{9,8},{10,11... | collective-permute-start | bytes 2494472 | tf_op jit(solution)/shard_map/ppermute | solution.py:18
  44.1 10.7 %collective-permute-start.15 = (bf16[24,3712]{1,0:T(8,128)(2,1)S(1)}, bf16[24,3712]{1,0:T(8,128)(2,1)S(1)}, u32[]{:S(2)}, u32[]{:S(2)}) collective-permute-start(bf16[24,3712]{1,0:T(8,128)(2,1)S(1)} %get-tuple-element.78), channel_id=1, source_target_pairs={{0,4},{1,5},{2,6},{3,7},{4,0},{5,1},{6,2},{7,3},{8,12},{9,13},{10,... | collective-permute-start | bytes 534536 | tf_op jit(solution)/shard_map/ppermute | solution.py:18
  45.0 9.8 %collective-permute-start.16 = (bf16[24,3712]{1,0:T(8,128)(2,1)S(1)}, bf16[24,3712]{1,0:T(8,128)(2,1)S(1)}, u32[]{:S(2)}, u32[]{:S(2)}) collective-permute-start(bf16[24,3712]{1,0:T(8,128)(2,1)S(1)} %get-tuple-element.79), channel_id=1, source_target_pairs={{0,6},{1,7},{2,4},{3,5},{4,2},{5,3},{6,0},{7,1},{8,14},{9,15},{10,... | collective-permute-start | bytes 534536 | tf_op jit(solution)/shard_map/ppermute | solution.py:18
  46.4 9.6 %collective-permute-start.14 = (bf16[24,3712]{1,0:T(8,128)(2,1)S(1)}, bf16[24,3712]{1,0:T(8,128)(2,1)S(1)}, u32[]{:S(2)}, u32[]{:S(2)}) collective-permute-start(bf16[24,3712]{1,0:T(8,128)(2,1)S(1)} %get-tuple-element.72.after_ref), channel_id=1, source_target_pairs={{0,2},{1,3},{2,0},{3,1},{4,6},{5,7},{6,4},{7,5},{8,10},{9,11},{10,... | collective-permute-start | bytes 534536 | tf_op jit(solution)/shard_map/ppermute | solution.py:18
  47.7 16.9 %copy-start = (s32[8,8]{1,0:T(8,128)S(1)}, s32[8,8]{1,0:T(8,128)}, u32[]{:S(2)}) copy-start(s32[8,8]{1,0:T(8,128)} %ids_ref.1) | copy-start | bytes 772
  53.6 7.2 %collective-permute-start.13 = (bf16[48,1792]{1,0:T(8,128)(2,1)S(1)}, bf16[48,1792]{1,0:T(8,128)(2,1)S(1)}, u32[]{:S(2)}, u32[]{:S(2)}) collective-permute-start(bf16[48,1792]{1,0:T(8,128)(2,1)S(1)} %get-tuple-element.75), channel_id=1, source_target_pairs={{0,1},{1,0},{2,3},{3,2},{4,5},{5,4},{6,7},{7,6},{8,9},{9,8},{10,11... | collective-permute-start | bytes 516104 | tf_op jit(solution)/shard_map/ppermute | solution.py:18
  56.3 4.5 %collective-permute-start.17 = (bf16[8,3712]{1,0:T(8,128)(2,1)S(1)}, bf16[8,3712]{1,0:T(8,128)(2,1)S(1)}, u32[]{:S(2)}, u32[]{:S(2)}) collective-permute-start(bf16[8,3712]{1,0:T(8,128)(2,1)S(1)} %get-tuple-element.81), channel_id=1, source_target_pairs={{0,8},{1,9},{2,10},{3,11},{4,12},{5,13},{6,14},{7,15},{8,0},{9,1},... | collective-permute-start | bytes 178184 | tf_op jit(solution)/shard_map/ppermute | solution.py:18
  56.4 5.4 %collective-permute-start.18 = (bf16[8,3712]{1,0:T(8,128)(2,1)S(1)}, bf16[8,3712]{1,0:T(8,128)(2,1)S(1)}, u32[]{:S(2)}, u32[]{:S(2)}) collective-permute-start(bf16[8,3712]{1,0:T(8,128)(2,1)S(1)} %get-tuple-element.82), channel_id=1, source_target_pairs={{0,16},{1,17},{2,18},{3,19},{4,20},{5,21},{6,22},{7,23},{8,24},{9,... | collective-permute-start | bytes 178184 | tf_op jit(solution)/shard_map/ppermute | solution.py:18
  58.6 6.0 %collective-permute-start.19 = (bf16[8,3712]{1,0:T(8,128)(2,1)S(1)}, bf16[8,3712]{1,0:T(8,128)(2,1)S(1)}, u32[]{:S(2)}, u32[]{:S(2)}) collective-permute-start(bf16[8,3712]{1,0:T(8,128)(2,1)S(1)} %get-tuple-element.83), channel_id=1, source_target_pairs={{0,24},{1,25},{2,26},{3,27},{4,28},{5,29},{6,30},{7,31},{8,16},{9,... | collective-permute-start | bytes 178184 | tf_op jit(solution)/shard_map/ppermute | solution.py:18

commit v4 on v3

--- a/solution.py
+++ b/solution.py
@@ -1,4 +1,5 @@
 import functools
+import math
 
 import jax
 import jax.numpy as jnp
@@ -138,9 +139,10 @@
     count, lanes = extra.shape
     slots = count // rows * capacity
     named = (extra > 0.0).astype(B16)
-    lane = lax.broadcasted_iota(jnp.int32, (8, lanes), 1)
-    line = lax.broadcasted_iota(jnp.int32, (8, lanes), 0)
-    wanted = jnp.zeros((8, lanes), F32)
+    kinds = -(-len(wanted_experts) // 8) * 8
+    lane = lax.broadcasted_iota(jnp.int32, (kinds, lanes), 1)
+    line = lax.broadcasted_iota(jnp.int32, (kinds, lanes), 0)
+    wanted = jnp.zeros((kinds, lanes), F32)
     for i, expert in enumerate(wanted_experts):
         wanted = jnp.where((line == i) & (lane == expert), 1.0, wanted)
     chosen = dot32(wanted.astype(B16), named, NT)
@@ -159,38 +161,77 @@
     return picks
 
 
-def pack_kernel(masks, rows, capacity, waits, *refs):
-    refs, ways = refs[waits:], min(len(masks), 2)
-    pieces, (tokens_out, cot_out, pick_out), outs = (
-        refs[: -3 - ways], refs[-3 - ways : -ways], refs[-ways:]
-    )
-    block = stacked(pieces)
+def folds_of(rows, capacity, lanes):
+    folds = rows // math.gcd(rows, capacity)
+    return folds, -(-lanes // (128 * folds)) * 128
+
+
+def write_rows(outs, rows):
+    first = 0
+    for out in outs:
+        out[...] = rows[first : first + out.shape[0]].astype(B16)
+        first += out.shape[0]
+
+
+def pack_kernel(masks, offsets, rows, capacity, after_ref, *refs):
+    del after_ref
+    crossing = len(masks) > 2
+    taken = len(refs) - 3 - len(masks[:2]) - crossing * len(offsets)
+    blocks, refs = refs[:taken], refs[taken:]
+    tokens_out, cot_out, pick_out, outs = *refs[:3], refs[3:]
+    block = stacked(blocks[crossing:])
     held = block.astype(B16)
     full, width = tokens_out.shape[1], cot_out.shape[1]
     tokens_out[...] = held[:, :full]
     cot_out[...] = held[:, full:]
     me = lax.axis_index("expert")
-    wanted = [(me ^ mask) // 2 for mask in masks]
-    picks = picks_of(block[:, width:full], wanted, rows, capacity)
-    for pick, out in zip(picks, outs):
-        out[...] = dot32(pick.astype(B16), held).astype(B16)
+    picks = picks_of(block[:, width:full], [(me ^ m) // 2 for m in masks], rows, capacity)
     pick_out[...] = jnp.concatenate(picks, axis=0)
-
-
-def stack_kernel(tokens_ref, cot_ref, *refs):
-    pieces, (tokens_out, cot_out) = refs[:-2], refs[-2:]
-    full = tokens_out.shape[1]
-    for out, first, own in ((tokens_out, 0, tokens_ref), (cot_out, full, cot_ref)):
-        parts = [own[...].astype(F32)]
-        parts += [piece[:, first : first + out.shape[1]].astype(F32) for piece in pieces]
+    write_rows(outs[: len(picks[:2])], dot32(jnp.concatenate(picks[:2], axis=0).astype(B16), held))
+    if crossing:
+        block = blocks[0][...].astype(F32)
+        lanes = block.shape[1]
+        folds, step = folds_of(rows, capacity, lanes)
+        extra = jnp.concatenate([block[:, width:full]] * folds, axis=0)
+        if folds * step > lanes:
+            block = jnp.concatenate([block, jnp.zeros((rows, folds * step - lanes), F32)], axis=1)
+        pieces = [block[:, i * step : (i + 1) * step] for i in range(folds)]
+        laid = jnp.concatenate(pieces, axis=0).astype(B16)
+        picks = picks_of(extra, [(me ^ offset) // 2 for offset in offsets], rows, capacity)
+        write_rows(outs[2:], dot32(jnp.concatenate(picks, axis=0).astype(B16), laid))
+
+
+def unfolded(refs, folds):
+    laid = stacked(refs).astype(B16)
+    total, blocks = laid.shape[0], len(refs)
+    capacity = total // (folds * blocks)
+    to = lax.broadcasted_iota(jnp.int32, (total, total), 0)
+    of = lax.broadcasted_iota(jnp.int32, (total, total), 1)
+    same = to % capacity == of % capacity
+    same &= to // (blocks * capacity) == of // capacity % folds
+    same &= to // capacity % blocks == of // (folds * capacity)
+    moved = dot32(jnp.where(same, 1.0, 0.0).astype(B16), laid)
+    slots = blocks * capacity
+    return jnp.concatenate([moved[i * slots : (i + 1) * slots] for i in range(folds)], axis=1)
+
+
+def stack_kernel(folds, beside, order, tokens_ref, cot_ref, *refs):
+    came, (tokens_out, cot_out) = refs[:-2], refs[-2:]
+    came = [came[order.index(i)] for i in range(len(order))]
+    near, folded = came[:beside], came[beside:]
+    pieces = [ref[...].astype(F32) for ref in near]
+    if folded:
+        pieces.append(unfolded(folded, folds))
+    full, both = tokens_out.shape[1], tokens_out.shape[1] + cot_out.shape[1]
+    for out, lanes, own in (
+        (tokens_out, slice(0, full), tokens_ref), (cot_out, slice(full, both), cot_ref)
+    ):
+        parts = [own[...].astype(F32)] + [piece[:, lanes] for piece in pieces]
         out[...] = jnp.concatenate(parts, axis=0).astype(B16)
 
 
-def pre_kernel(experts, width, rows, capacity, gate_ref, up_ref, *refs):
-    pieces, (x_ref, prob_ref, pre_gate_ref, pre_up_ref, pick_ref) = refs[:-5], refs[-5:]
-    count = pick_ref.shape[1]
-    crossed = pieces[0][:, width:].astype(F32)[-count:]
-    (pick_ref[...],) = picks_of(crossed, [lax.axis_index("expert") // 2], rows, capacity)
+def pre_kernel(experts, width, gate_ref, up_ref, *refs):
+    pieces, (x_ref, prob_ref, pre_gate_ref, pre_up_ref) = refs[:-4], refs[-4:]
     for part in chunks_of(width):
         x_ref[:, part] = jnp.concatenate(
             [piece[:, part].astype(F32) for piece in pieces], axis=0
@@ -242,7 +283,7 @@
     give_ref[:, width:] = extra[half:].astype(B16)
 
 
-def first_sum_kernel(experts, width, mine_ref, other_ref, pick_ref, after_ref, own_ref, *outs):
+def first_sum_kernel(experts, width, mine_ref, other_ref, after_ref, own_ref, *outs):
     del after_ref
     total = mine_ref[...].astype(F32) + other_ref[...].astype(F32)
     count = own_ref.shape[0]
@@ -253,18 +294,14 @@
     extra = extra + pltpu.roll(lost, experts, 1) - lost
     slots = outs[0].shape[0]
     for i, out in enumerate(outs):
-        if i < 2:
-            part = slice(i * slots, (i + 1) * slots)
-            out[:, :width] = total[count:, :width][part].astype(B16)
-            out[:, width:] = extra[part].astype(B16)
-        else:
-            pick = pick_ref[...].astype(B16)
-            out[:, :width] = dot32(pick, total[-count:, :width].astype(B16)).astype(B16)
-            out[:, width:] = dot32(pick, extra[-count:].astype(B16)).astype(B16)
+        part = slice(i * slots, (i + 1) * slots)
+        out[:, :width] = total[count:, :width][part].astype(B16)
+        out[:, width:] = extra[part].astype(B16)
 
 
 def second_sum_kernel(ways, pick_ref, own_ref, *refs):
     came, own_out, outs = refs[: -2 - ways], refs[-1 - ways], refs[len(refs) - ways :]
+    came = came[1:] + came[:1]
     total = own_ref[...] + dot32(pick_ref[...].astype(B16), stacked(came).astype(B16), TN)
     count = own_out.shape[0]
     own_out[...] = total[:count]
@@ -313,8 +350,12 @@
         give_out[...] = wide_all[:, :half].astype(B16)
 
 
-def last_kernel(experts, width, ids_ref, keep_ref, given_ref, own_ref, *refs):
-    came, (tokens_out, probs_out, wide_out) = refs[:-3], refs[-3:]
+def wide_kernel(keep_ref, given_ref, wide_out):
+    wide_out[...] = keep_ref[...] + given_ref[...].astype(F32)
+
+
+def last_kernel(experts, width, ids_ref, own_ref, *refs):
+    came, (tokens_out, probs_out) = refs[:-2], refs[-2:]
     total = own_ref[...]
     for ref in came:
         total = total + ref[...].astype(F32)
@@ -328,7 +369,6 @@
         found = jnp.where((lane == wanted) | (lane == wanted + experts), extra, 0.0)
         probs = jnp.where(spot == k, jnp.sum(found, axis=1, keepdims=True), probs)
     probs_out[...] = probs
-    wide_out[...] = keep_ref[...] + given_ref[...].astype(F32)
 
 
 def body(
@@ -352,7 +392,10 @@
     near, far = stages()[0], stages()[1:]
     count = rows * devices // 2 // (len(near) + 1)
     slots = count // rows * capacity
-    half = count + len(near[:2]) * slots + len(near[2:]) * count
+    half = count + len(near) * slots
+    offsets = [0]
+    for masks in far:
+        offsets = [first ^ mask for first in offsets for mask in (0, *masks)]
     lanes = -(-2 * experts // 128) * 128
     full = width + lanes
 
@@ -391,28 +434,34 @@
             pltpu.SemaphoreType.DMA((12,)),
         ],
     )
+    folds, step = folds_of(rows, capacity, full + width)
+    crossing = len(offsets) if crossed else 0
     held, cot_held, pick, *packed = in_vmem(
-        functools.partial(pack_kernel, near, rows, capacity, 1 + len(crossed)),
+        functools.partial(pack_kernel, near, offsets, rows, capacity),
         [((count, full), B16), ((count, width), B16), ((len(near) * slots, count), F32)]
-        + [((slots, full + width), B16)] * len(near[:2]),
+        + [((slots, full + width), B16)] * len(near[:2])
+        + [((folds * capacity, step), B16)] * crossing,
         [wide] + crossed + pieces,
     )
-    came = [send(block, mask) for block, mask in zip(packed, near)]
-    for block in crossed:
-        came += pieces_of(block)
+    came = [send(block, mask) for block, mask in zip(packed, near[:2])]
+    folded = packed[2 : 2 + crossing]
+    came += folded[:1] + [send(block, mask) for block, mask in zip(folded[1:], offsets[1:])]
+    order = list(range(len(came)))
+    if len(came) > 5:
+        order = [0, 4, 1, 5, *order[6:], 3, 2]
     mine_rows, cot_mine = in_vmem(
-        stack_kernel, [((half, full), B16), ((half, width), B16)], [held, cot_held, *came]
+        functools.partial(stack_kernel, folds, len(near[:2]), order),
+        [((half, full), B16), ((half, width), B16)],
+        [held, cot_held, *[came[i] for i in order]],
     )
     token_rows = [mine_rows, send(mine_rows, 1)]
     cot_rows = [cot_mine, send(cot_mine, 1)]
     packed_type = [((slots, full), B16)] * len(near)
 
     wide_type, unit_type = ((2 * half, width), B16), ((2 * half, hidden_units), B16)
-    x, probs, pre_gate, pre_up, cross_pick = in_vmem(
-        functools.partial(pre_kernel, experts, width, rows, capacity),
-        [wide_type, ((2 * half, 128), F32)]
-        + [((2 * half, hidden_units), F32)] * 2
-        + [((slots, count), F32)],
+    x, probs, pre_gate, pre_up = in_vmem(
+        functools.partial(pre_kernel, experts, width),
+        [wide_type, ((2 * half, 128), F32)] + [((2 * half, hidden_units), F32)] * 2,
         (gate_eff, up_eff, *token_rows),
         2 * matmul,
     )
@@ -432,12 +481,12 @@
     own, *parts = in_vmem(
         functools.partial(first_sum_kernel, experts, width),
         [((count, full), F32)] + packed_type,
-        (mine, other, cross_pick, down_narrow),
+        (mine, other, down_narrow),
     )
     grad_narrow, keep, give = in_vmem(
         feature_grads_kernel,
         [((3 * rank, hidden_units), F32), ((3 * rank, width // 2), F32), ((3 * rank, width // 2), B16)],
-        (x, grad_gate, grad_up, gate_raw, up_raw, narrow, wide, parts[0], down_narrow, down_wide),
+        (x, grad_gate, grad_up, gate_raw, up_raw, narrow, wide, parts[-2], down_narrow, down_wide),
         4 * matmul,
         results=(0,),
         scratch=[pltpu.VMEM((3 * rank, width), F32)],
@@ -446,7 +495,7 @@
     own, *parts = in_vmem(
         functools.partial(second_sum_kernel, ways),
         [((count // (ways + 1), full), F32)] + [((count // (ways + 1), full), B16)] * ways,
-        (pick, own, *[send(part, mask) for part, mask in zip(parts, near)], keep),
+        (pick, own, *[send(part, mask) for part, mask in zip(parts[-1:] + parts, near[-1:] + near[:-1])], keep),
     )
     came = [send(part, mask) for part, mask in zip(parts, far[0] if far else ())]
     for masks in far[1:]:
@@ -455,11 +504,14 @@
             total = total + part.astype(F32)
         own, *parts = jnp.split(total, len(masks) + 1, axis=0)
         came = [send(part.astype(B16), mask) for part, mask in zip(parts, masks)]
-    grad_tokens, grad_probs, grad_wide = in_vmem(
+    (grad_wide,) = in_vmem(
+        wide_kernel, [((3 * rank, width // 2), F32)], (keep, send(give, 1)), results=(0,)
+    )
+    grad_tokens, grad_probs = in_vmem(
         functools.partial(last_kernel, experts, width),
-        [((rows, width), B16), (expert_ids.shape, F32), ((3 * rank, width // 2), F32)],
-        (expert_ids, keep, send(give, 1), own, *came),
-        results=(0, 1, 2),
+        [((rows, width), B16), (expert_ids.shape, F32)],
+        (expert_ids, own, *came[1:], *came[:1]),
+        results=(0, 1),
     )
     return (
         grad_tokens,

time: 65.7 us -> 63.6 us (0.968)
  waiting for transfers between devices: 15.6 us -> 13.9 us
  starting transfers between devices: 24.6 us -> 23.3 us
  Pallas kernels: 24.5 us -> 25.5 us
    ppermute x20, waiting for transfers between devices: 15.6 us -> 13.9 us  [send(): return lax.ppermute(value, 'expert', pairs)]
    ppermute x20, starting transfers between devices: 24.6 us -> 23.3 us  [send(): return lax.ppermute(value, 'expert', pairs)]
    pallas_call x11 -> x12, Pallas kernels: 24.5 us -> 25.5 us  [in_vmem(): pl.pallas_call(kernel, out_shape=[(jax.ShapeDtypeStruct if i in results e...]
  transfers between devices with their start and end apart: 20 -> 20, of which waited for: 7 -> 8; matrix products, arithmetic and copies ran while one was open for 0% -> 0% of each run, Pallas kernels for 29% -> 31%
where the time goes in v4:
time: 63.6 us; the launch traced here: 63.4 us
  Pallas kernels  25.5 us (40%)
  starting transfers between devices  23.3 us (37%)
  waiting for transfers between devices  13.9 us (22%)
  between operations  0.76 us (1%)
    pallas_call x12, Pallas kernels, in_vmem(): pl.pallas_call(kernel, out_shape=[(jax.ShapeDtypeStruct if i in results e...  25.5 us
    ppermute x20, starting transfers between devices, send(): return lax.ppermute(value, 'expert', pairs)  23.3 us
    ppermute x20, waiting for transfers between devices, send(): return lax.ppermute(value, 'expert', pairs)  13.9 us
  transfers between devices with their start and end apart: 20, of which 8 were waited for; matrix products, arithmetic and copies ran while one was open for 0% of the time, Pallas kernels for 31%

profile of v4, /device:TPU:0, one launch (start us, length us, event | category | flops | bytes accessed | tf_op | source)
XLA Modules:
  0.0 63.4 jit_solution(13357302286890019976)
XLA Ops:
  0.6 0.5 collective-permute-start
  1.1 0.9 %shard_map.121.refs_1_ = bf16[8,7296]{1,0:T(8,128)(2,1)S(1)} custom-call(bf16[8,3584]{1,0:T(8,128)(2,1)} %refs_0_.1, bf16[8,3584]{1,0:T(8,128)(2,1)} %refs_1_.1, f32[8,8]{1,0:T(8,128)} %refs_2_.1, s32[8,8]{1,0:T(8,128)} %ids_ref.1), custom_call_target="tpu_custom_call" | custom-call | bytes 115200 | tf_op jit(solution)/shard_map/pallas_call | solution.py:40
  2.1 4.7 %collective-permute-start.4 = (bf16[8,7296]{1,0:T(8,128)(2,1)S(1)}, bf16[8,7296]{1,0:T(8,128)(2,1)S(1)}, u32[]{:S(2)}, u32[]{:S(2)}) collective-permute-start(bf16[8,7296]{1,0:T(8,128)(2,1)S(1)} %shard_map.121.refs_1_), channel_id=1, source_target_pairs={{0,24},{1,25},{2,26},{3,27},{4,28},{5,29},{6,30},{7,31},{8,16},{9,... | collective-permute-start | bytes 350216 | tf_op jit(solution)/shard_map/ppermute | solution.py:19
  6.7 0.0 collective-permute-start.3
  6.7 0.6 %collective-permute-start.2 = (bf16[8,7296]{1,0:T(8,128)(2,1)S(1)}, bf16[8,7296]{1,0:T(8,128)(2,1)S(1)}, u32[]{:S(2)}, u32[]{:S(2)}) collective-permute-start(bf16[8,7296]{1,0:T(8,128)(2,1)S(1)} %shard_map.121.refs_1_), channel_id=1, source_target_pairs={{0,8},{1,9},{2,10},{3,11},{4,12},{5,13},{6,14},{7,15},{8,0},{9,1},... | collective-permute-start | bytes 350216 | tf_op jit(solution)/shard_map/ppermute | solution.py:19
  7.4 2.6 %collective-permute-start.1 = (bf16[8,7296]{1,0:T(8,128)(2,1)S(1)}, bf16[8,7296]{1,0:T(8,128)(2,1)S(1)}, u32[]{:S(2)}, u32[]{:S(2)}) collective-permute-start(bf16[8,7296]{1,0:T(8,128)(2,1)S(1)} %shard_map.121.refs_1_), channel_id=1, source_target_pairs={{0,6},{1,7},{2,4},{3,5},{4,2},{5,3},{6,0},{7,1},{8,14},{9,15},{10,... | collective-permute-start | bytes 350216 | tf_op jit(solution)/shard_map/ppermute | solution.py:19
  10.0 0.0 collective-permute-done.other_ref
  10.0 7.3 %shard_map.120 = (bf16[3584,512]{1,0:T(8,128)(2,1)S(1)}, bf16[3584,512]{1,0:T(8,128)(2,1)S(1)}, bf16[512,3584]{1,0:T(8,128)(2,1)S(1)}, bf16[3584,512]{1,0:T(8,12...) custom-call(bf16[3584,512]{1,0:T(8,128)(2,1)} %gate_ref.1, ...), custom_call_target="tpu_custom_call" | custom-call | flops 2290089984 | bytes 11403264 | tf_op jit(solution)/shard_map/pallas_call | solution.py:40
  17.3 0.0 collective-permute-done.4.refs_4_
  17.3 0.0 collective-permute-done.3.refs_3_
  17.3 0.0 collective-permute-done.2.refs_2_
  17.4 0.0 collective-permute-done.1.refs_0_
  17.4 0.9 %shard_map.122 = (bf16[32,3712]{1,0:T(8,128)(2,1)S(1)}, bf16[32,3584]{1,0:T(8,128)(2,1)S(1)}, f32[72,32]{1,0:T(8,128)S(1)}, bf16[24,7296]{1,0:T(8,128)(2,1)S(1)}...) custom-call(bf16[3,16,3584]{2,1,0:T(8,128)(2,1)S(1)} %get-tuple-elem, ...), custom_call_target="tpu_custom_call" | custom-call | bytes 927744 | tf_op jit(solution)/shard_map/pallas_call | solution.py:40
  18.3 1.4 %collective-permute-start.5 = (bf16[24,7296]{1,0:T(8,128)(2,1)S(1)}, bf16[24,7296]{1,0:T(8,128)(2,1)S(1)}, u32[]{:S(2)}, u32[]{:S(2)}) collective-permute-start(bf16[24,7296]{1,0:T(8,128)(2,1)S(1)} %get-tuple-element.55), channel_id=1, source_target_pairs={{0,2},{1,3},{2,0},{3,1},{4,6},{5,7},{6,4},{7,5},{8,10},{9,11},{10,... | collective-permute-start | bytes 1050632 | tf_op jit(solution)/shard_map/ppermute | solution.py:19
  19.7 1.5 %collective-permute-start.7 = (bf16[24,7296]{1,0:T(8,128)(2,1)S(1)}, bf16[24,7296]{1,0:T(8,128)(2,1)S(1)}, u32[]{:S(2)}, u32[]{:S(2)}) collective-permute-start(bf16[24,7296]{1,0:T(8,128)(2,1)S(1)} %get-tuple-element.57), channel_id=1, source_target_pairs={{0,4},{1,5},{2,6},{3,7},{4,0},{5,1},{6,2},{7,3},{8,12},{9,13},{10,... | collective-permute-start | bytes 1050632 | tf_op jit(solution)/shard_map/ppermute | solution.py:19
  21.2 0.3 collective-permute-start.6
  21.5 2.2 %collective-permute-start.8 = (bf16[24,1920]{1,0:T(8,128)(2,1)S(1)}, bf16[24,1920]{1,0:T(8,128)(2,1)S(1)}, u32[]{:S(2)}, u32[]{:S(2)}) collective-permute-start(bf16[24,1920]{1,0:T(8,128)(2,1)S(1)} %get-tuple-element.58), channel_id=1, source_target_pairs={{0,24},{1,25},{2,26},{3,27},{4,28},{5,29},{6,30},{7,31},{8,16},{9,... | collective-permute-start | bytes 276488 | tf_op jit(solution)/shard_map/ppermute | solution.py:19
  23.8 1.0 %collective-permute-start.9 = (bf16[24,1920]{1,0:T(8,128)(2,1)S(1)}, bf16[24,1920]{1,0:T(8,128)(2,1)S(1)}, u32[]{:S(2)}, u32[]{:S(2)}) collective-permute-start(bf16[24,1920]{1,0:T(8,128)(2,1)S(1)} %get-tuple-element.59), channel_id=1, source_target_pairs={{0,8},{1,9},{2,10},{3,11},{4,12},{5,13},{6,14},{7,15},{8,0},{9,1},... | collective-permute-start | bytes 276488 | tf_op jit(solution)/shard_map/ppermute | solution.py:19
  24.7 5.0 %collective-permute-done.6.refs_1_ = bf16[24,1920]{1,0:T(8,128)(2,1)S(1)} collective-permute-done((bf16[24,1920]{1,0:T(8,128)(2,1)S(1)}, bf16[24,1920]{1,0:T(8,128)(2,1)S(1)}, u32[]{:S(2)}, u32[]{:S(2)}) %collective-permute-start.6) | collective-permute-done | bytes 92192 | tf_op jit(solution)/shard_map/ppermute | solution.py:19
  29.7 0.0 collective-permute-done.8.refs_3_
  29.7 0.9 %collective-permute-done.9.refs_4_ = bf16[24,1920]{1,0:T(8,128)(2,1)S(1)} collective-permute-done((bf16[24,1920]{1,0:T(8,128)(2,1)S(1)}, bf16[24,1920]{1,0:T(8,128)(2,1)S(1)}, u32[]{:S(2)}, u32[]{:S(2)}) %collective-permute-start.9) | collective-permute-done | bytes 92192 | tf_op jit(solution)/shard_map/ppermute | solution.py:19
  30.6 0.0 collective-permute-done.5.refs_0_
  30.6 0.0 collective-permute-done.7.refs_2_
  30.6 0.3 shard_map.123
  30.9 0.1 collective-permute-start.10
  31.0 0.5 collective-permute-start.11
  31.5 1.8 %collective-permute-done.10.refs_1_ = bf16[104,3712]{1,0:T(8,128)(2,1)S(1)} collective-permute-done((bf16[104,3712]{1,0:T(8,128)(2,1)S(1)}, bf16[104,3712]{1,0:T(8,128)(2,1)S(1)}, u32[]{:S(2)}, u32[]{:S(2)}) %collective-permute-start.10) | collective-permute-done | bytes 772128 | tf_op jit(solution)/shard_map/ppermute | solution.py:19
  33.3 1.7 %shard_map.124 = (bf16[208,3584]{1,0:T(8,128)(2,1)S(1)}, f32[208,128]{1,0:T(8,128)S(1)}, f32[208,512]{1,0:T(8,128)S(1)}, f32[208,512]{1,0:T(8,128)S(1)}) custom-call(bf16[3584,512]{1,0:T(8,128)(2,1)S(1)} %get-tuple-element.50.gate_ref, bf16[3584,512]{1,0:T(8,128)(2,1)S(1)} %get-tuple-element.51.up_ref, bf16[104,3712]{1,0:T(8,128)(2,1)S(1)} %get-tuple-element.61.refs_0_, ...), custom_call_target="tpu_custom_call" | custom-call | flops 1526726656 | bytes 8884224 | tf_op jit(solution)/shard_map/pallas_call | solution.py:40
  35.0 0.0 collective-permute-done.11.refs_1_
  35.0 3.8 %shard_map.125 = (bf16[208,3584]{1,0:T(8,128)(2,1)S(1)}, bf16[208,512]{1,0:T(8,128)(2,1)S(1)}, bf16[208,512]{1,0:T(8,128)(2,1)S(1)}, bf16[208,512]{1,0:T(8,128)(...) custom-call(bf16[3584,512]{1,0:T(8,128)(2,1)S(1)} %get-tuple-element.50.gate_ref, ...), custom_call_target="tpu_custom_call" | custom-call | flops 2290089984 | bytes 13459456 | tf_op jit(solution)/shard_map/pallas_call | solution.py:40
  38.8 0.3 collective-permute-start.12
  39.1 2.5 %shard_map.126 = (f32[16,512]{1,0:T(8,128)S(1)}, f32[16,3584]{1,0:T(8,128)S(1)}) custom-call(bf16[208,3584]{1,0:T(8,128)(2,1)S(1)} %get-tuple-element.68.y_ref, bf16[208,512]{1,0:T(8,128)(2,1)S(1)} %get-tuple-element.69.hidden_ref, bf16[512,3584]{1,0:T(8,128)(2,1)S(1)} %get-tuple-element.70.down_ref, bf16[3,16,512]{2,1,0:T(8,128)(2,1)S(1)} %get-tuple-element.71.narrow_ref, ...), custom_call_target="tpu_custom_call" | custom-call | flops 1526726656 | bytes 5767168 | tf_op jit(solution)/shard_map/pallas_call | solution.py:40
  41.6 0.0 collective-permute-done.12.other_ref
  41.6 0.3 shard_map.127
  41.9 1.0 %collective-permute-start.13 = (bf16[24,3712]{1,0:T(8,128)(2,1)S(1)}, bf16[24,3712]{1,0:T(8,128)(2,1)S(1)}, u32[]{:S(2)}, u32[]{:S(2)}) collective-permute-start(bf16[24,3712]{1,0:T(8,128)(2,1)S(1)} %get-tuple-element.74), channel_id=1, source_target_pairs={{0,6},{1,7},{2,4},{3,5},{4,2},{5,3},{6,0},{7,1},{8,14},{9,15},{10,... | collective-permute-start | bytes 534536 | tf_op jit(solution)/shard_map/ppermute | solution.py:19
  42.9 1.1 %collective-permute-start.14 = (bf16[24,3712]{1,0:T(8,128)(2,1)S(1)}, bf16[24,3712]{1,0:T(8,128)(2,1)S(1)}, u32[]{:S(2)}, u32[]{:S(2)}) collective-permute-start(bf16[24,3712]{1,0:T(8,128)(2,1)S(1)} %get-tuple-element.75), channel_id=1, source_target_pairs={{0,2},{1,3},{2,0},{3,1},{4,6},{5,7},{6,4},{7,5},{8,10},{9,11},{10,... | collective-permute-start | bytes 534536 | tf_op jit(solution)/shard_map/ppermute | solution.py:19
  44.0 1.5 %collective-permute-start.15 = (bf16[24,3712]{1,0:T(8,128)(2,1)S(1)}, bf16[24,3712]{1,0:T(8,128)(2,1)S(1)}, u32[]{:S(2)}, u32[]{:S(2)}) collective-permute-start(bf16[24,3712]{1,0:T(8,128)(2,1)S(1)} %get-tuple-element.76.after_ref), channel_id=1, source_target_pairs={{0,4},{1,5},{2,6},{3,7},{4,0},{5,1},{6,2},{7,3},{8,12},{9,13},{10,... | collective-permute-start | bytes 534536 | tf_op jit(solution)/shard_map/ppermute | solution.py:19
  45.5 0.0 copy-start
  45.5 5.9 %shard_map.128 = (f32[48,512]{1,0:T(8,128)}, f32[48,1792]{1,0:T(8,128)S(1)}, bf16[48,1792]{1,0:T(8,128)(2,1)S(1)}) custom-call(bf16[208,3584]{1,0:T(8,128)(2,1)S(1)} %get-tuple-element.77.x_ref, bf16[208,512]{1,0:T(8,128)(2,1)S(1)} %get-tuple-element.78.grad_gate_ref, bf16[208,512]{1,0:T(8,128)(2,1)S(1)} %get-tuple-element.79.grad_up_ref, ...), custom_call_target="tpu_custom_call" | custom-call | flops 3053453312 | bytes 10090496 | tf_op jit(solution)/shard_map/pallas_call | solution.py:40
  51.4 0.0 collective-permute-start.19
  51.4 0.0 collective-permute-done.13.refs_0_
  51.4 1.1 %collective-permute-done.14.refs_1_ = bf16[24,3712]{1,0:T(8,128)(2,1)S(1)} collective-permute-done((bf16[24,3712]{1,0:T(8,128)(2,1)S(1)}, bf16[24,3712]{1,0:T(8,128)(2,1)S(1)}, u32[]{:S(2)}, u32[]{:S(2)}) %collective-permute-start.14) | collective-permute-done | bytes 178208 | tf_op jit(solution)/shard_map/ppermute | solution.py:19
  52.5 0.9 %collective-permute-done.15.refs_2_ = bf16[24,3712]{1,0:T(8,128)(2,1)S(1)} collective-permute-done((bf16[24,3712]{1,0:T(8,128)(2,1)S(1)}, bf16[24,3712]{1,0:T(8,128)(2,1)S(1)}, u32[]{:S(2)}, u32[]{:S(2)}) %collective-permute-start.15) | collective-permute-done | bytes 178208 | tf_op jit(solution)/shard_map/ppermute | solution.py:19
  53.4 0.3 shard_map.129
  53.7 1.8 %collective-permute-start.16 = (bf16[8,3712]{1,0:T(8,128)(2,1)S(1)}, bf16[8,3712]{1,0:T(8,128)(2,1)S(1)}, u32[]{:S(2)}, u32[]{:S(2)}) collective-permute-start(bf16[8,3712]{1,0:T(8,128)(2,1)S(1)} %get-tuple-element.85), channel_id=1, source_target_pairs={{0,16},{1,17},{2,18},{3,19},{4,20},{5,21},{6,22},{7,23},{8,24},{9,... | collective-permute-start | bytes 178184 | tf_op jit(solution)/shard_map/ppermute | solution.py:19
  55.6 2.2 %collective-permute-start.17 = (bf16[8,3712]{1,0:T(8,128)(2,1)S(1)}, bf16[8,3712]{1,0:T(8,128)(2,1)S(1)}, u32[]{:S(2)}, u32[]{:S(2)}) collective-permute-start(bf16[8,3712]{1,0:T(8,128)(2,1)S(1)} %get-tuple-element.86), channel_id=1, source_target_pairs={{0,24},{1,25},{2,26},{3,27},{4,28},{5,29},{6,30},{7,31},{8,16},{9,... | collective-permute-start | bytes 178184 | tf_op jit(solution)/shard_map/ppermute | solution.py:19
  57.8 0.0 collective-permute-start.18
  57.8 0.0 collective-permute-done.19.given_ref
  57.8 0.8 %shard_map.131 = f32[48,1792]{1,0:T(8,128)} custom-call(f32[48,1792]{1,0:T(8,128)S(1)} %get-tuple-element.83.refs_3_.keep_ref, bf16[48,1792]{1,0:T(8,128)(2,1)S(1)} %collective-permute-done.19.given_ref), custom_call_target="tpu_custom_call" | custom-call | bytes 516096 | tf_op jit(solution)/shard_map/pallas_call | solution.py:40
  58.5 2.8 %collective-permute-done.16.refs_0_ = bf16[8,3712]{1,0:T(8,128)(2,1)S(1)} collective-permute-done((bf16[8,3712]{1,0:T(8,128)(2,1)S(1)}, bf16[8,3712]{1,0:T(8,128)(2,1)S(1)}, u32[]{:S(2)}, u32[]{:S(2)}) %collective-permute-start.16) | collective-permute-done | bytes 59424 | tf_op jit(solution)/shard_map/ppermute | solution.py:19
  61.3 0.6 collective-permute-done.17.refs_1_
  61.9 0.8 %collective-permute-done.18.refs_2_ = bf16[8,3712]{1,0:T(8,128)(2,1)S(1)} collective-permute-done((bf16[8,3712]{1,0:T(8,128)(2,1)S(1)}, bf16[8,3712]{1,0:T(8,128)(2,1)S(1)}, u32[]{:S(2)}, u32[]{:S(2)}) %collective-permute-start.18) | collective-permute-done | bytes 59424 | tf_op jit(solution)/shard_map/ppermute | solution.py:19
  62.7 0.0 copy-done
  62.7 0.8 %shard_map.130 = (bf16[8,3584]{1,0:T(8,128)(2,1)}, f32[8,8]{1,0:T(8,128)}) custom-call(s32[8,8]{1,0:T(8,128)S(1)} %copy-done, f32[8,3712]{1,0:T(8,128)S(1)} %get-tuple-element.84.own_ref, bf16[8,3712]{1,0:T(8,128)(2,1)S(1)} %collective-permute-done.16.refs_0_, bf16[8,3712]{1,0:T(8,128)(2,1)S(1)} %collective-permute-done.17.refs_1_, ...), custom_call_target="tpu_custom_call" | custom-call | bytes 297216 | tf_op jit(solution)/shard_map/pallas_call | solution.py:40
Async XLA Ops:
  0.6 9.3 %collective-permute-start = (bf16[3,16,1792]{2,1,0:T(8,128)(2,1)}, bf16[3,16,1792]{2,1,0:T(8,128)(2,1)S(1)}, u32[]{:S(2)}, u32[]{:S(2)}) collective-permute-start(bf16[3,16,1792]{2,1,0:T(8,128)(2,1)} %mine_hbm.1), channel_id=1, source_target_pairs={{0,1},{1,0},{2,3},{3,2},{4,5},{5,4},{6,7},{7,6},{8,9},{9,8},{10,11... | collective-permute-start | bytes 516104 | tf_op jit(solution)/shard_map/ppermute | solution.py:19
  2.1 15.3 %collective-permute-start.4 = (bf16[8,7296]{1,0:T(8,128)(2,1)S(1)}, bf16[8,7296]{1,0:T(8,128)(2,1)S(1)}, u32[]{:S(2)}, u32[]{:S(2)}) collective-permute-start(bf16[8,7296]{1,0:T(8,128)(2,1)S(1)} %shard_map.121.refs_1_), channel_id=1, source_target_pairs={{0,24},{1,25},{2,26},{3,27},{4,28},{5,29},{6,30},{7,31},{8,16},{9,... | collective-permute-start | bytes 350216 | tf_op jit(solution)/shard_map/ppermute | solution.py:19
  6.7 10.6 %collective-permute-start.3 = (bf16[8,7296]{1,0:T(8,128)(2,1)S(1)}, bf16[8,7296]{1,0:T(8,128)(2,1)S(1)}, u32[]{:S(2)}, u32[]{:S(2)}) collective-permute-start(bf16[8,7296]{1,0:T(8,128)(2,1)S(1)} %shard_map.121.refs_1_), channel_id=1, source_target_pairs={{0,16},{1,17},{2,18},{3,19},{4,20},{5,21},{6,22},{7,23},{8,24},{9,... | collective-permute-start | bytes 350216 | tf_op jit(solution)/shard_map/ppermute | solution.py:19
  6.7 10.6 %collective-permute-start.2 = (bf16[8,7296]{1,0:T(8,128)(2,1)S(1)}, bf16[8,7296]{1,0:T(8,128)(2,1)S(1)}, u32[]{:S(2)}, u32[]{:S(2)}) collective-permute-start(bf16[8,7296]{1,0:T(8,128)(2,1)S(1)} %shard_map.121.refs_1_), channel_id=1, source_target_pairs={{0,8},{1,9},{2,10},{3,11},{4,12},{5,13},{6,14},{7,15},{8,0},{9,1},... | collective-permute-start | bytes 350216 | tf_op jit(solution)/shard_map/ppermute | solution.py:19
  7.4 10.0 %collective-permute-start.1 = (bf16[8,7296]{1,0:T(8,128)(2,1)S(1)}, bf16[8,7296]{1,0:T(8,128)(2,1)S(1)}, u32[]{:S(2)}, u32[]{:S(2)}) collective-permute-start(bf16[8,7296]{1,0:T(8,128)(2,1)S(1)} %shard_map.121.refs_1_), channel_id=1, source_target_pairs={{0,6},{1,7},{2,4},{3,5},{4,2},{5,3},{6,0},{7,1},{8,14},{9,15},{10,... | collective-permute-start | bytes 350216 | tf_op jit(solution)/shard_map/ppermute | solution.py:19
  18.3 12.3 %collective-permute-start.5 = (bf16[24,7296]{1,0:T(8,128)(2,1)S(1)}, bf16[24,7296]{1,0:T(8,128)(2,1)S(1)}, u32[]{:S(2)}, u32[]{:S(2)}) collective-permute-start(bf16[24,7296]{1,0:T(8,128)(2,1)S(1)} %get-tuple-element.55), channel_id=1, source_target_pairs={{0,2},{1,3},{2,0},{3,1},{4,6},{5,7},{6,4},{7,5},{8,10},{9,11},{10,... | collective-permute-start | bytes 1050632 | tf_op jit(solution)/shard_map/ppermute | solution.py:19
  19.7 10.9 %collective-permute-start.7 = (bf16[24,7296]{1,0:T(8,128)(2,1)S(1)}, bf16[24,7296]{1,0:T(8,128)(2,1)S(1)}, u32[]{:S(2)}, u32[]{:S(2)}) collective-permute-start(bf16[24,7296]{1,0:T(8,128)(2,1)S(1)} %get-tuple-element.57), channel_id=1, source_target_pairs={{0,4},{1,5},{2,6},{3,7},{4,0},{5,1},{6,2},{7,3},{8,12},{9,13},{10,... | collective-permute-start | bytes 1050632 | tf_op jit(solution)/shard_map/ppermute | solution.py:19
  21.2 8.5 %collective-permute-start.6 = (bf16[24,1920]{1,0:T(8,128)(2,1)S(1)}, bf16[24,1920]{1,0:T(8,128)(2,1)S(1)}, u32[]{:S(2)}, u32[]{:S(2)}) collective-permute-start(bf16[24,1920]{1,0:T(8,128)(2,1)S(1)} %get-tuple-element.56), channel_id=1, source_target_pairs={{0,16},{1,17},{2,18},{3,19},{4,20},{5,21},{6,22},{7,23},{8,24},{9,... | collective-permute-start | bytes 276488 | tf_op jit(solution)/shard_map/ppermute | solution.py:19
  21.5 8.2 %collective-permute-start.8 = (bf16[24,1920]{1,0:T(8,128)(2,1)S(1)}, bf16[24,1920]{1,0:T(8,128)(2,1)S(1)}, u32[]{:S(2)}, u32[]{:S(2)}) collective-permute-start(bf16[24,1920]{1,0:T(8,128)(2,1)S(1)} %get-tuple-element.58), channel_id=1, source_target_pairs={{0,24},{1,25},{2,26},{3,27},{4,28},{5,29},{6,30},{7,31},{8,16},{9,... | collective-permute-start | bytes 276488 | tf_op jit(solution)/shard_map/ppermute | solution.py:19
  23.8 6.9 %collective-permute-start.9 = (bf16[24,1920]{1,0:T(8,128)(2,1)S(1)}, bf16[24,1920]{1,0:T(8,128)(2,1)S(1)}, u32[]{:S(2)}, u32[]{:S(2)}) collective-permute-start(bf16[24,1920]{1,0:T(8,128)(2,1)S(1)} %get-tuple-element.59), channel_id=1, source_target_pairs={{0,8},{1,9},{2,10},{3,11},{4,12},{5,13},{6,14},{7,15},{8,0},{9,1},... | collective-permute-start | bytes 276488 | tf_op jit(solution)/shard_map/ppermute | solution.py:19
  30.9 2.3 %collective-permute-start.10 = (bf16[104,3712]{1,0:T(8,128)(2,1)S(1)}, bf16[104,3712]{1,0:T(8,128)(2,1)S(1)}, u32[]{:S(2)}, u32[]{:S(2)}) collective-permute-start(bf16[104,3712]{1,0:T(8,128)(2,1)S(1)} %get-tuple-element.61.refs_0_), channel_id=1, source_target_pairs={{0,1},{1,0},{2,3},{3,2},{4,5},{5,4},{6,7},{7,6},{8,9},{9,8},{10,11... | collective-permute-start | bytes 2316296 | tf_op jit(solution)/shard_map/ppermute | solution.py:19
  31.0 4.0 %collective-permute-start.11 = (bf16[104,3584]{1,0:T(8,128)(2,1)S(1)}, bf16[104,3584]{1,0:T(8,128)(2,1)S(1)}, u32[]{:S(2)}, u32[]{:S(2)}) collective-permute-start(bf16[104,3584]{1,0:T(8,128)(2,1)S(1)} %get-tuple-element.65.refs_0_), channel_id=1, source_target_pairs={{0,1},{1,0},{2,3},{3,2},{4,5},{5,4},{6,7},{7,6},{8,9},{9,8},{10,11... | collective-permute-start | bytes 2236424 | tf_op jit(solution)/shard_map/ppermute | solution.py:19
  38.8 2.8 %collective-permute-start.12 = (bf16[104,3712]{1,0:T(8,128)(2,1)S(1)}, bf16[104,3712]{1,0:T(8,128)(2,1)S(1)}, u32[]{:S(2)}, u32[]{:S(2)}) collective-permute-start(bf16[104,3712]{1,0:T(8,128)(2,1)S(1)} %get-tuple-element.67), channel_id=1, source_target_pairs={{0,1},{1,0},{2,3},{3,2},{4,5},{5,4},{6,7},{7,6},{8,9},{9,8},{10,11... | collective-permute-start | bytes 2316296 | tf_op jit(solution)/shard_map/ppermute | solution.py:19
  41.9 9.5 %collective-permute-start.13 = (bf16[24,3712]{1,0:T(8,128)(2,1)S(1)}, bf16[24,3712]{1,0:T(8,128)(2,1)S(1)}, u32[]{:S(2)}, u32[]{:S(2)}) collective-permute-start(bf16[24,3712]{1,0:T(8,128)(2,1)S(1)} %get-tuple-element.74), channel_id=1, source_target_pairs={{0,6},{1,7},{2,4},{3,5},{4,2},{5,3},{6,0},{7,1},{8,14},{9,15},{10,... | collective-permute-start | bytes 534536 | tf_op jit(solution)/shard_map/ppermute | solution.py:19
  42.9 9.6 %collective-permute-start.14 = (bf16[24,3712]{1,0:T(8,128)(2,1)S(1)}, bf16[24,3712]{1,0:T(8,128)(2,1)S(1)}, u32[]{:S(2)}, u32[]{:S(2)}) collective-permute-start(bf16[24,3712]{1,0:T(8,128)(2,1)S(1)} %get-tuple-element.75), channel_id=1, source_target_pairs={{0,2},{1,3},{2,0},{3,1},{4,6},{5,7},{6,4},{7,5},{8,10},{9,11},{10,... | collective-permute-start | bytes 534536 | tf_op jit(solution)/shard_map/ppermute | solution.py:19
  44.0 9.5 %collective-permute-start.15 = (bf16[24,3712]{1,0:T(8,128)(2,1)S(1)}, bf16[24,3712]{1,0:T(8,128)(2,1)S(1)}, u32[]{:S(2)}, u32[]{:S(2)}) collective-permute-start(bf16[24,3712]{1,0:T(8,128)(2,1)S(1)} %get-tuple-element.76.after_ref), channel_id=1, source_target_pairs={{0,4},{1,5},{2,6},{3,7},{4,0},{5,1},{6,2},{7,3},{8,12},{9,13},{10,... | collective-permute-start | bytes 534536 | tf_op jit(solution)/shard_map/ppermute | solution.py:19
  45.5 17.2 %copy-start = (s32[8,8]{1,0:T(8,128)S(1)}, s32[8,8]{1,0:T(8,128)}, u32[]{:S(2)}) copy-start(s32[8,8]{1,0:T(8,128)} %ids_ref.1) | copy-start | bytes 772
  51.4 6.3 %collective-permute-start.19 = (bf16[48,1792]{1,0:T(8,128)(2,1)S(1)}, bf16[48,1792]{1,0:T(8,128)(2,1)S(1)}, u32[]{:S(2)}, u32[]{:S(2)}) collective-permute-start(bf16[48,1792]{1,0:T(8,128)(2,1)S(1)} %get-tuple-element.91), channel_id=1, source_target_pairs={{0,1},{1,0},{2,3},{3,2},{4,5},{5,4},{6,7},{7,6},{8,9},{9,8},{10,11... | collective-permute-start | bytes 516104 | tf_op jit(solution)/shard_map/ppermute | solution.py:19
  53.7 7.6 %collective-permute-start.16 = (bf16[8,3712]{1,0:T(8,128)(2,1)S(1)}, bf16[8,3712]{1,0:T(8,128)(2,1)S(1)}, u32[]{:S(2)}, u32[]{:S(2)}) collective-permute-start(bf16[8,3712]{1,0:T(8,128)(2,1)S(1)} %get-tuple-element.85), channel_id=1, source_target_pairs={{0,16},{1,17},{2,18},{3,19},{4,20},{5,21},{6,22},{7,23},{8,24},{9,... | collective-permute-start | bytes 178184 | tf_op jit(solution)/shard_map/ppermute | solution.py:19
  55.6 6.3 %collective-permute-start.17 = (bf16[8,3712]{1,0:T(8,128)(2,1)S(1)}, bf16[8,3712]{1,0:T(8,128)(2,1)S(1)}, u32[]{:S(2)}, u32[]{:S(2)}) collective-permute-start(bf16[8,3712]{1,0:T(8,128)(2,1)S(1)} %get-tuple-element.86), channel_id=1, source_target_pairs={{0,24},{1,25},{2,26},{3,27},{4,28},{5,29},{6,30},{7,31},{8,16},{9,... | collective-permute-start | bytes 178184 | tf_op jit(solution)/shard_map/ppermute | solution.py:19
  57.8 4.9 %collective-permute-start.18 = (bf16[8,3712]{1,0:T(8,128)(2,1)S(1)}, bf16[8,3712]{1,0:T(8,128)(2,1)S(1)}, u32[]{:S(2)}, u32[]{:S(2)}) collective-permute-start(bf16[8,3712]{1,0:T(8,128)(2,1)S(1)} %get-tuple-element.87), channel_id=1, source_target_pairs={{0,8},{1,9},{2,10},{3,11},{4,12},{5,13},{6,14},{7,15},{8,0},{9,1},... | collective-permute-start | bytes 178184 | tf_op jit(solution)/shard_map/ppermute | solution.py:19

commit v5 on v4

--- a/solution.py
+++ b/solution.py
@@ -115,8 +115,8 @@
                 out[rows, lanes] = (raw[rows, lanes].astype(F32) * factor).astype(B16)
 
 
-def weights_kernel(gate_ref, up_ref, down_ref, narrow_hbm, mine_hbm, other_ref, *refs):
-    raws, outs, (narrow_out, wide_out, mine_ref, small_sems, sems) = refs[:3], refs[3:6], refs[6:]
+def up_side_kernel(gate_ref, up_ref, narrow_hbm, mine_hbm, other_ref, *refs):
+    raws, outs, (narrow_out, wide_out, mine_ref, small_sems, sems) = refs[:2], refs[2:4], refs[4:]
     for copy in copied((narrow_hbm, mine_hbm), (narrow_out, mine_ref), small_sems):
         copy.wait()
     half = mine_ref.shape[2]
@@ -132,7 +132,12 @@
         wide_out[:, :, :half] = other_ref[...]
         wide_out[:, :, half:] = mine_ref[...]
 
-    weights_into(0, (gate_ref, up_ref, down_ref), raws, outs, narrow_out, wide_out, sems)
+    weights_into(0, (gate_ref, up_ref), raws, outs, narrow_out, wide_out, sems)
+
+
+def down_side_kernel(down_ref, narrow_ref, wide_ref, after_ref, raw, out, sems):
+    del after_ref
+    weights_into(2, (down_ref,), (raw,), (out,), narrow_ref, wide_ref, sems)
 
 
 def picks_of(extra, wanted_experts, rows, capacity):
@@ -173,32 +178,31 @@
         first += out.shape[0]
 
 
-def pack_kernel(masks, offsets, rows, capacity, after_ref, *refs):
+def pack_kernel(masks, rows, capacity, lanes, waits, *refs):
+    refs = refs[waits:]
+    sent = len(masks[:3])
+    blocks, pick_out, outs = refs[: -1 - sent], refs[-1 - sent], refs[-sent:]
+    block = stacked(blocks)
+    me = lax.axis_index("expert")
+    picks = picks_of(block[:, lanes], [(me ^ mask) // 2 for mask in masks], rows, capacity)
+    pick_out[...] = jnp.concatenate(picks, axis=0)
+    picks = jnp.concatenate(picks[:sent], axis=0).astype(B16)
+    write_rows(outs, dot32(picks, block.astype(B16)))
+
+
+def cross_kernel(offsets, rows, capacity, lanes, after_ref, block_ref, *outs):
     del after_ref
-    crossing = len(masks) > 2
-    taken = len(refs) - 3 - len(masks[:2]) - crossing * len(offsets)
-    blocks, refs = refs[:taken], refs[taken:]
-    tokens_out, cot_out, pick_out, outs = *refs[:3], refs[3:]
-    block = stacked(blocks[crossing:])
-    held = block.astype(B16)
-    full, width = tokens_out.shape[1], cot_out.shape[1]
-    tokens_out[...] = held[:, :full]
-    cot_out[...] = held[:, full:]
+    block = block_ref[...].astype(F32)
+    width = block.shape[1]
+    folds, step = folds_of(rows, capacity, width)
+    extra = jnp.concatenate([block[:, lanes]] * folds, axis=0)
+    if folds * step > width:
+        block = jnp.concatenate([block, jnp.zeros((rows, folds * step - width), F32)], axis=1)
+    pieces = [block[:, i * step : (i + 1) * step] for i in range(folds)]
+    laid = jnp.concatenate(pieces, axis=0).astype(B16)
     me = lax.axis_index("expert")
-    picks = picks_of(block[:, width:full], [(me ^ m) // 2 for m in masks], rows, capacity)
-    pick_out[...] = jnp.concatenate(picks, axis=0)
-    write_rows(outs[: len(picks[:2])], dot32(jnp.concatenate(picks[:2], axis=0).astype(B16), held))
-    if crossing:
-        block = blocks[0][...].astype(F32)
-        lanes = block.shape[1]
-        folds, step = folds_of(rows, capacity, lanes)
-        extra = jnp.concatenate([block[:, width:full]] * folds, axis=0)
-        if folds * step > lanes:
-            block = jnp.concatenate([block, jnp.zeros((rows, folds * step - lanes), F32)], axis=1)
-        pieces = [block[:, i * step : (i + 1) * step] for i in range(folds)]
-        laid = jnp.concatenate(pieces, axis=0).astype(B16)
-        picks = picks_of(extra, [(me ^ offset) // 2 for offset in offsets], rows, capacity)
-        write_rows(outs[2:], dot32(jnp.concatenate(picks, axis=0).astype(B16), laid))
+    picks = picks_of(extra, [(me ^ offset) // 2 for offset in offsets], rows, capacity)
+    write_rows(outs, dot32(jnp.concatenate(picks, axis=0).astype(B16), laid))
 
 
 def unfolded(refs, folds):
@@ -215,7 +219,8 @@
     return jnp.concatenate([moved[i * slots : (i + 1) * slots] for i in range(folds)], axis=1)
 
 
-def stack_kernel(folds, beside, order, tokens_ref, cot_ref, *refs):
+def stack_kernel(folds, beside, order, after_ref, *refs):
+    del after_ref
     came, (tokens_out, cot_out) = refs[:-2], refs[-2:]
     came = [came[order.index(i)] for i in range(len(order))]
     near, folded = came[:beside], came[beside:]
@@ -223,11 +228,8 @@
     if folded:
         pieces.append(unfolded(folded, folds))
     full, both = tokens_out.shape[1], tokens_out.shape[1] + cot_out.shape[1]
-    for out, lanes, own in (
-        (tokens_out, slice(0, full), tokens_ref), (cot_out, slice(full, both), cot_ref)
-    ):
-        parts = [own[...].astype(F32)] + [piece[:, lanes] for piece in pieces]
-        out[...] = jnp.concatenate(parts, axis=0).astype(B16)
+    for out, lanes in ((tokens_out, slice(0, full)), (cot_out, slice(full, both))):
+        out[...] = jnp.concatenate([piece[:, lanes] for piece in pieces], axis=0).astype(B16)
 
 
 def pre_kernel(experts, width, gate_ref, up_ref, *refs):
@@ -283,26 +285,24 @@
     give_ref[:, width:] = extra[half:].astype(B16)
 
 
-def first_sum_kernel(experts, width, mine_ref, other_ref, after_ref, own_ref, *outs):
+def first_sum_kernel(experts, width, mine_ref, other_ref, after_ref, *outs):
     del after_ref
     total = mine_ref[...].astype(F32) + other_ref[...].astype(F32)
-    count = own_ref.shape[0]
-    own_ref[...] = total[:count]
-    extra = total[count:, width:]
+    rows, extra = total[:, :width], total[:, width:]
     lane = lax.broadcasted_iota(jnp.int32, extra.shape, 1)
     lost = jnp.where(lane < experts, extra - extra.astype(B16).astype(F32), 0.0)
     extra = extra + pltpu.roll(lost, experts, 1) - lost
     slots = outs[0].shape[0]
     for i, out in enumerate(outs):
         part = slice(i * slots, (i + 1) * slots)
-        out[:, :width] = total[count:, :width][part].astype(B16)
+        out[:, :width] = rows[part].astype(B16)
         out[:, width:] = extra[part].astype(B16)
 
 
 def second_sum_kernel(ways, pick_ref, own_ref, *refs):
     came, own_out, outs = refs[: -2 - ways], refs[-1 - ways], refs[len(refs) - ways :]
-    came = came[1:] + came[:1]
-    total = own_ref[...] + dot32(pick_ref[...].astype(B16), stacked(came).astype(B16), TN)
+    came = (own_ref,) + came[1:] + came[:1]
+    total = dot32(pick_ref[...].astype(B16), stacked(came).astype(B16), TN)
     count = own_out.shape[0]
     own_out[...] = total[:count]
     for i, out in enumerate(outs):
@@ -392,7 +392,7 @@
     near, far = stages()[0], stages()[1:]
     count = rows * devices // 2 // (len(near) + 1)
     slots = count // rows * capacity
-    half = count + len(near) * slots
+    half = (1 + len(near)) * slots
     offsets = [0]
     for masks in far:
         offsets = [first ^ mask for first in offsets for mask in (0, *masks)]
@@ -420,43 +420,57 @@
     pieces = pieces_of(message)
     crossed = [send(message, mask) for mask in near[2:]]
     matmul = 2 * 2 * half * width * hidden_units
-    weights = (gate_weight, up_weight, down_weight)
-    gate_raw, up_raw, down_raw, gate_eff, up_eff, down_eff, narrow, wide = in_vmem(
-        weights_kernel,
-        [(weight.shape, B16) for weight in weights] * 2
-        + [(narrow.shape, B16), ((3, rank, width), B16)],
-        (*weights, narrow, wide_factors, send(wide_factors, 1)),
-        3 * matmul,
-        outside=5,
+    gate_raw, up_raw, gate_eff, up_eff, narrow, wide = in_vmem(
+        up_side_kernel,
+        [(gate_weight.shape, B16)] * 4 + [(narrow.shape, B16), ((3, rank, width), B16)],
+        (gate_weight, up_weight, narrow, wide_factors, send(wide_factors, 1)),
+        2 * matmul,
+        outside=4,
         scratch=[
             pltpu.VMEM(wide_factors.shape, B16),
             pltpu.SemaphoreType.DMA((2,)),
-            pltpu.SemaphoreType.DMA((12,)),
+            pltpu.SemaphoreType.DMA((8,)),
         ],
     )
     folds, step = folds_of(rows, capacity, full + width)
-    crossing = len(offsets) if crossed else 0
-    held, cot_held, pick, *packed = in_vmem(
-        functools.partial(pack_kernel, near, offsets, rows, capacity),
-        [((count, full), B16), ((count, width), B16), ((len(near) * slots, count), F32)]
-        + [((slots, full + width), B16)] * len(near[:2])
-        + [((folds * capacity, step), B16)] * crossing,
-        [wide] + crossed + pieces,
-    )
-    came = [send(block, mask) for block, mask in zip(packed, near[:2])]
-    folded = packed[2 : 2 + crossing]
+    probs_at = slice(width, full)
+    folded = []
+    for block in crossed:
+        folded += in_vmem(
+            functools.partial(cross_kernel, offsets, rows, capacity, probs_at),
+            [((folds * capacity, step), B16)] * len(offsets),
+            [wide, block],
+        )
+    beside = near[:2]
+    pick, *packed = in_vmem(
+        functools.partial(
+            pack_kernel, (0, *near), rows, capacity, probs_at, 1 + len(folded[:1])
+        ),
+        [(((1 + len(near)) * slots, count), F32)]
+        + [((slots, full + width), B16)] * (1 + len(beside)),
+        [wide] + folded[:1] + pieces,
+    )
+    came = packed[:1] + [send(block, mask) for block, mask in zip(packed[1:], beside)]
     came += folded[:1] + [send(block, mask) for block, mask in zip(folded[1:], offsets[1:])]
     order = list(range(len(came)))
-    if len(came) > 5:
-        order = [0, 4, 1, 5, *order[6:], 3, 2]
+    if len(came) > 6:
+        order = [0, 1, 5, 2, 6, *order[7:], 4, 3]
+    down_raw, down_eff = in_vmem(
+        down_side_kernel,
+        [(down_weight.shape, B16)] * 2,
+        (down_weight, narrow, wide, pick),
+        matmul,
+        outside=1,
+        scratch=[pltpu.SemaphoreType.DMA((4,))],
+    )
     mine_rows, cot_mine = in_vmem(
-        functools.partial(stack_kernel, folds, len(near[:2]), order),
+        functools.partial(stack_kernel, folds, 1 + len(beside), order),
         [((half, full), B16), ((half, width), B16)],
-        [held, cot_held, *[came[i] for i in order]],
+        [down_eff] + [came[i] for i in order],
     )
     token_rows = [mine_rows, send(mine_rows, 1)]
     cot_rows = [cot_mine, send(cot_mine, 1)]
-    packed_type = [((slots, full), B16)] * len(near)
+    packed_type = [((slots, full), B16)] * (1 + len(near))
 
     wide_type, unit_type = ((2 * half, width), B16), ((2 * half, hidden_units), B16)
     x, probs, pre_gate, pre_up = in_vmem(
@@ -480,7 +494,7 @@
     )
     own, *parts = in_vmem(
         functools.partial(first_sum_kernel, experts, width),
-        [((count, full), F32)] + packed_type,
+        packed_type,
         (mine, other, down_narrow),
     )
     grad_narrow, keep, give = in_vmem(

time: 63.6 us -> 63.3 us (level)
  waiting for transfers between devices: 13.9 us -> 12.1 us
  Pallas kernels: 25.5 us -> 26.9 us
    ppermute x20, waiting for transfers between devices: 13.9 us -> 12.1 us  [send(): return lax.ppermute(value, 'expert', pairs)]
    pallas_call x12 -> x14, Pallas kernels: 25.5 us -> 26.9 us  [in_vmem(): pl.pallas_call(kernel, out_shape=[(jax.ShapeDtypeStruct if i in results e...]
  transfers between devices with their start and end apart: 20 -> 20, of which waited for: 8 -> 9; matrix products, arithmetic and copies ran while one was open for 0% -> 0% of each run, Pallas kernels for 31% -> 33%
where the time goes in v5:
time: 63.3 us; the launch traced here: 63.1 us
  Pallas kernels  26.9 us (42%)
  starting transfers between devices  23.3 us (37%)
  waiting for transfers between devices  12.1 us (19%)
  between operations  0.75 us (1%)
    pallas_call x14, Pallas kernels, in_vmem(): pl.pallas_call(kernel, out_shape=[(jax.ShapeDtypeStruct if i in results e...  26.9 us
    ppermute x20, starting transfers between devices, send(): return lax.ppermute(value, 'expert', pairs)  23.3 us
    ppermute x20, waiting for transfers between devices, send(): return lax.ppermute(value, 'expert', pairs)  12.1 us
  transfers between devices with their start and end apart: 20, of which 9 were waited for; matrix products, arithmetic and copies ran while one was open for 0% of the time, Pallas kernels for 33%

profile of v5, /device:TPU:0, one launch (start us, length us, event | category | flops | bytes accessed | tf_op | source)
XLA Modules:
  0.0 63.1 jit_solution(10774824776659174455)
XLA Ops:
  0.6 0.5 collective-permute-start
  1.1 0.9 %shard_map.121.refs_2_ = bf16[8,7296]{1,0:T(8,128)(2,1)S(1)} custom-call(bf16[8,3584]{1,0:T(8,128)(2,1)} %refs_0_.1, bf16[8,3584]{1,0:T(8,128)(2,1)} %refs_1_.1, f32[8,8]{1,0:T(8,128)} %refs_2_.1, s32[8,8]{1,0:T(8,128)} %ids_ref.1), custom_call_target="tpu_custom_call" | custom-call | bytes 115200 | tf_op jit(solution)/shard_map/pallas_call | solution.py:40
  2.1 4.7 %collective-permute-start.4 = (bf16[8,7296]{1,0:T(8,128)(2,1)S(1)}, bf16[8,7296]{1,0:T(8,128)(2,1)S(1)}, u32[]{:S(2)}, u32[]{:S(2)}) collective-permute-start(bf16[8,7296]{1,0:T(8,128)(2,1)S(1)} %shard_map.121.refs_2_), channel_id=1, source_target_pairs={{0,24},{1,25},{2,26},{3,27},{4,28},{5,29},{6,30},{7,31},{8,16},{9,... | collective-permute-start | bytes 350216 | tf_op jit(solution)/shard_map/ppermute | solution.py:19
  6.7 0.0 collective-permute-start.3
  6.7 0.6 %collective-permute-start.2 = (bf16[8,7296]{1,0:T(8,128)(2,1)S(1)}, bf16[8,7296]{1,0:T(8,128)(2,1)S(1)}, u32[]{:S(2)}, u32[]{:S(2)}) collective-permute-start(bf16[8,7296]{1,0:T(8,128)(2,1)S(1)} %shard_map.121.refs_2_), channel_id=1, source_target_pairs={{0,8},{1,9},{2,10},{3,11},{4,12},{5,13},{6,14},{7,15},{8,0},{9,1},... | collective-permute-start | bytes 350216 | tf_op jit(solution)/shard_map/ppermute | solution.py:19
  7.4 2.6 %collective-permute-start.1 = (bf16[8,7296]{1,0:T(8,128)(2,1)S(1)}, bf16[8,7296]{1,0:T(8,128)(2,1)S(1)}, u32[]{:S(2)}, u32[]{:S(2)}) collective-permute-start(bf16[8,7296]{1,0:T(8,128)(2,1)S(1)} %shard_map.121.refs_2_), channel_id=1, source_target_pairs={{0,6},{1,7},{2,4},{3,5},{4,2},{5,3},{6,0},{7,1},{8,14},{9,15},{10,... | collective-permute-start | bytes 350216 | tf_op jit(solution)/shard_map/ppermute | solution.py:19
  10.0 0.0 collective-permute-done.other_ref
  10.0 5.6 %shard_map.120 = (bf16[3584,512]{1,0:T(8,128)(2,1)S(1)}, bf16[3584,512]{1,0:T(8,128)(2,1)S(1)}, bf16[3584,512]{1,0:T(8,128)(2,1)S(1)}, bf16[3584,512]{1,0:T(8,12...) custom-call(bf16[3584,512]{1,0:T(8,128)(2,1)} %gate_ref.1, bf16[3584,512]{1,0:T(8,128)(2,1)} %up_ref.1, ...), custom_call_target="tpu_custom_call" | custom-call | flops 1409286144 | bytes 7733248 | tf_op jit(solution)/shard_map/pallas_call | solution.py:40
  15.6 0.0 collective-permute-done.1.block_ref
  15.6 0.5 shard_map.122
  16.1 0.0 collective-permute-done.4.refs_5_
  16.1 1.1 %collective-permute-done.3.refs_4_ = bf16[8,7296]{1,0:T(8,128)(2,1)S(1)} collective-permute-done((bf16[8,7296]{1,0:T(8,128)(2,1)S(1)}, bf16[8,7296]{1,0:T(8,128)(2,1)S(1)}, u32[]{:S(2)}, u32[]{:S(2)}) %collective-permute-start.3) | collective-permute-done | bytes 116768 | tf_op jit(solution)/shard_map/ppermute | solution.py:19
  17.2 0.0 collective-permute-done.2.refs_3_
  17.2 0.7 %shard_map.123 = (f32[96,32]{1,0:T(8,128)S(1)}, bf16[24,7296]{1,0:T(8,128)(2,1)S(1)}, bf16[24,7296]{1,0:T(8,128)(2,1)S(1)}, bf16[24,7296]{1,0:T(8,128)(2,1)S(1)}) custom-call(bf16[3,16,3584]{2,1,0:T(8,128)(2,1)S(1)} %get-tuple-element.47.after_ref.refs_0_.wide_ref, bf16[24,1920]{1,0:T(8,128)(2,1)S(1)} %get-tuple-element.48.refs_1_.refs_6_, ...), custom_call_target="tpu_custom_call" | custom-call | bytes 903168 | tf_op jit(solution)/shard_map/pallas_call | solution.py:40
  18.0 1.6 %collective-permute-start.5 = (bf16[24,7296]{1,0:T(8,128)(2,1)S(1)}, bf16[24,7296]{1,0:T(8,128)(2,1)S(1)}, u32[]{:S(2)}, u32[]{:S(2)}) collective-permute-start(bf16[24,7296]{1,0:T(8,128)(2,1)S(1)} %get-tuple-element.55), channel_id=1, source_target_pairs={{0,2},{1,3},{2,0},{3,1},{4,6},{5,7},{6,4},{7,5},{8,10},{9,11},{10,... | collective-permute-start | bytes 1050632 | tf_op jit(solution)/shard_map/ppermute | solution.py:19
  19.5 1.5 %collective-permute-start.7 = (bf16[24,7296]{1,0:T(8,128)(2,1)S(1)}, bf16[24,7296]{1,0:T(8,128)(2,1)S(1)}, u32[]{:S(2)}, u32[]{:S(2)}) collective-permute-start(bf16[24,7296]{1,0:T(8,128)(2,1)S(1)} %get-tuple-element.57), channel_id=1, source_target_pairs={{0,4},{1,5},{2,6},{3,7},{4,0},{5,1},{6,2},{7,3},{8,12},{9,13},{10,... | collective-permute-start | bytes 1050632 | tf_op jit(solution)/shard_map/ppermute | solution.py:19
  21.0 0.0 collective-permute-start.6
  21.0 2.5 %collective-permute-start.8 = (bf16[24,1920]{1,0:T(8,128)(2,1)S(1)}, bf16[24,1920]{1,0:T(8,128)(2,1)S(1)}, u32[]{:S(2)}, u32[]{:S(2)}) collective-permute-start(bf16[24,1920]{1,0:T(8,128)(2,1)S(1)} %get-tuple-element.58), channel_id=1, source_target_pairs={{0,24},{1,25},{2,26},{3,27},{4,28},{5,29},{6,30},{7,31},{8,16},{9,... | collective-permute-start | bytes 276488 | tf_op jit(solution)/shard_map/ppermute | solution.py:19
  23.6 1.0 %collective-permute-start.9 = (bf16[24,1920]{1,0:T(8,128)(2,1)S(1)}, bf16[24,1920]{1,0:T(8,128)(2,1)S(1)}, u32[]{:S(2)}, u32[]{:S(2)}) collective-permute-start(bf16[24,1920]{1,0:T(8,128)(2,1)S(1)} %get-tuple-element.59), channel_id=1, source_target_pairs={{0,8},{1,9},{2,10},{3,11},{4,12},{5,13},{6,14},{7,15},{8,0},{9,1},... | collective-permute-start | bytes 276488 | tf_op jit(solution)/shard_map/ppermute | solution.py:19
  24.5 2.9 %shard_map.124 = (bf16[512,3584]{1,0:T(8,128)(2,1)S(1)}, bf16[512,3584]{1,0:T(8,128)(2,1)S(1)}) custom-call(bf16[512,3584]{1,0:T(8,128)(2,1)} %down_ref.1, bf16[3,16,512]{2,1,0:T(8,128)(2,1)S(1)} %get-tuple-element.52.narrow_ref, bf16[3,16,3584]{2,1,0:T(8,128)(2,1)S(1)} %get-tuple-element.47.after_ref.refs_0_.wide_ref, ...), custom_call_target="tpu_custom_call" | custom-call | flops 704643072 | bytes 4075520 | tf_op jit(solution)/shard_map/pallas_call | solution.py:40
  27.4 2.1 %collective-permute-done.6.refs_2_ = bf16[24,1920]{1,0:T(8,128)(2,1)S(1)} collective-permute-done((bf16[24,1920]{1,0:T(8,128)(2,1)S(1)}, bf16[24,1920]{1,0:T(8,128)(2,1)S(1)}, u32[]{:S(2)}, u32[]{:S(2)}) %collective-permute-start.6) | collective-permute-done | bytes 92192 | tf_op jit(solution)/shard_map/ppermute | solution.py:19
  29.5 0.0 collective-permute-done.8.refs_4_
  29.5 0.9 %collective-permute-done.9.refs_5_ = bf16[24,1920]{1,0:T(8,128)(2,1)S(1)} collective-permute-done((bf16[24,1920]{1,0:T(8,128)(2,1)S(1)}, bf16[24,1920]{1,0:T(8,128)(2,1)S(1)}, u32[]{:S(2)}, u32[]{:S(2)}) %collective-permute-start.9) | collective-permute-done | bytes 92192 | tf_op jit(solution)/shard_map/ppermute | solution.py:19
  30.4 0.0 collective-permute-done.5.refs_1_
  30.4 0.0 collective-permute-done.7.refs_3_
  30.4 0.3 shard_map.125
  30.7 0.1 collective-permute-start.10
  30.8 0.5 collective-permute-start.11
  31.3 1.7 %collective-permute-done.10.refs_1_ = bf16[96,3712]{1,0:T(8,128)(2,1)S(1)} collective-permute-done((bf16[96,3712]{1,0:T(8,128)(2,1)S(1)}, bf16[96,3712]{1,0:T(8,128)(2,1)S(1)}, u32[]{:S(2)}, u32[]{:S(2)}) %collective-permute-start.10) | collective-permute-done | bytes 712736 | tf_op jit(solution)/shard_map/ppermute | solution.py:19
  33.0 1.6 %shard_map.126 = (bf16[192,3584]{1,0:T(8,128)(2,1)S(1)}, f32[192,128]{1,0:T(8,128)S(1)}, f32[192,512]{1,0:T(8,128)S(1)}, f32[192,512]{1,0:T(8,128)S(1)}) custom-call(bf16[3584,512]{1,0:T(8,128)(2,1)S(1)} %get-tuple-element.50.gate_ref, bf16[3584,512]{1,0:T(8,128)(2,1)S(1)} %get-tuple-element.51.up_ref, bf16[96,3712]{1,0:T(8,128)(2,1)S(1)} %get-tuple-element.60.refs_0_, ...), custom_call_target="tpu_custom_call" | custom-call | flops 1409286144 | bytes 8765440 | tf_op jit(solution)/shard_map/pallas_call | solution.py:40
  34.6 0.0 collective-permute-done.11.refs_1_
  34.6 3.9 %shard_map.127 = (bf16[192,3584]{1,0:T(8,128)(2,1)S(1)}, bf16[192,512]{1,0:T(8,128)(2,1)S(1)}, bf16[192,512]{1,0:T(8,128)(2,1)S(1)}, bf16[192,512]{1,0:T(8,128)(...) custom-call(bf16[3584,512]{1,0:T(8,128)(2,1)S(1)} %get-tuple-element.50.gate_ref, ...), custom_call_target="tpu_custom_call" | custom-call | flops 2113929216 | bytes 13271040 | tf_op jit(solution)/shard_map/pallas_call | solution.py:40
  38.5 0.2 collective-permute-start.12
  38.7 2.5 %shard_map.128 = (f32[16,512]{1,0:T(8,128)S(1)}, f32[16,3584]{1,0:T(8,128)S(1)}) custom-call(bf16[192,3584]{1,0:T(8,128)(2,1)S(1)} %get-tuple-element.67.y_ref, bf16[192,512]{1,0:T(8,128)(2,1)S(1)} %get-tuple-element.68.hidden_ref, bf16[512,3584]{1,0:T(8,128)(2,1)S(1)} %get-tuple-element.69.down_ref, bf16[3,16,512]{2,1,0:T(8,128)(2,1)S(1)} %get-tuple-element.52.narrow_ref, ...), custom_call_target="tpu_custom_call" | custom-call | flops 1409286144 | bytes 5636096 | tf_op jit(solution)/shard_map/pallas_call | solution.py:40
  41.2 0.0 collective-permute-done.12.other_ref
  41.2 0.4 shard_map.129
  41.6 0.6 collective-permute-start.13
  42.1 1.5 %collective-permute-start.14 = (bf16[24,3712]{1,0:T(8,128)(2,1)S(1)}, bf16[24,3712]{1,0:T(8,128)(2,1)S(1)}, u32[]{:S(2)}, u32[]{:S(2)}) collective-permute-start(bf16[24,3712]{1,0:T(8,128)(2,1)S(1)} %get-tuple-element.73), channel_id=1, source_target_pairs={{0,2},{1,3},{2,0},{3,1},{4,6},{5,7},{6,4},{7,5},{8,10},{9,11},{10,... | collective-permute-start | bytes 534536 | tf_op jit(solution)/shard_map/ppermute | solution.py:19
  43.6 1.5 %collective-permute-start.15 = (bf16[24,3712]{1,0:T(8,128)(2,1)S(1)}, bf16[24,3712]{1,0:T(8,128)(2,1)S(1)}, u32[]{:S(2)}, u32[]{:S(2)}) collective-permute-start(bf16[24,3712]{1,0:T(8,128)(2,1)S(1)} %get-tuple-element.74.after_ref), channel_id=1, source_target_pairs={{0,4},{1,5},{2,6},{3,7},{4,0},{5,1},{6,2},{7,3},{8,12},{9,13},{10,... | collective-permute-start | bytes 534536 | tf_op jit(solution)/shard_map/ppermute | solution.py:19
  45.1 0.0 copy-start
  45.1 5.9 %shard_map.130 = (f32[48,512]{1,0:T(8,128)}, f32[48,1792]{1,0:T(8,128)S(1)}, bf16[48,1792]{1,0:T(8,128)(2,1)S(1)}) custom-call(bf16[192,3584]{1,0:T(8,128)(2,1)S(1)} %get-tuple-element.75.x_ref, bf16[192,512]{1,0:T(8,128)(2,1)S(1)} %get-tuple-element.76.grad_gate_ref, bf16[192,512]{1,0:T(8,128)(2,1)S(1)} %get-tuple-element.77.grad_up_ref, ...), custom_call_target="tpu_custom_call" | custom-call | flops 2818572288 | bytes 9943040 | tf_op jit(solution)/shard_map/pallas_call | solution.py:40
  51.0 0.0 collective-permute-start.19
  51.0 0.0 collective-permute-done.13.refs_0_
  51.0 1.2 %collective-permute-done.14.refs_1_ = bf16[24,3712]{1,0:T(8,128)(2,1)S(1)} collective-permute-done((bf16[24,3712]{1,0:T(8,128)(2,1)S(1)}, bf16[24,3712]{1,0:T(8,128)(2,1)S(1)}, u32[]{:S(2)}, u32[]{:S(2)}) %collective-permute-start.14) | collective-permute-done | bytes 178208 | tf_op jit(solution)/shard_map/ppermute | solution.py:19
  52.2 0.9 %collective-permute-done.15.refs_2_ = bf16[24,3712]{1,0:T(8,128)(2,1)S(1)} collective-permute-done((bf16[24,3712]{1,0:T(8,128)(2,1)S(1)}, bf16[24,3712]{1,0:T(8,128)(2,1)S(1)}, u32[]{:S(2)}, u32[]{:S(2)}) %collective-permute-start.15) | collective-permute-done | bytes 178208 | tf_op jit(solution)/shard_map/ppermute | solution.py:19
  53.1 0.3 shard_map.131
  53.4 1.8 %collective-permute-start.16 = (bf16[8,3712]{1,0:T(8,128)(2,1)S(1)}, bf16[8,3712]{1,0:T(8,128)(2,1)S(1)}, u32[]{:S(2)}, u32[]{:S(2)}) collective-permute-start(bf16[8,3712]{1,0:T(8,128)(2,1)S(1)} %get-tuple-element.83), channel_id=1, source_target_pairs={{0,16},{1,17},{2,18},{3,19},{4,20},{5,21},{6,22},{7,23},{8,24},{9,... | collective-permute-start | bytes 178184 | tf_op jit(solution)/shard_map/ppermute | solution.py:19
  55.2 2.2 %collective-permute-start.17 = (bf16[8,3712]{1,0:T(8,128)(2,1)S(1)}, bf16[8,3712]{1,0:T(8,128)(2,1)S(1)}, u32[]{:S(2)}, u32[]{:S(2)}) collective-permute-start(bf16[8,3712]{1,0:T(8,128)(2,1)S(1)} %get-tuple-element.84), channel_id=1, source_target_pairs={{0,24},{1,25},{2,26},{3,27},{4,28},{5,29},{6,30},{7,31},{8,16},{9,... | collective-permute-start | bytes 178184 | tf_op jit(solution)/shard_map/ppermute | solution.py:19
  57.4 0.0 collective-permute-start.18
  57.4 0.0 collective-permute-done.19.given_ref
  57.4 0.8 %shard_map.133 = f32[48,1792]{1,0:T(8,128)} custom-call(f32[48,1792]{1,0:T(8,128)S(1)} %get-tuple-element.81.refs_3_.keep_ref, bf16[48,1792]{1,0:T(8,128)(2,1)S(1)} %collective-permute-done.19.given_ref), custom_call_target="tpu_custom_call" | custom-call | bytes 516096 | tf_op jit(solution)/shard_map/pallas_call | solution.py:40
  58.2 2.9 %collective-permute-done.16.refs_0_ = bf16[8,3712]{1,0:T(8,128)(2,1)S(1)} collective-permute-done((bf16[8,3712]{1,0:T(8,128)(2,1)S(1)}, bf16[8,3712]{1,0:T(8,128)(2,1)S(1)}, u32[]{:S(2)}, u32[]{:S(2)}) %collective-permute-start.16) | collective-permute-done | bytes 59424 | tf_op jit(solution)/shard_map/ppermute | solution.py:19
  61.0 0.5 collective-permute-done.17.refs_1_
  61.5 0.8 %collective-permute-done.18.refs_2_ = bf16[8,3712]{1,0:T(8,128)(2,1)S(1)} collective-permute-done((bf16[8,3712]{1,0:T(8,128)(2,1)S(1)}, bf16[8,3712]{1,0:T(8,128)(2,1)S(1)}, u32[]{:S(2)}, u32[]{:S(2)}) %collective-permute-start.18) | collective-permute-done | bytes 59424 | tf_op jit(solution)/shard_map/ppermute | solution.py:19
  62.4 0.0 copy-done
  62.4 0.8 %shard_map.132 = (bf16[8,3584]{1,0:T(8,128)(2,1)}, f32[8,8]{1,0:T(8,128)}) custom-call(s32[8,8]{1,0:T(8,128)S(1)} %copy-done, f32[8,3712]{1,0:T(8,128)S(1)} %get-tuple-element.82.own_ref, bf16[8,3712]{1,0:T(8,128)(2,1)S(1)} %collective-permute-done.16.refs_0_, bf16[8,3712]{1,0:T(8,128)(2,1)S(1)} %collective-permute-done.17.refs_1_, ...), custom_call_target="tpu_custom_call" | custom-call | bytes 297216 | tf_op jit(solution)/shard_map/pallas_call | solution.py:40
Async XLA Ops:
  0.6 9.3 %collective-permute-start = (bf16[3,16,1792]{2,1,0:T(8,128)(2,1)}, bf16[3,16,1792]{2,1,0:T(8,128)(2,1)S(1)}, u32[]{:S(2)}, u32[]{:S(2)}) collective-permute-start(bf16[3,16,1792]{2,1,0:T(8,128)(2,1)} %mine_hbm.1), channel_id=1, source_target_pairs={{0,1},{1,0},{2,3},{3,2},{4,5},{5,4},{6,7},{7,6},{8,9},{9,8},{10,11... | collective-permute-start | bytes 516104 | tf_op jit(solution)/shard_map/ppermute | solution.py:19
  2.1 14.1 %collective-permute-start.4 = (bf16[8,7296]{1,0:T(8,128)(2,1)S(1)}, bf16[8,7296]{1,0:T(8,128)(2,1)S(1)}, u32[]{:S(2)}, u32[]{:S(2)}) collective-permute-start(bf16[8,7296]{1,0:T(8,128)(2,1)S(1)} %shard_map.121.refs_2_), channel_id=1, source_target_pairs={{0,24},{1,25},{2,26},{3,27},{4,28},{5,29},{6,30},{7,31},{8,16},{9,... | collective-permute-start | bytes 350216 | tf_op jit(solution)/shard_map/ppermute | solution.py:19
  6.7 10.5 %collective-permute-start.3 = (bf16[8,7296]{1,0:T(8,128)(2,1)S(1)}, bf16[8,7296]{1,0:T(8,128)(2,1)S(1)}, u32[]{:S(2)}, u32[]{:S(2)}) collective-permute-start(bf16[8,7296]{1,0:T(8,128)(2,1)S(1)} %shard_map.121.refs_2_), channel_id=1, source_target_pairs={{0,16},{1,17},{2,18},{3,19},{4,20},{5,21},{6,22},{7,23},{8,24},{9,... | collective-permute-start | bytes 350216 | tf_op jit(solution)/shard_map/ppermute | solution.py:19
  6.7 10.5 %collective-permute-start.2 = (bf16[8,7296]{1,0:T(8,128)(2,1)S(1)}, bf16[8,7296]{1,0:T(8,128)(2,1)S(1)}, u32[]{:S(2)}, u32[]{:S(2)}) collective-permute-start(bf16[8,7296]{1,0:T(8,128)(2,1)S(1)} %shard_map.121.refs_2_), channel_id=1, source_target_pairs={{0,8},{1,9},{2,10},{3,11},{4,12},{5,13},{6,14},{7,15},{8,0},{9,1},... | collective-permute-start | bytes 350216 | tf_op jit(solution)/shard_map/ppermute | solution.py:19
  7.4 8.2 %collective-permute-start.1 = (bf16[8,7296]{1,0:T(8,128)(2,1)S(1)}, bf16[8,7296]{1,0:T(8,128)(2,1)S(1)}, u32[]{:S(2)}, u32[]{:S(2)}) collective-permute-start(bf16[8,7296]{1,0:T(8,128)(2,1)S(1)} %shard_map.121.refs_2_), channel_id=1, source_target_pairs={{0,6},{1,7},{2,4},{3,5},{4,2},{5,3},{6,0},{7,1},{8,14},{9,15},{10,... | collective-permute-start | bytes 350216 | tf_op jit(solution)/shard_map/ppermute | solution.py:19
  18.0 12.5 %collective-permute-start.5 = (bf16[24,7296]{1,0:T(8,128)(2,1)S(1)}, bf16[24,7296]{1,0:T(8,128)(2,1)S(1)}, u32[]{:S(2)}, u32[]{:S(2)}) collective-permute-start(bf16[24,7296]{1,0:T(8,128)(2,1)S(1)} %get-tuple-element.55), channel_id=1, source_target_pairs={{0,2},{1,3},{2,0},{3,1},{4,6},{5,7},{6,4},{7,5},{8,10},{9,11},{10,... | collective-permute-start | bytes 1050632 | tf_op jit(solution)/shard_map/ppermute | solution.py:19
  19.5 10.9 %collective-permute-start.7 = (bf16[24,7296]{1,0:T(8,128)(2,1)S(1)}, bf16[24,7296]{1,0:T(8,128)(2,1)S(1)}, u32[]{:S(2)}, u32[]{:S(2)}) collective-permute-start(bf16[24,7296]{1,0:T(8,128)(2,1)S(1)} %get-tuple-element.57), channel_id=1, source_target_pairs={{0,4},{1,5},{2,6},{3,7},{4,0},{5,1},{6,2},{7,3},{8,12},{9,13},{10,... | collective-permute-start | bytes 1050632 | tf_op jit(solution)/shard_map/ppermute | solution.py:19
  21.0 8.5 %collective-permute-start.6 = (bf16[24,1920]{1,0:T(8,128)(2,1)S(1)}, bf16[24,1920]{1,0:T(8,128)(2,1)S(1)}, u32[]{:S(2)}, u32[]{:S(2)}) collective-permute-start(bf16[24,1920]{1,0:T(8,128)(2,1)S(1)} %get-tuple-element.56), channel_id=1, source_target_pairs={{0,16},{1,17},{2,18},{3,19},{4,20},{5,21},{6,22},{7,23},{8,24},{9,... | collective-permute-start | bytes 276488 | tf_op jit(solution)/shard_map/ppermute | solution.py:19
  21.0 8.5 %collective-permute-start.8 = (bf16[24,1920]{1,0:T(8,128)(2,1)S(1)}, bf16[24,1920]{1,0:T(8,128)(2,1)S(1)}, u32[]{:S(2)}, u32[]{:S(2)}) collective-permute-start(bf16[24,1920]{1,0:T(8,128)(2,1)S(1)} %get-tuple-element.58), channel_id=1, source_target_pairs={{0,24},{1,25},{2,26},{3,27},{4,28},{5,29},{6,30},{7,31},{8,16},{9,... | collective-permute-start | bytes 276488 | tf_op jit(solution)/shard_map/ppermute | solution.py:19
  23.6 6.9 %collective-permute-start.9 = (bf16[24,1920]{1,0:T(8,128)(2,1)S(1)}, bf16[24,1920]{1,0:T(8,128)(2,1)S(1)}, u32[]{:S(2)}, u32[]{:S(2)}) collective-permute-start(bf16[24,1920]{1,0:T(8,128)(2,1)S(1)} %get-tuple-element.59), channel_id=1, source_target_pairs={{0,8},{1,9},{2,10},{3,11},{4,12},{5,13},{6,14},{7,15},{8,0},{9,1},... | collective-permute-start | bytes 276488 | tf_op jit(solution)/shard_map/ppermute | solution.py:19
  30.7 2.2 %collective-permute-start.10 = (bf16[96,3712]{1,0:T(8,128)(2,1)S(1)}, bf16[96,3712]{1,0:T(8,128)(2,1)S(1)}, u32[]{:S(2)}, u32[]{:S(2)}) collective-permute-start(bf16[96,3712]{1,0:T(8,128)(2,1)S(1)} %get-tuple-element.60.refs_0_), channel_id=1, source_target_pairs={{0,1},{1,0},{2,3},{3,2},{4,5},{5,4},{6,7},{7,6},{8,9},{9,8},{10,11... | collective-permute-start | bytes 2138120 | tf_op jit(solution)/shard_map/ppermute | solution.py:19
  30.8 3.8 %collective-permute-start.11 = (bf16[96,3584]{1,0:T(8,128)(2,1)S(1)}, bf16[96,3584]{1,0:T(8,128)(2,1)S(1)}, u32[]{:S(2)}, u32[]{:S(2)}) collective-permute-start(bf16[96,3584]{1,0:T(8,128)(2,1)S(1)} %get-tuple-element.64.refs_0_), channel_id=1, source_target_pairs={{0,1},{1,0},{2,3},{3,2},{4,5},{5,4},{6,7},{7,6},{8,9},{9,8},{10,11... | collective-permute-start | bytes 2064392 | tf_op jit(solution)/shard_map/ppermute | solution.py:19
  38.5 2.7 %collective-permute-start.12 = (bf16[96,3712]{1,0:T(8,128)(2,1)S(1)}, bf16[96,3712]{1,0:T(8,128)(2,1)S(1)}, u32[]{:S(2)}, u32[]{:S(2)}) collective-permute-start(bf16[96,3712]{1,0:T(8,128)(2,1)S(1)} %get-tuple-element.66), channel_id=1, source_target_pairs={{0,1},{1,0},{2,3},{3,2},{4,5},{5,4},{6,7},{7,6},{8,9},{9,8},{10,11... | collective-permute-start | bytes 2138120 | tf_op jit(solution)/shard_map/ppermute | solution.py:19
  41.6 9.4 %collective-permute-start.13 = (bf16[24,3712]{1,0:T(8,128)(2,1)S(1)}, bf16[24,3712]{1,0:T(8,128)(2,1)S(1)}, u32[]{:S(2)}, u32[]{:S(2)}) collective-permute-start(bf16[24,3712]{1,0:T(8,128)(2,1)S(1)} %get-tuple-element.72), channel_id=1, source_target_pairs={{0,6},{1,7},{2,4},{3,5},{4,2},{5,3},{6,0},{7,1},{8,14},{9,15},{10,... | collective-permute-start | bytes 534536 | tf_op jit(solution)/shard_map/ppermute | solution.py:19
  42.1 10.1 %collective-permute-start.14 = (bf16[24,3712]{1,0:T(8,128)(2,1)S(1)}, bf16[24,3712]{1,0:T(8,128)(2,1)S(1)}, u32[]{:S(2)}, u32[]{:S(2)}) collective-permute-start(bf16[24,3712]{1,0:T(8,128)(2,1)S(1)} %get-tuple-element.73), channel_id=1, source_target_pairs={{0,2},{1,3},{2,0},{3,1},{4,6},{5,7},{6,4},{7,5},{8,10},{9,11},{10,... | collective-permute-start | bytes 534536 | tf_op jit(solution)/shard_map/ppermute | solution.py:19
  43.6 9.5 %collective-permute-start.15 = (bf16[24,3712]{1,0:T(8,128)(2,1)S(1)}, bf16[24,3712]{1,0:T(8,128)(2,1)S(1)}, u32[]{:S(2)}, u32[]{:S(2)}) collective-permute-start(bf16[24,3712]{1,0:T(8,128)(2,1)S(1)} %get-tuple-element.74.after_ref), channel_id=1, source_target_pairs={{0,4},{1,5},{2,6},{3,7},{4,0},{5,1},{6,2},{7,3},{8,12},{9,13},{10,... | collective-permute-start | bytes 534536 | tf_op jit(solution)/shard_map/ppermute | solution.py:19
  45.1 17.2 %copy-start = (s32[8,8]{1,0:T(8,128)S(1)}, s32[8,8]{1,0:T(8,128)}, u32[]{:S(2)}) copy-start(s32[8,8]{1,0:T(8,128)} %ids_ref.1) | copy-start | bytes 772
  51.0 6.4 %collective-permute-start.19 = (bf16[48,1792]{1,0:T(8,128)(2,1)S(1)}, bf16[48,1792]{1,0:T(8,128)(2,1)S(1)}, u32[]{:S(2)}, u32[]{:S(2)}) collective-permute-start(bf16[48,1792]{1,0:T(8,128)(2,1)S(1)} %get-tuple-element.89), channel_id=1, source_target_pairs={{0,1},{1,0},{2,3},{3,2},{4,5},{5,4},{6,7},{7,6},{8,9},{9,8},{10,11... | collective-permute-start | bytes 516104 | tf_op jit(solution)/shard_map/ppermute | solution.py:19
  53.4 7.6 %collective-permute-start.16 = (bf16[8,3712]{1,0:T(8,128)(2,1)S(1)}, bf16[8,3712]{1,0:T(8,128)(2,1)S(1)}, u32[]{:S(2)}, u32[]{:S(2)}) collective-permute-start(bf16[8,3712]{1,0:T(8,128)(2,1)S(1)} %get-tuple-element.83), channel_id=1, source_target_pairs={{0,16},{1,17},{2,18},{3,19},{4,20},{5,21},{6,22},{7,23},{8,24},{9,... | collective-permute-start | bytes 178184 | tf_op jit(solution)/shard_map/ppermute | solution.py:19
  55.2 6.3 %collective-permute-start.17 = (bf16[8,3712]{1,0:T(8,128)(2,1)S(1)}, bf16[8,3712]{1,0:T(8,128)(2,1)S(1)}, u32[]{:S(2)}, u32[]{:S(2)}) collective-permute-start(bf16[8,3712]{1,0:T(8,128)(2,1)S(1)} %get-tuple-element.84), channel_id=1, source_target_pairs={{0,24},{1,25},{2,26},{3,27},{4,28},{5,29},{6,30},{7,31},{8,16},{9,... | collective-permute-start | bytes 178184 | tf_op jit(solution)/shard_map/ppermute | solution.py:19
  57.4 5.0 %collective-permute-start.18 = (bf16[8,3712]{1,0:T(8,128)(2,1)S(1)}, bf16[8,3712]{1,0:T(8,128)(2,1)S(1)}, u32[]{:S(2)}, u32[]{:S(2)}) collective-permute-start(bf16[8,3712]{1,0:T(8,128)(2,1)S(1)} %get-tuple-element.85), channel_id=1, source_target_pairs={{0,8},{1,9},{2,10},{3,11},{4,12},{5,13},{6,14},{7,15},{8,0},{9,1},... | collective-permute-start | bytes 178184 | tf_op jit(solution)/shard_map/ppermute | solution.py:19

commit v6 on v5

--- a/solution.py
+++ b/solution.py
@@ -196,27 +196,39 @@
     width = block.shape[1]
     folds, step = folds_of(rows, capacity, width)
     extra = jnp.concatenate([block[:, lanes]] * folds, axis=0)
+    laid = lane_pieces(block, folds, step).astype(B16)
+    me = lax.axis_index("expert")
+    picks = picks_of(extra, [(me ^ offset) // 2 for offset in offsets], rows, capacity)
+    picks = jnp.concatenate(picks, axis=0)
+    outs[0][...] = picks
+    write_rows(outs[1:], dot32(picks.astype(B16), laid))
+
+
+def lane_pieces(block, folds, step):
+    rows, width = block.shape
     if folds * step > width:
         block = jnp.concatenate([block, jnp.zeros((rows, folds * step - width), F32)], axis=1)
-    pieces = [block[:, i * step : (i + 1) * step] for i in range(folds)]
-    laid = jnp.concatenate(pieces, axis=0).astype(B16)
-    me = lax.axis_index("expert")
-    picks = picks_of(extra, [(me ^ offset) // 2 for offset in offsets], rows, capacity)
-    write_rows(outs, dot32(jnp.concatenate(picks, axis=0).astype(B16), laid))
-
-
-def unfolded(refs, folds):
-    laid = stacked(refs).astype(B16)
-    total, blocks = laid.shape[0], len(refs)
+    return jnp.concatenate([block[:, i * step : (i + 1) * step] for i in range(folds)], axis=0)
+
+
+def piece_order(total, folds, blocks, back):
     capacity = total // (folds * blocks)
-    to = lax.broadcasted_iota(jnp.int32, (total, total), 0)
-    of = lax.broadcasted_iota(jnp.int32, (total, total), 1)
+    to = lax.broadcasted_iota(jnp.int32, (total, total), 1 if back else 0)
+    of = lax.broadcasted_iota(jnp.int32, (total, total), 0 if back else 1)
     same = to % capacity == of % capacity
     same &= to // (blocks * capacity) == of // capacity % folds
     same &= to // capacity % blocks == of // (folds * capacity)
-    moved = dot32(jnp.where(same, 1.0, 0.0).astype(B16), laid)
-    slots = blocks * capacity
-    return jnp.concatenate([moved[i * slots : (i + 1) * slots] for i in range(folds)], axis=1)
+    return jnp.where(same, 1.0, 0.0).astype(B16)
+
+
+def beside_lanes(laid, folds):
+    rows = laid.shape[0] // folds
+    return jnp.concatenate([laid[i * rows : (i + 1) * rows] for i in range(folds)], axis=1)
+
+
+def unfolded(refs, folds):
+    laid = stacked(refs).astype(B16)
+    return beside_lanes(dot32(piece_order(laid.shape[0], folds, len(refs), False), laid), folds)
 
 
 def stack_kernel(folds, beside, order, after_ref, *refs):
@@ -285,57 +297,63 @@
     give_ref[:, width:] = extra[half:].astype(B16)
 
 
-def first_sum_kernel(experts, width, mine_ref, other_ref, after_ref, *outs):
+def first_sum_kernel(experts, width, near, folds, mine_ref, other_ref, after_ref, *outs):
     del after_ref
     total = mine_ref[...].astype(F32) + other_ref[...].astype(F32)
-    rows, extra = total[:, :width], total[:, width:]
+    extra = total[:, width:]
     lane = lax.broadcasted_iota(jnp.int32, extra.shape, 1)
     lost = jnp.where(lane < experts, extra - extra.astype(B16).astype(F32), 0.0)
     extra = extra + pltpu.roll(lost, experts, 1) - lost
     slots = outs[0].shape[0]
-    for i, out in enumerate(outs):
+    for i, out in enumerate(outs[:near]):
         part = slice(i * slots, (i + 1) * slots)
-        out[:, :width] = rows[part].astype(B16)
+        out[:, :width] = total[part, :width].astype(B16)
         out[:, width:] = extra[part].astype(B16)
-
-
-def second_sum_kernel(ways, pick_ref, own_ref, *refs):
-    came, own_out, outs = refs[: -2 - ways], refs[-1 - ways], refs[len(refs) - ways :]
-    came = (own_ref,) + came[1:] + came[:1]
+    if outs[near:]:
+        rest = jnp.concatenate([total[near * slots :, :width], extra[near * slots :]], axis=1)
+        laid = lane_pieces(rest, folds, outs[near].shape[1]).astype(B16)
+        write_rows(outs[near:], dot32(piece_order(laid.shape[0], folds, len(outs[near:]), True), laid))
+
+
+def second_sum_kernel(near, folds, crossing, ways, give_ref, pick_ref, *refs):
+    refs[-1][...] = give_ref[...]
+    refs = refs[:-1]
+    came, refs = refs[:near], refs[near:]
     total = dot32(pick_ref[...].astype(B16), stacked(came).astype(B16), TN)
+    if crossing:
+        cross_pick, came, refs = refs[0], refs[1 : 1 + crossing], refs[1 + crossing :]
+        block = dot32(cross_pick[...].astype(B16), stacked(came).astype(B16), TN)
+        refs[-1][...] = beside_lanes(block, folds)[:, : total.shape[1]].astype(B16)
+    own_out, outs = refs[0], refs[1 : 1 + ways]
     count = own_out.shape[0]
     own_out[...] = total[:count]
     for i, out in enumerate(outs):
         out[...] = total[(i + 1) * count : (i + 2) * count].astype(B16)
 
 
-def down_grads_kernel(y_ref, hidden_ref, down_ref, narrow_ref, wide_ref, narrow_out, wide_out):
+def down_grads_kernel(y_ref, hidden_ref, down_ref, narrow_ref, masked_out, wide_out):
     width = y_ref.shape[1]
-    narrow_out[...] = jnp.zeros_like(narrow_out)
     for part in chunks_of(width, width // 2):
         masked = dot32(hidden_ref[...], y_ref[:, part], TN) * down_ref[:, part].astype(F32)
         masked = masked.astype(B16)
-        narrow_out[...] += dot32(wide_ref[2, :, part], masked, NT)
+        masked_out[:, part] = masked
         wide_out[:, part] = dot32(narrow_ref[2], masked)
 
 
 def feature_grads_kernel(
-    x_ref, grad_gate_ref, grad_up_ref, gate_ref, up_ref, narrow_ref, wide_ref, after_ref,
-    down_narrow_ref, down_wide_ref, narrow_out, keep_out, give_out, wide_all,
+    x_ref, grad_gate_ref, grad_up_ref, gate_ref, up_ref, narrow_ref, after_ref, down_wide_ref,
+    masked_gate, masked_up, keep_out, give_out, wide_all,
 ):
     del after_ref
     width, rank = x_ref.shape[1], narrow_ref.shape[1]
-    lines = pl.ds(2 * rank, rank)
-    narrow_out[lines, :] = down_narrow_ref[...]
-    wide_all[lines, :] = down_wide_ref[...]
-    for i, (grad, raw) in enumerate(((grad_gate_ref, gate_ref), (grad_up_ref, up_ref))):
-        lines = pl.ds(i * rank, rank)
-        narrow_out[lines, :] = jnp.zeros((rank, narrow_out.shape[1]), F32)
+    wide_all[pl.ds(2 * rank, rank), :] = down_wide_ref[...]
+    sides = ((grad_gate_ref, gate_ref, masked_gate), (grad_up_ref, up_ref, masked_up))
+    for i, (grad, raw, out) in enumerate(sides):
         for part in chunks_of(width, width // 2):
             masked = dot32(x_ref[:, part], grad[...], TN) * raw[part, :].astype(F32)
             masked = masked.astype(B16)
-            narrow_out[lines, :] += dot32(wide_ref[i, :, part], masked)
-            wide_all[lines, part] = dot32(narrow_ref[i], masked, NT)
+            out[part, :] = masked
+            wide_all[pl.ds(i * rank, rank), part] = dot32(narrow_ref[i], masked, NT)
     half = keep_out.shape[1]
     is_lower = lax.axis_index("expert") % 2 == 0
 
@@ -350,12 +368,16 @@
         give_out[...] = wide_all[:, :half].astype(B16)
 
 
-def wide_kernel(keep_ref, given_ref, wide_out):
+def narrow_kernel(masked_gate, masked_up, masked_down, wide_ref, after_ref, narrow_out):
+    del after_ref
+    rank = wide_ref.shape[1]
+    for i, (masked, dims) in enumerate(((masked_gate, NN), (masked_up, NN), (masked_down, NT))):
+        narrow_out[pl.ds(i * rank, rank), :] = dot32(wide_ref[i], masked[...], dims)
+
+
+def last_kernel(experts, width, ids_ref, keep_ref, own_ref, *refs):
+    came, given_ref, (tokens_out, probs_out, wide_out) = refs[:-4], refs[-4], refs[-3:]
     wide_out[...] = keep_ref[...] + given_ref[...].astype(F32)
-
-
-def last_kernel(experts, width, ids_ref, own_ref, *refs):
-    came, (tokens_out, probs_out) = refs[:-2], refs[-2:]
     total = own_ref[...]
     for ref in came:
         total = total + ref[...].astype(F32)
@@ -434,19 +456,21 @@
     )
     folds, step = folds_of(rows, capacity, full + width)
     probs_at = slice(width, full)
-    folded = []
+    cross_pick, folded = [], []
     for block in crossed:
-        folded += in_vmem(
+        picked, *folded = in_vmem(
             functools.partial(cross_kernel, offsets, rows, capacity, probs_at),
-            [((folds * capacity, step), B16)] * len(offsets),
+            [((len(offsets) * folds * capacity, folds * rows), F32)]
+            + [((folds * capacity, step), B16)] * len(offsets),
             [wide, block],
         )
+        cross_pick = [picked]
     beside = near[:2]
     pick, *packed = in_vmem(
         functools.partial(
-            pack_kernel, (0, *near), rows, capacity, probs_at, 1 + len(folded[:1])
+            pack_kernel, (0, *beside), rows, capacity, probs_at, 1 + len(folded[:1])
         ),
-        [(((1 + len(near)) * slots, count), F32)]
+        [(((1 + len(beside)) * slots, count), F32)]
         + [((slots, full + width), B16)] * (1 + len(beside)),
         [wide] + folded[:1] + pieces,
     )
@@ -470,7 +494,6 @@
     )
     token_rows = [mine_rows, send(mine_rows, 1)]
     cot_rows = [cot_mine, send(cot_mine, 1)]
-    packed_type = [((slots, full), B16)] * (1 + len(near))
 
     wide_type, unit_type = ((2 * half, width), B16), ((2 * half, hidden_units), B16)
     x, probs, pre_gate, pre_up = in_vmem(
@@ -486,46 +509,63 @@
         3 * matmul,
     )
     other = send(give, 1)
-    down_narrow, down_wide = in_vmem(
+    masked_down, down_wide = in_vmem(
         down_grads_kernel,
-        [((rank, hidden_units), F32), ((rank, width), F32)],
-        (y, hidden, down_raw, narrow, wide),
+        [(down_weight.shape, B16), ((rank, width), F32)],
+        (y, hidden, down_raw, narrow),
         2 * matmul,
     )
-    own, *parts = in_vmem(
-        functools.partial(first_sum_kernel, experts, width),
-        packed_type,
-        (mine, other, down_narrow),
-    )
-    grad_narrow, keep, give = in_vmem(
+    near_count, cross_count = 1 + len(beside), len(folded)
+    fold_step = folds_of(rows, capacity, full)[1]
+    sums = in_vmem(
+        functools.partial(first_sum_kernel, experts, width, near_count, folds),
+        [((slots, full), B16)] * near_count
+        + [((folds * capacity, fold_step), B16)] * cross_count,
+        (mine, other, down_wide),
+    )
+    masked_gate, masked_up, keep, give = in_vmem(
         feature_grads_kernel,
-        [((3 * rank, hidden_units), F32), ((3 * rank, width // 2), F32), ((3 * rank, width // 2), B16)],
-        (x, grad_gate, grad_up, gate_raw, up_raw, narrow, wide, parts[-2], down_narrow, down_wide),
+        [(gate_weight.shape, B16)] * 2
+        + [((3 * rank, width // 2), F32), ((3 * rank, width // 2), B16)],
+        (x, grad_gate, grad_up, gate_raw, up_raw, narrow, sums[0], down_wide),
         4 * matmul,
-        results=(0,),
         scratch=[pltpu.VMEM((3 * rank, width), F32)],
     )
+    came = [sums[0]] + [send(part, mask) for part, mask in zip(sums[1:near_count], beside)]
+    crossing = sums[near_count:]
+    came += [*cross_pick, *crossing[:1]]
+    came += [send(part, mask) for part, mask in zip(crossing[1:], offsets[1:])]
     ways = len(far[0]) if far else 0
     own, *parts = in_vmem(
-        functools.partial(second_sum_kernel, ways),
-        [((count // (ways + 1), full), F32)] + [((count // (ways + 1), full), B16)] * ways,
-        (pick, own, *[send(part, mask) for part, mask in zip(parts[-1:] + parts, near[-1:] + near[:-1])], keep),
-    )
-    came = [send(part, mask) for part, mask in zip(parts, far[0] if far else ())]
+        functools.partial(second_sum_kernel, near_count, folds, cross_count, ways),
+        [((count // (ways + 1), full), F32)]
+        + [((count // (ways + 1), full), B16)] * ways
+        + [((rows, full), B16)] * len(crossed)
+        + [(give.shape, B16)],
+        (give, pick, *came),
+    )
+    *parts, give = parts
+    (grad_narrow,) = in_vmem(
+        narrow_kernel,
+        [((3 * rank, hidden_units), F32)],
+        (masked_gate, masked_up, masked_down, wide, parts[-1]),
+        2 * matmul,
+        results=(0,),
+    )
+    from_cross = [send(part, mask) for part, mask in zip(parts[ways:], near[2:])]
+    came = [send(part, mask) for part, mask in zip(parts[:ways], far[0] if far else ())]
     for masks in far[1:]:
         total = own
         for part in came:
             total = total + part.astype(F32)
         own, *parts = jnp.split(total, len(masks) + 1, axis=0)
         came = [send(part.astype(B16), mask) for part, mask in zip(parts, masks)]
-    (grad_wide,) = in_vmem(
-        wide_kernel, [((3 * rank, width // 2), F32)], (keep, send(give, 1)), results=(0,)
-    )
-    grad_tokens, grad_probs = in_vmem(
+    came = came[1:] + from_cross + came[:1]
+    grad_tokens, grad_probs, grad_wide = in_vmem(
         functools.partial(last_kernel, experts, width),
-        [((rows, width), B16), (expert_ids.shape, F32)],
-        (expert_ids, own, *came[1:], *came[:1]),
-        results=(0, 1),
+        [((rows, width), B16), (expert_ids.shape, F32), ((3 * rank, width // 2), F32)],
+        (expert_ids, keep, own, *came, send(give, 1)),
+        results=(0, 1, 2),
     )
     return (
         grad_tokens,

time: 63.3 us -> 62.2 us (0.983)
  waiting for transfers between devices: 12.1 us -> 8.35 us
  starting transfers between devices: 23.3 us -> 26.5 us
    ppermute x20 -> x23, waiting for transfers between devices: 12.1 us -> 8.35 us  [send(): return lax.ppermute(value, 'expert', pairs)]
    ppermute x20 -> x23, starting transfers between devices: 23.3 us -> 26.5 us  [send(): return lax.ppermute(value, 'expert', pairs)]
  transfers between devices with their start and end apart: 20 -> 23, of which waited for: 9 -> 9; matrix products, arithmetic and copies ran while one was open for 0% -> 0% of each run, Pallas kernels for 33% -> 32%
where the time goes in v6:
time: 62.2 us; the launch traced here: 62 us
  starting transfers between devices  26.5 us (43%)
  Pallas kernels  26.3 us (42%)
  waiting for transfers between devices  8.35 us (13%)
  between operations  0.8 us (1%)
    ppermute x23, starting transfers between devices, send(): return lax.ppermute(value, 'expert', pairs)  26.5 us
    pallas_call x14, Pallas kernels, in_vmem(): pl.pallas_call(kernel, out_shape=[(jax.ShapeDtypeStruct if i in results e...  26.3 us
    ppermute x23, waiting for transfers between devices, send(): return lax.ppermute(value, 'expert', pairs)  8.35 us
  transfers between devices with their start and end apart: 23, of which 9 were waited for; matrix products, arithmetic and copies ran while one was open for 0% of the time, Pallas kernels for 32%

profile of v6, /device:TPU:0, one launch (start us, length us, event | category | flops | bytes accessed | tf_op | source)
XLA Modules:
  0.0 62.0 jit_solution(17783768970403481972)
XLA Ops:
  0.6 0.5 collective-permute-start
  1.1 0.9 %shard_map.121.refs_2_ = bf16[8,7296]{1,0:T(8,128)(2,1)S(1)} custom-call(bf16[8,3584]{1,0:T(8,128)(2,1)} %refs_0_.1, bf16[8,3584]{1,0:T(8,128)(2,1)} %refs_1_.1, f32[8,8]{1,0:T(8,128)} %refs_2_.1, s32[8,8]{1,0:T(8,128)} %ids_ref.1), custom_call_target="tpu_custom_call" | custom-call | bytes 115200 | tf_op jit(solution)/shard_map/pallas_call | solution.py:40
  2.1 4.7 %collective-permute-start.4 = (bf16[8,7296]{1,0:T(8,128)(2,1)S(1)}, bf16[8,7296]{1,0:T(8,128)(2,1)S(1)}, u32[]{:S(2)}, u32[]{:S(2)}) collective-permute-start(bf16[8,7296]{1,0:T(8,128)(2,1)S(1)} %shard_map.121.refs_2_), channel_id=1, source_target_pairs={{0,24},{1,25},{2,26},{3,27},{4,28},{5,29},{6,30},{7,31},{8,16},{9,... | collective-permute-start | bytes 350216 | tf_op jit(solution)/shard_map/ppermute | solution.py:19
  6.7 0.0 collective-permute-start.3
  6.7 0.6 %collective-permute-start.2 = (bf16[8,7296]{1,0:T(8,128)(2,1)S(1)}, bf16[8,7296]{1,0:T(8,128)(2,1)S(1)}, u32[]{:S(2)}, u32[]{:S(2)}) collective-permute-start(bf16[8,7296]{1,0:T(8,128)(2,1)S(1)} %shard_map.121.refs_2_), channel_id=1, source_target_pairs={{0,8},{1,9},{2,10},{3,11},{4,12},{5,13},{6,14},{7,15},{8,0},{9,1},... | collective-permute-start | bytes 350216 | tf_op jit(solution)/shard_map/ppermute | solution.py:19
  7.4 2.6 %collective-permute-start.1 = (bf16[8,7296]{1,0:T(8,128)(2,1)S(1)}, bf16[8,7296]{1,0:T(8,128)(2,1)S(1)}, u32[]{:S(2)}, u32[]{:S(2)}) collective-permute-start(bf16[8,7296]{1,0:T(8,128)(2,1)S(1)} %shard_map.121.refs_2_), channel_id=1, source_target_pairs={{0,6},{1,7},{2,4},{3,5},{4,2},{5,3},{6,0},{7,1},{8,14},{9,15},{10,... | collective-permute-start | bytes 350216 | tf_op jit(solution)/shard_map/ppermute | solution.py:19
  10.0 0.0 collective-permute-done.other_ref
  10.0 5.6 %shard_map.120 = (bf16[3584,512]{1,0:T(8,128)(2,1)S(1)}, bf16[3584,512]{1,0:T(8,128)(2,1)S(1)}, bf16[3584,512]{1,0:T(8,128)(2,1)S(1)}, bf16[3584,512]{1,0:T(8,12...) custom-call(bf16[3584,512]{1,0:T(8,128)(2,1)} %gate_ref.1, bf16[3584,512]{1,0:T(8,128)(2,1)} %up_ref.1, ...), custom_call_target="tpu_custom_call" | custom-call | flops 1409286144 | bytes 7733248 | tf_op jit(solution)/shard_map/pallas_call | solution.py:40
  15.6 0.0 collective-permute-done.1.block_ref
  15.6 0.5 shard_map.122
  16.1 0.0 collective-permute-done.4.refs_5_
  16.1 1.1 %collective-permute-done.3.refs_4_ = bf16[8,7296]{1,0:T(8,128)(2,1)S(1)} collective-permute-done((bf16[8,7296]{1,0:T(8,128)(2,1)S(1)}, bf16[8,7296]{1,0:T(8,128)(2,1)S(1)}, u32[]{:S(2)}, u32[]{:S(2)}) %collective-permute-start.3) | collective-permute-done | bytes 116768 | tf_op jit(solution)/shard_map/ppermute | solution.py:19
  17.2 0.0 collective-permute-done.2.refs_3_
  17.2 0.7 %shard_map.123 = (f32[72,32]{1,0:T(8,128)S(1)}, bf16[24,7296]{1,0:T(8,128)(2,1)S(1)}, bf16[24,7296]{1,0:T(8,128)(2,1)S(1)}, bf16[24,7296]{1,0:T(8,128)(2,1)S(1)}) custom-call(bf16[3,16,3584]{2,1,0:T(8,128)(2,1)S(1)} %get-tuple-element.58.after_ref.refs_0_.wide_ref, bf16[24,1920]{1,0:T(8,128)(2,1)S(1)} %get-tuple-element.59.refs_1_.refs_6_, ...), custom_call_target="tpu_custom_call" | custom-call | bytes 903168 | tf_op jit(solution)/shard_map/pallas_call | solution.py:40
  17.9 1.6 %collective-permute-start.5 = (bf16[24,7296]{1,0:T(8,128)(2,1)S(1)}, bf16[24,7296]{1,0:T(8,128)(2,1)S(1)}, u32[]{:S(2)}, u32[]{:S(2)}) collective-permute-start(bf16[24,7296]{1,0:T(8,128)(2,1)S(1)} %get-tuple-element.63), channel_id=1, source_target_pairs={{0,2},{1,3},{2,0},{3,1},{4,6},{5,7},{6,4},{7,5},{8,10},{9,11},{10,... | collective-permute-start | bytes 1050632 | tf_op jit(solution)/shard_map/ppermute | solution.py:19
  19.5 1.5 %collective-permute-start.7 = (bf16[24,7296]{1,0:T(8,128)(2,1)S(1)}, bf16[24,7296]{1,0:T(8,128)(2,1)S(1)}, u32[]{:S(2)}, u32[]{:S(2)}) collective-permute-start(bf16[24,7296]{1,0:T(8,128)(2,1)S(1)} %get-tuple-element.65), channel_id=1, source_target_pairs={{0,4},{1,5},{2,6},{3,7},{4,0},{5,1},{6,2},{7,3},{8,12},{9,13},{10,... | collective-permute-start | bytes 1050632 | tf_op jit(solution)/shard_map/ppermute | solution.py:19
  21.0 0.0 collective-permute-start.6
  21.0 2.5 %collective-permute-start.8 = (bf16[24,1920]{1,0:T(8,128)(2,1)S(1)}, bf16[24,1920]{1,0:T(8,128)(2,1)S(1)}, u32[]{:S(2)}, u32[]{:S(2)}) collective-permute-start(bf16[24,1920]{1,0:T(8,128)(2,1)S(1)} %get-tuple-element.66), channel_id=1, source_target_pairs={{0,24},{1,25},{2,26},{3,27},{4,28},{5,29},{6,30},{7,31},{8,16},{9,... | collective-permute-start | bytes 276488 | tf_op jit(solution)/shard_map/ppermute | solution.py:19
  23.6 1.0 %collective-permute-start.9 = (bf16[24,1920]{1,0:T(8,128)(2,1)S(1)}, bf16[24,1920]{1,0:T(8,128)(2,1)S(1)}, u32[]{:S(2)}, u32[]{:S(2)}) collective-permute-start(bf16[24,1920]{1,0:T(8,128)(2,1)S(1)} %get-tuple-element.67), channel_id=1, source_target_pairs={{0,8},{1,9},{2,10},{3,11},{4,12},{5,13},{6,14},{7,15},{8,0},{9,1},... | collective-permute-start | bytes 276488 | tf_op jit(solution)/shard_map/ppermute | solution.py:19
  24.5 2.9 %shard_map.124 = (bf16[512,3584]{1,0:T(8,128)(2,1)S(1)}, bf16[512,3584]{1,0:T(8,128)(2,1)S(1)}) custom-call(bf16[512,3584]{1,0:T(8,128)(2,1)} %down_ref.1, bf16[3,16,512]{2,1,0:T(8,128)(2,1)S(1)} %get-tuple-element.57.narrow_ref, bf16[3,16,3584]{2,1,0:T(8,128)(2,1)S(1)} %get-tuple-element.58.after_ref.refs_0_.wide_ref, ...), custom_call_target="tpu_custom_call" | custom-call | flops 704643072 | bytes 4072448 | tf_op jit(solution)/shard_map/pallas_call | solution.py:40
  27.4 2.1 %collective-permute-done.6.refs_2_ = bf16[24,1920]{1,0:T(8,128)(2,1)S(1)} collective-permute-done((bf16[24,1920]{1,0:T(8,128)(2,1)S(1)}, bf16[24,1920]{1,0:T(8,128)(2,1)S(1)}, u32[]{:S(2)}, u32[]{:S(2)}) %collective-permute-start.6) | collective-permute-done | bytes 92192 | tf_op jit(solution)/shard_map/ppermute | solution.py:19
  29.5 0.0 collective-permute-done.8.refs_4_
  29.5 0.9 %collective-permute-done.9.refs_5_ = bf16[24,1920]{1,0:T(8,128)(2,1)S(1)} collective-permute-done((bf16[24,1920]{1,0:T(8,128)(2,1)S(1)}, bf16[24,1920]{1,0:T(8,128)(2,1)S(1)}, u32[]{:S(2)}, u32[]{:S(2)}) %collective-permute-start.9) | collective-permute-done | bytes 92192 | tf_op jit(solution)/shard_map/ppermute | solution.py:19
  30.4 0.0 collective-permute-done.5.refs_1_
  30.4 0.0 collective-permute-done.7.refs_3_
  30.4 0.3 shard_map.125
  30.7 0.1 collective-permute-start.10
  30.8 0.5 collective-permute-start.11
  31.3 1.7 %collective-permute-done.10.refs_1_ = bf16[96,3712]{1,0:T(8,128)(2,1)S(1)} collective-permute-done((bf16[96,3712]{1,0:T(8,128)(2,1)S(1)}, bf16[96,3712]{1,0:T(8,128)(2,1)S(1)}, u32[]{:S(2)}, u32[]{:S(2)}) %collective-permute-start.10) | collective-permute-done | bytes 712736 | tf_op jit(solution)/shard_map/ppermute | solution.py:19
  33.0 1.6 %shard_map.126 = (bf16[192,3584]{1,0:T(8,128)(2,1)S(1)}, f32[192,128]{1,0:T(8,128)S(1)}, f32[192,512]{1,0:T(8,128)S(1)}, f32[192,512]{1,0:T(8,128)S(1)}) custom-call(bf16[3584,512]{1,0:T(8,128)(2,1)S(1)} %get-tuple-element.55.gate_ref, bf16[3584,512]{1,0:T(8,128)(2,1)S(1)} %get-tuple-element.56.up_ref, bf16[96,3712]{1,0:T(8,128)(2,1)S(1)} %get-tuple-element.68.refs_0_, ...), custom_call_target="tpu_custom_call" | custom-call | flops 1409286144 | bytes 8765440 | tf_op jit(solution)/shard_map/pallas_call | solution.py:40
  34.6 0.0 collective-permute-done.11.refs_1_
  34.6 3.9 %shard_map.127 = (bf16[192,3584]{1,0:T(8,128)(2,1)S(1)}, bf16[192,512]{1,0:T(8,128)(2,1)S(1)}, bf16[192,512]{1,0:T(8,128)(2,1)S(1)}, bf16[192,512]{1,0:T(8,128)(...) custom-call(bf16[3584,512]{1,0:T(8,128)(2,1)S(1)} %get-tuple-element.55.gate_ref, ...), custom_call_target="tpu_custom_call" | custom-call | flops 2113929216 | bytes 13271040 | tf_op jit(solution)/shard_map/pallas_call | solution.py:40
  38.5 0.2 collective-permute-start.12
  38.7 1.6 %shard_map.128 = (bf16[512,3584]{1,0:T(8,128)(2,1)S(1)}, f32[16,3584]{1,0:T(8,128)S(1)}) custom-call(bf16[192,3584]{1,0:T(8,128)(2,1)S(1)} %get-tuple-element.80.y_ref, bf16[192,512]{1,0:T(8,128)(2,1)S(1)} %get-tuple-element.81.hidden_ref, bf16[512,3584]{1,0:T(8,128)(2,1)S(1)} %get-tuple-element.82.down_ref, bf16[3,16,512]{2,1,0:T(8,128)(2,1)S(1)} %get-tuple-element.57.narrow_ref), custom_call_target="tpu_custom_call" | custom-call | flops 1409286144 | bytes 5292032 | tf_op jit(solution)/shard_map/pallas_call | solution.py:40
  40.3 0.4 collective-permute-done.12.other_ref
  40.7 0.4 shard_map.129
  41.1 1.6 %collective-permute-start.15 = (bf16[24,1024]{1,0:T(8,128)(2,1)S(1)}, bf16[24,1024]{1,0:T(8,128)(2,1)S(1)}, u32[]{:S(2)}, u32[]{:S(2)}) collective-permute-start(bf16[24,1024]{1,0:T(8,128)(2,1)S(1)} %get-tuple-element.91), channel_id=1, source_target_pairs={{0,8},{1,9},{2,10},{3,11},{4,12},{5,13},{6,14},{7,15},{8,0},{9,1},... | collective-permute-start | bytes 147464 | tf_op jit(solution)/shard_map/ppermute | solution.py:19
  42.8 0.7 %collective-permute-start.16 = (bf16[24,1024]{1,0:T(8,128)(2,1)S(1)}, bf16[24,1024]{1,0:T(8,128)(2,1)S(1)}, u32[]{:S(2)}, u32[]{:S(2)}) collective-permute-start(bf16[24,1024]{1,0:T(8,128)(2,1)S(1)} %get-tuple-element.92), channel_id=1, source_target_pairs={{0,16},{1,17},{2,18},{3,19},{4,20},{5,21},{6,22},{7,23},{8,24},{9,... | collective-permute-start | bytes 147464 | tf_op jit(solution)/shard_map/ppermute | solution.py:19
  43.4 2.2 %collective-permute-start.17 = (bf16[24,1024]{1,0:T(8,128)(2,1)S(1)}, bf16[24,1024]{1,0:T(8,128)(2,1)S(1)}, u32[]{:S(2)}, u32[]{:S(2)}) collective-permute-start(bf16[24,1024]{1,0:T(8,128)(2,1)S(1)} %get-tuple-element.93), channel_id=1, source_target_pairs={{0,24},{1,25},{2,26},{3,27},{4,28},{5,29},{6,30},{7,31},{8,16},{9,... | collective-permute-start | bytes 147464 | tf_op jit(solution)/shard_map/ppermute | solution.py:19
  45.6 0.5 collective-permute-start.13
  46.1 0.5 collective-permute-start.14
  46.6 4.1 %shard_map.130 = (bf16[3584,512]{1,0:T(8,128)(2,1)S(1)}, bf16[3584,512]{1,0:T(8,128)(2,1)S(1)}, f32[48,1792]{1,0:T(8,128)S(1)}, bf16[48,1792]{1,0:T(8,128)(2,1)S(1)}) custom-call(bf16[192,3584]{1,0:T(8,128)(2,1)S(1)} %get-tuple-element.69.x_ref, bf16[192,512]{1,0:T(8,128)(2,1)S(1)} %get-tuple-element.74.grad_gate_ref, ...), custom_call_target="tpu_custom_call" | custom-call | flops 2818572288 | bytes 9566208 | tf_op jit(solution)/shard_map/pallas_call | solution.py:40
  50.7 0.0 collective-permute-done.15.refs_5_
  50.7 0.0 collective-permute-done.16.refs_6_
  50.7 0.0 collective-permute-done.17.refs_7_
  50.7 0.6 collective-permute-done.13.refs_1_
  51.3 0.3 collective-permute-done.14.refs_2_
  51.6 0.3 shard_map.131
  51.9 0.1 collective-permute-start.22
  52.0 0.9 %collective-permute-start.18 = (bf16[8,3712]{1,0:T(8,128)(2,1)S(1)}, bf16[8,3712]{1,0:T(8,128)(2,1)S(1)}, u32[]{:S(2)}, u32[]{:S(2)}) collective-permute-start(bf16[8,3712]{1,0:T(8,128)(2,1)S(1)} %get-tuple-element.95), channel_id=1, source_target_pairs={{0,16},{1,17},{2,18},{3,19},{4,20},{5,21},{6,22},{7,23},{8,24},{9,... | collective-permute-start | bytes 178184 | tf_op jit(solution)/shard_map/ppermute | solution.py:19
  52.9 2.2 %collective-permute-start.19 = (bf16[8,3712]{1,0:T(8,128)(2,1)S(1)}, bf16[8,3712]{1,0:T(8,128)(2,1)S(1)}, u32[]{:S(2)}, u32[]{:S(2)}) collective-permute-start(bf16[8,3712]{1,0:T(8,128)(2,1)S(1)} %get-tuple-element.96), channel_id=1, source_target_pairs={{0,24},{1,25},{2,26},{3,27},{4,28},{5,29},{6,30},{7,31},{8,16},{9,... | collective-permute-start | bytes 178184 | tf_op jit(solution)/shard_map/ppermute | solution.py:19
  55.1 0.5 collective-permute-start.21
  55.5 1.6 %collective-permute-start.20 = (bf16[8,3712]{1,0:T(8,128)(2,1)S(1)}, bf16[8,3712]{1,0:T(8,128)(2,1)S(1)}, u32[]{:S(2)}, u32[]{:S(2)}) collective-permute-start(bf16[8,3712]{1,0:T(8,128)(2,1)S(1)} %get-tuple-element.97.after_ref), channel_id=1, source_target_pairs={{0,6},{1,7},{2,4},{3,5},{4,2},{5,3},{6,0},{7,1},{8,14},{9,15},{10,... | collective-permute-start | bytes 178184 | tf_op jit(solution)/shard_map/ppermute | solution.py:19
  57.1 0.0 copy-start
  57.1 2.6 %shard_map.133 = f32[48,512]{1,0:T(8,128)} custom-call(bf16[3584,512]{1,0:T(8,128)(2,1)S(1)} %get-tuple-element.102.masked_gate, bf16[3584,512]{1,0:T(8,128)(2,1)S(1)} %get-tuple-element.103.masked_up, bf16[512,3584]{1,0:T(8,128)(2,1)S(1)} %get-tuple-element.104.masked_down, bf16[3,16,3584]{2,1,0:T(8,128)(2,1)S(1)} %get-tuple-element.58.after_ref.refs_0_.wide_ref, ...), custom_call_target="tpu_custom_call" | custom-call | flops 1409286144 | bytes 11413504 | tf_op jit(solution)/shard_map/pallas_call | solution.py:40
  59.8 0.2 collective-permute-done.18.refs_0_
  60.0 0.0 collective-permute-done.19.refs_1_
  60.0 1.0 %collective-permute-done.21.refs_3_ = bf16[8,3712]{1,0:T(8,128)(2,1)S(1)} collective-permute-done((bf16[8,3712]{1,0:T(8,128)(2,1)S(1)}, bf16[8,3712]{1,0:T(8,128)(2,1)S(1)}, u32[]{:S(2)}, u32[]{:S(2)}) %collective-permute-start.21) | collective-permute-done | bytes 59424 | tf_op jit(solution)/shard_map/ppermute | solution.py:19
  61.1 0.0 collective-permute-done.20.refs_2_
  61.1 0.0 collective-permute-done.22.refs_4_
  61.1 0.0 copy-done
  61.1 0.9 %shard_map.132 = (bf16[8,3584]{1,0:T(8,128)(2,1)}, f32[8,8]{1,0:T(8,128)}, f32[48,1792]{1,0:T(8,128)}) custom-call(s32[8,8]{1,0:T(8,128)S(1)} %copy-done, f32[48,1792]{1,0:T(8,128)S(1)} %get-tuple-element.85.keep_ref, f32[8,3712]{1,0:T(8,128)S(1)} %get-tuple-element.94.own_ref, bf16[8,3712]{1,0:T(8,128)(2,1)S(1)} %collective-permute-done.18.refs_0_, ...), custom_call_target="tpu_custom_call" | custom-call | bytes 872704 | tf_op jit(solution)/shard_map/pallas_call | solution.py:40
Async XLA Ops:
  0.6 9.3 %collective-permute-start = (bf16[3,16,1792]{2,1,0:T(8,128)(2,1)}, bf16[3,16,1792]{2,1,0:T(8,128)(2,1)S(1)}, u32[]{:S(2)}, u32[]{:S(2)}) collective-permute-start(bf16[3,16,1792]{2,1,0:T(8,128)(2,1)} %mine_hbm.1), channel_id=1, source_target_pairs={{0,1},{1,0},{2,3},{3,2},{4,5},{5,4},{6,7},{7,6},{8,9},{9,8},{10,11... | collective-permute-start | bytes 516104 | tf_op jit(solution)/shard_map/ppermute | solution.py:19
  2.1 14.1 %collective-permute-start.4 = (bf16[8,7296]{1,0:T(8,128)(2,1)S(1)}, bf16[8,7296]{1,0:T(8,128)(2,1)S(1)}, u32[]{:S(2)}, u32[]{:S(2)}) collective-permute-start(bf16[8,7296]{1,0:T(8,128)(2,1)S(1)} %shard_map.121.refs_2_), channel_id=1, source_target_pairs={{0,24},{1,25},{2,26},{3,27},{4,28},{5,29},{6,30},{7,31},{8,16},{9,... | collective-permute-start | bytes 350216 | tf_op jit(solution)/shard_map/ppermute | solution.py:19
  6.7 10.5 %collective-permute-start.3 = (bf16[8,7296]{1,0:T(8,128)(2,1)S(1)}, bf16[8,7296]{1,0:T(8,128)(2,1)S(1)}, u32[]{:S(2)}, u32[]{:S(2)}) collective-permute-start(bf16[8,7296]{1,0:T(8,128)(2,1)S(1)} %shard_map.121.refs_2_), channel_id=1, source_target_pairs={{0,16},{1,17},{2,18},{3,19},{4,20},{5,21},{6,22},{7,23},{8,24},{9,... | collective-permute-start | bytes 350216 | tf_op jit(solution)/shard_map/ppermute | solution.py:19
  6.7 10.5 %collective-permute-start.2 = (bf16[8,7296]{1,0:T(8,128)(2,1)S(1)}, bf16[8,7296]{1,0:T(8,128)(2,1)S(1)}, u32[]{:S(2)}, u32[]{:S(2)}) collective-permute-start(bf16[8,7296]{1,0:T(8,128)(2,1)S(1)} %shard_map.121.refs_2_), channel_id=1, source_target_pairs={{0,8},{1,9},{2,10},{3,11},{4,12},{5,13},{6,14},{7,15},{8,0},{9,1},... | collective-permute-start | bytes 350216 | tf_op jit(solution)/shard_map/ppermute | solution.py:19
  7.4 8.2 %collective-permute-start.1 = (bf16[8,7296]{1,0:T(8,128)(2,1)S(1)}, bf16[8,7296]{1,0:T(8,128)(2,1)S(1)}, u32[]{:S(2)}, u32[]{:S(2)}) collective-permute-start(bf16[8,7296]{1,0:T(8,128)(2,1)S(1)} %shard_map.121.refs_2_), channel_id=1, source_target_pairs={{0,6},{1,7},{2,4},{3,5},{4,2},{5,3},{6,0},{7,1},{8,14},{9,15},{10,... | collective-permute-start | bytes 350216 | tf_op jit(solution)/shard_map/ppermute | solution.py:19
  17.9 12.5 %collective-permute-start.5 = (bf16[24,7296]{1,0:T(8,128)(2,1)S(1)}, bf16[24,7296]{1,0:T(8,128)(2,1)S(1)}, u32[]{:S(2)}, u32[]{:S(2)}) collective-permute-start(bf16[24,7296]{1,0:T(8,128)(2,1)S(1)} %get-tuple-element.63), channel_id=1, source_target_pairs={{0,2},{1,3},{2,0},{3,1},{4,6},{5,7},{6,4},{7,5},{8,10},{9,11},{10,... | collective-permute-start | bytes 1050632 | tf_op jit(solution)/shard_map/ppermute | solution.py:19
  19.5 10.9 %collective-permute-start.7 = (bf16[24,7296]{1,0:T(8,128)(2,1)S(1)}, bf16[24,7296]{1,0:T(8,128)(2,1)S(1)}, u32[]{:S(2)}, u32[]{:S(2)}) collective-permute-start(bf16[24,7296]{1,0:T(8,128)(2,1)S(1)} %get-tuple-element.65), channel_id=1, source_target_pairs={{0,4},{1,5},{2,6},{3,7},{4,0},{5,1},{6,2},{7,3},{8,12},{9,13},{10,... | collective-permute-start | bytes 1050632 | tf_op jit(solution)/shard_map/ppermute | solution.py:19
  21.0 8.5 %collective-permute-start.6 = (bf16[24,1920]{1,0:T(8,128)(2,1)S(1)}, bf16[24,1920]{1,0:T(8,128)(2,1)S(1)}, u32[]{:S(2)}, u32[]{:S(2)}) collective-permute-start(bf16[24,1920]{1,0:T(8,128)(2,1)S(1)} %get-tuple-element.64), channel_id=1, source_target_pairs={{0,16},{1,17},{2,18},{3,19},{4,20},{5,21},{6,22},{7,23},{8,24},{9,... | collective-permute-start | bytes 276488 | tf_op jit(solution)/shard_map/ppermute | solution.py:19
  21.0 8.5 %collective-permute-start.8 = (bf16[24,1920]{1,0:T(8,128)(2,1)S(1)}, bf16[24,1920]{1,0:T(8,128)(2,1)S(1)}, u32[]{:S(2)}, u32[]{:S(2)}) collective-permute-start(bf16[24,1920]{1,0:T(8,128)(2,1)S(1)} %get-tuple-element.66), channel_id=1, source_target_pairs={{0,24},{1,25},{2,26},{3,27},{4,28},{5,29},{6,30},{7,31},{8,16},{9,... | collective-permute-start | bytes 276488 | tf_op jit(solution)/shard_map/ppermute | solution.py:19
  23.6 6.9 %collective-permute-start.9 = (bf16[24,1920]{1,0:T(8,128)(2,1)S(1)}, bf16[24,1920]{1,0:T(8,128)(2,1)S(1)}, u32[]{:S(2)}, u32[]{:S(2)}) collective-permute-start(bf16[24,1920]{1,0:T(8,128)(2,1)S(1)} %get-tuple-element.67), channel_id=1, source_target_pairs={{0,8},{1,9},{2,10},{3,11},{4,12},{5,13},{6,14},{7,15},{8,0},{9,1},... | collective-permute-start | bytes 276488 | tf_op jit(solution)/shard_map/ppermute | solution.py:19
  30.7 2.2 %collective-permute-start.10 = (bf16[96,3712]{1,0:T(8,128)(2,1)S(1)}, bf16[96,3712]{1,0:T(8,128)(2,1)S(1)}, u32[]{:S(2)}, u32[]{:S(2)}) collective-permute-start(bf16[96,3712]{1,0:T(8,128)(2,1)S(1)} %get-tuple-element.68.refs_0_), channel_id=1, source_target_pairs={{0,1},{1,0},{2,3},{3,2},{4,5},{5,4},{6,7},{7,6},{8,9},{9,8},{10,11... | collective-permute-start | bytes 2138120 | tf_op jit(solution)/shard_map/ppermute | solution.py:19
  30.8 3.8 %collective-permute-start.11 = (bf16[96,3584]{1,0:T(8,128)(2,1)S(1)}, bf16[96,3584]{1,0:T(8,128)(2,1)S(1)}, u32[]{:S(2)}, u32[]{:S(2)}) collective-permute-start(bf16[96,3584]{1,0:T(8,128)(2,1)S(1)} %get-tuple-element.73.refs_0_), channel_id=1, source_target_pairs={{0,1},{1,0},{2,3},{3,2},{4,5},{5,4},{6,7},{7,6},{8,9},{9,8},{10,11... | collective-permute-start | bytes 2064392 | tf_op jit(solution)/shard_map/ppermute | solution.py:19
  38.5 2.2 %collective-permute-start.12 = (bf16[96,3712]{1,0:T(8,128)(2,1)S(1)}, bf16[96,3712]{1,0:T(8,128)(2,1)S(1)}, u32[]{:S(2)}, u32[]{:S(2)}) collective-permute-start(bf16[96,3712]{1,0:T(8,128)(2,1)S(1)} %get-tuple-element.79), channel_id=1, source_target_pairs={{0,1},{1,0},{2,3},{3,2},{4,5},{5,4},{6,7},{7,6},{8,9},{9,8},{10,11... | collective-permute-start | bytes 2138120 | tf_op jit(solution)/shard_map/ppermute | solution.py:19
  41.1 9.6 %collective-permute-start.15 = (bf16[24,1024]{1,0:T(8,128)(2,1)S(1)}, bf16[24,1024]{1,0:T(8,128)(2,1)S(1)}, u32[]{:S(2)}, u32[]{:S(2)}) collective-permute-start(bf16[24,1024]{1,0:T(8,128)(2,1)S(1)} %get-tuple-element.91), channel_id=1, source_target_pairs={{0,8},{1,9},{2,10},{3,11},{4,12},{5,13},{6,14},{7,15},{8,0},{9,1},... | collective-permute-start | bytes 147464 | tf_op jit(solution)/shard_map/ppermute | solution.py:19
  42.8 8.0 %collective-permute-start.16 = (bf16[24,1024]{1,0:T(8,128)(2,1)S(1)}, bf16[24,1024]{1,0:T(8,128)(2,1)S(1)}, u32[]{:S(2)}, u32[]{:S(2)}) collective-permute-start(bf16[24,1024]{1,0:T(8,128)(2,1)S(1)} %get-tuple-element.92), channel_id=1, source_target_pairs={{0,16},{1,17},{2,18},{3,19},{4,20},{5,21},{6,22},{7,23},{8,24},{9,... | collective-permute-start | bytes 147464 | tf_op jit(solution)/shard_map/ppermute | solution.py:19
  43.4 7.3 %collective-permute-start.17 = (bf16[24,1024]{1,0:T(8,128)(2,1)S(1)}, bf16[24,1024]{1,0:T(8,128)(2,1)S(1)}, u32[]{:S(2)}, u32[]{:S(2)}) collective-permute-start(bf16[24,1024]{1,0:T(8,128)(2,1)S(1)} %get-tuple-element.93), channel_id=1, source_target_pairs={{0,24},{1,25},{2,26},{3,27},{4,28},{5,29},{6,30},{7,31},{8,16},{9,... | collective-permute-start | bytes 147464 | tf_op jit(solution)/shard_map/ppermute | solution.py:19
  45.6 5.7 %collective-permute-start.13 = (bf16[24,3712]{1,0:T(8,128)(2,1)S(1)}, bf16[24,3712]{1,0:T(8,128)(2,1)S(1)}, u32[]{:S(2)}, u32[]{:S(2)}) collective-permute-start(bf16[24,3712]{1,0:T(8,128)(2,1)S(1)} %get-tuple-element.87), channel_id=1, source_target_pairs={{0,2},{1,3},{2,0},{3,1},{4,6},{5,7},{6,4},{7,5},{8,10},{9,11},{10,... | collective-permute-start | bytes 534536 | tf_op jit(solution)/shard_map/ppermute | solution.py:19
  46.1 5.5 %collective-permute-start.14 = (bf16[24,3712]{1,0:T(8,128)(2,1)S(1)}, bf16[24,3712]{1,0:T(8,128)(2,1)S(1)}, u32[]{:S(2)}, u32[]{:S(2)}) collective-permute-start(bf16[24,3712]{1,0:T(8,128)(2,1)S(1)} %get-tuple-element.88), channel_id=1, source_target_pairs={{0,4},{1,5},{2,6},{3,7},{4,0},{5,1},{6,2},{7,3},{8,12},{9,13},{10,... | collective-permute-start | bytes 534536 | tf_op jit(solution)/shard_map/ppermute | solution.py:19
  51.9 9.2 %collective-permute-start.22 = (bf16[48,1792]{1,0:T(8,128)(2,1)S(1)}, bf16[48,1792]{1,0:T(8,128)(2,1)S(1)}, u32[]{:S(2)}, u32[]{:S(2)}) collective-permute-start(bf16[48,1792]{1,0:T(8,128)(2,1)S(1)} %get-tuple-element.99), channel_id=1, source_target_pairs={{0,1},{1,0},{2,3},{3,2},{4,5},{5,4},{6,7},{7,6},{8,9},{9,8},{10,11... | collective-permute-start | bytes 516104 | tf_op jit(solution)/shard_map/ppermute | solution.py:19
  52.0 8.1 %collective-permute-start.18 = (bf16[8,3712]{1,0:T(8,128)(2,1)S(1)}, bf16[8,3712]{1,0:T(8,128)(2,1)S(1)}, u32[]{:S(2)}, u32[]{:S(2)}) collective-permute-start(bf16[8,3712]{1,0:T(8,128)(2,1)S(1)} %get-tuple-element.95), channel_id=1, source_target_pairs={{0,16},{1,17},{2,18},{3,19},{4,20},{5,21},{6,22},{7,23},{8,24},{9,... | collective-permute-start | bytes 178184 | tf_op jit(solution)/shard_map/ppermute | solution.py:19
  52.9 7.1 %collective-permute-start.19 = (bf16[8,3712]{1,0:T(8,128)(2,1)S(1)}, bf16[8,3712]{1,0:T(8,128)(2,1)S(1)}, u32[]{:S(2)}, u32[]{:S(2)}) collective-permute-start(bf16[8,3712]{1,0:T(8,128)(2,1)S(1)} %get-tuple-element.96), channel_id=1, source_target_pairs={{0,24},{1,25},{2,26},{3,27},{4,28},{5,29},{6,30},{7,31},{8,16},{9,... | collective-permute-start | bytes 178184 | tf_op jit(solution)/shard_map/ppermute | solution.py:19
  55.1 6.0 %collective-permute-start.21 = (bf16[8,3712]{1,0:T(8,128)(2,1)S(1)}, bf16[8,3712]{1,0:T(8,128)(2,1)S(1)}, u32[]{:S(2)}, u32[]{:S(2)}) collective-permute-start(bf16[8,3712]{1,0:T(8,128)(2,1)S(1)} %get-tuple-element.98), channel_id=1, source_target_pairs={{0,8},{1,9},{2,10},{3,11},{4,12},{5,13},{6,14},{7,15},{8,0},{9,1},... | collective-permute-start | bytes 178184 | tf_op jit(solution)/shard_map/ppermute | solution.py:19
  55.5 5.5 %collective-permute-start.20 = (bf16[8,3712]{1,0:T(8,128)(2,1)S(1)}, bf16[8,3712]{1,0:T(8,128)(2,1)S(1)}, u32[]{:S(2)}, u32[]{:S(2)}) collective-permute-start(bf16[8,3712]{1,0:T(8,128)(2,1)S(1)} %get-tuple-element.97.after_ref), channel_id=1, source_target_pairs={{0,6},{1,7},{2,4},{3,5},{4,2},{5,3},{6,0},{7,1},{8,14},{9,15},{10,... | collective-permute-start | bytes 178184 | tf_op jit(solution)/shard_map/ppermute | solution.py:19
  57.1 3.9 %copy-start = (s32[8,8]{1,0:T(8,128)S(1)}, s32[8,8]{1,0:T(8,128)}, u32[]{:S(2)}) copy-start(s32[8,8]{1,0:T(8,128)} %ids_ref.1) | copy-start | bytes 772

commit v7 on v6

--- a/solution.py
+++ b/solution.py
@@ -46,7 +46,7 @@
         in_specs=[pl.BlockSpec(memory_space=space) for space in spaces],
         out_specs=[pl.BlockSpec(memory_space=pltpu.VMEM)] * len(outs),
         scratch_shapes=list(scratch),
-        compiler_params=pltpu.CompilerParams(vmem_limit_bytes=20 * 2**20),
+        compiler_params=pltpu.CompilerParams(vmem_limit_bytes=8 * 2**20),
         cost_estimate=pl.CostEstimate(flops=flops, bytes_accessed=moved, transcendentals=0),
     )(*[pltpu.with_memory_space_constraint(a, space) for a, space in zip(args, spaces)])
 
@@ -87,32 +87,17 @@
         copy.wait()
 
 
-def weights_into(which, sources, raws, outs, narrow_ref, wide_ref, sems):
-    pieces = sems.shape[0] // len(sources)
-    parts = []
+def started(sources, raws, sems, ahead):
+    pieces, parts = sems.shape[0] // len(sources), []
     for i, (source, raw) in enumerate(zip(sources, raws)):
         step = source.shape[0] // pieces
         for j in range(pieces):
             rows = pl.ds(j * step, step)
             sem = sems.at[i * pieces + j]
             parts.append((i, rows, pltpu.make_async_copy(source.at[rows, :], raw.at[rows, :], sem)))
-    ahead = 5
     for _, _, copy in parts[:ahead]:
         copy.start()
-    for at, (i, rows, copy) in enumerate(parts):
-        copy.wait()
-        if at + ahead < len(parts):
-            parts[at + ahead][2].start()
-        raw, out, kind = raws[i], outs[i], which + i
-        if kind < 2:
-            for line in range(rows.start, rows.start + rows.size, 128):
-                lines = pl.ds(line, 128)
-                factor = 1.0 + dot32(wide_ref[kind, :, lines], narrow_ref[kind], TN)
-                out[lines, :] = (raw[lines, :].astype(F32) * factor).astype(B16)
-        else:
-            for lanes in chunks_of(raw.shape[1]):
-                factor = 1.0 + dot32(narrow_ref[kind, :, rows], wide_ref[kind, :, lanes], TN)
-                out[rows, lanes] = (raw[rows, lanes].astype(F32) * factor).astype(B16)
+    return parts
 
 
 def up_side_kernel(gate_ref, up_ref, narrow_hbm, mine_hbm, other_ref, *refs):
@@ -132,12 +117,31 @@
         wide_out[:, :, :half] = other_ref[...]
         wide_out[:, :, half:] = mine_ref[...]
 
-    weights_into(0, (gate_ref, up_ref), raws, outs, narrow_out, wide_out, sems)
-
-
-def down_side_kernel(down_ref, narrow_ref, wide_ref, after_ref, raw, out, sems):
+    ahead = 5
+    parts = started((gate_ref, up_ref), raws, sems, ahead)
+    for at, (i, rows, copy) in enumerate(parts):
+        copy.wait()
+        if at + ahead < len(parts):
+            parts[at + ahead][2].start()
+        for line in range(rows.start, rows.start + rows.size, 128):
+            lines = pl.ds(line, 128)
+            factor = 1.0 + dot32(wide_out[i, :, lines], narrow_out[i], TN)
+            outs[i][lines, :] = (raws[i][lines, :].astype(F32) * factor).astype(B16)
+
+
+def down_side_kernel(
+    down_ref, narrow_ref, wide_ref, gate_ref, up_ref, after_ref, raw, down_out, gate_out, up_out, sems
+):
     del after_ref
-    weights_into(2, (down_ref,), (raw,), (out,), narrow_ref, wide_ref, sems)
+    parts = started((down_ref,), (raw,), sems, sems.shape[0])
+    for source, out in ((gate_ref, gate_out), (up_ref, up_out)):
+        for lines in chunks_of(source.shape[0]):
+            out[:, lines] = source[lines, :].T
+    for _, rows, copy in parts:
+        copy.wait()
+        for lanes in chunks_of(raw.shape[1]):
+            factor = 1.0 + dot32(narrow_ref[2, :, rows], wide_ref[2, :, lanes], TN)
+            down_out[lanes, rows] = (raw[rows, lanes].astype(F32) * factor).astype(B16).T
 
 
 def picks_of(extra, wanted_experts, rows, capacity):
@@ -178,30 +182,26 @@
         first += out.shape[0]
 
 
-def pack_kernel(masks, rows, capacity, lanes, waits, *refs):
-    refs = refs[waits:]
-    sent = len(masks[:3])
-    blocks, pick_out, outs = refs[: -1 - sent], refs[-1 - sent], refs[-sent:]
-    block = stacked(blocks)
+def pack_kernel(masks, offsets, rows, capacity, lanes, blocks, after_ref, *refs):
+    del after_ref
+    came, refs = refs[:blocks], refs[blocks:]
+    crossing = refs[0].shape[0] == rows and len(refs) > 1 + len(masks)
+    crossed, (pick_out, *outs) = (refs[:1], refs[1:]) if crossing else ((), refs)
+    block = stacked(came[::-1])
     me = lax.axis_index("expert")
     picks = picks_of(block[:, lanes], [(me ^ mask) // 2 for mask in masks], rows, capacity)
-    pick_out[...] = jnp.concatenate(picks, axis=0)
-    picks = jnp.concatenate(picks[:sent], axis=0).astype(B16)
-    write_rows(outs, dot32(picks, block.astype(B16)))
-
-
-def cross_kernel(offsets, rows, capacity, lanes, after_ref, block_ref, *outs):
-    del after_ref
-    block = block_ref[...].astype(F32)
-    width = block.shape[1]
-    folds, step = folds_of(rows, capacity, width)
-    extra = jnp.concatenate([block[:, lanes]] * folds, axis=0)
-    laid = lane_pieces(block, folds, step).astype(B16)
-    me = lax.axis_index("expert")
-    picks = picks_of(extra, [(me ^ offset) // 2 for offset in offsets], rows, capacity)
     picks = jnp.concatenate(picks, axis=0)
-    outs[0][...] = picks
-    write_rows(outs[1:], dot32(picks.astype(B16), laid))
+    pick_out[...] = picks
+    write_rows(outs[: len(masks)], dot32(picks.astype(B16), block.astype(B16)))
+    for ref in crossed:
+        block = ref[...].astype(F32)
+        folds, step = folds_of(rows, capacity, block.shape[1])
+        extra = jnp.concatenate([block[:, lanes]] * folds, axis=0)
+        picks = picks_of(extra, [(me ^ offset) // 2 for offset in offsets], rows, capacity)
+        picks = jnp.concatenate(picks, axis=0)
+        outs[len(masks)][...] = picks
+        laid = lane_pieces(block, folds, step).astype(B16)
+        write_rows(outs[len(masks) + 1 :], dot32(picks.astype(B16), laid))
 
 
 def lane_pieces(block, folds, step):
@@ -268,7 +268,7 @@
         y_ref[:, part] = jnp.concatenate(
             [piece[:, part].astype(F32) for piece in pieces], axis=0
         ).astype(B16)
-    grad_full = dot32(y_ref[...], down_ref[...], NT)
+    grad_full = dot32(y_ref[...], down_ref[...])
     pre_gate, pre_up = pre_gate_ref[...], pre_up_ref[...]
     probs = prob_ref[:, :1]
     routed = probs > 0.0
@@ -284,8 +284,8 @@
     grad_up_ref[...] = jnp.where(routed, grad_hidden * activated, 0.0).astype(B16)
     half = mine_ref.shape[0]
     for part in chunks_of(width):
-        product = dot32(grad_gate_ref[...], gate_ref[part, :], NT)
-        product = product + dot32(grad_up_ref[...], up_ref[part, :], NT)
+        product = dot32(grad_gate_ref[...], gate_ref[:, part])
+        product = product + dot32(grad_up_ref[...], up_ref[:, part])
         mine_ref[:, part] = product[:half].astype(B16)
         give_ref[:, part] = product[half:].astype(B16)
     lanes = mine_ref.shape[1] - width
@@ -315,10 +315,11 @@
         write_rows(outs[near:], dot32(piece_order(laid.shape[0], folds, len(outs[near:]), True), laid))
 
 
-def second_sum_kernel(near, folds, crossing, ways, give_ref, pick_ref, *refs):
+def second_sum_kernel(near, folds, crossing, ways, order, give_ref, pick_ref, *refs):
     refs[-1][...] = give_ref[...]
     refs = refs[:-1]
-    came, refs = refs[:near], refs[near:]
+    came = [refs[order.index(i)] for i in range(len(order))]
+    came, refs = came[:near], (*came[near:], *refs[len(order) :])
     total = dot32(pick_ref[...].astype(B16), stacked(came).astype(B16), TN)
     if crossing:
         cross_pick, came, refs = refs[0], refs[1 : 1 + crossing], refs[1 + crossing :]
@@ -331,29 +332,31 @@
         out[...] = total[(i + 1) * count : (i + 2) * count].astype(B16)
 
 
-def down_grads_kernel(y_ref, hidden_ref, down_ref, narrow_ref, masked_out, wide_out):
-    width = y_ref.shape[1]
+def up_grads_kernel(x_ref, grad_ref, raw_ref, narrow_ref, masked_out, wide_out):
+    width = x_ref.shape[1]
     for part in chunks_of(width, width // 2):
-        masked = dot32(hidden_ref[...], y_ref[:, part], TN) * down_ref[:, part].astype(F32)
+        masked = dot32(x_ref[:, part], grad_ref[...], TN) * raw_ref[part, :].astype(F32)
         masked = masked.astype(B16)
-        masked_out[:, part] = masked
-        wide_out[:, part] = dot32(narrow_ref[2], masked)
-
-
-def feature_grads_kernel(
-    x_ref, grad_gate_ref, grad_up_ref, gate_ref, up_ref, narrow_ref, after_ref, down_wide_ref,
-    masked_gate, masked_up, keep_out, give_out, wide_all,
+        masked_out[part, :] = masked
+        wide_out[:, part] = dot32(narrow_ref[1], masked, NT)
+
+
+def other_grads_kernel(
+    x_ref, grad_ref, gate_ref, y_ref, hidden_ref, down_ref, narrow_ref, after_ref, up_wide_ref,
+    masked_gate, masked_down, keep_out, give_out, wide_all,
 ):
     del after_ref
     width, rank = x_ref.shape[1], narrow_ref.shape[1]
-    wide_all[pl.ds(2 * rank, rank), :] = down_wide_ref[...]
-    sides = ((grad_gate_ref, gate_ref, masked_gate), (grad_up_ref, up_ref, masked_up))
-    for i, (grad, raw, out) in enumerate(sides):
-        for part in chunks_of(width, width // 2):
-            masked = dot32(x_ref[:, part], grad[...], TN) * raw[part, :].astype(F32)
-            masked = masked.astype(B16)
-            out[part, :] = masked
-            wide_all[pl.ds(i * rank, rank), part] = dot32(narrow_ref[i], masked, NT)
+    wide_all[pl.ds(rank, rank), :] = up_wide_ref[...]
+    for part in chunks_of(width, width // 2):
+        masked = dot32(x_ref[:, part], grad_ref[...], TN) * gate_ref[part, :].astype(F32)
+        masked = masked.astype(B16)
+        masked_gate[part, :] = masked
+        wide_all[pl.ds(0, rank), part] = dot32(narrow_ref[0], masked, NT)
+        masked = dot32(hidden_ref[...], y_ref[:, part], TN) * down_ref[:, part].astype(F32)
+        masked = masked.astype(B16)
+        masked_down[:, part] = masked
+        wide_all[pl.ds(2 * rank, rank), part] = dot32(narrow_ref[2], masked)
     half = keep_out.shape[1]
     is_lower = lax.axis_index("expert") % 2 == 0
 
@@ -456,33 +459,28 @@
     )
     folds, step = folds_of(rows, capacity, full + width)
     probs_at = slice(width, full)
-    cross_pick, folded = [], []
-    for block in crossed:
-        picked, *folded = in_vmem(
-            functools.partial(cross_kernel, offsets, rows, capacity, probs_at),
-            [((len(offsets) * folds * capacity, folds * rows), F32)]
-            + [((folds * capacity, step), B16)] * len(offsets),
-            [wide, block],
-        )
-        cross_pick = [picked]
     beside = near[:2]
     pick, *packed = in_vmem(
         functools.partial(
-            pack_kernel, (0, *beside), rows, capacity, probs_at, 1 + len(folded[:1])
+            pack_kernel, (0, *beside), offsets, rows, capacity, probs_at, len(pieces)
         ),
         [(((1 + len(beside)) * slots, count), F32)]
-        + [((slots, full + width), B16)] * (1 + len(beside)),
-        [wide] + folded[:1] + pieces,
-    )
+        + [((slots, full + width), B16)] * (1 + len(beside))
+        + [((len(offsets) * folds * capacity, folds * rows), F32)] * len(crossed)
+        + [((folds * capacity, step), B16)] * (len(offsets) * len(crossed)),
+        [wide] + pieces[::-1] + crossed,
+    )
+    packed, cross_pick, folded = packed[: 1 + len(beside)], packed[1 + len(beside) :], []
+    cross_pick, folded = cross_pick[:1], cross_pick[1:]
     came = packed[:1] + [send(block, mask) for block, mask in zip(packed[1:], beside)]
     came += folded[:1] + [send(block, mask) for block, mask in zip(folded[1:], offsets[1:])]
     order = list(range(len(came)))
     if len(came) > 6:
         order = [0, 1, 5, 2, 6, *order[7:], 4, 3]
-    down_raw, down_eff = in_vmem(
+    down_raw, down_turned, gate_turned, up_turned = in_vmem(
         down_side_kernel,
-        [(down_weight.shape, B16)] * 2,
-        (down_weight, narrow, wide, pick),
+        [(down_weight.shape, B16), (gate_weight.shape, B16)] + [(down_weight.shape, B16)] * 2,
+        (down_weight, narrow, wide, gate_eff, up_eff, pick),
         matmul,
         outside=1,
         scratch=[pltpu.SemaphoreType.DMA((4,))],
@@ -490,7 +488,7 @@
     mine_rows, cot_mine = in_vmem(
         functools.partial(stack_kernel, folds, 1 + len(beside), order),
         [((half, full), B16), ((half, width), B16)],
-        [down_eff] + [came[i] for i in order],
+        [down_turned] + [came[i] for i in order],
     )
     token_rows = [mine_rows, send(mine_rows, 1)]
     cot_rows = [cot_mine, send(cot_mine, 1)]
@@ -505,14 +503,14 @@
     y, hidden, grad_gate, grad_up, mine, give = in_vmem(
         functools.partial(mid_kernel, experts, width),
         [wide_type] + [unit_type] * 3 + [((half, full), B16)] * 2,
-        (gate_eff, up_eff, down_eff, probs, pre_gate, pre_up, *cot_rows),
+        (gate_turned, up_turned, down_turned, probs, pre_gate, pre_up, *cot_rows),
         3 * matmul,
     )
     other = send(give, 1)
-    masked_down, down_wide = in_vmem(
-        down_grads_kernel,
-        [(down_weight.shape, B16), ((rank, width), F32)],
-        (y, hidden, down_raw, narrow),
+    masked_up, up_wide = in_vmem(
+        up_grads_kernel,
+        [(up_weight.shape, B16), ((rank, width), F32)],
+        (x, grad_up, up_raw, narrow),
         2 * matmul,
     )
     near_count, cross_count = 1 + len(beside), len(folded)
@@ -521,13 +519,13 @@
         functools.partial(first_sum_kernel, experts, width, near_count, folds),
         [((slots, full), B16)] * near_count
         + [((folds * capacity, fold_step), B16)] * cross_count,
-        (mine, other, down_wide),
-    )
-    masked_gate, masked_up, keep, give = in_vmem(
-        feature_grads_kernel,
-        [(gate_weight.shape, B16)] * 2
+        (mine, other, up_wide),
+    )
+    masked_gate, masked_down, keep, give = in_vmem(
+        other_grads_kernel,
+        [(gate_weight.shape, B16), (down_weight.shape, B16)]
         + [((3 * rank, width // 2), F32), ((3 * rank, width // 2), B16)],
-        (x, grad_gate, grad_up, gate_raw, up_raw, narrow, sums[0], down_wide),
+        (x, grad_gate, gate_raw, y, hidden, down_raw, narrow, sums[0], up_wide),
         4 * matmul,
         scratch=[pltpu.VMEM((3 * rank, width), F32)],
     )
@@ -535,14 +533,17 @@
     crossing = sums[near_count:]
     came += [*cross_pick, *crossing[:1]]
     came += [send(part, mask) for part, mask in zip(crossing[1:], offsets[1:])]
+    order = list(range(len(came)))
+    if len(came) > 7:
+        order = [0, 3, 4, 1, 6, 2, 7, *order[8:], 5]
     ways = len(far[0]) if far else 0
     own, *parts = in_vmem(
-        functools.partial(second_sum_kernel, near_count, folds, cross_count, ways),
+        functools.partial(second_sum_kernel, near_count, folds, cross_count, ways, order),
         [((count // (ways + 1), full), F32)]
         + [((count // (ways + 1), full), B16)] * ways
         + [((rows, full), B16)] * len(crossed)
         + [(give.shape, B16)],
-        (give, pick, *came),
+        (give, pick, *[came[i] for i in order]),
     )
     *parts, give = parts
     (grad_narrow,) = in_vmem(

time: 62.2 us -> 61.7 us (level)
  waiting for transfers between devices: 8.35 us -> 7.26 us
    ppermute x23, waiting for transfers between devices: 8.35 us -> 7.26 us  [send(): return lax.ppermute(value, 'expert', pairs)]
    pallas_call x14 -> x13, Pallas kernels: 26.3 us -> 26.4 us  [in_vmem(): pl.pallas_call(kernel, out_shape=[(jax.ShapeDtypeStruct if i in results e...]
  transfers between devices with their start and end apart: 23 -> 23, of which waited for: 9 -> 7; matrix products, arithmetic and copies ran while one was open for 0% -> 0% of each run, Pallas kernels for 32% -> 34%
where the time goes in v7:
time: 61.7 us; the launch traced here: 61.5 us
  starting transfers between devices  27.1 us (44%)
  Pallas kernels  26.4 us (43%)
  waiting for transfers between devices  7.26 us (12%)
  between operations  0.76 us (1%)
    ppermute x23, starting transfers between devices, send(): return lax.ppermute(value, 'expert', pairs)  27.1 us
    pallas_call x13, Pallas kernels, in_vmem(): pl.pallas_call(kernel, out_shape=[(jax.ShapeDtypeStruct if i in results e...  26.4 us
    ppermute x23, waiting for transfers between devices, send(): return lax.ppermute(value, 'expert', pairs)  7.26 us
  transfers between devices with their start and end apart: 23, of which 7 were waited for; matrix products, arithmetic and copies ran while one was open for 0% of the time, Pallas kernels for 34%

profile of v7, /device:TPU:0, one launch (start us, length us, event | category | flops | bytes accessed | tf_op | source)
XLA Modules:
  0.0 61.5 jit_solution(14423679158012695596)
XLA Ops:
  0.6 0.5 collective-permute-start
  1.1 0.9 %shard_map.121.refs_3_ = bf16[8,7296]{1,0:T(8,128)(2,1)S(1)} custom-call(bf16[8,3584]{1,0:T(8,128)(2,1)} %refs_0_.1, bf16[8,3584]{1,0:T(8,128)(2,1)} %refs_1_.1, f32[8,8]{1,0:T(8,128)} %refs_2_.1, s32[8,8]{1,0:T(8,128)} %ids_ref.1), custom_call_target="tpu_custom_call" | custom-call | bytes 115200 | tf_op jit(solution)/shard_map/pallas_call | solution.py:40
  2.1 4.7 %collective-permute-start.1 = (bf16[8,7296]{1,0:T(8,128)(2,1)S(1)}, bf16[8,7296]{1,0:T(8,128)(2,1)S(1)}, u32[]{:S(2)}, u32[]{:S(2)}) collective-permute-start(bf16[8,7296]{1,0:T(8,128)(2,1)S(1)} %shard_map.121.refs_3_), channel_id=1, source_target_pairs={{0,24},{1,25},{2,26},{3,27},{4,28},{5,29},{6,30},{7,31},{8,16},{9,... | collective-permute-start | bytes 350216 | tf_op jit(solution)/shard_map/ppermute | solution.py:19
  6.7 0.0 collective-permute-start.2
  6.7 0.6 %collective-permute-start.3 = (bf16[8,7296]{1,0:T(8,128)(2,1)S(1)}, bf16[8,7296]{1,0:T(8,128)(2,1)S(1)}, u32[]{:S(2)}, u32[]{:S(2)}) collective-permute-start(bf16[8,7296]{1,0:T(8,128)(2,1)S(1)} %shard_map.121.refs_3_), channel_id=1, source_target_pairs={{0,8},{1,9},{2,10},{3,11},{4,12},{5,13},{6,14},{7,15},{8,0},{9,1},... | collective-permute-start | bytes 350216 | tf_op jit(solution)/shard_map/ppermute | solution.py:19
  7.4 2.6 %collective-permute-start.4 = (bf16[8,7296]{1,0:T(8,128)(2,1)S(1)}, bf16[8,7296]{1,0:T(8,128)(2,1)S(1)}, u32[]{:S(2)}, u32[]{:S(2)}) collective-permute-start(bf16[8,7296]{1,0:T(8,128)(2,1)S(1)} %shard_map.121.refs_3_), channel_id=1, source_target_pairs={{0,6},{1,7},{2,4},{3,5},{4,2},{5,3},{6,0},{7,1},{8,14},{9,15},{10,... | collective-permute-start | bytes 350216 | tf_op jit(solution)/shard_map/ppermute | solution.py:19
  10.0 0.0 collective-permute-done.other_ref
  10.0 5.6 %shard_map.120 = (bf16[3584,512]{1,0:T(8,128)(2,1)S(1)}, bf16[3584,512]{1,0:T(8,128)(2,1)S(1)}, bf16[3584,512]{1,0:T(8,128)(2,1)S(1)}, bf16[3584,512]{1,0:T(8,12...) custom-call(bf16[3584,512]{1,0:T(8,128)(2,1)} %gate_ref.1, bf16[3584,512]{1,0:T(8,128)(2,1)} %up_ref.1, ...), custom_call_target="tpu_custom_call" | custom-call | flops 1409286144 | bytes 7733248 | tf_op jit(solution)/shard_map/pallas_call | solution.py:40
  15.6 0.0 collective-permute-done.1.refs_0_
  15.6 1.6 %collective-permute-done.2.refs_1_ = bf16[8,7296]{1,0:T(8,128)(2,1)S(1)} collective-permute-done((bf16[8,7296]{1,0:T(8,128)(2,1)S(1)}, bf16[8,7296]{1,0:T(8,128)(2,1)S(1)}, u32[]{:S(2)}, u32[]{:S(2)}) %collective-permute-start.2) | collective-permute-done | bytes 116768 | tf_op jit(solution)/shard_map/ppermute | solution.py:19
  17.2 0.0 collective-permute-done.3.refs_2_
  17.2 0.0 collective-permute-done.4.refs_4_
  17.2 1.0 %shard_map.122 = (f32[72,32]{1,0:T(8,128)S(1)}, bf16[24,7296]{1,0:T(8,128)(2,1)S(1)}, bf16[24,7296]{1,0:T(8,128)(2,1)S(1)}, bf16[24,7296]{1,0:T(8,128)(2,1)S(1)}...) custom-call(bf16[3,16,3584]{2,1,0:T(8,128)(2,1)S(1)} %get-tuple-elem, ...), custom_call_target="tpu_custom_call" | custom-call | bytes 927744 | tf_op jit(solution)/shard_map/pallas_call | solution.py:40
  18.3 1.6 %collective-permute-start.5 = (bf16[24,7296]{1,0:T(8,128)(2,1)S(1)}, bf16[24,7296]{1,0:T(8,128)(2,1)S(1)}, u32[]{:S(2)}, u32[]{:S(2)}) collective-permute-start(bf16[24,7296]{1,0:T(8,128)(2,1)S(1)} %get-tuple-element.64), channel_id=1, source_target_pairs={{0,2},{1,3},{2,0},{3,1},{4,6},{5,7},{6,4},{7,5},{8,10},{9,11},{10,... | collective-permute-start | bytes 1050632 | tf_op jit(solution)/shard_map/ppermute | solution.py:19
  19.8 1.5 %collective-permute-start.7 = (bf16[24,7296]{1,0:T(8,128)(2,1)S(1)}, bf16[24,7296]{1,0:T(8,128)(2,1)S(1)}, u32[]{:S(2)}, u32[]{:S(2)}) collective-permute-start(bf16[24,7296]{1,0:T(8,128)(2,1)S(1)} %get-tuple-element.66), channel_id=1, source_target_pairs={{0,4},{1,5},{2,6},{3,7},{4,0},{5,1},{6,2},{7,3},{8,12},{9,13},{10,... | collective-permute-start | bytes 1050632 | tf_op jit(solution)/shard_map/ppermute | solution.py:19
  21.3 0.0 collective-permute-start.6
  21.4 2.6 %collective-permute-start.8 = (bf16[24,1920]{1,0:T(8,128)(2,1)S(1)}, bf16[24,1920]{1,0:T(8,128)(2,1)S(1)}, u32[]{:S(2)}, u32[]{:S(2)}) collective-permute-start(bf16[24,1920]{1,0:T(8,128)(2,1)S(1)} %get-tuple-element.67), channel_id=1, source_target_pairs={{0,24},{1,25},{2,26},{3,27},{4,28},{5,29},{6,30},{7,31},{8,16},{9,... | collective-permute-start | bytes 276488 | tf_op jit(solution)/shard_map/ppermute | solution.py:19
  23.9 0.9 %collective-permute-start.9 = (bf16[24,1920]{1,0:T(8,128)(2,1)S(1)}, bf16[24,1920]{1,0:T(8,128)(2,1)S(1)}, u32[]{:S(2)}, u32[]{:S(2)}) collective-permute-start(bf16[24,1920]{1,0:T(8,128)(2,1)S(1)} %get-tuple-element.68), channel_id=1, source_target_pairs={{0,8},{1,9},{2,10},{3,11},{4,12},{5,13},{6,14},{7,15},{8,0},{9,1},... | collective-permute-start | bytes 276488 | tf_op jit(solution)/shard_map/ppermute | solution.py:19
  24.8 4.2 %shard_map.123 = (bf16[512,3584]{1,0:T(8,128)(2,1)S(1)}, bf16[3584,512]{1,0:T(8,128)(2,1)S(1)}, bf16[512,3584]{1,0:T(8,128)(2,1)S(1)}, bf16[512,3584]{1,0:T(8,128)(2,1)S(1)}) custom-call(bf16[512,3584]{1,0:T(8,128)(2,1)} %down_ref.1, bf16[3,16,512]{2,1,0:T(8,128)(2,1)S(1)} %get-tuple-element.59.narrow_ref, ...), custom_call_target="tpu_custom_call" | custom-call | flops 704643072 | bytes 11412480 | tf_op jit(solution)/shard_map/pallas_call | solution.py:40
  29.1 0.8 %collective-permute-done.6.refs_2_ = bf16[24,1920]{1,0:T(8,128)(2,1)S(1)} collective-permute-done((bf16[24,1920]{1,0:T(8,128)(2,1)S(1)}, bf16[24,1920]{1,0:T(8,128)(2,1)S(1)}, u32[]{:S(2)}, u32[]{:S(2)}) %collective-permute-start.6) | collective-permute-done | bytes 92192 | tf_op jit(solution)/shard_map/ppermute | solution.py:19
  29.9 0.0 collective-permute-done.8.refs_4_
  29.9 0.9 %collective-permute-done.9.refs_5_ = bf16[24,1920]{1,0:T(8,128)(2,1)S(1)} collective-permute-done((bf16[24,1920]{1,0:T(8,128)(2,1)S(1)}, bf16[24,1920]{1,0:T(8,128)(2,1)S(1)}, u32[]{:S(2)}, u32[]{:S(2)}) %collective-permute-start.9) | collective-permute-done | bytes 92192 | tf_op jit(solution)/shard_map/ppermute | solution.py:19
  30.7 0.0 collective-permute-done.5.refs_1_
  30.7 0.0 collective-permute-done.7.refs_3_
  30.8 0.3 shard_map.124
  31.1 0.1 collective-permute-start.10
  31.2 0.5 collective-permute-start.11
  31.7 1.7 %collective-permute-done.10.refs_1_ = bf16[96,3712]{1,0:T(8,128)(2,1)S(1)} collective-permute-done((bf16[96,3712]{1,0:T(8,128)(2,1)S(1)}, bf16[96,3712]{1,0:T(8,128)(2,1)S(1)}, u32[]{:S(2)}, u32[]{:S(2)}) %collective-permute-start.10) | collective-permute-done | bytes 712736 | tf_op jit(solution)/shard_map/ppermute | solution.py:19
  33.3 1.6 %shard_map.125 = (bf16[192,3584]{1,0:T(8,128)(2,1)S(1)}, f32[192,128]{1,0:T(8,128)S(1)}, f32[192,512]{1,0:T(8,128)S(1)}, f32[192,512]{1,0:T(8,128)S(1)}) custom-call(bf16[3584,512]{1,0:T(8,128)(2,1)S(1)} %get-tuple-element.57.gate_ref, bf16[3584,512]{1,0:T(8,128)(2,1)S(1)} %get-tuple-element.58.up_ref, bf16[96,3712]{1,0:T(8,128)(2,1)S(1)} %get-tuple-element.70.refs_0_, ...), custom_call_target="tpu_custom_call" | custom-call | flops 1409286144 | bytes 8765440 | tf_op jit(solution)/shard_map/pallas_call | solution.py:40
  34.9 0.0 collective-permute-done.11.refs_1_
  34.9 2.6 %shard_map.126 = (bf16[192,3584]{1,0:T(8,128)(2,1)S(1)}, bf16[192,512]{1,0:T(8,128)(2,1)S(1)}, bf16[192,512]{1,0:T(8,128)(2,1)S(1)}, bf16[192,512]{1,0:T(8,128)(...) custom-call(bf16[512,3584]{1,0:T(8,128)(2,1)S(1)} %get-tuple-element.72.gate_ref, ...), custom_call_target="tpu_custom_call" | custom-call | flops 2113929216 | bytes 13271040 | tf_op jit(solution)/shard_map/pallas_call | solution.py:40
  37.6 0.2 collective-permute-start.12
  37.8 2.0 %shard_map.127 = (bf16[3584,512]{1,0:T(8,128)(2,1)S(1)}, f32[16,3584]{1,0:T(8,128)S(1)}) custom-call(bf16[192,3584]{1,0:T(8,128)(2,1)S(1)} %get-tuple-element.71.x_ref, bf16[192,512]{1,0:T(8,128)(2,1)S(1)} %get-tuple-element.85.grad_ref, bf16[3584,512]{1,0:T(8,128)(2,1)S(1)} %get-tuple-element.86.raw_ref, bf16[3,16,512]{2,1,0:T(8,128)(2,1)S(1)} %get-tuple-element.59.narrow_ref), custom_call_target="tpu_custom_call" | custom-call | flops 1409286144 | bytes 5292032 | tf_op jit(solution)/shard_map/pallas_call | solution.py:40
  39.8 0.0 collective-permute-done.12.other_ref
  39.8 0.6 shard_map.128
  40.4 0.6 collective-permute-start.13
  41.0 0.5 collective-permute-start.15
  41.5 1.7 %collective-permute-start.14 = (bf16[24,1024]{1,0:T(8,128)(2,1)S(1)}, bf16[24,1024]{1,0:T(8,128)(2,1)S(1)}, u32[]{:S(2)}, u32[]{:S(2)}) collective-permute-start(bf16[24,1024]{1,0:T(8,128)(2,1)S(1)} %get-tuple-element.94), channel_id=1, source_target_pairs={{0,16},{1,17},{2,18},{3,19},{4,20},{5,21},{6,22},{7,23},{8,24},{9,... | collective-permute-start | bytes 147464 | tf_op jit(solution)/shard_map/ppermute | solution.py:19
  43.3 2.2 %collective-permute-start.16 = (bf16[24,1024]{1,0:T(8,128)(2,1)S(1)}, bf16[24,1024]{1,0:T(8,128)(2,1)S(1)}, u32[]{:S(2)}, u32[]{:S(2)}) collective-permute-start(bf16[24,1024]{1,0:T(8,128)(2,1)S(1)} %get-tuple-element.96), channel_id=1, source_target_pairs={{0,24},{1,25},{2,26},{3,27},{4,28},{5,29},{6,30},{7,31},{8,16},{9,... | collective-permute-start | bytes 147464 | tf_op jit(solution)/shard_map/ppermute | solution.py:19
  45.4 0.0 collective-permute-start.17
  45.5 3.6 %shard_map.129 = (bf16[3584,512]{1,0:T(8,128)(2,1)S(1)}, bf16[512,3584]{1,0:T(8,128)(2,1)S(1)}, f32[48,1792]{1,0:T(8,128)S(1)}, bf16[48,1792]{1,0:T(8,128)(2,1)S(1)}) custom-call(bf16[192,3584]{1,0:T(8,128)(2,1)S(1)} %get-tuple-element.71.x_ref, bf16[192,512]{1,0:T(8,128)(2,1)S(1)} %get-tuple-element.78.grad_ref, ...), custom_call_target="tpu_custom_call" | custom-call | flops 2818572288 | bytes 10942464 | tf_op jit(solution)/shard_map/pallas_call | solution.py:40
  49.0 0.0 collective-permute-done.14.refs_4_
  49.1 0.2 collective-permute-done.16.refs_6_
  49.3 0.5 collective-permute-done.17.refs_7_
  49.8 0.0 collective-permute-done.13.refs_3_
  49.8 0.0 collective-permute-done.15.refs_5_
  49.8 0.3 shard_map.130
  50.1 0.1 collective-permute-start.22
  50.2 1.6 %collective-permute-start.18 = (bf16[8,3712]{1,0:T(8,128)(2,1)S(1)}, bf16[8,3712]{1,0:T(8,128)(2,1)S(1)}, u32[]{:S(2)}, u32[]{:S(2)}) collective-permute-start(bf16[8,3712]{1,0:T(8,128)(2,1)S(1)} %get-tuple-element.99), channel_id=1, source_target_pairs={{0,16},{1,17},{2,18},{3,19},{4,20},{5,21},{6,22},{7,23},{8,24},{9,... | collective-permute-start | bytes 178184 | tf_op jit(solution)/shard_map/ppermute | solution.py:19
  51.8 2.2 %collective-permute-start.19 = (bf16[8,3712]{1,0:T(8,128)(2,1)S(1)}, bf16[8,3712]{1,0:T(8,128)(2,1)S(1)}, u32[]{:S(2)}, u32[]{:S(2)}) collective-permute-start(bf16[8,3712]{1,0:T(8,128)(2,1)S(1)} %get-tuple-element.100), channel_id=1, source_target_pairs={{0,24},{1,25},{2,26},{3,27},{4,28},{5,29},{6,30},{7,31},{8,16},{9,... | collective-permute-start | bytes 178184 | tf_op jit(solution)/shard_map/ppermute | solution.py:19
  53.9 2.4 %collective-permute-start.20 = (bf16[8,3712]{1,0:T(8,128)(2,1)S(1)}, bf16[8,3712]{1,0:T(8,128)(2,1)S(1)}, u32[]{:S(2)}, u32[]{:S(2)}) collective-permute-start(bf16[8,3712]{1,0:T(8,128)(2,1)S(1)} %get-tuple-element.101.after_ref), channel_id=1, source_target_pairs={{0,6},{1,7},{2,4},{3,5},{4,2},{5,3},{6,0},{7,1},{8,14},{9,15},{10,... | collective-permute-start | bytes 178184 | tf_op jit(solution)/shard_map/ppermute | solution.py:19
  56.4 0.0 collective-permute-start.21
  56.4 0.0 copy-start
  56.4 2.6 %shard_map.132 = f32[48,512]{1,0:T(8,128)} custom-call(bf16[3584,512]{1,0:T(8,128)(2,1)S(1)} %get-tuple-element.106.masked_gate, bf16[3584,512]{1,0:T(8,128)(2,1)S(1)} %get-tuple-element.107.masked_up, bf16[512,3584]{1,0:T(8,128)(2,1)S(1)} %get-tuple-element.108.masked_down, bf16[3,16,3584]{2,1,0:T(8,128)(2,1)S(1)} %get-tuple-element.60.after_ref.wide_ref, ...), custom_call_target="tpu_custom_call" | custom-call | flops 1409286144 | bytes 11413504 | tf_op jit(solution)/shard_map/pallas_call | solution.py:40
  59.0 0.0 collective-permute-done.18.refs_0_
  59.0 0.0 collective-permute-done.19.refs_1_
  59.0 0.0 collective-permute-done.20.refs_2_
  59.0 1.5 %collective-permute-done.21.refs_3_ = bf16[8,3712]{1,0:T(8,128)(2,1)S(1)} collective-permute-done((bf16[8,3712]{1,0:T(8,128)(2,1)S(1)}, bf16[8,3712]{1,0:T(8,128)(2,1)S(1)}, u32[]{:S(2)}, u32[]{:S(2)}) %collective-permute-start.21) | collective-permute-done | bytes 59424 | tf_op jit(solution)/shard_map/ppermute | solution.py:19
  60.6 0.0 collective-permute-done.22.refs_4_
  60.6 0.0 copy-done
  60.6 0.9 %shard_map.131 = (bf16[8,3584]{1,0:T(8,128)(2,1)}, f32[8,8]{1,0:T(8,128)}, f32[48,1792]{1,0:T(8,128)}) custom-call(s32[8,8]{1,0:T(8,128)S(1)} %copy-done, f32[48,1792]{1,0:T(8,128)S(1)} %get-tuple-element.89.keep_ref, f32[8,3712]{1,0:T(8,128)S(1)} %get-tuple-element.98.own_ref, bf16[8,3712]{1,0:T(8,128)(2,1)S(1)} %collective-permute-done.18.refs_0_, ...), custom_call_target="tpu_custom_call" | custom-call | bytes 872704 | tf_op jit(solution)/shard_map/pallas_call | solution.py:40
Async XLA Ops:
  0.6 9.3 %collective-permute-start = (bf16[3,16,1792]{2,1,0:T(8,128)(2,1)}, bf16[3,16,1792]{2,1,0:T(8,128)(2,1)S(1)}, u32[]{:S(2)}, u32[]{:S(2)}) collective-permute-start(bf16[3,16,1792]{2,1,0:T(8,128)(2,1)} %mine_hbm.1), channel_id=1, source_target_pairs={{0,1},{1,0},{2,3},{3,2},{4,5},{5,4},{6,7},{7,6},{8,9},{9,8},{10,11... | collective-permute-start | bytes 516104 | tf_op jit(solution)/shard_map/ppermute | solution.py:19
  2.1 13.6 %collective-permute-start.1 = (bf16[8,7296]{1,0:T(8,128)(2,1)S(1)}, bf16[8,7296]{1,0:T(8,128)(2,1)S(1)}, u32[]{:S(2)}, u32[]{:S(2)}) collective-permute-start(bf16[8,7296]{1,0:T(8,128)(2,1)S(1)} %shard_map.121.refs_3_), channel_id=1, source_target_pairs={{0,24},{1,25},{2,26},{3,27},{4,28},{5,29},{6,30},{7,31},{8,16},{9,... | collective-permute-start | bytes 350216 | tf_op jit(solution)/shard_map/ppermute | solution.py:19
  6.7 10.5 %collective-permute-start.2 = (bf16[8,7296]{1,0:T(8,128)(2,1)S(1)}, bf16[8,7296]{1,0:T(8,128)(2,1)S(1)}, u32[]{:S(2)}, u32[]{:S(2)}) collective-permute-start(bf16[8,7296]{1,0:T(8,128)(2,1)S(1)} %shard_map.121.refs_3_), channel_id=1, source_target_pairs={{0,16},{1,17},{2,18},{3,19},{4,20},{5,21},{6,22},{7,23},{8,24},{9,... | collective-permute-start | bytes 350216 | tf_op jit(solution)/shard_map/ppermute | solution.py:19
  6.7 10.5 %collective-permute-start.3 = (bf16[8,7296]{1,0:T(8,128)(2,1)S(1)}, bf16[8,7296]{1,0:T(8,128)(2,1)S(1)}, u32[]{:S(2)}, u32[]{:S(2)}) collective-permute-start(bf16[8,7296]{1,0:T(8,128)(2,1)S(1)} %shard_map.121.refs_3_), channel_id=1, source_target_pairs={{0,8},{1,9},{2,10},{3,11},{4,12},{5,13},{6,14},{7,15},{8,0},{9,1},... | collective-permute-start | bytes 350216 | tf_op jit(solution)/shard_map/ppermute | solution.py:19
  7.4 9.9 %collective-permute-start.4 = (bf16[8,7296]{1,0:T(8,128)(2,1)S(1)}, bf16[8,7296]{1,0:T(8,128)(2,1)S(1)}, u32[]{:S(2)}, u32[]{:S(2)}) collective-permute-start(bf16[8,7296]{1,0:T(8,128)(2,1)S(1)} %shard_map.121.refs_3_), channel_id=1, source_target_pairs={{0,6},{1,7},{2,4},{3,5},{4,2},{5,3},{6,0},{7,1},{8,14},{9,15},{10,... | collective-permute-start | bytes 350216 | tf_op jit(solution)/shard_map/ppermute | solution.py:19
  18.3 12.5 %collective-permute-start.5 = (bf16[24,7296]{1,0:T(8,128)(2,1)S(1)}, bf16[24,7296]{1,0:T(8,128)(2,1)S(1)}, u32[]{:S(2)}, u32[]{:S(2)}) collective-permute-start(bf16[24,7296]{1,0:T(8,128)(2,1)S(1)} %get-tuple-element.64), channel_id=1, source_target_pairs={{0,2},{1,3},{2,0},{3,1},{4,6},{5,7},{6,4},{7,5},{8,10},{9,11},{10,... | collective-permute-start | bytes 1050632 | tf_op jit(solution)/shard_map/ppermute | solution.py:19
  19.8 10.9 %collective-permute-start.7 = (bf16[24,7296]{1,0:T(8,128)(2,1)S(1)}, bf16[24,7296]{1,0:T(8,128)(2,1)S(1)}, u32[]{:S(2)}, u32[]{:S(2)}) collective-permute-start(bf16[24,7296]{1,0:T(8,128)(2,1)S(1)} %get-tuple-element.66), channel_id=1, source_target_pairs={{0,4},{1,5},{2,6},{3,7},{4,0},{5,1},{6,2},{7,3},{8,12},{9,13},{10,... | collective-permute-start | bytes 1050632 | tf_op jit(solution)/shard_map/ppermute | solution.py:19
  21.3 8.5 %collective-permute-start.6 = (bf16[24,1920]{1,0:T(8,128)(2,1)S(1)}, bf16[24,1920]{1,0:T(8,128)(2,1)S(1)}, u32[]{:S(2)}, u32[]{:S(2)}) collective-permute-start(bf16[24,1920]{1,0:T(8,128)(2,1)S(1)} %get-tuple-element.65), channel_id=1, source_target_pairs={{0,16},{1,17},{2,18},{3,19},{4,20},{5,21},{6,22},{7,23},{8,24},{9,... | collective-permute-start | bytes 276488 | tf_op jit(solution)/shard_map/ppermute | solution.py:19
  21.4 8.5 %collective-permute-start.8 = (bf16[24,1920]{1,0:T(8,128)(2,1)S(1)}, bf16[24,1920]{1,0:T(8,128)(2,1)S(1)}, u32[]{:S(2)}, u32[]{:S(2)}) collective-permute-start(bf16[24,1920]{1,0:T(8,128)(2,1)S(1)} %get-tuple-element.67), channel_id=1, source_target_pairs={{0,24},{1,25},{2,26},{3,27},{4,28},{5,29},{6,30},{7,31},{8,16},{9,... | collective-permute-start | bytes 276488 | tf_op jit(solution)/shard_map/ppermute | solution.py:19
  23.9 6.8 %collective-permute-start.9 = (bf16[24,1920]{1,0:T(8,128)(2,1)S(1)}, bf16[24,1920]{1,0:T(8,128)(2,1)S(1)}, u32[]{:S(2)}, u32[]{:S(2)}) collective-permute-start(bf16[24,1920]{1,0:T(8,128)(2,1)S(1)} %get-tuple-element.68), channel_id=1, source_target_pairs={{0,8},{1,9},{2,10},{3,11},{4,12},{5,13},{6,14},{7,15},{8,0},{9,1},... | collective-permute-start | bytes 276488 | tf_op jit(solution)/shard_map/ppermute | solution.py:19
  31.1 2.2 %collective-permute-start.10 = (bf16[96,3712]{1,0:T(8,128)(2,1)S(1)}, bf16[96,3712]{1,0:T(8,128)(2,1)S(1)}, u32[]{:S(2)}, u32[]{:S(2)}) collective-permute-start(bf16[96,3712]{1,0:T(8,128)(2,1)S(1)} %get-tuple-element.70.refs_0_), channel_id=1, source_target_pairs={{0,1},{1,0},{2,3},{3,2},{4,5},{5,4},{6,7},{7,6},{8,9},{9,8},{10,11... | collective-permute-start | bytes 2138120 | tf_op jit(solution)/shard_map/ppermute | solution.py:19
  31.2 3.8 %collective-permute-start.11 = (bf16[96,3584]{1,0:T(8,128)(2,1)S(1)}, bf16[96,3584]{1,0:T(8,128)(2,1)S(1)}, u32[]{:S(2)}, u32[]{:S(2)}) collective-permute-start(bf16[96,3584]{1,0:T(8,128)(2,1)S(1)} %get-tuple-element.77.refs_0_), channel_id=1, source_target_pairs={{0,1},{1,0},{2,3},{3,2},{4,5},{5,4},{6,7},{7,6},{8,9},{9,8},{10,11... | collective-permute-start | bytes 2064392 | tf_op jit(solution)/shard_map/ppermute | solution.py:19
  37.6 2.2 %collective-permute-start.12 = (bf16[96,3712]{1,0:T(8,128)(2,1)S(1)}, bf16[96,3712]{1,0:T(8,128)(2,1)S(1)}, u32[]{:S(2)}, u32[]{:S(2)}) collective-permute-start(bf16[96,3712]{1,0:T(8,128)(2,1)S(1)} %get-tuple-element.84), channel_id=1, source_target_pairs={{0,1},{1,0},{2,3},{3,2},{4,5},{5,4},{6,7},{7,6},{8,9},{9,8},{10,11... | collective-permute-start | bytes 2138120 | tf_op jit(solution)/shard_map/ppermute | solution.py:19
  40.4 9.4 %collective-permute-start.13 = (bf16[24,3712]{1,0:T(8,128)(2,1)S(1)}, bf16[24,3712]{1,0:T(8,128)(2,1)S(1)}, u32[]{:S(2)}, u32[]{:S(2)}) collective-permute-start(bf16[24,3712]{1,0:T(8,128)(2,1)S(1)} %get-tuple-element.93), channel_id=1, source_target_pairs={{0,2},{1,3},{2,0},{3,1},{4,6},{5,7},{6,4},{7,5},{8,10},{9,11},{10,... | collective-permute-start | bytes 534536 | tf_op jit(solution)/shard_map/ppermute | solution.py:19
  41.0 8.8 %collective-permute-start.15 = (bf16[24,3712]{1,0:T(8,128)(2,1)S(1)}, bf16[24,3712]{1,0:T(8,128)(2,1)S(1)}, u32[]{:S(2)}, u32[]{:S(2)}) collective-permute-start(bf16[24,3712]{1,0:T(8,128)(2,1)S(1)} %get-tuple-element.95), channel_id=1, source_target_pairs={{0,4},{1,5},{2,6},{3,7},{4,0},{5,1},{6,2},{7,3},{8,12},{9,13},{10,... | collective-permute-start | bytes 534536 | tf_op jit(solution)/shard_map/ppermute | solution.py:19
  41.5 7.5 %collective-permute-start.14 = (bf16[24,1024]{1,0:T(8,128)(2,1)S(1)}, bf16[24,1024]{1,0:T(8,128)(2,1)S(1)}, u32[]{:S(2)}, u32[]{:S(2)}) collective-permute-start(bf16[24,1024]{1,0:T(8,128)(2,1)S(1)} %get-tuple-element.94), channel_id=1, source_target_pairs={{0,16},{1,17},{2,18},{3,19},{4,20},{5,21},{6,22},{7,23},{8,24},{9,... | collective-permute-start | bytes 147464 | tf_op jit(solution)/shard_map/ppermute | solution.py:19
  43.3 6.0 %collective-permute-start.16 = (bf16[24,1024]{1,0:T(8,128)(2,1)S(1)}, bf16[24,1024]{1,0:T(8,128)(2,1)S(1)}, u32[]{:S(2)}, u32[]{:S(2)}) collective-permute-start(bf16[24,1024]{1,0:T(8,128)(2,1)S(1)} %get-tuple-element.96), channel_id=1, source_target_pairs={{0,24},{1,25},{2,26},{3,27},{4,28},{5,29},{6,30},{7,31},{8,16},{9,... | collective-permute-start | bytes 147464 | tf_op jit(solution)/shard_map/ppermute | solution.py:19
  45.4 4.3 %collective-permute-start.17 = (bf16[24,1024]{1,0:T(8,128)(2,1)S(1)}, bf16[24,1024]{1,0:T(8,128)(2,1)S(1)}, u32[]{:S(2)}, u32[]{:S(2)}) collective-permute-start(bf16[24,1024]{1,0:T(8,128)(2,1)S(1)} %get-tuple-element.97), channel_id=1, source_target_pairs={{0,8},{1,9},{2,10},{3,11},{4,12},{5,13},{6,14},{7,15},{8,0},{9,1},... | collective-permute-start | bytes 147464 | tf_op jit(solution)/shard_map/ppermute | solution.py:19
  50.1 10.5 %collective-permute-start.22 = (bf16[48,1792]{1,0:T(8,128)(2,1)S(1)}, bf16[48,1792]{1,0:T(8,128)(2,1)S(1)}, u32[]{:S(2)}, u32[]{:S(2)}) collective-permute-start(bf16[48,1792]{1,0:T(8,128)(2,1)S(1)} %get-tuple-element.103), channel_id=1, source_target_pairs={{0,1},{1,0},{2,3},{3,2},{4,5},{5,4},{6,7},{7,6},{8,9},{9,8},{10,11... | collective-permute-start | bytes 516104 | tf_op jit(solution)/shard_map/ppermute | solution.py:19
  50.2 8.9 %collective-permute-start.18 = (bf16[8,3712]{1,0:T(8,128)(2,1)S(1)}, bf16[8,3712]{1,0:T(8,128)(2,1)S(1)}, u32[]{:S(2)}, u32[]{:S(2)}) collective-permute-start(bf16[8,3712]{1,0:T(8,128)(2,1)S(1)} %get-tuple-element.99), channel_id=1, source_target_pairs={{0,16},{1,17},{2,18},{3,19},{4,20},{5,21},{6,22},{7,23},{8,24},{9,... | collective-permute-start | bytes 178184 | tf_op jit(solution)/shard_map/ppermute | solution.py:19
  51.8 7.3 %collective-permute-start.19 = (bf16[8,3712]{1,0:T(8,128)(2,1)S(1)}, bf16[8,3712]{1,0:T(8,128)(2,1)S(1)}, u32[]{:S(2)}, u32[]{:S(2)}) collective-permute-start(bf16[8,3712]{1,0:T(8,128)(2,1)S(1)} %get-tuple-element.100), channel_id=1, source_target_pairs={{0,24},{1,25},{2,26},{3,27},{4,28},{5,29},{6,30},{7,31},{8,16},{9,... | collective-permute-start | bytes 178184 | tf_op jit(solution)/shard_map/ppermute | solution.py:19
  53.9 5.1 %collective-permute-start.20 = (bf16[8,3712]{1,0:T(8,128)(2,1)S(1)}, bf16[8,3712]{1,0:T(8,128)(2,1)S(1)}, u32[]{:S(2)}, u32[]{:S(2)}) collective-permute-start(bf16[8,3712]{1,0:T(8,128)(2,1)S(1)} %get-tuple-element.101.after_ref), channel_id=1, source_target_pairs={{0,6},{1,7},{2,4},{3,5},{4,2},{5,3},{6,0},{7,1},{8,14},{9,15},{10,... | collective-permute-start | bytes 178184 | tf_op jit(solution)/shard_map/ppermute | solution.py:19
  56.4 4.2 %collective-permute-start.21 = (bf16[8,3712]{1,0:T(8,128)(2,1)S(1)}, bf16[8,3712]{1,0:T(8,128)(2,1)S(1)}, u32[]{:S(2)}, u32[]{:S(2)}) collective-permute-start(bf16[8,3712]{1,0:T(8,128)(2,1)S(1)} %get-tuple-element.102), channel_id=1, source_target_pairs={{0,8},{1,9},{2,10},{3,11},{4,12},{5,13},{6,14},{7,15},{8,0},{9,1},... | collective-permute-start | bytes 178184 | tf_op jit(solution)/shard_map/ppermute | solution.py:19
  56.4 4.2 %copy-start = (s32[8,8]{1,0:T(8,128)S(1)}, s32[8,8]{1,0:T(8,128)}, u32[]{:S(2)}) copy-start(s32[8,8]{1,0:T(8,128)} %ids_ref.1) | copy-start | bytes 772

commit v8 on v7

--- a/solution.py
+++ b/solution.py
@@ -66,13 +66,9 @@
     return copies
 
 
-def message_kernel(experts, width, *refs):
-    sources, out_ref, probs_ref, ids_ref, sems = refs[:4], refs[4], refs[5], refs[6], refs[7]
+def message_kernel(experts, tokens_ref, cot_ref, probs_ref, ids_ref, out_ref):
+    width = tokens_ref.shape[1]
     tail = out_ref.shape[1] - width
-    targets = (out_ref.at[:, :width], out_ref.at[:, tail:], probs_ref, ids_ref)
-    copies = copied(sources, targets, sems)
-    for copy in copies[2:]:
-        copy.wait()
     ids, probs = ids_ref[...], probs_ref[...]
     high = probs.astype(B16).astype(F32)
     low = probs - high
@@ -82,9 +78,9 @@
         one = slice(k, k + 1)
         extra = jnp.where(lane == ids[:, one], high[:, one], extra)
         extra = jnp.where(lane == ids[:, one] + experts, low[:, one], extra)
+    out_ref[:, :width] = tokens_ref[...]
     out_ref[:, width:tail] = extra.astype(B16)
-    for copy in copies[:2]:
-        copy.wait()
+    out_ref[:, tail:] = cot_ref[...]
 
 
 def started(sources, raws, sems, ahead):
@@ -431,17 +427,16 @@
             return [block] + [send(block, mask) for mask in far[0]]
         return [block]
 
-    (message,) = in_vmem(
-        functools.partial(message_kernel, experts, width),
-        [((rows, full + width), B16)],
-        (tokens, cotangent, route_probs, expert_ids),
-        outside=4,
-        scratch=[
-            pltpu.VMEM(route_probs.shape, F32),
-            pltpu.VMEM(expert_ids.shape, jnp.int32),
-            pltpu.SemaphoreType.DMA((4,)),
-        ],
-    )
+    sources = (tokens, cotangent, route_probs, expert_ids)
+    message = pl.pallas_call(
+        functools.partial(message_kernel, experts),
+        grid=(1,),
+        out_shape=pltpu.VMEM((rows, full + width), B16),
+        in_specs=[pl.BlockSpec(source.shape, lambda step: (0, 0)) for source in sources],
+        out_specs=pl.BlockSpec(memory_space=pltpu.VMEM),
+        compiler_params=pltpu.CompilerParams(vmem_limit_bytes=8 * 2**20),
+        cost_estimate=pl.CostEstimate(flops=0, bytes_accessed=4 * rows * (full + width), transcendentals=0),
+    )(*[pltpu.with_memory_space_constraint(source, pltpu.HBM) for source in sources])
     pieces = pieces_of(message)
     crossed = [send(message, mask) for mask in near[2:]]
     matmul = 2 * 2 * half * width * hidden_units

time: 61.7 us -> 61.7 us (level)
    pallas_call x0 -> x1, Pallas kernels: none -> 0.96 us  [body(): pl.pallas_call(functools.partial(message_kernel, experts), grid=(1,), out...]
    pallas_call x13 -> x12, Pallas kernels: 26.4 us -> 25.5 us  [in_vmem(): pl.pallas_call(kernel, out_shape=[(jax.ShapeDtypeStruct if i in results e...]
where the time goes in v8:
time: 61.7 us; the launch traced here: 61.6 us
  starting transfers between devices  27.1 us (44%)
  Pallas kernels  26.5 us (43%)
  waiting for transfers between devices  7.26 us (12%)
  between operations  0.75 us (1%)
    ppermute x23, starting transfers between devices, send(): return lax.ppermute(value, 'expert', pairs)  27.1 us
    pallas_call x12, Pallas kernels, in_vmem(): pl.pallas_call(kernel, out_shape=[(jax.ShapeDtypeStruct if i in results e...  25.5 us
    ppermute x23, waiting for transfers between devices, send(): return lax.ppermute(value, 'expert', pairs)  7.26 us
  transfers between devices with their start and end apart: 23, of which 7 were waited for; matrix products, arithmetic and copies ran while one was open for 0% of the time, Pallas kernels for 34%

profile of v8, /device:TPU:0, one launch (start us, length us, event | category | flops | bytes accessed | tf_op | source)
XLA Modules:
  0.0 61.6 jit_solution(11260057447925408748)
XLA Ops:
  0.6 0.5 collective-permute-start
  1.1 1.0 %shard_map.121.refs_3_ = bf16[8,7296]{1,0:T(8,128)(2,1)S(1)} custom-call(bf16[8,3584]{1,0:T(8,128)(2,1)} %tokens_ref.1, bf16[8,3584]{1,0:T(8,128)(2,1)} %cot_ref.1, f32[8,8]{1,0:T(8,128)} %probs_ref.1, s32[8,8]{1,0:T(8,128)} %ids_ref.3), custom_call_target="tpu_custom_call" | custom-call | bytes 233472 | tf_op jit(solution)/shard_map/pallas_call | solution.py:431
  2.1 4.7 %collective-permute-start.1 = (bf16[8,7296]{1,0:T(8,128)(2,1)S(1)}, bf16[8,7296]{1,0:T(8,128)(2,1)S(1)}, u32[]{:S(2)}, u32[]{:S(2)}) collective-permute-start(bf16[8,7296]{1,0:T(8,128)(2,1)S(1)} %shard_map.121.refs_3_), channel_id=1, source_target_pairs={{0,24},{1,25},{2,26},{3,27},{4,28},{5,29},{6,30},{7,31},{8,16},{9,... | collective-permute-start | bytes 350216 | tf_op jit(solution)/shard_map/ppermute | solution.py:19
  6.8 0.0 collective-permute-start.2
  6.8 0.6 %collective-permute-start.3 = (bf16[8,7296]{1,0:T(8,128)(2,1)S(1)}, bf16[8,7296]{1,0:T(8,128)(2,1)S(1)}, u32[]{:S(2)}, u32[]{:S(2)}) collective-permute-start(bf16[8,7296]{1,0:T(8,128)(2,1)S(1)} %shard_map.121.refs_3_), channel_id=1, source_target_pairs={{0,8},{1,9},{2,10},{3,11},{4,12},{5,13},{6,14},{7,15},{8,0},{9,1},... | collective-permute-start | bytes 350216 | tf_op jit(solution)/shard_map/ppermute | solution.py:19
  7.4 2.6 %collective-permute-start.4 = (bf16[8,7296]{1,0:T(8,128)(2,1)S(1)}, bf16[8,7296]{1,0:T(8,128)(2,1)S(1)}, u32[]{:S(2)}, u32[]{:S(2)}) collective-permute-start(bf16[8,7296]{1,0:T(8,128)(2,1)S(1)} %shard_map.121.refs_3_), channel_id=1, source_target_pairs={{0,6},{1,7},{2,4},{3,5},{4,2},{5,3},{6,0},{7,1},{8,14},{9,15},{10,... | collective-permute-start | bytes 350216 | tf_op jit(solution)/shard_map/ppermute | solution.py:19
  10.0 0.0 collective-permute-done.other_ref
  10.0 5.6 %shard_map.120 = (bf16[3584,512]{1,0:T(8,128)(2,1)S(1)}, bf16[3584,512]{1,0:T(8,128)(2,1)S(1)}, bf16[3584,512]{1,0:T(8,128)(2,1)S(1)}, bf16[3584,512]{1,0:T(8,12...) custom-call(bf16[3584,512]{1,0:T(8,128)(2,1)} %gate_ref.1, bf16[3584,512]{1,0:T(8,128)(2,1)} %up_ref.1, ...), custom_call_target="tpu_custom_call" | custom-call | flops 1409286144 | bytes 7733248 | tf_op jit(solution)/shard_map/pallas_call | solution.py:40
  15.7 0.0 collective-permute-done.1.refs_0_
  15.7 1.6 %collective-permute-done.2.refs_1_ = bf16[8,7296]{1,0:T(8,128)(2,1)S(1)} collective-permute-done((bf16[8,7296]{1,0:T(8,128)(2,1)S(1)}, bf16[8,7296]{1,0:T(8,128)(2,1)S(1)}, u32[]{:S(2)}, u32[]{:S(2)}) %collective-permute-start.2) | collective-permute-done | bytes 116768 | tf_op jit(solution)/shard_map/ppermute | solution.py:19
  17.3 0.0 collective-permute-done.3.refs_2_
  17.3 0.0 collective-permute-done.4.refs_4_
  17.3 1.0 %shard_map.122 = (f32[72,32]{1,0:T(8,128)S(1)}, bf16[24,7296]{1,0:T(8,128)(2,1)S(1)}, bf16[24,7296]{1,0:T(8,128)(2,1)S(1)}, bf16[24,7296]{1,0:T(8,128)(2,1)S(1)}...) custom-call(bf16[3,16,3584]{2,1,0:T(8,128)(2,1)S(1)} %get-tuple-elem, ...), custom_call_target="tpu_custom_call" | custom-call | bytes 927744 | tf_op jit(solution)/shard_map/pallas_call | solution.py:40
  18.3 1.5 %collective-permute-start.5 = (bf16[24,7296]{1,0:T(8,128)(2,1)S(1)}, bf16[24,7296]{1,0:T(8,128)(2,1)S(1)}, u32[]{:S(2)}, u32[]{:S(2)}) collective-permute-start(bf16[24,7296]{1,0:T(8,128)(2,1)S(1)} %get-tuple-element.64), channel_id=1, source_target_pairs={{0,2},{1,3},{2,0},{3,1},{4,6},{5,7},{6,4},{7,5},{8,10},{9,11},{10,... | collective-permute-start | bytes 1050632 | tf_op jit(solution)/shard_map/ppermute | solution.py:19
  19.9 1.5 %collective-permute-start.7 = (bf16[24,7296]{1,0:T(8,128)(2,1)S(1)}, bf16[24,7296]{1,0:T(8,128)(2,1)S(1)}, u32[]{:S(2)}, u32[]{:S(2)}) collective-permute-start(bf16[24,7296]{1,0:T(8,128)(2,1)S(1)} %get-tuple-element.66), channel_id=1, source_target_pairs={{0,4},{1,5},{2,6},{3,7},{4,0},{5,1},{6,2},{7,3},{8,12},{9,13},{10,... | collective-permute-start | bytes 1050632 | tf_op jit(solution)/shard_map/ppermute | solution.py:19
  21.4 0.0 collective-permute-start.6
  21.4 2.5 %collective-permute-start.8 = (bf16[24,1920]{1,0:T(8,128)(2,1)S(1)}, bf16[24,1920]{1,0:T(8,128)(2,1)S(1)}, u32[]{:S(2)}, u32[]{:S(2)}) collective-permute-start(bf16[24,1920]{1,0:T(8,128)(2,1)S(1)} %get-tuple-element.67), channel_id=1, source_target_pairs={{0,24},{1,25},{2,26},{3,27},{4,28},{5,29},{6,30},{7,31},{8,16},{9,... | collective-permute-start | bytes 276488 | tf_op jit(solution)/shard_map/ppermute | solution.py:19
  23.9 0.9 %collective-permute-start.9 = (bf16[24,1920]{1,0:T(8,128)(2,1)S(1)}, bf16[24,1920]{1,0:T(8,128)(2,1)S(1)}, u32[]{:S(2)}, u32[]{:S(2)}) collective-permute-start(bf16[24,1920]{1,0:T(8,128)(2,1)S(1)} %get-tuple-element.68), channel_id=1, source_target_pairs={{0,8},{1,9},{2,10},{3,11},{4,12},{5,13},{6,14},{7,15},{8,0},{9,1},... | collective-permute-start | bytes 276488 | tf_op jit(solution)/shard_map/ppermute | solution.py:19
  24.9 4.2 %shard_map.123 = (bf16[512,3584]{1,0:T(8,128)(2,1)S(1)}, bf16[3584,512]{1,0:T(8,128)(2,1)S(1)}, bf16[512,3584]{1,0:T(8,128)(2,1)S(1)}, bf16[512,3584]{1,0:T(8,128)(2,1)S(1)}) custom-call(bf16[512,3584]{1,0:T(8,128)(2,1)} %down_ref.1, bf16[3,16,512]{2,1,0:T(8,128)(2,1)S(1)} %get-tuple-element.59.narrow_ref, ...), custom_call_target="tpu_custom_call" | custom-call | flops 704643072 | bytes 11412480 | tf_op jit(solution)/shard_map/pallas_call | solution.py:40
  29.1 0.8 %collective-permute-done.6.refs_2_ = bf16[24,1920]{1,0:T(8,128)(2,1)S(1)} collective-permute-done((bf16[24,1920]{1,0:T(8,128)(2,1)S(1)}, bf16[24,1920]{1,0:T(8,128)(2,1)S(1)}, u32[]{:S(2)}, u32[]{:S(2)}) %collective-permute-start.6) | collective-permute-done | bytes 92192 | tf_op jit(solution)/shard_map/ppermute | solution.py:19
  29.9 0.0 collective-permute-done.8.refs_4_
  29.9 0.9 %collective-permute-done.9.refs_5_ = bf16[24,1920]{1,0:T(8,128)(2,1)S(1)} collective-permute-done((bf16[24,1920]{1,0:T(8,128)(2,1)S(1)}, bf16[24,1920]{1,0:T(8,128)(2,1)S(1)}, u32[]{:S(2)}, u32[]{:S(2)}) %collective-permute-start.9) | collective-permute-done | bytes 92192 | tf_op jit(solution)/shard_map/ppermute | solution.py:19
  30.8 0.0 collective-permute-done.5.refs_1_
  30.8 0.0 collective-permute-done.7.refs_3_
  30.8 0.3 shard_map.124
  31.1 0.1 collective-permute-start.10
  31.2 0.5 collective-permute-start.11
  31.7 1.7 %collective-permute-done.10.refs_1_ = bf16[96,3712]{1,0:T(8,128)(2,1)S(1)} collective-permute-done((bf16[96,3712]{1,0:T(8,128)(2,1)S(1)}, bf16[96,3712]{1,0:T(8,128)(2,1)S(1)}, u32[]{:S(2)}, u32[]{:S(2)}) %collective-permute-start.10) | collective-permute-done | bytes 712736 | tf_op jit(solution)/shard_map/ppermute | solution.py:19
  33.4 1.6 %shard_map.125 = (bf16[192,3584]{1,0:T(8,128)(2,1)S(1)}, f32[192,128]{1,0:T(8,128)S(1)}, f32[192,512]{1,0:T(8,128)S(1)}, f32[192,512]{1,0:T(8,128)S(1)}) custom-call(bf16[3584,512]{1,0:T(8,128)(2,1)S(1)} %get-tuple-element.57.gate_ref, bf16[3584,512]{1,0:T(8,128)(2,1)S(1)} %get-tuple-element.58.up_ref, bf16[96,3712]{1,0:T(8,128)(2,1)S(1)} %get-tuple-element.70.refs_0_, ...), custom_call_target="tpu_custom_call" | custom-call | flops 1409286144 | bytes 8765440 | tf_op jit(solution)/shard_map/pallas_call | solution.py:40
  35.0 0.0 collective-permute-done.11.refs_1_
  35.0 2.6 %shard_map.126 = (bf16[192,3584]{1,0:T(8,128)(2,1)S(1)}, bf16[192,512]{1,0:T(8,128)(2,1)S(1)}, bf16[192,512]{1,0:T(8,128)(2,1)S(1)}, bf16[192,512]{1,0:T(8,128)(...) custom-call(bf16[512,3584]{1,0:T(8,128)(2,1)S(1)} %get-tuple-element.72.gate_ref, ...), custom_call_target="tpu_custom_call" | custom-call | flops 2113929216 | bytes 13271040 | tf_op jit(solution)/shard_map/pallas_call | solution.py:40
  37.7 0.2 collective-permute-start.12
  37.9 2.0 %shard_map.127 = (bf16[3584,512]{1,0:T(8,128)(2,1)S(1)}, f32[16,3584]{1,0:T(8,128)S(1)}) custom-call(bf16[192,3584]{1,0:T(8,128)(2,1)S(1)} %get-tuple-element.71.x_ref, bf16[192,512]{1,0:T(8,128)(2,1)S(1)} %get-tuple-element.85.grad_ref, bf16[3584,512]{1,0:T(8,128)(2,1)S(1)} %get-tuple-element.86.raw_ref, bf16[3,16,512]{2,1,0:T(8,128)(2,1)S(1)} %get-tuple-element.59.narrow_ref), custom_call_target="tpu_custom_call" | custom-call | flops 1409286144 | bytes 5292032 | tf_op jit(solution)/shard_map/pallas_call | solution.py:40
  39.9 0.0 collective-permute-done.12.other_ref
  39.9 0.6 shard_map.128
  40.5 0.6 %collective-permute-start.13 = (bf16[24,3712]{1,0:T(8,128)(2,1)S(1)}, bf16[24,3712]{1,0:T(8,128)(2,1)S(1)}, u32[]{:S(2)}, u32[]{:S(2)}) collective-permute-start(bf16[24,3712]{1,0:T(8,128)(2,1)S(1)} %get-tuple-element.93), channel_id=1, source_target_pairs={{0,2},{1,3},{2,0},{3,1},{4,6},{5,7},{6,4},{7,5},{8,10},{9,11},{10,... | collective-permute-start | bytes 534536 | tf_op jit(solution)/shard_map/ppermute | solution.py:19
  41.1 0.5 collective-permute-start.15
  41.6 1.7 %collective-permute-start.14 = (bf16[24,1024]{1,0:T(8,128)(2,1)S(1)}, bf16[24,1024]{1,0:T(8,128)(2,1)S(1)}, u32[]{:S(2)}, u32[]{:S(2)}) collective-permute-start(bf16[24,1024]{1,0:T(8,128)(2,1)S(1)} %get-tuple-element.94), channel_id=1, source_target_pairs={{0,16},{1,17},{2,18},{3,19},{4,20},{5,21},{6,22},{7,23},{8,24},{9,... | collective-permute-start | bytes 147464 | tf_op jit(solution)/shard_map/ppermute | solution.py:19
  43.3 2.2 %collective-permute-start.16 = (bf16[24,1024]{1,0:T(8,128)(2,1)S(1)}, bf16[24,1024]{1,0:T(8,128)(2,1)S(1)}, u32[]{:S(2)}, u32[]{:S(2)}) collective-permute-start(bf16[24,1024]{1,0:T(8,128)(2,1)S(1)} %get-tuple-element.96), channel_id=1, source_target_pairs={{0,24},{1,25},{2,26},{3,27},{4,28},{5,29},{6,30},{7,31},{8,16},{9,... | collective-permute-start | bytes 147464 | tf_op jit(solution)/shard_map/ppermute | solution.py:19
  45.5 0.0 collective-permute-start.17
  45.5 3.6 %shard_map.129 = (bf16[3584,512]{1,0:T(8,128)(2,1)S(1)}, bf16[512,3584]{1,0:T(8,128)(2,1)S(1)}, f32[48,1792]{1,0:T(8,128)S(1)}, bf16[48,1792]{1,0:T(8,128)(2,1)S(1)}) custom-call(bf16[192,3584]{1,0:T(8,128)(2,1)S(1)} %get-tuple-element.71.x_ref, bf16[192,512]{1,0:T(8,128)(2,1)S(1)} %get-tuple-element.78.grad_ref, ...), custom_call_target="tpu_custom_call" | custom-call | flops 2818572288 | bytes 10942464 | tf_op jit(solution)/shard_map/pallas_call | solution.py:40
  49.1 0.0 collective-permute-done.14.refs_4_
  49.1 0.2 collective-permute-done.16.refs_6_
  49.4 0.5 collective-permute-done.17.refs_7_
  49.9 0.0 collective-permute-done.13.refs_3_
  49.9 0.0 collective-permute-done.15.refs_5_
  49.9 0.3 shard_map.130
  50.2 0.1 collective-permute-start.22
  50.2 1.6 %collective-permute-start.18 = (bf16[8,3712]{1,0:T(8,128)(2,1)S(1)}, bf16[8,3712]{1,0:T(8,128)(2,1)S(1)}, u32[]{:S(2)}, u32[]{:S(2)}) collective-permute-start(bf16[8,3712]{1,0:T(8,128)(2,1)S(1)} %get-tuple-element.99), channel_id=1, source_target_pairs={{0,16},{1,17},{2,18},{3,19},{4,20},{5,21},{6,22},{7,23},{8,24},{9,... | collective-permute-start | bytes 178184 | tf_op jit(solution)/shard_map/ppermute | solution.py:19
  51.8 2.2 %collective-permute-start.19 = (bf16[8,3712]{1,0:T(8,128)(2,1)S(1)}, bf16[8,3712]{1,0:T(8,128)(2,1)S(1)}, u32[]{:S(2)}, u32[]{:S(2)}) collective-permute-start(bf16[8,3712]{1,0:T(8,128)(2,1)S(1)} %get-tuple-element.100), channel_id=1, source_target_pairs={{0,24},{1,25},{2,26},{3,27},{4,28},{5,29},{6,30},{7,31},{8,16},{9,... | collective-permute-start | bytes 178184 | tf_op jit(solution)/shard_map/ppermute | solution.py:19
  54.0 2.4 %collective-permute-start.20 = (bf16[8,3712]{1,0:T(8,128)(2,1)S(1)}, bf16[8,3712]{1,0:T(8,128)(2,1)S(1)}, u32[]{:S(2)}, u32[]{:S(2)}) collective-permute-start(bf16[8,3712]{1,0:T(8,128)(2,1)S(1)} %get-tuple-element.101.after_ref), channel_id=1, source_target_pairs={{0,6},{1,7},{2,4},{3,5},{4,2},{5,3},{6,0},{7,1},{8,14},{9,15},{10,... | collective-permute-start | bytes 178184 | tf_op jit(solution)/shard_map/ppermute | solution.py:19
  56.4 0.0 collective-permute-start.21
  56.4 0.0 copy-start
  56.4 2.6 %shard_map.132 = f32[48,512]{1,0:T(8,128)} custom-call(bf16[3584,512]{1,0:T(8,128)(2,1)S(1)} %get-tuple-element.106.masked_gate, bf16[3584,512]{1,0:T(8,128)(2,1)S(1)} %get-tuple-element.107.masked_up, bf16[512,3584]{1,0:T(8,128)(2,1)S(1)} %get-tuple-element.108.masked_down, bf16[3,16,3584]{2,1,0:T(8,128)(2,1)S(1)} %get-tuple-element.60.after_ref.wide_ref, ...), custom_call_target="tpu_custom_call" | custom-call | flops 1409286144 | bytes 11413504 | tf_op jit(solution)/shard_map/pallas_call | solution.py:40
  59.1 0.0 collective-permute-done.18.refs_0_
  59.1 0.0 collective-permute-done.19.refs_1_
  59.1 0.0 collective-permute-done.20.refs_2_
  59.1 1.5 %collective-permute-done.21.refs_3_ = bf16[8,3712]{1,0:T(8,128)(2,1)S(1)} collective-permute-done((bf16[8,3712]{1,0:T(8,128)(2,1)S(1)}, bf16[8,3712]{1,0:T(8,128)(2,1)S(1)}, u32[]{:S(2)}, u32[]{:S(2)}) %collective-permute-start.21) | collective-permute-done | bytes 59424 | tf_op jit(solution)/shard_map/ppermute | solution.py:19
  60.6 0.0 collective-permute-done.22.refs_4_
  60.6 0.0 copy-done
  60.6 0.9 %shard_map.131 = (bf16[8,3584]{1,0:T(8,128)(2,1)}, f32[8,8]{1,0:T(8,128)}, f32[48,1792]{1,0:T(8,128)}) custom-call(s32[8,8]{1,0:T(8,128)S(1)} %copy-done, f32[48,1792]{1,0:T(8,128)S(1)} %get-tuple-element.89.keep_ref, f32[8,3712]{1,0:T(8,128)S(1)} %get-tuple-element.98.own_ref, bf16[8,3712]{1,0:T(8,128)(2,1)S(1)} %collective-permute-done.18.refs_0_, ...), custom_call_target="tpu_custom_call" | custom-call | bytes 872704 | tf_op jit(solution)/shard_map/pallas_call | solution.py:40
Async XLA Ops:
  0.6 9.4 %collective-permute-start = (bf16[3,16,1792]{2,1,0:T(8,128)(2,1)}, bf16[3,16,1792]{2,1,0:T(8,128)(2,1)S(1)}, u32[]{:S(2)}, u32[]{:S(2)}) collective-permute-start(bf16[3,16,1792]{2,1,0:T(8,128)(2,1)} %mine_hbm.1), channel_id=1, source_target_pairs={{0,1},{1,0},{2,3},{3,2},{4,5},{5,4},{6,7},{7,6},{8,9},{9,8},{10,11... | collective-permute-start | bytes 516104 | tf_op jit(solution)/shard_map/ppermute | solution.py:19
  2.1 13.6 %collective-permute-start.1 = (bf16[8,7296]{1,0:T(8,128)(2,1)S(1)}, bf16[8,7296]{1,0:T(8,128)(2,1)S(1)}, u32[]{:S(2)}, u32[]{:S(2)}) collective-permute-start(bf16[8,7296]{1,0:T(8,128)(2,1)S(1)} %shard_map.121.refs_3_), channel_id=1, source_target_pairs={{0,24},{1,25},{2,26},{3,27},{4,28},{5,29},{6,30},{7,31},{8,16},{9,... | collective-permute-start | bytes 350216 | tf_op jit(solution)/shard_map/ppermute | solution.py:19
  6.8 10.5 %collective-permute-start.2 = (bf16[8,7296]{1,0:T(8,128)(2,1)S(1)}, bf16[8,7296]{1,0:T(8,128)(2,1)S(1)}, u32[]{:S(2)}, u32[]{:S(2)}) collective-permute-start(bf16[8,7296]{1,0:T(8,128)(2,1)S(1)} %shard_map.121.refs_3_), channel_id=1, source_target_pairs={{0,16},{1,17},{2,18},{3,19},{4,20},{5,21},{6,22},{7,23},{8,24},{9,... | collective-permute-start | bytes 350216 | tf_op jit(solution)/shard_map/ppermute | solution.py:19
  6.8 10.5 %collective-permute-start.3 = (bf16[8,7296]{1,0:T(8,128)(2,1)S(1)}, bf16[8,7296]{1,0:T(8,128)(2,1)S(1)}, u32[]{:S(2)}, u32[]{:S(2)}) collective-permute-start(bf16[8,7296]{1,0:T(8,128)(2,1)S(1)} %shard_map.121.refs_3_), channel_id=1, source_target_pairs={{0,8},{1,9},{2,10},{3,11},{4,12},{5,13},{6,14},{7,15},{8,0},{9,1},... | collective-permute-start | bytes 350216 | tf_op jit(solution)/shard_map/ppermute | solution.py:19
  7.4 9.9 %collective-permute-start.4 = (bf16[8,7296]{1,0:T(8,128)(2,1)S(1)}, bf16[8,7296]{1,0:T(8,128)(2,1)S(1)}, u32[]{:S(2)}, u32[]{:S(2)}) collective-permute-start(bf16[8,7296]{1,0:T(8,128)(2,1)S(1)} %shard_map.121.refs_3_), channel_id=1, source_target_pairs={{0,6},{1,7},{2,4},{3,5},{4,2},{5,3},{6,0},{7,1},{8,14},{9,15},{10,... | collective-permute-start | bytes 350216 | tf_op jit(solution)/shard_map/ppermute | solution.py:19
  18.3 12.5 %collective-permute-start.5 = (bf16[24,7296]{1,0:T(8,128)(2,1)S(1)}, bf16[24,7296]{1,0:T(8,128)(2,1)S(1)}, u32[]{:S(2)}, u32[]{:S(2)}) collective-permute-start(bf16[24,7296]{1,0:T(8,128)(2,1)S(1)} %get-tuple-element.64), channel_id=1, source_target_pairs={{0,2},{1,3},{2,0},{3,1},{4,6},{5,7},{6,4},{7,5},{8,10},{9,11},{10,... | collective-permute-start | bytes 1050632 | tf_op jit(solution)/shard_map/ppermute | solution.py:19
  19.9 10.9 %collective-permute-start.7 = (bf16[24,7296]{1,0:T(8,128)(2,1)S(1)}, bf16[24,7296]{1,0:T(8,128)(2,1)S(1)}, u32[]{:S(2)}, u32[]{:S(2)}) collective-permute-start(bf16[24,7296]{1,0:T(8,128)(2,1)S(1)} %get-tuple-element.66), channel_id=1, source_target_pairs={{0,4},{1,5},{2,6},{3,7},{4,0},{5,1},{6,2},{7,3},{8,12},{9,13},{10,... | collective-permute-start | bytes 1050632 | tf_op jit(solution)/shard_map/ppermute | solution.py:19
  21.4 8.5 %collective-permute-start.6 = (bf16[24,1920]{1,0:T(8,128)(2,1)S(1)}, bf16[24,1920]{1,0:T(8,128)(2,1)S(1)}, u32[]{:S(2)}, u32[]{:S(2)}) collective-permute-start(bf16[24,1920]{1,0:T(8,128)(2,1)S(1)} %get-tuple-element.65), channel_id=1, source_target_pairs={{0,16},{1,17},{2,18},{3,19},{4,20},{5,21},{6,22},{7,23},{8,24},{9,... | collective-permute-start | bytes 276488 | tf_op jit(solution)/shard_map/ppermute | solution.py:19
  21.4 8.5 %collective-permute-start.8 = (bf16[24,1920]{1,0:T(8,128)(2,1)S(1)}, bf16[24,1920]{1,0:T(8,128)(2,1)S(1)}, u32[]{:S(2)}, u32[]{:S(2)}) collective-permute-start(bf16[24,1920]{1,0:T(8,128)(2,1)S(1)} %get-tuple-element.67), channel_id=1, source_target_pairs={{0,24},{1,25},{2,26},{3,27},{4,28},{5,29},{6,30},{7,31},{8,16},{9,... | collective-permute-start | bytes 276488 | tf_op jit(solution)/shard_map/ppermute | solution.py:19
  23.9 6.9 %collective-permute-start.9 = (bf16[24,1920]{1,0:T(8,128)(2,1)S(1)}, bf16[24,1920]{1,0:T(8,128)(2,1)S(1)}, u32[]{:S(2)}, u32[]{:S(2)}) collective-permute-start(bf16[24,1920]{1,0:T(8,128)(2,1)S(1)} %get-tuple-element.68), channel_id=1, source_target_pairs={{0,8},{1,9},{2,10},{3,11},{4,12},{5,13},{6,14},{7,15},{8,0},{9,1},... | collective-permute-start | bytes 276488 | tf_op jit(solution)/shard_map/ppermute | solution.py:19
  31.1 2.2 %collective-permute-start.10 = (bf16[96,3712]{1,0:T(8,128)(2,1)S(1)}, bf16[96,3712]{1,0:T(8,128)(2,1)S(1)}, u32[]{:S(2)}, u32[]{:S(2)}) collective-permute-start(bf16[96,3712]{1,0:T(8,128)(2,1)S(1)} %get-tuple-element.70.refs_0_), channel_id=1, source_target_pairs={{0,1},{1,0},{2,3},{3,2},{4,5},{5,4},{6,7},{7,6},{8,9},{9,8},{10,11... | collective-permute-start | bytes 2138120 | tf_op jit(solution)/shard_map/ppermute | solution.py:19
  31.2 3.8 %collective-permute-start.11 = (bf16[96,3584]{1,0:T(8,128)(2,1)S(1)}, bf16[96,3584]{1,0:T(8,128)(2,1)S(1)}, u32[]{:S(2)}, u32[]{:S(2)}) collective-permute-start(bf16[96,3584]{1,0:T(8,128)(2,1)S(1)} %get-tuple-element.77.refs_0_), channel_id=1, source_target_pairs={{0,1},{1,0},{2,3},{3,2},{4,5},{5,4},{6,7},{7,6},{8,9},{9,8},{10,11... | collective-permute-start | bytes 2064392 | tf_op jit(solution)/shard_map/ppermute | solution.py:19
  37.7 2.2 %collective-permute-start.12 = (bf16[96,3712]{1,0:T(8,128)(2,1)S(1)}, bf16[96,3712]{1,0:T(8,128)(2,1)S(1)}, u32[]{:S(2)}, u32[]{:S(2)}) collective-permute-start(bf16[96,3712]{1,0:T(8,128)(2,1)S(1)} %get-tuple-element.84), channel_id=1, source_target_pairs={{0,1},{1,0},{2,3},{3,2},{4,5},{5,4},{6,7},{7,6},{8,9},{9,8},{10,11... | collective-permute-start | bytes 2138120 | tf_op jit(solution)/shard_map/ppermute | solution.py:19
  40.5 9.4 %collective-permute-start.13 = (bf16[24,3712]{1,0:T(8,128)(2,1)S(1)}, bf16[24,3712]{1,0:T(8,128)(2,1)S(1)}, u32[]{:S(2)}, u32[]{:S(2)}) collective-permute-start(bf16[24,3712]{1,0:T(8,128)(2,1)S(1)} %get-tuple-element.93), channel_id=1, source_target_pairs={{0,2},{1,3},{2,0},{3,1},{4,6},{5,7},{6,4},{7,5},{8,10},{9,11},{10,... | collective-permute-start | bytes 534536 | tf_op jit(solution)/shard_map/ppermute | solution.py:19
  41.1 8.8 %collective-permute-start.15 = (bf16[24,3712]{1,0:T(8,128)(2,1)S(1)}, bf16[24,3712]{1,0:T(8,128)(2,1)S(1)}, u32[]{:S(2)}, u32[]{:S(2)}) collective-permute-start(bf16[24,3712]{1,0:T(8,128)(2,1)S(1)} %get-tuple-element.95), channel_id=1, source_target_pairs={{0,4},{1,5},{2,6},{3,7},{4,0},{5,1},{6,2},{7,3},{8,12},{9,13},{10,... | collective-permute-start | bytes 534536 | tf_op jit(solution)/shard_map/ppermute | solution.py:19
  41.6 7.5 %collective-permute-start.14 = (bf16[24,1024]{1,0:T(8,128)(2,1)S(1)}, bf16[24,1024]{1,0:T(8,128)(2,1)S(1)}, u32[]{:S(2)}, u32[]{:S(2)}) collective-permute-start(bf16[24,1024]{1,0:T(8,128)(2,1)S(1)} %get-tuple-element.94), channel_id=1, source_target_pairs={{0,16},{1,17},{2,18},{3,19},{4,20},{5,21},{6,22},{7,23},{8,24},{9,... | collective-permute-start | bytes 147464 | tf_op jit(solution)/shard_map/ppermute | solution.py:19
  43.3 6.0 %collective-permute-start.16 = (bf16[24,1024]{1,0:T(8,128)(2,1)S(1)}, bf16[24,1024]{1,0:T(8,128)(2,1)S(1)}, u32[]{:S(2)}, u32[]{:S(2)}) collective-permute-start(bf16[24,1024]{1,0:T(8,128)(2,1)S(1)} %get-tuple-element.96), channel_id=1, source_target_pairs={{0,24},{1,25},{2,26},{3,27},{4,28},{5,29},{6,30},{7,31},{8,16},{9,... | collective-permute-start | bytes 147464 | tf_op jit(solution)/shard_map/ppermute | solution.py:19
  45.5 4.3 %collective-permute-start.17 = (bf16[24,1024]{1,0:T(8,128)(2,1)S(1)}, bf16[24,1024]{1,0:T(8,128)(2,1)S(1)}, u32[]{:S(2)}, u32[]{:S(2)}) collective-permute-start(bf16[24,1024]{1,0:T(8,128)(2,1)S(1)} %get-tuple-element.97), channel_id=1, source_target_pairs={{0,8},{1,9},{2,10},{3,11},{4,12},{5,13},{6,14},{7,15},{8,0},{9,1},... | collective-permute-start | bytes 147464 | tf_op jit(solution)/shard_map/ppermute | solution.py:19
  50.2 10.5 %collective-permute-start.22 = (bf16[48,1792]{1,0:T(8,128)(2,1)S(1)}, bf16[48,1792]{1,0:T(8,128)(2,1)S(1)}, u32[]{:S(2)}, u32[]{:S(2)}) collective-permute-start(bf16[48,1792]{1,0:T(8,128)(2,1)S(1)} %get-tuple-element.103), channel_id=1, source_target_pairs={{0,1},{1,0},{2,3},{3,2},{4,5},{5,4},{6,7},{7,6},{8,9},{9,8},{10,11... | collective-permute-start | bytes 516104 | tf_op jit(solution)/shard_map/ppermute | solution.py:19
  50.2 8.9 %collective-permute-start.18 = (bf16[8,3712]{1,0:T(8,128)(2,1)S(1)}, bf16[8,3712]{1,0:T(8,128)(2,1)S(1)}, u32[]{:S(2)}, u32[]{:S(2)}) collective-permute-start(bf16[8,3712]{1,0:T(8,128)(2,1)S(1)} %get-tuple-element.99), channel_id=1, source_target_pairs={{0,16},{1,17},{2,18},{3,19},{4,20},{5,21},{6,22},{7,23},{8,24},{9,... | collective-permute-start | bytes 178184 | tf_op jit(solution)/shard_map/ppermute | solution.py:19
  51.8 7.3 %collective-permute-start.19 = (bf16[8,3712]{1,0:T(8,128)(2,1)S(1)}, bf16[8,3712]{1,0:T(8,128)(2,1)S(1)}, u32[]{:S(2)}, u32[]{:S(2)}) collective-permute-start(bf16[8,3712]{1,0:T(8,128)(2,1)S(1)} %get-tuple-element.100), channel_id=1, source_target_pairs={{0,24},{1,25},{2,26},{3,27},{4,28},{5,29},{6,30},{7,31},{8,16},{9,... | collective-permute-start | bytes 178184 | tf_op jit(solution)/shard_map/ppermute | solution.py:19
  54.0 5.1 %collective-permute-start.20 = (bf16[8,3712]{1,0:T(8,128)(2,1)S(1)}, bf16[8,3712]{1,0:T(8,128)(2,1)S(1)}, u32[]{:S(2)}, u32[]{:S(2)}) collective-permute-start(bf16[8,3712]{1,0:T(8,128)(2,1)S(1)} %get-tuple-element.101.after_ref), channel_id=1, source_target_pairs={{0,6},{1,7},{2,4},{3,5},{4,2},{5,3},{6,0},{7,1},{8,14},{9,15},{10,... | collective-permute-start | bytes 178184 | tf_op jit(solution)/shard_map/ppermute | solution.py:19
  56.4 4.2 %collective-permute-start.21 = (bf16[8,3712]{1,0:T(8,128)(2,1)S(1)}, bf16[8,3712]{1,0:T(8,128)(2,1)S(1)}, u32[]{:S(2)}, u32[]{:S(2)}) collective-permute-start(bf16[8,3712]{1,0:T(8,128)(2,1)S(1)} %get-tuple-element.102), channel_id=1, source_target_pairs={{0,8},{1,9},{2,10},{3,11},{4,12},{5,13},{6,14},{7,15},{8,0},{9,1},... | collective-permute-start | bytes 178184 | tf_op jit(solution)/shard_map/ppermute | solution.py:19
  56.4 4.2 %copy-start = (s32[8,8]{1,0:T(8,128)S(1)}, s32[8,8]{1,0:T(8,128)}, u32[]{:S(2)}) copy-start(s32[8,8]{1,0:T(8,128)} %ids_ref.3) | copy-start | bytes 772

commit v9 on v8

--- a/solution.py
+++ b/solution.py
@@ -328,10 +328,12 @@
         out[...] = total[(i + 1) * count : (i + 2) * count].astype(B16)
 
 
-def up_grads_kernel(x_ref, grad_ref, raw_ref, narrow_ref, masked_out, wide_out):
+def up_grads_kernel(x_ref, grad_ref, raw_ref, narrow_ref, masked_out, wide_out, turned_out):
     width = x_ref.shape[1]
     for part in chunks_of(width, width // 2):
-        masked = dot32(x_ref[:, part], grad_ref[...], TN) * raw_ref[part, :].astype(F32)
+        turned = x_ref[:, part].T
+        turned_out[part, :] = turned
+        masked = dot32(turned, grad_ref[...]) * raw_ref[part, :].astype(F32)
         masked = masked.astype(B16)
         masked_out[part, :] = masked
         wide_out[:, part] = dot32(narrow_ref[1], masked, NT)
@@ -342,10 +344,10 @@
     masked_gate, masked_down, keep_out, give_out, wide_all,
 ):
     del after_ref
-    width, rank = x_ref.shape[1], narrow_ref.shape[1]
+    width, rank = x_ref.shape[0], narrow_ref.shape[1]
     wide_all[pl.ds(rank, rank), :] = up_wide_ref[...]
     for part in chunks_of(width, width // 2):
-        masked = dot32(x_ref[:, part], grad_ref[...], TN) * gate_ref[part, :].astype(F32)
+        masked = dot32(x_ref[part, :], grad_ref[...]) * gate_ref[part, :].astype(F32)
         masked = masked.astype(B16)
         masked_gate[part, :] = masked
         wide_all[pl.ds(0, rank), part] = dot32(narrow_ref[0], masked, NT)
@@ -502,9 +504,9 @@
         3 * matmul,
     )
     other = send(give, 1)
-    masked_up, up_wide = in_vmem(
+    masked_up, up_wide, turned = in_vmem(
         up_grads_kernel,
-        [(up_weight.shape, B16), ((rank, width), F32)],
+        [(up_weight.shape, B16), ((rank, width), F32), ((width, 2 * half), B16)],
         (x, grad_up, up_raw, narrow),
         2 * matmul,
     )
@@ -520,7 +522,7 @@
         other_grads_kernel,
         [(gate_weight.shape, B16), (down_weight.shape, B16)]
         + [((3 * rank, width // 2), F32), ((3 * rank, width // 2), B16)],
-        (x, grad_gate, gate_raw, y, hidden, down_raw, narrow, sums[0], up_wide),
+        (turned, grad_gate, gate_raw, y, hidden, down_raw, narrow, sums[0], up_wide),
         4 * matmul,
         scratch=[pltpu.VMEM((3 * rank, width), F32)],
     )

time: 61.7 us -> 61.7 us (level)
  no operation moved by 1% of the time
where the time goes in v9:
time: 61.7 us; the launch traced here: 61.5 us
  starting transfers between devices  27 us (44%)
  Pallas kernels  26.4 us (43%)
  waiting for transfers between devices  7.28 us (12%)
  between operations  0.75 us (1%)
    ppermute x23, starting transfers between devices, send(): return lax.ppermute(value, 'expert', pairs)  27 us
    pallas_call x12, Pallas kernels, in_vmem(): pl.pallas_call(kernel, out_shape=[(jax.ShapeDtypeStruct if i in results e...  25.4 us
    ppermute x23, waiting for transfers between devices, send(): return lax.ppermute(value, 'expert', pairs)  7.28 us
  transfers between devices with their start and end apart: 23, of which 7 were waited for; matrix products, arithmetic and copies ran while one was open for 0% of the time, Pallas kernels for 34%

profile of v9, /device:TPU:0, one launch (start us, length us, event | category | flops | bytes accessed | tf_op | source)
XLA Modules:
  0.0 61.5 jit_solution(12412428511462340123)
XLA Ops:
  0.6 0.5 collective-permute-start
  1.1 1.0 %shard_map.121.refs_3_ = bf16[8,7296]{1,0:T(8,128)(2,1)S(1)} custom-call(bf16[8,3584]{1,0:T(8,128)(2,1)} %tokens_ref.1, bf16[8,3584]{1,0:T(8,128)(2,1)} %cot_ref.1, f32[8,8]{1,0:T(8,128)} %probs_ref.1, s32[8,8]{1,0:T(8,128)} %ids_ref.3), custom_call_target="tpu_custom_call" | custom-call | bytes 233472 | tf_op jit(solution)/shard_map/pallas_call | solution.py:433
  2.1 4.7 %collective-permute-start.1 = (bf16[8,7296]{1,0:T(8,128)(2,1)S(1)}, bf16[8,7296]{1,0:T(8,128)(2,1)S(1)}, u32[]{:S(2)}, u32[]{:S(2)}) collective-permute-start(bf16[8,7296]{1,0:T(8,128)(2,1)S(1)} %shard_map.121.refs_3_), channel_id=1, source_target_pairs={{0,24},{1,25},{2,26},{3,27},{4,28},{5,29},{6,30},{7,31},{8,16},{9,... | collective-permute-start | bytes 350216 | tf_op jit(solution)/shard_map/ppermute | solution.py:19
  6.8 0.0 collective-permute-start.2
  6.8 0.6 %collective-permute-start.3 = (bf16[8,7296]{1,0:T(8,128)(2,1)S(1)}, bf16[8,7296]{1,0:T(8,128)(2,1)S(1)}, u32[]{:S(2)}, u32[]{:S(2)}) collective-permute-start(bf16[8,7296]{1,0:T(8,128)(2,1)S(1)} %shard_map.121.refs_3_), channel_id=1, source_target_pairs={{0,8},{1,9},{2,10},{3,11},{4,12},{5,13},{6,14},{7,15},{8,0},{9,1},... | collective-permute-start | bytes 350216 | tf_op jit(solution)/shard_map/ppermute | solution.py:19
  7.4 2.6 %collective-permute-start.4 = (bf16[8,7296]{1,0:T(8,128)(2,1)S(1)}, bf16[8,7296]{1,0:T(8,128)(2,1)S(1)}, u32[]{:S(2)}, u32[]{:S(2)}) collective-permute-start(bf16[8,7296]{1,0:T(8,128)(2,1)S(1)} %shard_map.121.refs_3_), channel_id=1, source_target_pairs={{0,6},{1,7},{2,4},{3,5},{4,2},{5,3},{6,0},{7,1},{8,14},{9,15},{10,... | collective-permute-start | bytes 350216 | tf_op jit(solution)/shard_map/ppermute | solution.py:19
  10.0 0.0 collective-permute-done.other_ref
  10.0 5.6 %shard_map.120 = (bf16[3584,512]{1,0:T(8,128)(2,1)S(1)}, bf16[3584,512]{1,0:T(8,128)(2,1)S(1)}, bf16[3584,512]{1,0:T(8,128)(2,1)S(1)}, bf16[3584,512]{1,0:T(8,12...) custom-call(bf16[3584,512]{1,0:T(8,128)(2,1)} %gate_ref.1, bf16[3584,512]{1,0:T(8,128)(2,1)} %up_ref.1, ...), custom_call_target="tpu_custom_call" | custom-call | flops 1409286144 | bytes 7733248 | tf_op jit(solution)/shard_map/pallas_call | solution.py:40
  15.7 0.0 collective-permute-done.1.refs_0_
  15.7 1.6 %collective-permute-done.2.refs_1_ = bf16[8,7296]{1,0:T(8,128)(2,1)S(1)} collective-permute-done((bf16[8,7296]{1,0:T(8,128)(2,1)S(1)}, bf16[8,7296]{1,0:T(8,128)(2,1)S(1)}, u32[]{:S(2)}, u32[]{:S(2)}) %collective-permute-start.2) | collective-permute-done | bytes 116768 | tf_op jit(solution)/shard_map/ppermute | solution.py:19
  17.3 0.0 collective-permute-done.3.refs_2_
  17.3 0.0 collective-permute-done.4.refs_4_
  17.3 1.0 %shard_map.122 = (f32[72,32]{1,0:T(8,128)S(1)}, bf16[24,7296]{1,0:T(8,128)(2,1)S(1)}, bf16[24,7296]{1,0:T(8,128)(2,1)S(1)}, bf16[24,7296]{1,0:T(8,128)(2,1)S(1)}...) custom-call(bf16[3,16,3584]{2,1,0:T(8,128)(2,1)S(1)} %get-tuple-elem, ...), custom_call_target="tpu_custom_call" | custom-call | bytes 927744 | tf_op jit(solution)/shard_map/pallas_call | solution.py:40
  18.3 1.5 %collective-permute-start.5 = (bf16[24,7296]{1,0:T(8,128)(2,1)S(1)}, bf16[24,7296]{1,0:T(8,128)(2,1)S(1)}, u32[]{:S(2)}, u32[]{:S(2)}) collective-permute-start(bf16[24,7296]{1,0:T(8,128)(2,1)S(1)} %get-tuple-element.65), channel_id=1, source_target_pairs={{0,2},{1,3},{2,0},{3,1},{4,6},{5,7},{6,4},{7,5},{8,10},{9,11},{10,... | collective-permute-start | bytes 1050632 | tf_op jit(solution)/shard_map/ppermute | solution.py:19
  19.9 1.5 %collective-permute-start.7 = (bf16[24,7296]{1,0:T(8,128)(2,1)S(1)}, bf16[24,7296]{1,0:T(8,128)(2,1)S(1)}, u32[]{:S(2)}, u32[]{:S(2)}) collective-permute-start(bf16[24,7296]{1,0:T(8,128)(2,1)S(1)} %get-tuple-element.67), channel_id=1, source_target_pairs={{0,4},{1,5},{2,6},{3,7},{4,0},{5,1},{6,2},{7,3},{8,12},{9,13},{10,... | collective-permute-start | bytes 1050632 | tf_op jit(solution)/shard_map/ppermute | solution.py:19
  21.4 0.0 collective-permute-start.6
  21.4 2.5 %collective-permute-start.8 = (bf16[24,1920]{1,0:T(8,128)(2,1)S(1)}, bf16[24,1920]{1,0:T(8,128)(2,1)S(1)}, u32[]{:S(2)}, u32[]{:S(2)}) collective-permute-start(bf16[24,1920]{1,0:T(8,128)(2,1)S(1)} %get-tuple-element.68), channel_id=1, source_target_pairs={{0,24},{1,25},{2,26},{3,27},{4,28},{5,29},{6,30},{7,31},{8,16},{9,... | collective-permute-start | bytes 276488 | tf_op jit(solution)/shard_map/ppermute | solution.py:19
  23.9 0.9 %collective-permute-start.9 = (bf16[24,1920]{1,0:T(8,128)(2,1)S(1)}, bf16[24,1920]{1,0:T(8,128)(2,1)S(1)}, u32[]{:S(2)}, u32[]{:S(2)}) collective-permute-start(bf16[24,1920]{1,0:T(8,128)(2,1)S(1)} %get-tuple-element.69), channel_id=1, source_target_pairs={{0,8},{1,9},{2,10},{3,11},{4,12},{5,13},{6,14},{7,15},{8,0},{9,1},... | collective-permute-start | bytes 276488 | tf_op jit(solution)/shard_map/ppermute | solution.py:19
  24.9 4.2 %shard_map.123 = (bf16[512,3584]{1,0:T(8,128)(2,1)S(1)}, bf16[3584,512]{1,0:T(8,128)(2,1)S(1)}, bf16[512,3584]{1,0:T(8,128)(2,1)S(1)}, bf16[512,3584]{1,0:T(8,128)(2,1)S(1)}) custom-call(bf16[512,3584]{1,0:T(8,128)(2,1)} %down_ref.1, bf16[3,16,512]{2,1,0:T(8,128)(2,1)S(1)} %get-tuple-element.60.narrow_ref, ...), custom_call_target="tpu_custom_call" | custom-call | flops 704643072 | bytes 11412480 | tf_op jit(solution)/shard_map/pallas_call | solution.py:40
  29.1 0.8 %collective-permute-done.6.refs_2_ = bf16[24,1920]{1,0:T(8,128)(2,1)S(1)} collective-permute-done((bf16[24,1920]{1,0:T(8,128)(2,1)S(1)}, bf16[24,1920]{1,0:T(8,128)(2,1)S(1)}, u32[]{:S(2)}, u32[]{:S(2)}) %collective-permute-start.6) | collective-permute-done | bytes 92192 | tf_op jit(solution)/shard_map/ppermute | solution.py:19
  29.9 0.0 collective-permute-done.8.refs_4_
  29.9 0.9 %collective-permute-done.9.refs_5_ = bf16[24,1920]{1,0:T(8,128)(2,1)S(1)} collective-permute-done((bf16[24,1920]{1,0:T(8,128)(2,1)S(1)}, bf16[24,1920]{1,0:T(8,128)(2,1)S(1)}, u32[]{:S(2)}, u32[]{:S(2)}) %collective-permute-start.9) | collective-permute-done | bytes 92192 | tf_op jit(solution)/shard_map/ppermute | solution.py:19
  30.8 0.0 collective-permute-done.5.refs_1_
  30.8 0.0 collective-permute-done.7.refs_3_
  30.8 0.3 shard_map.124
  31.1 0.1 collective-permute-start.10
  31.2 0.5 collective-permute-start.11
  31.7 1.7 %collective-permute-done.10.refs_1_ = bf16[96,3712]{1,0:T(8,128)(2,1)S(1)} collective-permute-done((bf16[96,3712]{1,0:T(8,128)(2,1)S(1)}, bf16[96,3712]{1,0:T(8,128)(2,1)S(1)}, u32[]{:S(2)}, u32[]{:S(2)}) %collective-permute-start.10) | collective-permute-done | bytes 712736 | tf_op jit(solution)/shard_map/ppermute | solution.py:19
  33.4 1.6 %shard_map.125 = (bf16[192,3584]{1,0:T(8,128)(2,1)S(1)}, f32[192,128]{1,0:T(8,128)S(1)}, f32[192,512]{1,0:T(8,128)S(1)}, f32[192,512]{1,0:T(8,128)S(1)}) custom-call(bf16[3584,512]{1,0:T(8,128)(2,1)S(1)} %get-tuple-element.58.gate_ref, bf16[3584,512]{1,0:T(8,128)(2,1)S(1)} %get-tuple-element.59.up_ref, bf16[96,3712]{1,0:T(8,128)(2,1)S(1)} %get-tuple-element.71.refs_0_, ...), custom_call_target="tpu_custom_call" | custom-call | flops 1409286144 | bytes 8765440 | tf_op jit(solution)/shard_map/pallas_call | solution.py:40
  35.0 0.0 collective-permute-done.11.refs_1_
  35.0 2.6 %shard_map.126 = (bf16[192,3584]{1,0:T(8,128)(2,1)S(1)}, bf16[192,512]{1,0:T(8,128)(2,1)S(1)}, bf16[192,512]{1,0:T(8,128)(2,1)S(1)}, bf16[192,512]{1,0:T(8,128)(...) custom-call(bf16[512,3584]{1,0:T(8,128)(2,1)S(1)} %get-tuple-element.73.gate_ref, ...), custom_call_target="tpu_custom_call" | custom-call | flops 2113929216 | bytes 13271040 | tf_op jit(solution)/shard_map/pallas_call | solution.py:40
  37.6 0.2 collective-permute-start.12
  37.8 2.1 %shard_map.127 = (bf16[3584,512]{1,0:T(8,128)(2,1)S(1)}, f32[16,3584]{1,0:T(8,128)S(1)}, bf16[3584,192]{1,0:T(8,128)(2,1)S(1)}) custom-call(bf16[192,3584]{1,0:T(8,128)(2,1)S(1)} %get-tuple-element.72.x_ref, bf16[192,512]{1,0:T(8,128)(2,1)S(1)} %get-tuple-element.79.grad_ref, bf16[3584,512]{1,0:T(8,128)(2,1)S(1)} %get-tuple-element.80.raw_ref, ...), custom_call_target="tpu_custom_call" | custom-call | flops 1409286144 | bytes 5292032 | tf_op jit(solution)/shard_map/pallas_call | solution.py:40
  39.9 0.0 collective-permute-done.12.other_ref
  39.9 0.5 shard_map.128
  40.4 0.6 %collective-permute-start.13 = (bf16[24,3712]{1,0:T(8,128)(2,1)S(1)}, bf16[24,3712]{1,0:T(8,128)(2,1)S(1)}, u32[]{:S(2)}, u32[]{:S(2)}) collective-permute-start(bf16[24,3712]{1,0:T(8,128)(2,1)S(1)} %get-tuple-element.95), channel_id=1, source_target_pairs={{0,2},{1,3},{2,0},{3,1},{4,6},{5,7},{6,4},{7,5},{8,10},{9,11},{10,... | collective-permute-start | bytes 534536 | tf_op jit(solution)/shard_map/ppermute | solution.py:19
  41.0 0.5 collective-permute-start.15
  41.5 1.8 %collective-permute-start.14 = (bf16[24,1024]{1,0:T(8,128)(2,1)S(1)}, bf16[24,1024]{1,0:T(8,128)(2,1)S(1)}, u32[]{:S(2)}, u32[]{:S(2)}) collective-permute-start(bf16[24,1024]{1,0:T(8,128)(2,1)S(1)} %get-tuple-element.96), channel_id=1, source_target_pairs={{0,16},{1,17},{2,18},{3,19},{4,20},{5,21},{6,22},{7,23},{8,24},{9,... | collective-permute-start | bytes 147464 | tf_op jit(solution)/shard_map/ppermute | solution.py:19
  43.3 2.2 %collective-permute-start.16 = (bf16[24,1024]{1,0:T(8,128)(2,1)S(1)}, bf16[24,1024]{1,0:T(8,128)(2,1)S(1)}, u32[]{:S(2)}, u32[]{:S(2)}) collective-permute-start(bf16[24,1024]{1,0:T(8,128)(2,1)S(1)} %get-tuple-element.98), channel_id=1, source_target_pairs={{0,24},{1,25},{2,26},{3,27},{4,28},{5,29},{6,30},{7,31},{8,16},{9,... | collective-permute-start | bytes 147464 | tf_op jit(solution)/shard_map/ppermute | solution.py:19
  45.5 0.0 collective-permute-start.17
  45.5 3.6 %shard_map.129 = (bf16[3584,512]{1,0:T(8,128)(2,1)S(1)}, bf16[512,3584]{1,0:T(8,128)(2,1)S(1)}, f32[48,1792]{1,0:T(8,128)S(1)}, bf16[48,1792]{1,0:T(8,128)(2,1)S(1)}) custom-call(bf16[3584,192]{1,0:T(8,128)(2,1)S(1)} %get-tuple-element.81.x_ref, bf16[192,512]{1,0:T(8,128)(2,1)S(1)} %get-tuple-element.82.grad_ref, ...), custom_call_target="tpu_custom_call" | custom-call | flops 2818572288 | bytes 10942464 | tf_op jit(solution)/shard_map/pallas_call | solution.py:40
  49.0 0.0 collective-permute-done.14.refs_4_
  49.0 0.3 collective-permute-done.16.refs_6_
  49.3 0.5 collective-permute-done.17.refs_7_
  49.8 0.0 collective-permute-done.13.refs_3_
  49.8 0.0 collective-permute-done.15.refs_5_
  49.8 0.3 shard_map.130
  50.1 0.1 collective-permute-start.22
  50.2 1.6 %collective-permute-start.18 = (bf16[8,3712]{1,0:T(8,128)(2,1)S(1)}, bf16[8,3712]{1,0:T(8,128)(2,1)S(1)}, u32[]{:S(2)}, u32[]{:S(2)}) collective-permute-start(bf16[8,3712]{1,0:T(8,128)(2,1)S(1)} %get-tuple-element.101), channel_id=1, source_target_pairs={{0,16},{1,17},{2,18},{3,19},{4,20},{5,21},{6,22},{7,23},{8,24},{9,... | collective-permute-start | bytes 178184 | tf_op jit(solution)/shard_map/ppermute | solution.py:19
  51.7 2.2 %collective-permute-start.19 = (bf16[8,3712]{1,0:T(8,128)(2,1)S(1)}, bf16[8,3712]{1,0:T(8,128)(2,1)S(1)}, u32[]{:S(2)}, u32[]{:S(2)}) collective-permute-start(bf16[8,3712]{1,0:T(8,128)(2,1)S(1)} %get-tuple-element.102), channel_id=1, source_target_pairs={{0,24},{1,25},{2,26},{3,27},{4,28},{5,29},{6,30},{7,31},{8,16},{9,... | collective-permute-start | bytes 178184 | tf_op jit(solution)/shard_map/ppermute | solution.py:19
  53.9 2.5 %collective-permute-start.20 = (bf16[8,3712]{1,0:T(8,128)(2,1)S(1)}, bf16[8,3712]{1,0:T(8,128)(2,1)S(1)}, u32[]{:S(2)}, u32[]{:S(2)}) collective-permute-start(bf16[8,3712]{1,0:T(8,128)(2,1)S(1)} %get-tuple-element.103.after_ref), channel_id=1, source_target_pairs={{0,6},{1,7},{2,4},{3,5},{4,2},{5,3},{6,0},{7,1},{8,14},{9,15},{10,... | collective-permute-start | bytes 178184 | tf_op jit(solution)/shard_map/ppermute | solution.py:19
  56.4 0.0 collective-permute-start.21
  56.4 0.0 copy-start
  56.4 2.6 %shard_map.132 = f32[48,512]{1,0:T(8,128)} custom-call(bf16[3584,512]{1,0:T(8,128)(2,1)S(1)} %get-tuple-element.108.masked_gate, bf16[3584,512]{1,0:T(8,128)(2,1)S(1)} %get-tuple-element.109.masked_up, bf16[512,3584]{1,0:T(8,128)(2,1)S(1)} %get-tuple-element.110.masked_down, bf16[3,16,3584]{2,1,0:T(8,128)(2,1)S(1)} %get-tuple-element.61.after_ref.wide_ref, ...), custom_call_target="tpu_custom_call" | custom-call | flops 1409286144 | bytes 11413504 | tf_op jit(solution)/shard_map/pallas_call | solution.py:40
  59.0 0.0 collective-permute-done.18.refs_0_
  59.0 0.0 collective-permute-done.19.refs_1_
  59.0 0.0 collective-permute-done.20.refs_2_
  59.0 1.5 %collective-permute-done.21.refs_3_ = bf16[8,3712]{1,0:T(8,128)(2,1)S(1)} collective-permute-done((bf16[8,3712]{1,0:T(8,128)(2,1)S(1)}, bf16[8,3712]{1,0:T(8,128)(2,1)S(1)}, u32[]{:S(2)}, u32[]{:S(2)}) %collective-permute-start.21) | collective-permute-done | bytes 59424 | tf_op jit(solution)/shard_map/ppermute | solution.py:19
  60.6 0.0 collective-permute-done.22.refs_4_
  60.6 0.0 copy-done
  60.6 0.9 %shard_map.131 = (bf16[8,3584]{1,0:T(8,128)(2,1)}, f32[8,8]{1,0:T(8,128)}, f32[48,1792]{1,0:T(8,128)}) custom-call(s32[8,8]{1,0:T(8,128)S(1)} %copy-done, f32[48,1792]{1,0:T(8,128)S(1)} %get-tuple-element.91.keep_ref, f32[8,3712]{1,0:T(8,128)S(1)} %get-tuple-element.100.own_ref, bf16[8,3712]{1,0:T(8,128)(2,1)S(1)} %collective-permute-done.18.refs_0_, ...), custom_call_target="tpu_custom_call" | custom-call | bytes 872704 | tf_op jit(solution)/shard_map/pallas_call | solution.py:40
Async XLA Ops:
  0.6 9.4 %collective-permute-start = (bf16[3,16,1792]{2,1,0:T(8,128)(2,1)}, bf16[3,16,1792]{2,1,0:T(8,128)(2,1)S(1)}, u32[]{:S(2)}, u32[]{:S(2)}) collective-permute-start(bf16[3,16,1792]{2,1,0:T(8,128)(2,1)} %mine_hbm.1), channel_id=1, source_target_pairs={{0,1},{1,0},{2,3},{3,2},{4,5},{5,4},{6,7},{7,6},{8,9},{9,8},{10,11... | collective-permute-start | bytes 516104 | tf_op jit(solution)/shard_map/ppermute | solution.py:19
  2.1 13.6 %collective-permute-start.1 = (bf16[8,7296]{1,0:T(8,128)(2,1)S(1)}, bf16[8,7296]{1,0:T(8,128)(2,1)S(1)}, u32[]{:S(2)}, u32[]{:S(2)}) collective-permute-start(bf16[8,7296]{1,0:T(8,128)(2,1)S(1)} %shard_map.121.refs_3_), channel_id=1, source_target_pairs={{0,24},{1,25},{2,26},{3,27},{4,28},{5,29},{6,30},{7,31},{8,16},{9,... | collective-permute-start | bytes 350216 | tf_op jit(solution)/shard_map/ppermute | solution.py:19
  6.8 10.5 %collective-permute-start.2 = (bf16[8,7296]{1,0:T(8,128)(2,1)S(1)}, bf16[8,7296]{1,0:T(8,128)(2,1)S(1)}, u32[]{:S(2)}, u32[]{:S(2)}) collective-permute-start(bf16[8,7296]{1,0:T(8,128)(2,1)S(1)} %shard_map.121.refs_3_), channel_id=1, source_target_pairs={{0,16},{1,17},{2,18},{3,19},{4,20},{5,21},{6,22},{7,23},{8,24},{9,... | collective-permute-start | bytes 350216 | tf_op jit(solution)/shard_map/ppermute | solution.py:19
  6.8 10.5 %collective-permute-start.3 = (bf16[8,7296]{1,0:T(8,128)(2,1)S(1)}, bf16[8,7296]{1,0:T(8,128)(2,1)S(1)}, u32[]{:S(2)}, u32[]{:S(2)}) collective-permute-start(bf16[8,7296]{1,0:T(8,128)(2,1)S(1)} %shard_map.121.refs_3_), channel_id=1, source_target_pairs={{0,8},{1,9},{2,10},{3,11},{4,12},{5,13},{6,14},{7,15},{8,0},{9,1},... | collective-permute-start | bytes 350216 | tf_op jit(solution)/shard_map/ppermute | solution.py:19
  7.4 9.9 %collective-permute-start.4 = (bf16[8,7296]{1,0:T(8,128)(2,1)S(1)}, bf16[8,7296]{1,0:T(8,128)(2,1)S(1)}, u32[]{:S(2)}, u32[]{:S(2)}) collective-permute-start(bf16[8,7296]{1,0:T(8,128)(2,1)S(1)} %shard_map.121.refs_3_), channel_id=1, source_target_pairs={{0,6},{1,7},{2,4},{3,5},{4,2},{5,3},{6,0},{7,1},{8,14},{9,15},{10,... | collective-permute-start | bytes 350216 | tf_op jit(solution)/shard_map/ppermute | solution.py:19
  18.3 12.5 %collective-permute-start.5 = (bf16[24,7296]{1,0:T(8,128)(2,1)S(1)}, bf16[24,7296]{1,0:T(8,128)(2,1)S(1)}, u32[]{:S(2)}, u32[]{:S(2)}) collective-permute-start(bf16[24,7296]{1,0:T(8,128)(2,1)S(1)} %get-tuple-element.65), channel_id=1, source_target_pairs={{0,2},{1,3},{2,0},{3,1},{4,6},{5,7},{6,4},{7,5},{8,10},{9,11},{10,... | collective-permute-start | bytes 1050632 | tf_op jit(solution)/shard_map/ppermute | solution.py:19
  19.9 10.9 %collective-permute-start.7 = (bf16[24,7296]{1,0:T(8,128)(2,1)S(1)}, bf16[24,7296]{1,0:T(8,128)(2,1)S(1)}, u32[]{:S(2)}, u32[]{:S(2)}) collective-permute-start(bf16[24,7296]{1,0:T(8,128)(2,1)S(1)} %get-tuple-element.67), channel_id=1, source_target_pairs={{0,4},{1,5},{2,6},{3,7},{4,0},{5,1},{6,2},{7,3},{8,12},{9,13},{10,... | collective-permute-start | bytes 1050632 | tf_op jit(solution)/shard_map/ppermute | solution.py:19
  21.4 8.5 %collective-permute-start.6 = (bf16[24,1920]{1,0:T(8,128)(2,1)S(1)}, bf16[24,1920]{1,0:T(8,128)(2,1)S(1)}, u32[]{:S(2)}, u32[]{:S(2)}) collective-permute-start(bf16[24,1920]{1,0:T(8,128)(2,1)S(1)} %get-tuple-element.66), channel_id=1, source_target_pairs={{0,16},{1,17},{2,18},{3,19},{4,20},{5,21},{6,22},{7,23},{8,24},{9,... | collective-permute-start | bytes 276488 | tf_op jit(solution)/shard_map/ppermute | solution.py:19
  21.4 8.5 %collective-permute-start.8 = (bf16[24,1920]{1,0:T(8,128)(2,1)S(1)}, bf16[24,1920]{1,0:T(8,128)(2,1)S(1)}, u32[]{:S(2)}, u32[]{:S(2)}) collective-permute-start(bf16[24,1920]{1,0:T(8,128)(2,1)S(1)} %get-tuple-element.68), channel_id=1, source_target_pairs={{0,24},{1,25},{2,26},{3,27},{4,28},{5,29},{6,30},{7,31},{8,16},{9,... | collective-permute-start | bytes 276488 | tf_op jit(solution)/shard_map/ppermute | solution.py:19
  23.9 6.9 %collective-permute-start.9 = (bf16[24,1920]{1,0:T(8,128)(2,1)S(1)}, bf16[24,1920]{1,0:T(8,128)(2,1)S(1)}, u32[]{:S(2)}, u32[]{:S(2)}) collective-permute-start(bf16[24,1920]{1,0:T(8,128)(2,1)S(1)} %get-tuple-element.69), channel_id=1, source_target_pairs={{0,8},{1,9},{2,10},{3,11},{4,12},{5,13},{6,14},{7,15},{8,0},{9,1},... | collective-permute-start | bytes 276488 | tf_op jit(solution)/shard_map/ppermute | solution.py:19
  31.1 2.2 %collective-permute-start.10 = (bf16[96,3712]{1,0:T(8,128)(2,1)S(1)}, bf16[96,3712]{1,0:T(8,128)(2,1)S(1)}, u32[]{:S(2)}, u32[]{:S(2)}) collective-permute-start(bf16[96,3712]{1,0:T(8,128)(2,1)S(1)} %get-tuple-element.71.refs_0_), channel_id=1, source_target_pairs={{0,1},{1,0},{2,3},{3,2},{4,5},{5,4},{6,7},{7,6},{8,9},{9,8},{10,11... | collective-permute-start | bytes 2138120 | tf_op jit(solution)/shard_map/ppermute | solution.py:19
  31.2 3.8 %collective-permute-start.11 = (bf16[96,3584]{1,0:T(8,128)(2,1)S(1)}, bf16[96,3584]{1,0:T(8,128)(2,1)S(1)}, u32[]{:S(2)}, u32[]{:S(2)}) collective-permute-start(bf16[96,3584]{1,0:T(8,128)(2,1)S(1)} %get-tuple-element.78.refs_0_), channel_id=1, source_target_pairs={{0,1},{1,0},{2,3},{3,2},{4,5},{5,4},{6,7},{7,6},{8,9},{9,8},{10,11... | collective-permute-start | bytes 2064392 | tf_op jit(solution)/shard_map/ppermute | solution.py:19
  37.6 2.2 %collective-permute-start.12 = (bf16[96,3712]{1,0:T(8,128)(2,1)S(1)}, bf16[96,3712]{1,0:T(8,128)(2,1)S(1)}, u32[]{:S(2)}, u32[]{:S(2)}) collective-permute-start(bf16[96,3712]{1,0:T(8,128)(2,1)S(1)} %get-tuple-element.88), channel_id=1, source_target_pairs={{0,1},{1,0},{2,3},{3,2},{4,5},{5,4},{6,7},{7,6},{8,9},{9,8},{10,11... | collective-permute-start | bytes 2138120 | tf_op jit(solution)/shard_map/ppermute | solution.py:19
  40.4 9.4 %collective-permute-start.13 = (bf16[24,3712]{1,0:T(8,128)(2,1)S(1)}, bf16[24,3712]{1,0:T(8,128)(2,1)S(1)}, u32[]{:S(2)}, u32[]{:S(2)}) collective-permute-start(bf16[24,3712]{1,0:T(8,128)(2,1)S(1)} %get-tuple-element.95), channel_id=1, source_target_pairs={{0,2},{1,3},{2,0},{3,1},{4,6},{5,7},{6,4},{7,5},{8,10},{9,11},{10,... | collective-permute-start | bytes 534536 | tf_op jit(solution)/shard_map/ppermute | solution.py:19
  41.0 8.8 %collective-permute-start.15 = (bf16[24,3712]{1,0:T(8,128)(2,1)S(1)}, bf16[24,3712]{1,0:T(8,128)(2,1)S(1)}, u32[]{:S(2)}, u32[]{:S(2)}) collective-permute-start(bf16[24,3712]{1,0:T(8,128)(2,1)S(1)} %get-tuple-element.97), channel_id=1, source_target_pairs={{0,4},{1,5},{2,6},{3,7},{4,0},{5,1},{6,2},{7,3},{8,12},{9,13},{10,... | collective-permute-start | bytes 534536 | tf_op jit(solution)/shard_map/ppermute | solution.py:19
  41.5 7.5 %collective-permute-start.14 = (bf16[24,1024]{1,0:T(8,128)(2,1)S(1)}, bf16[24,1024]{1,0:T(8,128)(2,1)S(1)}, u32[]{:S(2)}, u32[]{:S(2)}) collective-permute-start(bf16[24,1024]{1,0:T(8,128)(2,1)S(1)} %get-tuple-element.96), channel_id=1, source_target_pairs={{0,16},{1,17},{2,18},{3,19},{4,20},{5,21},{6,22},{7,23},{8,24},{9,... | collective-permute-start | bytes 147464 | tf_op jit(solution)/shard_map/ppermute | solution.py:19
  43.3 6.0 %collective-permute-start.16 = (bf16[24,1024]{1,0:T(8,128)(2,1)S(1)}, bf16[24,1024]{1,0:T(8,128)(2,1)S(1)}, u32[]{:S(2)}, u32[]{:S(2)}) collective-permute-start(bf16[24,1024]{1,0:T(8,128)(2,1)S(1)} %get-tuple-element.98), channel_id=1, source_target_pairs={{0,24},{1,25},{2,26},{3,27},{4,28},{5,29},{6,30},{7,31},{8,16},{9,... | collective-permute-start | bytes 147464 | tf_op jit(solution)/shard_map/ppermute | solution.py:19
  45.5 4.3 %collective-permute-start.17 = (bf16[24,1024]{1,0:T(8,128)(2,1)S(1)}, bf16[24,1024]{1,0:T(8,128)(2,1)S(1)}, u32[]{:S(2)}, u32[]{:S(2)}) collective-permute-start(bf16[24,1024]{1,0:T(8,128)(2,1)S(1)} %get-tuple-element.99), channel_id=1, source_target_pairs={{0,8},{1,9},{2,10},{3,11},{4,12},{5,13},{6,14},{7,15},{8,0},{9,1},... | collective-permute-start | bytes 147464 | tf_op jit(solution)/shard_map/ppermute | solution.py:19
  50.1 10.5 %collective-permute-start.22 = (bf16[48,1792]{1,0:T(8,128)(2,1)S(1)}, bf16[48,1792]{1,0:T(8,128)(2,1)S(1)}, u32[]{:S(2)}, u32[]{:S(2)}) collective-permute-start(bf16[48,1792]{1,0:T(8,128)(2,1)S(1)} %get-tuple-element.105), channel_id=1, source_target_pairs={{0,1},{1,0},{2,3},{3,2},{4,5},{5,4},{6,7},{7,6},{8,9},{9,8},{10,11... | collective-permute-start | bytes 516104 | tf_op jit(solution)/shard_map/ppermute | solution.py:19
  50.2 8.8 %collective-permute-start.18 = (bf16[8,3712]{1,0:T(8,128)(2,1)S(1)}, bf16[8,3712]{1,0:T(8,128)(2,1)S(1)}, u32[]{:S(2)}, u32[]{:S(2)}) collective-permute-start(bf16[8,3712]{1,0:T(8,128)(2,1)S(1)} %get-tuple-element.101), channel_id=1, source_target_pairs={{0,16},{1,17},{2,18},{3,19},{4,20},{5,21},{6,22},{7,23},{8,24},{9,... | collective-permute-start | bytes 178184 | tf_op jit(solution)/shard_map/ppermute | solution.py:19
  51.7 7.3 %collective-permute-start.19 = (bf16[8,3712]{1,0:T(8,128)(2,1)S(1)}, bf16[8,3712]{1,0:T(8,128)(2,1)S(1)}, u32[]{:S(2)}, u32[]{:S(2)}) collective-permute-start(bf16[8,3712]{1,0:T(8,128)(2,1)S(1)} %get-tuple-element.102), channel_id=1, source_target_pairs={{0,24},{1,25},{2,26},{3,27},{4,28},{5,29},{6,30},{7,31},{8,16},{9,... | collective-permute-start | bytes 178184 | tf_op jit(solution)/shard_map/ppermute | solution.py:19
  53.9 5.1 %collective-permute-start.20 = (bf16[8,3712]{1,0:T(8,128)(2,1)S(1)}, bf16[8,3712]{1,0:T(8,128)(2,1)S(1)}, u32[]{:S(2)}, u32[]{:S(2)}) collective-permute-start(bf16[8,3712]{1,0:T(8,128)(2,1)S(1)} %get-tuple-element.103.after_ref), channel_id=1, source_target_pairs={{0,6},{1,7},{2,4},{3,5},{4,2},{5,3},{6,0},{7,1},{8,14},{9,15},{10,... | collective-permute-start | bytes 178184 | tf_op jit(solution)/shard_map/ppermute | solution.py:19
  56.4 4.2 %collective-permute-start.21 = (bf16[8,3712]{1,0:T(8,128)(2,1)S(1)}, bf16[8,3712]{1,0:T(8,128)(2,1)S(1)}, u32[]{:S(2)}, u32[]{:S(2)}) collective-permute-start(bf16[8,3712]{1,0:T(8,128)(2,1)S(1)} %get-tuple-element.104), channel_id=1, source_target_pairs={{0,8},{1,9},{2,10},{3,11},{4,12},{5,13},{6,14},{7,15},{8,0},{9,1},... | collective-permute-start | bytes 178184 | tf_op jit(solution)/shard_map/ppermute | solution.py:19
  56.4 4.2 %copy-start = (s32[8,8]{1,0:T(8,128)S(1)}, s32[8,8]{1,0:T(8,128)}, u32[]{:S(2)}) copy-start(s32[8,8]{1,0:T(8,128)} %ids_ref.3) | copy-start | bytes 772
